TPU v7x, 32 devices: a whole 2x2x4 slice. The times are simulated.
32 devices in a mesh: fsdp: 16 (over z, x, core), seq: 2 (over y).
Axes of the slice: x: 2, y: 2, z: 4, core: 2. Of those that a mesh axis runs over, the one named last changes fastest.
Arguments:
- tokens: bfloat16 [32768, 512], P(('fsdp', 'seq')), may hold values from -6 to 6
- w_query: bfloat16 [512, 512], P('fsdp'), may hold values from -0.5 to 0.5
- w_key: bfloat16 [512, 512], P('fsdp'), may hold values from -0.25 to 0.25
- w_value: bfloat16 [512, 512], P('fsdp'), may hold values from -0.25 to 0.25
- w_control: bfloat16 [512, 512], P('fsdp'), may hold values from -0.5 to 0.5
- w_out: bfloat16 [512, 512], P('fsdp'), may hold values from -0.75 to 0.75
- w_up: bfloat16 [512, 2048], P('fsdp'), may hold values from -0.25 to 0.25
- w_down: bfloat16 [2048, 512], P('fsdp'), may hold values from -0.1875 to 0.1875
- gain_attn: bfloat16 [512], P('fsdp'), may hold values from 0.5 to 1.5
- gain_ffn: bfloat16 [512], P('fsdp'), may hold values from 0.5 to 1.5
- bias_up: bfloat16 [2048], P('fsdp'), may hold values from -3 to 3
- bias_down: bfloat16 [512], P('fsdp'), may hold values from -3 to 3
- cotangent: bfloat16 [32768, 512], P(('fsdp', 'seq')), may hold values from -6 to 6
Outputs:
- layer_out: bfloat16 [32768, 512], P(('fsdp', 'seq'))
- grad_tokens: float32 [32768, 512], P(('fsdp', 'seq'))
- grad_w_query: float32 [512, 512], P('fsdp')
- grad_w_key: float32 [512, 512], P('fsdp')
- grad_w_value: float32 [512, 512], P('fsdp')
- grad_w_control: float32 [512, 512], P('fsdp')
- grad_w_out: float32 [512, 512], P('fsdp')
- grad_w_up: float32 [512, 2048], P('fsdp')
- grad_w_down: float32 [2048, 512], P('fsdp')
- grad_gain_attn: float32 [512], P('fsdp')
- grad_gain_ffn: float32 [512], P('fsdp')
- grad_bias_up: float32 [2048], P('fsdp')
- grad_bias_down: float32 [512], P('fsdp')
All inputs are finite; a program needn't handle non-finite values.
Results may differ from a plain program's by a relative error of at most 0.02.
The roundings to bfloat16 on the way count: a program that leaves them out, or rounds other values in their place, can miss the bound.
Values may be sent and summed in bfloat16 or wider, within the bound.
No kernel may reach another device: no remote copies, remote signals or barrier semaphores. Data moves between devices by JAX's collectives and lax.ppermute only.
A program may use at most 128 MiB of HBM per device.

v0:
```python
from functools import partial

import jax
import jax.numpy as jnp
from jax import lax
from jax.sharding import PartitionSpec as P

H = 8
HEAD = 64
SLOTS = 64


exact_precision = lax.Precision.HIGHEST


def normalize(source):
    average = jnp.mean(source, axis=-1, keepdims=True)
    centred = source - average
    spread = jnp.mean(centred * centred, axis=-1, keepdims=True)
    factor = lax.rsqrt(spread + 1e-05)
    return (centred * factor, factor)


def norm_back(grad_normed, normed, factor):
    first_mean = jnp.mean(grad_normed, axis=-1, keepdims=True)
    second_mean = jnp.mean(grad_normed * normed, axis=-1, keepdims=True)
    return factor * (grad_normed - first_mean - normed * second_mean)


def over_rows(first_op, second_op):
    return lax.dot_general(
        first_op, second_op, (((0,), (0,)), ((), ())), preferred_element_type=jnp.float32
    )


def by_columns(first_op, second_op):
    return lax.dot_general(
        first_op, second_op, (((1,), (1,)), ((), ())), preferred_element_type=jnp.float32
    )


def joined_weights(full_query, full_key, full_value, full_control):
    width = full_query.shape[0]
    return jnp.concatenate(
        [
            full_query.reshape(width, H, HEAD),
            full_key.reshape(width, H, HEAD),
            full_value.reshape(width, H, HEAD),
            full_control.reshape(width, H, SLOTS),
        ],
        axis=2,
    ).reshape(width, H * (3 * HEAD + SLOTS))


def mix_block(rounded_inputs, carry, block):
    memory_slot_keys, memory_slot_values, totals = carry
    block_rows = block.shape[0]
    query_segment = block[:, :, 0:HEAD]
    key_segment = block[:, :, HEAD : 2 * HEAD]
    value_segment = block[:, :, 2 * HEAD : 3 * HEAD]
    stored_entries = jnp.exp(block[:, :, 3 * HEAD : 3 * HEAD + SLOTS])
    places = jnp.arange(block_rows)
    lower_mask = (places[:, None] >= places[None, :]).astype(jnp.float32)
    if rounded_inputs:
        pair_scores = (
            jnp.einsum(
                "thd,ihd->hti",
                query_segment.astype(jnp.bfloat16),
                key_segment.astype(jnp.bfloat16),
                preferred_element_type=jnp.float32,
            )
            * lower_mask[None]
        )
    else:
        pair_scores = (
            jnp.einsum("thd,ihd->hti", query_segment, key_segment, precision=exact_precision)
            * lower_mask[None]
        )
    running = (
        jnp.einsum("ti,ihm->thm", lower_mask, stored_entries, precision=exact_precision)
        + totals[None]
    )
    fraction_top = jnp.einsum(
        "hti,ihm->thm", pair_scores, stored_entries, precision=exact_precision
    )
    fraction_top = fraction_top + jnp.einsum(
        "aek,exk->aex", query_segment, memory_slot_keys, precision=exact_precision
    )
    slot_score = fraction_top * HEAD ** (-0.5) / running
    read_weight = jax.nn.softmax(slot_score, axis=-1)
    weight_scaled_rows = read_weight / running
    recall = (
        jnp.einsum("thm,ihm->hti", weight_scaled_rows, stored_entries, precision=exact_precision)
        * lower_mask[None]
    )
    output_segment = jnp.einsum("hti,ihd->thd", recall, value_segment, precision=exact_precision)
    output_segment = output_segment + jnp.einsum(
        "jkx,kxo->jko", weight_scaled_rows, memory_slot_values, precision=exact_precision
    )
    memory_slot_keys = memory_slot_keys + jnp.einsum(
        "uwz,uwq->wzq", stored_entries, key_segment, precision=exact_precision
    )
    memory_slot_values = memory_slot_values + jnp.einsum(
        "uwz,uwq->wzq", stored_entries, value_segment, precision=exact_precision
    )
    totals = totals + jnp.sum(stored_entries, axis=0)
    return ((memory_slot_keys, memory_slot_values, totals), output_segment)


def run_mixer(packed, rounded_inputs):
    length, heads, width = packed.shape
    block_rows = min(512, length)
    blocks = packed.reshape(length // block_rows, block_rows, heads, width)
    start = (
        jnp.zeros((heads, SLOTS, HEAD), jnp.float32),
        jnp.zeros((heads, SLOTS, HEAD), jnp.float32),
        jnp.zeros((heads, SLOTS), jnp.float32),
    )
    _, outputs = lax.scan(jax.checkpoint(partial(mix_block, rounded_inputs)), start, blocks)
    return outputs.reshape(length, heads, HEAD)


def mixer(packed):
    return run_mixer(packed, False)


def on_device(
    tokens,
    w_query,
    w_key,
    w_value,
    w_control,
    w_out,
    w_up,
    w_down,
    gain_attn,
    gain_ffn,
    bias_up,
    bias_down,
    cotangent,
):
    packed_width = 3 * HEAD + SLOTS
    full_query, full_key, full_value, full_control, full_out, full_gain_attn = (
        lax.all_gather(w_query, "fsdp", axis=0, tiled=True),
        lax.all_gather(w_key, "fsdp", axis=0, tiled=True),
        lax.all_gather(w_value, "fsdp", axis=0, tiled=True),
        lax.all_gather(w_control, "fsdp", axis=0, tiled=True),
        lax.all_gather(w_out, "fsdp", axis=0, tiled=True),
        lax.all_gather(gain_attn, "fsdp", axis=0, tiled=True),
    )
    packed_weights = joined_weights(full_query, full_key, full_value, full_control)
    source = tokens.astype(jnp.float32)
    normed_a, factor_a = normalize(source)
    attn_input = (normed_a * full_gain_attn.astype(jnp.float32)).astype(jnp.bfloat16)
    packed = jnp.dot(attn_input, packed_weights, preferred_element_type=jnp.float32).astype(
        jnp.bfloat16
    )
    by_head = lax.all_to_all(packed, "seq", split_axis=1, concat_axis=0, tiled=True)
    length = by_head.shape[0]
    local_heads = by_head.shape[1] // packed_width
    head_input = by_head.reshape(length, local_heads, packed_width).astype(jnp.float32)
    mixed_heads = (
        run_mixer(head_input, True).astype(jnp.bfloat16).reshape(length, local_heads * HEAD)
    )
    mixed = lax.all_to_all(mixed_heads, "seq", split_axis=0, concat_axis=1, tiled=True)
    branch = jnp.dot(mixed, full_out, preferred_element_type=jnp.float32)
    resid = source + branch
    full_up, full_down, full_gain_ffn, full_bias_up, full_bias_down = (
        lax.all_gather(w_up, "fsdp", axis=0, tiled=True),
        lax.all_gather(w_down, "fsdp", axis=0, tiled=True),
        lax.all_gather(gain_ffn, "fsdp", axis=0, tiled=True),
        lax.all_gather(bias_up, "fsdp", axis=0, tiled=True),
        lax.all_gather(bias_down, "fsdp", axis=0, tiled=True),
    )
    normed_f, factor_f = normalize(resid)
    ffn_input = (normed_f * full_gain_ffn.astype(jnp.float32)).astype(jnp.bfloat16)
    pre_act = jnp.dot(ffn_input, full_up, preferred_element_type=jnp.float32) + full_bias_up.astype(
        jnp.float32
    )
    hidden = jax.nn.silu(pre_act).astype(jnp.bfloat16)
    ffn_out = jnp.dot(
        hidden, full_down, preferred_element_type=jnp.float32
    ) + full_bias_down.astype(jnp.float32)
    layer_out = (resid + ffn_out).astype(jnp.bfloat16)
    back_up, back_down, back_gain_ffn, unused_up, unused_down = (
        lax.all_gather(w_up, "fsdp", axis=0, tiled=True),
        lax.all_gather(w_down, "fsdp", axis=0, tiled=True),
        lax.all_gather(gain_ffn, "fsdp", axis=0, tiled=True),
        lax.all_gather(bias_up, "fsdp", axis=0, tiled=True),
        lax.all_gather(bias_down, "fsdp", axis=0, tiled=True),
    )
    grad_bias_down = jnp.sum(cotangent.astype(jnp.float32), axis=0)
    grad_w_down = over_rows(hidden, cotangent)
    grad_hidden = by_columns(cotangent, back_down)
    sigmoid_act = jax.nn.sigmoid(pre_act)
    slope = sigmoid_act * (1.0 + pre_act * (1.0 - sigmoid_act))
    grad_pre = (grad_hidden * slope).astype(jnp.bfloat16)
    grad_bias_up = jnp.sum(grad_pre.astype(jnp.float32), axis=0)
    grad_w_up = over_rows(ffn_input, grad_pre)
    grad_ffn_in = by_columns(grad_pre, back_up)
    grad_gain_ffn = jnp.sum(grad_ffn_in * normed_f, axis=0)
    grad_resid = cotangent.astype(jnp.float32) + norm_back(
        grad_ffn_in * back_gain_ffn.astype(jnp.float32), normed_f, factor_f
    )
    share_up, share_down, share_gain_ffn, share_bias_up, share_bias_down = (
        lax.psum_scatter(
            grad_w_up.astype(jnp.bfloat16), "fsdp", scatter_dimension=0, tiled=True
        ).astype(jnp.float32),
        lax.psum_scatter(
            grad_w_down.astype(jnp.bfloat16), "fsdp", scatter_dimension=0, tiled=True
        ).astype(jnp.float32),
        lax.psum_scatter(
            grad_gain_ffn.astype(jnp.bfloat16), "fsdp", scatter_dimension=0, tiled=True
        ).astype(jnp.float32),
        lax.psum_scatter(
            grad_bias_up.astype(jnp.bfloat16), "fsdp", scatter_dimension=0, tiled=True
        ).astype(jnp.float32),
        lax.psum_scatter(
            grad_bias_down.astype(jnp.bfloat16), "fsdp", scatter_dimension=0, tiled=True
        ).astype(jnp.float32),
    )
    share_up, share_down, share_gain_ffn, share_bias_up, share_bias_down = lax.psum(
        (share_up, share_down, share_gain_ffn, share_bias_up, share_bias_down), "seq"
    )
    back_query, back_key, back_value, back_control, back_out, back_gain_attn = (
        lax.all_gather(w_query, "fsdp", axis=0, tiled=True),
        lax.all_gather(w_key, "fsdp", axis=0, tiled=True),
        lax.all_gather(w_value, "fsdp", axis=0, tiled=True),
        lax.all_gather(w_control, "fsdp", axis=0, tiled=True),
        lax.all_gather(w_out, "fsdp", axis=0, tiled=True),
        lax.all_gather(gain_attn, "fsdp", axis=0, tiled=True),
    )
    back_packed = joined_weights(back_query, back_key, back_value, back_control)
    grad_branch = grad_resid.astype(jnp.bfloat16)
    grad_w_out = over_rows(mixed, grad_branch)
    grad_mixed = by_columns(grad_branch, back_out).astype(jnp.bfloat16)
    grad_heads = lax.all_to_all(grad_mixed, "seq", split_axis=1, concat_axis=0, tiled=True)
    unused_out, pull = jax.vjp(mixer, head_input)
    (grad_head_input,) = pull(grad_heads.reshape(length, local_heads, HEAD).astype(jnp.float32))
    grad_head_input = grad_head_input.astype(jnp.bfloat16).reshape(
        length, local_heads * packed_width
    )
    grad_packed = lax.all_to_all(grad_head_input, "seq", split_axis=0, concat_axis=1, tiled=True)
    grad_joined = over_rows(attn_input, grad_packed).reshape(attn_input.shape[1], H, packed_width)
    width = attn_input.shape[1]
    grad_w_query = grad_joined[:, :, 0:HEAD].reshape(width, H * HEAD)
    grad_w_key = grad_joined[:, :, HEAD : 2 * HEAD].reshape(width, H * HEAD)
    grad_w_value = grad_joined[:, :, 2 * HEAD : 3 * HEAD].reshape(width, H * HEAD)
    grad_w_control = grad_joined[:, :, 3 * HEAD : packed_width].reshape(width, H * SLOTS)
    grad_attn_in = by_columns(grad_packed, back_packed)
    grad_gain_attn = jnp.sum(grad_attn_in * normed_a, axis=0)
    grad_tokens = grad_resid + norm_back(
        grad_attn_in * back_gain_attn.astype(jnp.float32), normed_a, factor_a
    )
    share_query, share_key, share_value, share_control, share_out, share_gain_attn = (
        lax.psum_scatter(
            grad_w_query.astype(jnp.bfloat16), "fsdp", scatter_dimension=0, tiled=True
        ).astype(jnp.float32),
        lax.psum_scatter(
            grad_w_key.astype(jnp.bfloat16), "fsdp", scatter_dimension=0, tiled=True
        ).astype(jnp.float32),
        lax.psum_scatter(
            grad_w_value.astype(jnp.bfloat16), "fsdp", scatter_dimension=0, tiled=True
        ).astype(jnp.float32),
        lax.psum_scatter(
            grad_w_control.astype(jnp.bfloat16), "fsdp", scatter_dimension=0, tiled=True
        ).astype(jnp.float32),
        lax.psum_scatter(
            grad_w_out.astype(jnp.bfloat16), "fsdp", scatter_dimension=0, tiled=True
        ).astype(jnp.float32),
        lax.psum_scatter(
            grad_gain_attn.astype(jnp.bfloat16), "fsdp", scatter_dimension=0, tiled=True
        ).astype(jnp.float32),
    )
    share_query, share_key, share_value, share_control, share_out, share_gain_attn = (
        lax.psum(share_query.astype(jnp.bfloat16), "seq").astype(jnp.float32),
        lax.psum(share_key.astype(jnp.bfloat16), "seq").astype(jnp.float32),
        lax.psum(share_value.astype(jnp.bfloat16), "seq").astype(jnp.float32),
        lax.psum(share_control.astype(jnp.bfloat16), "seq").astype(jnp.float32),
        lax.psum(share_out.astype(jnp.bfloat16), "seq").astype(jnp.float32),
        lax.psum(share_gain_attn.astype(jnp.bfloat16), "seq").astype(jnp.float32),
    )
    return (
        layer_out,
        grad_tokens,
        share_query,
        share_key,
        share_value,
        share_control,
        share_out,
        share_up,
        share_down,
        share_gain_attn,
        share_gain_ffn,
        share_bias_up,
        share_bias_down,
    )


def solution(mesh):
    in_specs = (
        P(("fsdp", "seq"), None),
        P("fsdp", None),
        P("fsdp", None),
        P("fsdp", None),
        P("fsdp", None),
        P("fsdp", None),
        P("fsdp", None),
        P("fsdp", None),
        P("fsdp"),
        P("fsdp"),
        P("fsdp"),
        P("fsdp"),
        P(("fsdp", "seq"), None),
    )
    out_specs = (
        P(("fsdp", "seq"), None),
        P(("fsdp", "seq"), None),
        P("fsdp", None),
        P("fsdp", None),
        P("fsdp", None),
        P("fsdp", None),
        P("fsdp", None),
        P("fsdp", None),
        P("fsdp", None),
        P("fsdp"),
        P("fsdp"),
        P("fsdp"),
        P("fsdp"),
    )
    return jax.shard_map(
        on_device, mesh=mesh, in_specs=in_specs, out_specs=out_specs, check_vma=False
    )
```

profile of v0, /device:TPU:0, one launch (start us, length us, event | category | flops | bytes accessed | tf_op | source)
XLA Modules:
  0.0 1122.2 jit_solution(11139686046345123835)
XLA Ops:
  7.9 25.1 %all_gather.43 = bf16[512,512]{1,0:T(8,128)(2,1)S(1)} all-gather(bf16[32,512]{1,0:T(8,128)(2,1)} %param.20), channel_id=1, replica_groups=mesh['fsdp'=16,'seq'=2] {'fsdp'}, dimensions={0}, use_global_device_ids=true | all-gather | bytes 557056 | tf_op jit(solution)/shard_map/all_gather | solution.py:144
  33.1 19.6 %all_gather.44 = bf16[512,512]{1,0:T(8,128)(2,1)S(1)} all-gather(bf16[32,512]{1,0:T(8,128)(2,1)} %param.21), channel_id=1, replica_groups=mesh['fsdp'=16,'seq'=2] {'fsdp'}, dimensions={0}, use_global_device_ids=true | all-gather | bytes 557056 | tf_op jit(solution)/shard_map/all_gather | solution.py:145
  52.7 21.4 %all_gather.45 = bf16[512,512]{1,0:T(8,128)(2,1)S(1)} all-gather(bf16[32,512]{1,0:T(8,128)(2,1)} %param.22), channel_id=1, replica_groups=mesh['fsdp'=16,'seq'=2] {'fsdp'}, dimensions={0}, use_global_device_ids=true | all-gather | bytes 557056 | tf_op jit(solution)/shard_map/all_gather | solution.py:146
  77.5 29.8 %all-reduce.13 = (bf16[512]{0:T(512)(128)(2,1)S(1)}, bf16[512]{0:T(512)(128)(2,1)S(1)}) all-reduce(bf16[512]{0:T(512)(128)(2,1)S(1)} %dynamic-update-slice, bf16[512]{0:T(512)(128)(2,1)S(1)} %dynamic-update-slice.1), channel_id=1, replica_groups=mesh['fsdp'=16,'seq'=2] {'fsdp'}, use_global_device_ids=true, to_apply=%add.4 | all-reduce | flops 1024 | bytes 4096
  108.0 18.8 %all_gather.46 = bf16[512,512]{1,0:T(8,128)(2,1)S(1)} all-gather(bf16[32,512]{1,0:T(8,128)(2,1)S(1)} %copy-done.24), channel_id=1, replica_groups=mesh['fsdp'=16,'seq'=2] {'fsdp'}, dimensions={0}, use_global_device_ids=true | all-gather | bytes 557056 | tf_op jit(solution)/shard_map/all_gather | solution.py:147
  141.1 47.4 %all-to-all-done = bf16[1024,2,1024]{2,0,1:T(8,128)(2,1)} async-done(((bf16[1024,2,1024]{2,0,1:T(8,128)(2,1)}), bf16[1024,2,1024]{2,0,1:T(8,128)(2,1)}, u32[]{:S(2)}, u32[]{:S(2)}) %all-to-all-start) | async-done | bytes 4194336 | tf_op jit(solution)/shard_map/all_to_all | solution.py:158
  194.9 10.5 reshape.186
  205.5 9.9 copy.108
  215.4 87.2 %while.59 = (s32[]{:T(128)}, f32[4,64,64]{2,1,0:T(8,128)S(1)}, f32[4,64,64]{2,1,0:T(8,128)S(1)}, f32[4,64]{1,0:T(4,128)S(1)}, bf16[4,512,4,64]{1,3,2,0:T(8,128)(...) while((s32[]{:T(128)}, f32[4,64,64]{2,1,0:T(8,128)S(1)}, f32[4,64,64]{2,1,0:T(8,128)S(1)}, ...), condition=%wide.region_6.7_spmd.clone, body=%wide.region_2.6_spmd.clone.sunk | while | flops 3763302656 | bytes 46270624 | solution.py:119
  310.9 18.7 %all-gather = bf16[16,1,128]{2,1,0:T(2,128)(2,1)S(1)} all-gather(bf16[1,1,128]{2,1,0:T(2,128)(2,1)S(1)} %bitcast.368), channel_id=1, replica_groups=mesh['fsdp'=16,'seq'=2] {'fsdp'}, dimensions={0}, use_global_device_ids=true | all-gather | bytes 4352 | tf_op jit(solution)/shard_map/all_gather | solution.py:172
  331.6 20.5 %all_gather.47 = bf16[512,512]{1,0:T(8,128)(2,1)} all-gather(bf16[32,512]{1,0:T(8,128)(2,1)} %param.24), channel_id=1, replica_groups=mesh['fsdp'=16,'seq'=2] {'fsdp'}, dimensions={0}, use_global_device_ids=true | all-gather | bytes 557056 | tf_op jit(solution)/shard_map/all_gather | solution.py:148
  355.5 8.6 multiply_convert_fusion.1
  364.1 7.7 fusion.187
  382.7 16.5 %while.60 = (s32[]{:T(128)}, f32[4,64,64]{2,1,0:T(8,128)S(1)}, f32[4,64,64]{2,1,0:T(8,128)S(1)}, f32[4,64]{1,0:T(4,128)S(1)}, f32[4,4,64,64]{3,2,1,0:T(8,128)}, ...) while((s32[]{:T(128)}, f32[4,64,64]{2,1,0:T(8,128)S(1)}, ...), condition=%wide.region_13.14_spmd.clone, body=%wide.region_11.13_spmd.clone.sunk | while | flops 201556480 | bytes 7611003 | solution.py:119
  406.5 229.7 %while.61 = (s32[]{:T(128)}, f32[4,64,64]{2,1,0:T(8,128)S(1)}, f32[4,64,64]{2,1,0:T(8,128)S(1)}, f32[4,64]{1,0:T(4,128)S(1)}, bf16[4,512,4,256]{1,3,2,0:T(8,128)...) while((s32[]{:T(128)}, f32[4,64,64]{2,1,0:T(8,128)S(1)}, ...), condition=%wide.region_19.20_spmd.clone, body=%wide.region_14.19_spmd.clone.sunk | while | flops 11391533056 | bytes 137714896 | solution.py:119
  643.7 7.7 convert_element_type.217
  659.0 46.6 %all-to-all-done.3 = bf16[2,1024,1024]{2,1,0:T(8,128)(2,1)} async-done(((bf16[2,1024,1024]{2,1,0:T(8,128)(2,1)}), bf16[2,1024,1024]{2,1,0:T(8,128)(2,1)}, u32[]{:S(2)}, u32[]{:S(2)}) %all-to-all-start.3) | async-done | bytes 4194336 | tf_op jit(solution)/shard_map/all_to_all | solution.py:243
  749.9 31.2 %all-reduce.12 = (bf16[512]{0:T(512)(128)(2,1)S(1)}, bf16[512]{0:T(512)(128)(2,1)S(1)}, bf16[2048]{0:T(1024)(128)(2,1)S(1)}, bf16[512]{0:T(512)(128)(2,1)S(1)}, bf16[512]{0:T(512)(128)(2,1)S(1)}) all-reduce(bf16[512]{0:T(512)(128)(2,1)S(1)} %dynamic-update-slice.2, ...), channel_id=1, replica_groups=mesh['fsdp'=16,'seq'=2] {'fsdp'}, use_global_device_ids=true, to_apply=%add.6 | all-reduce | flops 4096 | bytes 16384
  790.4 43.0 %reduce-scatter.12.cloned.1.call-done = bf16[32,512]{1,0:T(8,128)(2,1)} async-done(((bf16[512,512]{1,0:T(8,128)(2,1)}), bf16[32,512]{1,0:T(8,128)(2,1)}) %reduce-scatter.12.cloned.1.call-update) | async-done | bytes 32784 | tf_op jit(solution)/shard_map/reduce_scatter | solution.py:262
  833.4 58.6 %reduce-scatter.14.cloned.1.call-done = bf16[32,512]{1,0:T(8,128)(2,1)} async-done(((bf16[512,512]{1,0:T(8,128)(2,1)}), bf16[32,512]{1,0:T(8,128)(2,1)}) %reduce-scatter.14.cloned.1.call-update) | async-done | bytes 32784 | tf_op jit(solution)/shard_map/reduce_scatter | solution.py:265
  892.0 59.0 %reduce-scatter.8.cloned.1.call-done = bf16[32,512]{1,0:T(8,128)(2,1)} async-done(((bf16[512,512]{1,0:T(8,128)(2,1)}), bf16[32,512]{1,0:T(8,128)(2,1)}) %reduce-scatter.8.cloned.1.call-update) | async-done | bytes 32784 | tf_op jit(solution)/shard_map/reduce_scatter | solution.py:256
  954.2 61.6 %reduce-scatter.18.cloned.1.call-done = bf16[32,2048]{1,0:T(8,128)(2,1)} async-done(((bf16[512,2048]{1,0:T(8,128)(2,1)}), bf16[32,2048]{1,0:T(8,128)(2,1)}) %reduce-scatter.18.cloned.1.call-update) | async-done | bytes 131088 | tf_op jit(solution)/shard_map/reduce_scatter | solution.py:206
  1015.8 64.3 %reduce-scatter.20.cloned.1.call-done = bf16[128,512]{1,0:T(8,128)(2,1)} async-done(((bf16[2048,512]{1,0:T(8,128)(2,1)}), bf16[128,512]{1,0:T(8,128)(2,1)}) %reduce-scatter.20.cloned.1.call-update) | async-done | bytes 131088 | tf_op jit(solution)/shard_map/reduce_scatter | solution.py:209
  1080.1 19.2 %all-reduce.19 = (f32[32,2048]{1,0:T(8,128)}, f32[128,512]{1,0:T(8,128)}, f32[32]{0:T(128)}, f32[128]{0:T(128)}, f32[32]{0:T(128)}) all-reduce(bf16[32,2048]{1,0:T(8,128)(2,1)} %reduce-scatter.18.cloned.1.call-done, bf16[128,512]{1,0:T(8,128)(2,1)} %reduce-scatter.20.cloned.1.call-done, ...), channel_id=1, replica_groups=mesh['fsdp'=16,'seq'=2] {'seq'}, use_global_device_ids=true, to_apply=%region_33.34 | all-reduce | flops 131264 | bytes 787968 | tf_op jit(solution)/shard_map/psum | solution.py:222
  (469 shorter events, 452.2 us)
Async XLA Ops:
  7.2 68.5 %copy-start.35 = (u32[32]{0:T(128)S(1)}, u32[32]{0:T(128)}, u32[]{:S(2)}) copy-start(u32[32]{0:T(128)} %constant.145) | copy-start | bytes 388
  7.2 69.8 %copy-start.40 = (bf16[32]{0:T(256)(128)(2,1)S(1)}, bf16[32]{0:T(256)(128)(2,1)}, u32[]{:S(2)}) copy-start(bf16[32]{0:T(256)(128)(2,1)} %param.27) | copy-start | bytes 196
  7.2 70.1 %copy-start.41 = (bf16[32]{0:T(256)(128)(2,1)S(1)}, bf16[32]{0:T(256)(128)(2,1)}, u32[]{:S(2)}) copy-start(bf16[32]{0:T(256)(128)(2,1)} %param.28) | copy-start | bytes 196
  7.2 348.3 %all-gather.4.cloned.1.call-start = ((), (), s32[]{:S(2)}) async-start(), calls=%async_computation.11 | async-start | bytes 2228224 | tf_op jit(solution)/shard_map/all_gather | solution.py:169
  75.6 54.0 %copy-start.2 = (bf16[1024,512]{0,1:T(8,128)(2,1)}, bf16[1024,512]{0,1:T(8,128)(2,1)S(1)}, u32[]{:S(2)}) copy-start(bf16[1024,512]{0,1:T(8,128)(2,1)S(1)} %copy.102) | copy-start | bytes 3145732
  75.6 32.4 %copy-start.24 = (bf16[32,512]{1,0:T(8,128)(2,1)S(1)}, bf16[32,512]{1,0:T(8,128)(2,1)}, u32[]{:S(2)}) copy-start(bf16[32,512]{1,0:T(8,128)(2,1)} %param.23) | copy-start | bytes 98308
  107.4 22.2 %copy-start.30 = (f32[512]{0:T(512)}, f32[512]{0:T(512)S(1)}, u32[]{:S(2)}) copy-start(f32[512]{0:T(512)S(1)} %convert_element_type.195) | copy-start | bytes 6148
  134.6 53.8 %all-to-all-start = ((bf16[1024,2,1024]{2,0,1:T(8,128)(2,1)}), bf16[1024,2,1024]{2,0,1:T(8,128)(2,1)}, u32[]{:S(2)}, u32[]{:S(2)}) async-start(bf16[1024,2,1024]{2,0,1:T(8,128)(2,1)} %bitcast.348), calls=%async_computation | async-start | bytes 8388608 | tf_op jit(solution)/shard_map/all_to_all | solution.py:158
  140.3 223.8 %all-gather.6.cloned.1.call-start = ((), (), s32[]{:S(2)}) async-start(), calls=%async_computation.12 | async-start | bytes 2228224 | tf_op jit(solution)/shard_map/all_gather | solution.py:170
  305.3 24.9 %copy-start.13 = (bf16[1024,512]{1,0:T(8,128)(2,1)S(1)}, bf16[1024,512]{1,0:T(8,128)(2,1)}, u32[]{:S(2)}) copy-start(bf16[1024,512]{1,0:T(8,128)(2,1)} %param.31) | copy-start | bytes 3145732
  306.6 46.4 %copy-start.3 = (bf16[1024,512]{0,1:T(8,128)(2,1)S(1)}, bf16[1024,512]{0,1:T(8,128)(2,1)}, u32[]{:S(2)}) copy-start(bf16[1024,512]{0,1:T(8,128)(2,1)} %copy-done.2) | copy-start | bytes 3145732
  306.6 45.4 %all-to-all-start.1 = ((bf16[2,1024,256]{1,2,0:T(8,128)(2,1)}), bf16[2,1024,256]{1,2,0:T(8,128)(2,1)S(1)}, u32[]{:S(2)}, u32[]{:S(2)}) async-start(bf16[2,1024,256]{1,2,0:T(8,128)(2,1)} %copy.110), calls=%async_computation.1 | async-start | bytes 2097152 | tf_op jit(solution)/shard_map/all_to_all | solution.py:165
  355.1 20.1 %copy-start.5 = (f32[1024,512]{0,1:T(8,128)}, f32[1024,512]{0,1:T(8,128)S(1)}, u32[]{:S(2)}) copy-start(f32[1024,512]{0,1:T(8,128)S(1)} %get-tuple-element.622) | copy-start | bytes 6291460
  379.1 20.1 %all-to-all-start.2 = ((bf16[1024,2,256]{0,2,1:T(8,128)(2,1)}), bf16[1024,2,256]{0,2,1:T(8,128)(2,1)S(1)}, u32[]{:S(2)}, u32[]{:S(2)}) async-start(bf16[1024,2,256]{0,2,1:T(8,128)(2,1)} %bitcast.11), calls=%async_computation.2 | async-start | bytes 2097152 | tf_op jit(solution)/shard_map/all_to_all | solution.py:237
  651.4 54.2 %all-to-all-start.3 = ((bf16[2,1024,1024]{2,1,0:T(8,128)(2,1)}), bf16[2,1024,1024]{2,1,0:T(8,128)(2,1)}, u32[]{:S(2)}, u32[]{:S(2)}) async-start(bf16[2,1024,1024]{2,1,0:T(8,128)(2,1)} %convert_element_type.217), calls=%async_computation.3 | async-start | bytes 8388608 | tf_op jit(solution)/shard_map/all_to_all | solution.py:243
  657.3 133.1 %reduce-scatter.16.cloned.1.call-start = ((), (), s32[]{:S(2)}) async-start(), calls=%async_computation.17 | async-start | bytes 557056 | tf_op jit(solution)/shard_map/reduce_scatter | solution.py:268
  658.9 131.5 %reduce-scatter.10.cloned.1.call-start = ((), (), s32[]{:S(2)}) async-start(), calls=%async_computation.14 | async-start | bytes 557056 | tf_op jit(solution)/shard_map/reduce_scatter | solution.py:259
  720.2 113.2 %reduce-scatter.12.cloned.1.call-start = ((), (), s32[]{:S(2)}) async-start(), calls=%async_computation.15 | async-start | bytes 557056 | tf_op jit(solution)/shard_map/reduce_scatter | solution.py:262
  722.3 169.7 %reduce-scatter.14.cloned.1.call-start = ((), (), s32[]{:S(2)}) async-start(), calls=%async_computation.16 | async-start | bytes 557056 | tf_op jit(solution)/shard_map/reduce_scatter | solution.py:265
  724.5 226.5 %reduce-scatter.8.cloned.1.call-start = ((), (), s32[]{:S(2)}) async-start(), calls=%async_computation.13 | async-start | bytes 557056 | tf_op jit(solution)/shard_map/reduce_scatter | solution.py:256
  726.6 289.2 %reduce-scatter.18.cloned.1.call-start = ((), (), s32[]{:S(2)}) async-start(), calls=%async_computation.18 | async-start | bytes 2228224 | tf_op jit(solution)/shard_map/reduce_scatter | solution.py:206
  733.3 346.8 %reduce-scatter.20.cloned.1.call-start = ((), (), s32[]{:S(2)}) async-start(), calls=%async_computation.19 | async-start | bytes 2228224 | tf_op jit(solution)/shard_map/reduce_scatter | solution.py:209
  739.6 367.2 %all-reduce.18.cloned.1.call-start = ((), (), s32[]{:S(2)}) async-start(), calls=%async_computation.20 | async-start | bytes 328704 | tf_op jit(solution)/shard_map/psum | solution.py:276
  785.6 165.5 %copy-start.11 = (f32[1024,512]{0,1:T(8,128)S(1)}, f32[1024,512]{0,1:T(8,128)}, u32[]{:S(2)}) copy-start(f32[1024,512]{0,1:T(8,128)} %fusion.169) | copy-start | bytes 6291460
  (46 other events, 205.8 us)
Sparse Core Ops, SparseCore 0:
  10.2 46.1 all-gather.3
  143.3 40.2 all-gather.5
  661.7 54.7 reduce-scatter.15
  720.3 54.7 reduce-scatter.9
  778.5 54.8 reduce-scatter.11
  837.2 54.7 reduce-scatter.13
  896.1 54.8 reduce-scatter.7
  955.2 60.5 reduce-scatter.17
  1019.6 60.5 reduce-scatter.19
  1083.4 23.3 all-reduce.17
where the time goes:
time: 1130 us; the launch traced here: 1120 us
  waiting for transfers between devices  390 us (35%)
  matrix products  310 us (27%)
  blocking collectives  204 us (18%)
  local copies, waits for them, and re-layouts  123 us (11%)
  other arithmetic  34.6 us (3%)
  loops' own time  23.3 us (2%)
  starting transfers between devices  19.2 us (2%)
  between operations  17.3 us (2%)
    reduce_scatter x1, waiting for transfers between devices, on_device(): lax.psum_scatter(grad_w_down.astype(jnp.bfloat16), 'fsdp', scatter_dimens...  64.3 us
    reduce_scatter x1, waiting for transfers between devices, on_device(): lax.psum_scatter(grad_w_up.astype(jnp.bfloat16), 'fsdp', scatter_dimensio...  61.6 us
    unnamed x2, blocking collectives  61 us
    dot_general x16, matrix products, mix_block(): jnp.einsum('thm,ihm->hti', weight_scaled_rows, stored_entries, precision=...  60.2 us
    reduce_scatter x1, waiting for transfers between devices, on_device(): lax.psum_scatter(grad_w_query.astype(jnp.bfloat16), 'fsdp', scatter_dimen...  59 us
    reduce_scatter x1, waiting for transfers between devices, on_device(): lax.psum_scatter(grad_w_control.astype(jnp.bfloat16), 'fsdp', scatter_dim...  58.6 us
    dot_general x16, matrix products, mix_block(): jnp.einsum('hti,ihm->thm', pair_scores, stored_entries, precision=exact_p...  58.2 us
    all_to_all x1, waiting for transfers between devices, on_device(): lax.all_to_all(packed, 'seq', split_axis=1, concat_axis=0, tiled=True)  47.4 us
  transfers between devices with their start and end apart: 14, of which 8 were waited for; matrix products, arithmetic and copies ran while one was open for 18% of the time, Pallas kernels for 0%

commit v1 on v0

v1 whole, which is shorter than its diff:
```python
from functools import partial
import jax
import jax.numpy as jnp
from jax import lax
from jax.experimental import pallas as pl
from jax.experimental.pallas import tpu as pltpu
from jax.sharding import PartitionSpec as P

F32 = jnp.float32
BF16 = jnp.bfloat16
HEAD = 64
QUAD = 256
SCALE = HEAD ** -0.5
CHUNK = 128
VMEM_LIMIT = 60 * 1024 * 1024


def mm(a, b):
    return lax.dot_general(a, b, (((1,), (0,)), ((), ())), preferred_element_type=F32)


def mm_t(a, b):
    return lax.dot_general(a, b, (((1,), (1,)), ((), ())), preferred_element_type=F32)


def t_mm(a, b):
    return lax.dot_general(a, b, (((0,), (0,)), ((), ())), preferred_element_type=F32)


def iota(shape, dim):
    return lax.broadcasted_iota(jnp.int32, shape, dim)


def normalize(x):
    centred = x - jnp.mean(x, axis=-1, keepdims=True)
    spread = jnp.mean(centred * centred, axis=-1, keepdims=True)
    factor = lax.rsqrt(spread + 1e-05)
    return centred * factor, factor


def norm_back(g, normed, factor):
    first = jnp.mean(g, axis=-1, keepdims=True)
    second = jnp.mean(g * normed, axis=-1, keepdims=True)
    return factor * (g - first - normed * second)


def blocks_of(x):
    lane = iota(x.shape, 1) // HEAD
    zero = jnp.zeros_like(x)
    return jnp.concatenate([jnp.where(lane == h, x, zero) for h in range(4)], axis=0)


def tri(x, lower):
    c = x.shape[0]
    row, col = iota(x.shape, 0), iota(x.shape, 1) % c
    keep = row >= col if lower else row <= col
    return jnp.where(keep, x, 0.0).astype(BF16)


def per_head(x, op, neutral):
    parts = []
    for p in range(x.shape[1] // 128):
        v = x[:, p * 128 : (p + 1) * 128]
        low = iota(v.shape, 1) < HEAD
        a = op(jnp.where(low, v, neutral), axis=-1, keepdims=True)
        b = op(jnp.where(low, neutral, v), axis=-1, keepdims=True)
        parts.append(jnp.where(low, a, b))
    return jnp.concatenate(parts, axis=1)


def head_square():
    return iota((QUAD, QUAD), 0) // HEAD == iota((QUAD, QUAD), 1) // HEAD


STATE = 2 * HEAD + 8


def store_state(st_ref, first, second, total):
    square = head_square()
    for g in range(st_ref.shape[0]):
        for k, ref in enumerate((first, second)):
            x = jnp.where(square, ref[g], 0.0)
            st_ref[g, k * HEAD : (k + 1) * HEAD, :] = x[0:64] + x[64:128] + x[128:192] + x[192:256]
        st_ref[g, 2 * HEAD :, :] = jnp.broadcast_to(total[0:1, g * QUAD : (g + 1) * QUAD], (8, QUAD))


def load_state(st_ref, first, second, total):
    square = head_square()
    for g in range(st_ref.shape[0]):
        for k, ref in enumerate((first, second)):
            x = st_ref[g, k * HEAD : (k + 1) * HEAD, :]
            ref[g] = jnp.where(square, jnp.concatenate([x] * 4, axis=0), 0.0)
        total[:, g * QUAD : (g + 1) * QUAD] = st_ref[g, 2 * HEAD :, :]


def hi_lo(x):
    hi = x.astype(BF16)
    return hi, (x - hi.astype(F32)).astype(BF16)


def spread_vector(vecs, me, n, r, k, each, total):
    pick = (iota((n, n * r), 1) == iota((n, n * r), 0) * r + k).astype(BF16)
    rows = mm(pick, vecs).astype(BF16)
    tile = (iota((128, total), 1) % each == iota((128, total), 0)).astype(BF16)
    wide = mm(rows, tile)
    own = iota((n, total), 1) // each == (iota((n, total), 0) ^ me)
    return jnp.sum(jnp.where(own, wide, 0.0), axis=0, keepdims=True)


def gather_vector(vec, me, n, each):
    total = vec.shape[1]
    own = iota((n, total), 1) // each == (iota((n, total), 0) ^ me)
    wide = jnp.where(own, vec, 0.0).astype(BF16)
    tile = (iota((128, total), 1) % each == iota((128, total), 0)).astype(BF16)
    return mm_t(wide, tile).astype(BF16)


def project_kernel(n, r, me_ref, tok_ref, *refs):
    pieces = refs[:n]
    att_ref, pack_ref, st_ref, w_ref, vec_out, kt_ref, mv_ref, tot_ref, vecs, sems, vsems = refs[n:]
    d = w_ref.shape[0]
    wide = w_ref.shape[1]
    me = me_ref[0]

    @pl.when(pl.program_id(0) == 0)
    def _():
        copies = []
        for j in range(n):
            at = pl.multiple_of((me ^ j) * r, r)
            copies.append(pltpu.make_async_copy(pieces[j].at[:, pl.ds(0, wide)], w_ref.at[pl.ds(at, r), :], sems.at[j]))
            copies.append(pltpu.make_async_copy(pieces[j].at[:, pl.ds(wide, 128)], vecs.at[pl.ds(j * r, r), :], vsems.at[j]))
        for c in copies:
            c.start()
        kt_ref[...] = jnp.zeros_like(kt_ref)
        mv_ref[...] = jnp.zeros_like(mv_ref)
        tot_ref[...] = jnp.zeros_like(tot_ref)
        for c in copies:
            c.wait()
        vec_out[...] = vecs[...]

    gain = spread_vector(vecs[...], me, n, r, 0, r, d)
    normed, _ = normalize(tok_ref[...].astype(F32))
    att = (normed * gain).astype(BF16)
    att_ref[...] = att
    cols = []
    for p in range(4):
        full = mm(att, w_ref[:, p * d : (p + 1) * d]).astype(BF16)
        pack_ref[:, p * d : (p + 1) * d] = full
        cols.append(full)
    written = jnp.exp(cols[3].astype(F32)).astype(BF16)
    for g in range(d // QUAD):
        s = slice(g * QUAD, (g + 1) * QUAD)
        kt_ref[g] += t_mm(cols[1][:, s], written[:, s])
        mv_ref[g] += t_mm(written[:, s], cols[2][:, s])
    tot_ref[0:1, :] += jnp.sum(written.astype(F32), axis=0, keepdims=True)

    @pl.when(pl.program_id(0) == pl.num_programs(0) - 1)
    def _():
        store_state(st_ref, kt_ref, mv_ref, tot_ref)


def project(me, tokens, pieces, rows=256):
    t, d = tokens.shape
    n = len(pieces)
    r = pieces[0].shape[0]
    wide = 4 * d
    g = d // QUAD
    const = lambda *shape: pl.BlockSpec(shape, lambda i: (0,) * len(shape))
    return pl.pallas_call(
        partial(project_kernel, n, r),
        grid=(t // rows,),
        in_specs=[pl.BlockSpec(memory_space=pltpu.SMEM), pl.BlockSpec((rows, d), lambda i: (i, 0))]
        + [pl.BlockSpec(memory_space=pl.ANY)] * n,
        out_specs=[
            pl.BlockSpec((rows, d), lambda i: (i, 0)),
            pl.BlockSpec((rows, wide), lambda i: (i, 0)),
            const(g, STATE, QUAD),
            const(d, wide),
            const(n * r, 128),
        ],
        out_shape=[
            jax.ShapeDtypeStruct((t, d), BF16),
            jax.ShapeDtypeStruct((t, wide), BF16),
            jax.ShapeDtypeStruct((g, STATE, QUAD), F32),
            jax.ShapeDtypeStruct((d, wide), BF16),
            jax.ShapeDtypeStruct((n * r, 128), BF16),
        ],
        scratch_shapes=[
            pltpu.VMEM((g, QUAD, QUAD), F32),
            pltpu.VMEM((g, QUAD, QUAD), F32),
            pltpu.VMEM((8, d), F32),
            pltpu.VMEM((n * r, 128), BF16),
            pltpu.SemaphoreType.DMA((n,)),
            pltpu.SemaphoreType.DMA((n,)),
        ],
        compiler_params=pltpu.CompilerParams(vmem_limit_bytes=VMEM_LIMIT),
        cost_estimate=pl.CostEstimate(flops=2 * t * d * wide, bytes_accessed=12 << 20, transcendentals=t * d),
        name="project",
    )(me, tokens, *pieces)


def mix_kernel(pack_ref, st_in, mix_ref, read_ref, score_ref, inv_ref, kts_ref, mvs_ref, kt, mv, tot):
    d = mix_ref.shape[1]
    rows = mix_ref.shape[0]

    @pl.when(pl.program_id(0) == 0)
    def _():
        load_state(st_in, kt, mv, tot)

    c = CHUNK
    square = head_square()
    ones = (iota((c, c), 0) >= iota((c, c), 1)).astype(BF16)
    for b in range(rows // c):
        rr = slice(b * c, (b + 1) * c)
        for g in range(d // QUAD):
            s = slice(g * QUAD, (g + 1) * QUAD)
            q, k, v, u = (pack_ref[rr, p * d + g * QUAD : p * d + (g + 1) * QUAD] for p in range(4))
            written = jnp.exp(u.astype(F32)).astype(BF16)
            wb = blocks_of(written)
            pairs = tri(mm_t(q, blocks_of(k)), True)
            ktb, mvb = kt[g].astype(BF16), mv[g].astype(BF16)
            kts_ref[b, g] = ktb
            mvs_ref[b, g] = mvb
            top = mm(pairs, wb) + mm(q, ktb)
            total = mm(ones, written) + tot[0:1, s]
            inv = 1.0 / total
            score = top * SCALE * inv
            e = jnp.exp(score - per_head(score, jnp.max, -jnp.inf))
            read = e / per_head(e, jnp.sum, 0.0)
            scaled = (read * inv).astype(BF16)
            recall = tri(mm_t(scaled, wb), True)
            out = mm(recall, blocks_of(v)) + mm(scaled, mvb)
            mix_ref[rr, s] = out.astype(BF16)
            read_ref[rr, s] = read
            score_ref[rr, s] = score
            inv_ref[rr, s] = inv
            kt[g] += jnp.where(square, t_mm(k, written), 0.0)
            mv[g] += jnp.where(square, t_mm(written, v), 0.0)
            tot[0:1, s] = total[c - 1 : c, :]


def mix(packed, state, rows=256):
    t, wide = packed.shape
    d = wide // 4
    g = d // QUAD
    const = lambda *shape: pl.BlockSpec(shape, lambda i: (0,) * len(shape))
    per = rows // CHUNK
    row = lambda w: pl.BlockSpec((rows, w), lambda i: (i, 0))
    return pl.pallas_call(
        mix_kernel,
        grid=(t // rows,),
        in_specs=[row(wide), const(g, STATE, QUAD)],
        out_specs=[row(d)] * 4 + [pl.BlockSpec((per, g, QUAD, QUAD), lambda i: (i, 0, 0, 0))] * 2,
        out_shape=[jax.ShapeDtypeStruct((t, d), BF16)] + [jax.ShapeDtypeStruct((t, d), F32)] * 3
        + [jax.ShapeDtypeStruct((t // CHUNK, g, QUAD, QUAD), BF16)] * 2,
        scratch_shapes=[pltpu.VMEM((g, QUAD, QUAD), F32), pltpu.VMEM((g, QUAD, QUAD), F32), pltpu.VMEM((8, d), F32)],
        compiler_params=pltpu.CompilerParams(vmem_limit_bytes=VMEM_LIMIT),
        cost_estimate=pl.CostEstimate(flops=6 * 10**9, bytes_accessed=16 << 20, transcendentals=2 * t * d),
        name="mix",
    )(packed, state)


def ffn_kernel(n, r, me_ref, vec_ref, mixed_ref, tok_ref, cot_ref, *refs):
    pieces = refs[:n]
    out_ref, gres_ref, gmix_ref, even_ref, odd_ref = refs[n : n + 5]
    w_out, w_up, w_down, hid, gpre, fin, gbr, grads, sems, osems = refs[n + 5 :]
    t, d = mixed_ref.shape
    ff = w_up.shape[1]
    me = me_ref[0]
    mult = ff // d
    copies = []
    for j in range(n):
        own = me ^ j
        at = pl.multiple_of(own * r, r)
        copies.append(pltpu.make_async_copy(pieces[j].at[:, pl.ds(0, ff)], w_up.at[pl.ds(at, r), :], sems.at[0, j]))
        for m in range(mult):
            to = pl.multiple_of(own * r * mult + m * r, r)
            copies.append(
                pltpu.make_async_copy(pieces[j].at[:, pl.ds(ff + m * d, d)], w_down.at[pl.ds(to, r), :], sems.at[2 + m, j])
            )
        copies.append(pltpu.make_async_copy(pieces[j].at[:, pl.ds(2 * ff, d)], w_out.at[pl.ds(at, r), :], sems.at[1, j]))
    for c in copies:
        c.start()
    vecs = vec_ref[...]
    gain = spread_vector(vecs, me, n, r, 1, r, d)
    b_up = spread_vector(vecs, me, n, r, 2, r * mult, ff)
    b_down = spread_vector(vecs, me, n, r, 3, r, d)
    for c in copies:
        c.wait()

    rows = 256
    part = 512
    zero = jnp.zeros((1, d), F32)

    def body(i, carry):
        ggain, gbup, gbdown = carry
        at = pl.multiple_of(i * rows, rows)
        rs = pl.ds(at, rows)
        cot = cot_ref[rs, :]
        cotf = cot.astype(F32)
        resid = tok_ref[rs, :].astype(F32) + mm(mixed_ref[rs, :], w_out[...])
        normed, factor = normalize(resid)
        ffn_in = (normed * gain).astype(BF16)
        fin[rs, :] = ffn_in
        total = jnp.zeros((rows, d), F32)
        gin = jnp.zeros((rows, d), F32)
        sums = []
        for p in range(ff // part):
            ps = slice(p * part, (p + 1) * part)
            pre = mm(ffn_in, w_up[:, ps]) + b_up[:, ps]
            sig = 1.0 / (1.0 + jnp.exp(-pre))
            hidden = (pre * sig).astype(BF16)
            hid[rs, ps] = hidden
            total += mm(hidden, w_down[ps, :])
            gh = mm_t(cot, w_down[ps, :])
            gp = (gh * (sig * (1.0 + pre * (1.0 - sig)))).astype(BF16)
            gpre[rs, ps] = gp
            sums.append(jnp.sum(gp.astype(F32), axis=0, keepdims=True))
            gin += mm_t(gp, w_up[:, ps])
        out_ref[rs, :] = (resid + (total + b_down)).astype(BF16)
        gres = cotf + norm_back(gin * gain, normed, factor)
        gres_ref[rs, :] = gres
        gb = gres.astype(BF16)
        gbr[rs, :] = gb
        gmix_ref[rs, :] = mm_t(gb, w_out[...]).astype(BF16)
        return (
            ggain + jnp.sum(gin * normed, axis=0, keepdims=True),
            gbup + jnp.concatenate(sums, axis=1),
            gbdown + jnp.sum(cotf, axis=0, keepdims=True),
        )

    ggain, gbup, gbdown = lax.fori_loop(0, t // rows, body, (zero, jnp.zeros((1, ff), F32), zero))
    for p in range(ff // part):
        ps = slice(p * part, (p + 1) * part)
        w_up[:, ps] = t_mm(fin[...], gpre[:, ps]).astype(BF16)
        w_down[ps, :] = t_mm(hid[:, ps], cot_ref[...]).astype(BF16)
    w_out[...] = t_mm(mixed_ref[...], gbr[...]).astype(BF16)
    va = gather_vector(ggain, me, n, r)
    vb = gather_vector(gbup, me, n, r * mult)
    vc = gather_vector(gbdown, me, n, r)
    row = iota((n, r, 128), 1)
    grads[...] = jnp.where(
        row == 1, va[:, None, :].astype(F32),
        jnp.where(row == 2, vb[:, None, :].astype(F32), jnp.where(row == 3, vc[:, None, :].astype(F32), 0.0)),
    ).astype(BF16)
    outs = []
    for j in range(n):
        own = me ^ j
        at = pl.multiple_of(own * r, r)
        dst = (odd_ref if j % 2 else even_ref).at[j // 2]
        outs.append(pltpu.make_async_copy(w_up.at[pl.ds(at, r), :], dst.at[:, pl.ds(0, ff)], osems.at[0, j]))
        for m in range(mult):
            frm = pl.multiple_of(own * r * mult + m * r, r)
            outs.append(
                pltpu.make_async_copy(w_down.at[pl.ds(frm, r), :], dst.at[:, pl.ds(ff + m * d, d)], osems.at[3 + m, j])
            )
        outs.append(pltpu.make_async_copy(w_out.at[pl.ds(at, r), :], dst.at[:, pl.ds(2 * ff, d)], osems.at[1, j]))
        outs.append(pltpu.make_async_copy(grads.at[j], dst.at[:, pl.ds(2 * ff + d, 128)], osems.at[2, j]))
    for c in outs:
        c.start()
    for c in outs:
        c.wait()


def ffn(me, vecs, mixed, tokens, cot, pieces, ff):
    t, d = tokens.shape
    n = len(pieces)
    r = pieces[0].shape[0]
    whole = pl.BlockSpec(memory_space=pltpu.VMEM)
    hbm = pl.BlockSpec(memory_space=pl.ANY)
    width = 2 * ff + d + 128
    mult = ff // d
    return pl.pallas_call(
        partial(ffn_kernel, n, r),
        in_specs=[pl.BlockSpec(memory_space=pltpu.SMEM)] + [whole] * 4 + [hbm] * n,
        out_specs=[whole] * 3 + [hbm] * 2,
        out_shape=[
            jax.ShapeDtypeStruct((t, d), BF16),
            jax.ShapeDtypeStruct((t, d), F32),
            jax.ShapeDtypeStruct((t, d), BF16),
            jax.ShapeDtypeStruct((n // 2, r, width), BF16),
            jax.ShapeDtypeStruct((n // 2, r, width), BF16),
        ],
        scratch_shapes=[
            pltpu.VMEM((d, d), BF16),
            pltpu.VMEM((d, ff), BF16),
            pltpu.VMEM((ff, d), BF16),
            pltpu.VMEM((t, ff), BF16),
            pltpu.VMEM((t, ff), BF16),
            pltpu.VMEM((t, d), BF16),
            pltpu.VMEM((t, d), BF16),
            pltpu.VMEM((n, r, 128), BF16),
            pltpu.SemaphoreType.DMA((2 + mult, n)),
            pltpu.SemaphoreType.DMA((3 + mult, n)),
        ],
        compiler_params=pltpu.CompilerParams(vmem_limit_bytes=VMEM_LIMIT),
        cost_estimate=pl.CostEstimate(flops=12 * t * d * ff, bytes_accessed=20 << 20, transcendentals=t * ff),
        name="ffn",
    )(me, vecs, mixed, tokens, cot, *pieces)


def read_back_kernel(pack_ref, gmix_ref, read_ref, score_ref, inv_ref, kts_ref, mvs_ref,
                     gq_ref, a_ref, u_ref, gtot_ref, st_ref, gk_ref, gv_ref, gt_ref):
    rows, d = gmix_ref.shape

    @pl.when(pl.program_id(0) == 0)
    def _():
        gk_ref[...] = jnp.zeros_like(gk_ref)
        gv_ref[...] = jnp.zeros_like(gv_ref)
        gt_ref[...] = jnp.zeros_like(gt_ref)

    c = CHUNK
    for b in range(rows // c):
        rr = slice(b * c, (b + 1) * c)
        for g in range(d // QUAD):
            s = slice(g * QUAD, (g + 1) * QUAD)
            q, k, v, w = (pack_ref[rr, p * d + g * QUAD : p * d + (g + 1) * QUAD] for p in range(4))
            written = jnp.exp(w.astype(F32)).astype(BF16)
            wb = blocks_of(written)
            gm = gmix_ref[rr, s]
            read, score, inv = read_ref[rr, s], score_ref[rr, s], inv_ref[rr, s]
            gpair = tri(mm_t(gm, blocks_of(v)), True)
            gread = (mm(gpair, wb) + mm_t(gm, mvs_ref[b, g])) * inv
            weighted = read * gread
            gscore = weighted - read * per_head(weighted, jnp.sum, 0.0)
            a = (gscore * inv * SCALE).astype(BF16)
            u = (read * inv).astype(BF16)
            gtot = (gscore * score + weighted) * inv
            spair = tri(mm_t(a, wb), True)
            gq_ref[rr, s] = (mm(spair, blocks_of(k)) + mm_t(a, kts_ref[b, g])).astype(BF16)
            a_ref[rr, s] = a
            u_ref[rr, s] = u
            gtot_ref[rr, s] = gtot
            gk_ref[g] += t_mm(a, q)
            gv_ref[g] += t_mm(u, gm)
            gt_ref[0:1, s] += jnp.sum(gtot, axis=0, keepdims=True)

    @pl.when(pl.program_id(0) == pl.num_programs(0) - 1)
    def _():
        store_state(st_ref, gk_ref, gv_ref, gt_ref)


def read_back(packed, gmix, read, score, inv, kts, mvs, rows=256):
    t, wide = packed.shape
    d = wide // 4
    g = d // QUAD
    const = lambda *shape: pl.BlockSpec(shape, lambda i: (0,) * len(shape))
    per = rows // CHUNK
    row = lambda w: pl.BlockSpec((rows, w), lambda i: (i, 0))
    st = pl.BlockSpec((per, g, QUAD, QUAD), lambda i: (i, 0, 0, 0))
    return pl.pallas_call(
        read_back_kernel,
        grid=(t // rows,),
        in_specs=[row(wide), row(d), row(d), row(d), row(d), st, st],
        out_specs=[row(d)] * 4 + [const(g, STATE, QUAD)],
        out_shape=[jax.ShapeDtypeStruct((t, d), BF16)] * 3 + [jax.ShapeDtypeStruct((t, d), F32)]
        + [jax.ShapeDtypeStruct((g, STATE, QUAD), F32)],
        scratch_shapes=[pltpu.VMEM((g, QUAD, QUAD), F32), pltpu.VMEM((g, QUAD, QUAD), F32), pltpu.VMEM((8, d), F32)],
        compiler_params=pltpu.CompilerParams(vmem_limit_bytes=VMEM_LIMIT),
        cost_estimate=pl.CostEstimate(flops=6 * 10**9, bytes_accessed=20 << 20, transcendentals=t * d),
        name="read_back",
    )(packed, gmix, read, score, inv, kts, mvs)


def write_back_kernel(pack_ref, gmix_ref, a_ref, u_ref, gtot_ref, st_in, out_ref, gk, gv, gt):
    rows, d = gmix_ref.shape

    @pl.when(pl.program_id(0) == 0)
    def _():
        load_state(st_in, gk, gv, gt)

    c = CHUNK
    square = head_square()
    ones = (iota((c, c), 0) <= iota((c, c), 1)).astype(BF16)
    for b in reversed(range(rows // c)):
        rr = slice(b * c, (b + 1) * c)
        for g in range(d // QUAD):
            s = slice(g * QUAD, (g + 1) * QUAD)
            q, k, v, w = (pack_ref[rr, p * d + g * QUAD : p * d + (g + 1) * QUAD] for p in range(4))
            wf = jnp.exp(w.astype(F32))
            written = wf.astype(BF16)
            gm, a, u = gmix_ref[rr, s], a_ref[rr, s], u_ref[rr, s]
            gtot = gtot_ref[rr, s]
            hi, lo = hi_lo(gtot)
            after = mm(ones, hi) + mm(ones, lo) + gt[0:1, s]
            qb, gb, ab, ub = blocks_of(q), blocks_of(gm), blocks_of(a), blocks_of(u)
            gkb, gvb = gk[g].astype(BF16), gv[g].astype(BF16)
            pt = tri(mm_t(k, qb), False)
            gp = tri(mm_t(v, gb), False)
            st = tri(mm_t(written, ab), False)
            rt = tri(mm_t(written, ub), False)
            gw = mm(pt, ab) + mm(gp, ub) + mm_t(k, gkb) + mm_t(v, gvb)
            gkey = mm(st, qb) + mm(written, gkb)
            gval = mm(rt, gb) + mm(written, gvb)
            out_ref[rr, g * QUAD : (g + 1) * QUAD] = gkey.astype(BF16)
            out_ref[rr, d + g * QUAD : d + (g + 1) * QUAD] = gval.astype(BF16)
            out_ref[rr, 2 * d + g * QUAD : 2 * d + (g + 1) * QUAD] = (wf * (gw - after)).astype(BF16)
            gk[g] += jnp.where(square, t_mm(a, q), 0.0)
            gv[g] += jnp.where(square, t_mm(u, gm), 0.0)
            gt[0:1, s] = after[0:1, :]


def write_back(packed, gmix, a, u, gtot, state, rows=256):
    t, wide = packed.shape
    d = wide // 4
    g = d // QUAD
    last = t // rows - 1
    const = lambda *shape: pl.BlockSpec(shape, lambda i: (0,) * len(shape))
    row = lambda w: pl.BlockSpec((rows, w), lambda i: (last - i, 0))
    return pl.pallas_call(
        write_back_kernel,
        grid=(t // rows,),
        in_specs=[row(wide), row(d), row(d), row(d), row(d), const(g, STATE, QUAD)],
        out_specs=row(3 * d),
        out_shape=jax.ShapeDtypeStruct((t, 3 * d), BF16),
        scratch_shapes=[pltpu.VMEM((g, QUAD, QUAD), F32), pltpu.VMEM((g, QUAD, QUAD), F32), pltpu.VMEM((8, d), F32)],
        compiler_params=pltpu.CompilerParams(vmem_limit_bytes=VMEM_LIMIT),
        cost_estimate=pl.CostEstimate(flops=9 * 10**9, bytes_accessed=16 << 20, transcendentals=t * d),
        name="write_back",
    )(packed, gmix, a, u, gtot, state)


def weight_grad_kernel(n, r, me_ref, att_ref, gq_ref, gkvc_ref, even_ref, odd_ref, acc, sems):
    d = att_ref.shape[1]
    me = me_ref[0]
    acc[:, 0:d] = t_mm(att_ref[...], gq_ref[...]).astype(BF16)
    for p in range(3):
        acc[:, (p + 1) * d : (p + 2) * d] = t_mm(att_ref[...], gkvc_ref[:, p * d : (p + 1) * d]).astype(BF16)
    outs = []
    for j in range(n):
        at = pl.multiple_of((me ^ j) * r, r)
        dst = (odd_ref if j % 2 else even_ref).at[j // 2]
        outs.append(pltpu.make_async_copy(acc.at[pl.ds(at, r), :], dst, sems.at[j]))
    for c in outs:
        c.start()
    for c in outs:
        c.wait()


def weight_grad(me, att, gq, gkvc, n):
    t, d = att.shape
    r = d // n
    whole = pl.BlockSpec(memory_space=pltpu.VMEM)
    hbm = pl.BlockSpec(memory_space=pl.ANY)
    return pl.pallas_call(
        partial(weight_grad_kernel, n, r),
        in_specs=[pl.BlockSpec(memory_space=pltpu.SMEM)] + [whole] * 3,
        out_specs=[hbm] * 2,
        out_shape=[jax.ShapeDtypeStruct((n // 2, r, 4 * d), BF16)] * 2,
        scratch_shapes=[pltpu.VMEM((d, 4 * d), BF16), pltpu.SemaphoreType.DMA((n,))],
        compiler_params=pltpu.CompilerParams(vmem_limit_bytes=VMEM_LIMIT),
        cost_estimate=pl.CostEstimate(flops=8 * t * d * d, bytes_accessed=7 << 20, transcendentals=0),
        name="weight_grad",
    )(me, att, gq, gkvc)


def input_grad_kernel(n, r, me_ref, vec_ref, tok_ref, gq_ref, gkvc_ref, w_ref, gres_ref, out_ref):
    d = tok_ref.shape[1]
    gain = spread_vector(vec_ref[...], me_ref[0], n, r, 0, r, d)
    gin = mm_t(gq_ref[...], w_ref[:, 0:d]) + mm_t(gkvc_ref[...], w_ref[:, d:])
    normed, factor = normalize(tok_ref[...].astype(F32))
    out_ref[...] = gres_ref[...] + norm_back(gin * gain, normed, factor)


def input_grad(me, vecs, tokens, gq, gkvc, w, gres, n, rows=256):
    t, d = tokens.shape
    r = d // n
    const = lambda *shape: pl.BlockSpec(shape, lambda i: (0,) * len(shape))
    row = lambda w: pl.BlockSpec((rows, w), lambda i: (i, 0))
    return pl.pallas_call(
        partial(input_grad_kernel, n, r),
        grid=(t // rows,),
        in_specs=[pl.BlockSpec(memory_space=pltpu.SMEM), const(n * r, 128), row(d), row(d), row(3 * d), const(d, 4 * d), row(d)],
        out_specs=row(d),
        out_shape=jax.ShapeDtypeStruct((t, d), F32),
        compiler_params=pltpu.CompilerParams(vmem_limit_bytes=VMEM_LIMIT),
        cost_estimate=pl.CostEstimate(flops=8 * t * d * d, bytes_accessed=12 << 20, transcendentals=0),
        name="input_grad",
    )(me, vecs, tokens, gq, gkvc, w, gres)


def swap(x, mask, n):
    return lax.ppermute(x, "fsdp", [(i, i ^ mask) for i in range(n)])


def gather(shard, n):
    even = [shard] + [swap(shard, 2 * i, n) for i in range(1, n // 2)]
    odd = [swap(x, 1, n) for x in even]
    return [x for pair in zip(even, odd) for x in pair]


def scatter_sum(even, odd, n, seqs):
    mine = (even.astype(F32) + swap(odd, 1, n).astype(F32)).astype(BF16)
    parts = [mine[0]] + [swap(mine[i], 2 * i, n) for i in range(1, n // 2)]
    total = sum(p.astype(F32) for p in parts)
    step = 1
    while step < seqs:
        total = total + lax.ppermute(total, "seq", [(i, i ^ step) for i in range(seqs)])
        step *= 2
    return total


def shift(x, by, seqs):
    return lax.ppermute(x, "seq", [(i, i + by) for i in range(seqs) if 0 <= i + by < seqs])


def others(state, direction, seqs):
    if seqs == 1:
        return jnp.zeros_like(state)
    total = shift(state, direction, seqs)
    step = 1
    while step < seqs - 1:
        total = total + shift(total, direction * step, seqs)
        step *= 2
    return total


def on_device(n, seqs, tokens, w_query, w_key, w_value, w_control, w_out, w_up, w_down,
              gain_attn, gain_ffn, bias_up, bias_down, cotangent):
    r, d = w_query.shape
    ff = w_up.shape[1]
    mult = ff // d
    me = lax.axis_index("fsdp").astype(jnp.int32).reshape(1)
    lanes = lambda v: jnp.pad(v, (0, 128 - v.shape[0]))
    vec = jnp.pad(jnp.stack([lanes(gain_attn), lanes(gain_ffn), lanes(bias_up), lanes(bias_down)]), ((0, r - 4), (0, 0)))
    first = jnp.concatenate([w_query, w_key, w_value, w_control, vec], axis=1)
    second = jnp.concatenate([w_up] + [w_down[m * r : (m + 1) * r] for m in range(mult)] + [w_out], axis=1)
    att_pieces = gather(first, n)
    ffn_pieces = gather(second, n)
    att, packed, state, w_att, vecs = project(me, tokens, att_pieces)
    mixed, read, score, inv, kts, mvs = mix(packed, others(state, 1, seqs))
    layer_out, gres, gmix, even, odd = ffn(me, vecs, mixed, tokens, cotangent, ffn_pieces, ff)
    ffn_share = scatter_sum(even, odd, n, seqs)
    gq, a, u, gtot, gstate = read_back(packed, gmix, read, score, inv, kts, mvs)
    gkvc = write_back(packed, gmix, a, u, gtot, others(gstate, -1, seqs))
    even, odd = weight_grad(me, att, gq, gkvc, n)
    grad_tokens = input_grad(me, vecs, tokens, gq, gkvc, w_att, gres, n)
    att_share = scatter_sum(even, odd, n, seqs)
    gain_share = jnp.sum(att_share * first[:, : 4 * d].astype(F32), axis=1) / gain_attn.astype(F32)
    up, down, out, vec = (
        ffn_share[:, :ff],
        ffn_share[:, ff : 2 * ff],
        ffn_share[:, 2 * ff : 2 * ff + d],
        ffn_share[:, 2 * ff + d :],
    )
    down = jnp.concatenate([down[:, m * d : (m + 1) * d] for m in range(mult)], axis=0)
    return (
        layer_out,
        grad_tokens,
        att_share[:, 0:d],
        att_share[:, d : 2 * d],
        att_share[:, 2 * d : 3 * d],
        att_share[:, 3 * d :],
        out,
        up,
        down,
        gain_share,
        vec[1, :r],
        vec[2, : r * mult],
        vec[3, :r],
    )


def solution(mesh):
    tokens = P(("fsdp", "seq"), None)
    matrix = P("fsdp", None)
    vector = P("fsdp")
    return jax.shard_map(
        partial(on_device, mesh.shape["fsdp"], mesh.shape["seq"]),
        mesh=mesh,
        in_specs=(tokens,) + (matrix,) * 7 + (vector,) * 4 + (tokens,),
        out_specs=(tokens, tokens) + (matrix,) * 7 + (vector,) * 4,
        check_vma=False,
    )
```

time: 1130 us -> 313 us (0.28)
  matrix products: 310 us -> 0 us
  waiting for transfers between devices: 390 us -> 90.4 us
  blocking collectives: 204 us -> 0 us
  local copies, waits for them, and re-layouts: 123 us -> 18.6 us
  Pallas kernels: 0 us -> 99.2 us
  starting transfers between devices: 19.2 us -> 93.3 us
  other arithmetic: 34.6 us -> 8.86 us
  loops' own time: 23.3 us -> 0 us
  between operations: 17.3 us -> 1.21 us
    dot_general x132 -> x0, matrix products: 303 us -> none  [the longest x16 60.2 us: mix_block(): jnp.einsum('thm,ihm->hti', weight_scaled_rows, stored_entries, precision=...]
    reduce_scatter x7 -> x0, waiting for transfers between devices: 286 us -> none  [the longest x1 64.3 us: on_device(): lax.psum_scatter(grad_w_down.astype(jnp.bfloat16), 'fsdp', scatter_dimens...]
    all_gather x6 -> x0, blocking collectives: 124 us -> none  [the longest x1 25.1 us: on_device(): lax.all_gather(w_query, 'fsdp', axis=0, tiled=True)]
    pallas_call x0 -> x7, Pallas kernels: none -> 99.2 us  [the longest x1 31.6 us: ffn(): pl.pallas_call(partial(ffn_kernel, n, r), in_specs=[pl.BlockSpec(memory_s...]
    all_to_all x4 -> x0, waiting for transfers between devices: 94 us -> none  [the longest x1 47.4 us: on_device(): lax.all_to_all(packed, 'seq', split_axis=1, concat_axis=0, tiled=True)]
    ppermute x0 -> x50, starting transfers between devices: none -> 93.3 us  [the longest x46 88.5 us: swap(): return lax.ppermute(x, 'fsdp', [(i, i ^ mask) for i in range(n)])]
    ppermute x0 -> x50, waiting for transfers between devices: none -> 90.4 us  [the longest x46 63.6 us: swap(): return lax.ppermute(x, 'fsdp', [(i, i ^ mask) for i in range(n)])]
    unnamed x2 -> x0, blocking collectives: 61 us -> none
  transfers between devices with their start and end apart: 14 -> 50, of which waited for: 8 -> 15; matrix products, arithmetic and copies ran while one was open for 18% -> 5% of each run, Pallas kernels for 0% -> 17%
where the time goes in v1:
time: 313 us; the launch traced here: 312 us
  Pallas kernels  99.2 us (32%)
  starting transfers between devices  93.3 us (30%)
  waiting for transfers between devices  90.4 us (29%)
  local copies, waits for them, and re-layouts  18.6 us (6%)
  other arithmetic  8.86 us (3%)
    ppermute x46, starting transfers between devices, swap(): return lax.ppermute(x, 'fsdp', [(i, i ^ mask) for i in range(n)])  88.5 us
    ppermute x46, waiting for transfers between devices, swap(): return lax.ppermute(x, 'fsdp', [(i, i ^ mask) for i in range(n)])  63.6 us
    pallas_call x1, Pallas kernels, ffn(): pl.pallas_call(partial(ffn_kernel, n, r), in_specs=[pl.BlockSpec(memory_s...  31.6 us
    ppermute x2, waiting for transfers between devices, shift(): lax.ppermute(x, 'seq', [(i, i + by) for i in range(seqs) if 0 <= i + by <...  15.1 us
    pallas_call x1, Pallas kernels, mix(): pl.pallas_call(mix_kernel, grid=(t // rows,), in_specs=[row(wide), const(...  15 us
    pallas_call x1, Pallas kernels, read_back(): pl.pallas_call(read_back_kernel, grid=(t // rows,), in_specs=[row(wide),...  14.3 us
    pallas_call x1, Pallas kernels, write_back(): pl.pallas_call(write_back_kernel, grid=(t // rows,), in_specs=[row(wide),...  13.9 us
    ppermute x2, waiting for transfers between devices, scatter_sum(): lax.ppermute(total, 'seq', [(i, i ^ step) for i in range(seqs)])  11.7 us
  transfers between devices with their start and end apart: 50, of which 15 were waited for; matrix products, arithmetic and copies ran while one was open for 5% of the time, Pallas kernels for 17%

profile of v1, /device:TPU:0, one launch (start us, length us, event | category | flops | bytes accessed | tf_op | source)
XLA Modules:
  0.0 311.6 jit_solution(4104171056110783549)
XLA Ops:
  5.7 6.0 %collective-permute-start.13 = (bf16[32,2176]{1,0:T(8,128)(2,1)S(1)}, bf16[32,2176]{1,0:T(8,128)(2,1)S(1)}, u32[]{:S(2)}, u32[]{:S(2)}) collective-permute-start(bf16[32,2176]{1,0:T(8,128)(2,1)S(1)} %constant_dynamic-update-slice_fusion.refs_0_), channel_id=1, source_target_pairs={{0,28},{2,30},{4,24},{6,26},{8,20},{10,22},{12,16},{14,18},{16,12}... | collective-permute-start | bytes 417800 | tf_op jit(solution)/shard_map/ppermute | solution.py:583
  19.5 8.9 %collective-permute-start.3 = (bf16[32,2176]{1,0:T(8,128)(2,1)S(1)}, bf16[32,2176]{1,0:T(8,128)(2,1)S(1)}, u32[]{:S(2)}, u32[]{:S(2)}) collective-permute-start(bf16[32,2176]{1,0:T(8,128)(2,1)S(1)} %constant_dynamic-update-slice_fusion.refs_0_), channel_id=1, source_target_pairs={{0,8},{2,10},{4,12},{6,14},{8,0},{10,2},{12,4},{14,6},{16,24},{18,... | collective-permute-start | bytes 417800 | tf_op jit(solution)/shard_map/ppermute | solution.py:583
  30.6 3.0 collective-permute-done.9.refs_10_
  43.6 3.7 %collective-permute-start.23 = (bf16[32,4608]{1,0:T(8,128)(2,1)S(1)}, bf16[32,4608]{1,0:T(8,128)(2,1)S(1)}, u32[]{:S(2)}, u32[]{:S(2)}) collective-permute-start(bf16[32,4608]{1,0:T(8,128)(2,1)S(1)} %constant_dynamic-update-slice_fusion.5.refs_0_), channel_id=1, source_target_pairs={{0,16},{2,18},{4,20},{6,22},{8,24},{10,26},{12,28},{14,30},{16,0},... | collective-permute-start | bytes 884744 | tf_op jit(solution)/shard_map/ppermute | solution.py:583
  48.0 4.1 %collective-permute-done.29.refs_14_ = bf16[32,4608]{1,0:T(8,128)(2,1)S(1)} collective-permute-done((bf16[32,4608]{1,0:T(8,128)(2,1)S(1)}, bf16[32,4608]{1,0:T(8,128)(2,1)S(1)}, u32[]{:S(2)}, u32[]{:S(2)}) %collective-permute-start.29) | collective-permute-done | bytes 294944 | tf_op jit(solution)/shard_map/ppermute | solution.py:583
  52.1 25.4 %collective-permute-start.19 = (bf16[32,4608]{1,0:T(8,128)(2,1)S(1)}, bf16[32,4608]{1,0:T(8,128)(2,1)S(1)}, u32[]{:S(2)}, u32[]{:S(2)}) collective-permute-start(bf16[32,4608]{1,0:T(8,128)(2,1)S(1)} %constant_dynamic-update-slice_fusion.5.refs_0_), channel_id=1, source_target_pairs={{0,8},{2,10},{4,12},{6,14},{8,0},{10,2},{12,4},{14,6},{16,24},{18,... | collective-permute-start | bytes 884744 | tf_op jit(solution)/shard_map/ppermute | solution.py:583
  78.1 10.5 %collective-permute-done.25.refs_10_ = bf16[32,4608]{1,0:T(8,128)(2,1)S(1)} collective-permute-done((bf16[32,4608]{1,0:T(8,128)(2,1)S(1)}, bf16[32,4608]{1,0:T(8,128)(2,1)S(1)}, u32[]{:S(2)}, u32[]{:S(2)}) %collective-permute-start.25) | collective-permute-done | bytes 294944 | tf_op jit(solution)/shard_map/ppermute | solution.py:583
  88.7 5.0 %collective-permute-done.23.refs_8_ = bf16[32,4608]{1,0:T(8,128)(2,1)S(1)} collective-permute-done((bf16[32,4608]{1,0:T(8,128)(2,1)S(1)}, bf16[32,4608]{1,0:T(8,128)(2,1)S(1)}, u32[]{:S(2)}, u32[]{:S(2)}) %collective-permute-start.23) | collective-permute-done | bytes 294944 | tf_op jit(solution)/shard_map/ppermute | solution.py:583
  94.2 10.2 %project.1 = (bf16[1024,512]{1,0:T(8,128)(2,1)}, bf16[1024,2048]{1,0:T(8,128)(2,1)}, f32[2,136,256]{2,1,0:T(8,128)}, bf16[512,2048]{1,0:T(8,128)(2,1)}, bf16[512,128]{1,0:T(8,128)(2,1)}) custom-call(s32[1]{0:T(128)} %bitcast.me_ref, bf16[1024,512]{1,0:T(8,128)(2,1)} %tok_ref.5, bf16[32,2176]{1,0:T(8,128)(2,1)} %copy-done.11, bf16[32,2176]{1,0:T(8,128)(2,1)} %copy-done.36, ...), custom_call_target="tpu_custom_call" | custom-call | flops 2147483648 | bytes 12582912 | tf_op jit(solution)/shard_map/project/pallas_call | solution.py:169
  104.4 3.4 %collective-permute-start.15 = (f32[2,136,256]{2,1,0:T(8,128)}, f32[2,136,256]{2,1,0:T(8,128)S(1)}, u32[]{:S(2)}, u32[]{:S(2)}) collective-permute-start(f32[2,136,256]{2,1,0:T(8,128)} %get-tuple-element.38), channel_id=1, source_target_pairs={{0,1},{2,3},{4,5},{6,7},{8,9},{10,11},{12,13},{14,15},{16,17},{18,... | collective-permute-start | bytes 835592 | tf_op jit(solution)/shard_map/ppermute | solution.py:604
  108.5 5.8 %collective-permute-done.15.st_in = f32[2,136,256]{2,1,0:T(8,128)S(1)} collective-permute-done((f32[2,136,256]{2,1,0:T(8,128)}, f32[2,136,256]{2,1,0:T(8,128)S(1)}, u32[]{:S(2)}, u32[]{:S(2)}) %collective-permute-start.15) | collective-permute-done | bytes 278560 | tf_op jit(solution)/shard_map/ppermute | solution.py:604
  115.0 15.0 %mix.1 = (bf16[1024,512]{1,0:T(8,128)(2,1)}, f32[1024,512]{1,0:T(8,128)}, f32[1024,512]{1,0:T(8,128)}, f32[1024,512]{1,0:T(8,128)}, bf16[8,2,256,256]{3,2,1,0:T(8,128)(2,1)}, /*index=5*/bf16[8,2,256,256]{3,2,1,0:T(8,128)(2,1)}) custom-call(bf16[1024,2048]{1,0:T(8,128)(2,1)} %get-tuple-element.37.pack_ref, f32[2,136,256]{2,1,0:T(8,128)} %copy-done.27), custom_call_target="tpu_custom_call" | custom-call | flops 6000000000 | bytes 16777216 | tf_op jit(solution)/shard_map/mix/pallas_call | solution.py:249
  131.2 31.6 %ffn.1 = (bf16[1024,512]{1,0:T(8,128)(2,1)}, f32[1024,512]{1,0:T(8,128)}, bf16[1024,512]{1,0:T(8,128)(2,1)}, bf16[8,32,4736]{2,1,0:T(8,128)(2,1)}, bf16[8,32,4736]{2,1,0:T(8,128)(2,1)}) custom-call(s32[1]{0:T(128)} %bitcast.me_ref, bf16[512,128]{1,0:T(8,128)(2,1)} %get-tuple-element.36.vec_ref, bf16[1024,512]{1,0:T(8,128)(2,1)} %get-tuple-element.39.mixed_ref, ...), custom_call_target="tpu_custom_call" | custom-call | flops 12884901888 | bytes 20971520 | tf_op jit(solution)/shard_map/ffn/pallas_call | solution.py:373
  162.9 14.3 %read_back.1 = (bf16[1024,512]{1,0:T(8,128)(2,1)}, bf16[1024,512]{1,0:T(8,128)(2,1)}, bf16[1024,512]{1,0:T(8,128)(2,1)}, f32[1024,512]{1,0:T(8,128)}, f32[2,136,256]{2,1,0:T(8,128)}) custom-call(bf16[1024,2048]{1,0:T(8,128)(2,1)} %get-tuple-element.37.pack_ref, bf16[1024,512]{1,0:T(8,128)(2,1)} %get-tuple-element.41.gmix_ref, ...), custom_call_target="tpu_custom_call" | custom-call | flops 6000000000 | bytes 20971520 | tf_op jit(solution)/shard_map/read_back/pallas_call | solution.py:451
  178.9 9.3 %collective-permute-done.31.st_in = f32[2,136,256]{2,1,0:T(8,128)S(1)} collective-permute-done((f32[2,136,256]{2,1,0:T(8,128)}, f32[2,136,256]{2,1,0:T(8,128)S(1)}, u32[]{:S(2)}, u32[]{:S(2)}) %collective-permute-start.31) | collective-permute-done | bytes 278560 | tf_op jit(solution)/shard_map/ppermute | solution.py:604
  188.9 13.9 %write_back.1.gkvc_ref = bf16[1024,1536]{1,0:T(8,128)(2,1)} custom-call(bf16[1024,2048]{1,0:T(8,128)(2,1)} %get-tuple-element.37.pack_ref, bf16[1024,512]{1,0:T(8,128)(2,1)} %get-tuple-element.41.gmix_ref, bf16[1024,512]{1,0:T(8,128)(2,1)} %get-tuple-element.48.a_ref, bf16[1024,512]{1,0:T(8,128)(2,1)} %get-tuple-element.49.u_ref, ...), custom_call_target="tpu_custom_call" | custom-call | flops 8999999488 | bytes 16777216 | tf_op jit(solution)/shard_map/write_back/pallas_call | solution.py:510
  202.9 6.3 %weight_grad.1 = (bf16[8,32,2048]{2,1,0:T(8,128)(2,1)}, bf16[8,32,2048]{2,1,0:T(8,128)(2,1)}) custom-call(s32[1]{0:T(128)} %bitcast.me_ref, bf16[1024,512]{1,0:T(8,128)(2,1)} %get-tuple-element.54.att_ref, bf16[1024,512]{1,0:T(8,128)(2,1)} %get-tuple-element.47.gq_ref, bf16[1024,1536]{1,0:T(8,128)(2,1)} %write_back.1.gkvc_ref), custom_call_target="tpu_custom_call" | custom-call | flops 2147483648 | bytes 7340032 | tf_op jit(solution)/shard_map/weight_grad/pallas_call | solution.py:545
  216.1 3.0 collective-permute-start.39
  226.3 3.0 collective-permute-start.48
  231.8 10.4 %collective-permute-start.35 = (bf16[32,2048]{1,0:T(8,128)(2,1)}, bf16[32,2048]{1,0:T(8,128)(2,1)}, u32[]{:S(2)}, u32[]{:S(2)}) collective-permute-start(bf16[32,2048]{1,0:T(8,128)(2,1)} %get-tuple-element.73), channel_id=1, source_target_pairs={{0,12},{2,14},{4,8},{6,10},{8,4},{10,6},{12,0},{14,2},{16,28},{18,... | collective-permute-start | bytes 393224 | tf_op jit(solution)/shard_map/ppermute | solution.py:583
  245.0 7.9 %input_grad.1 = f32[1024,512]{1,0:T(8,128)} custom-call(s32[1]{0:T(128)} %bitcast.me_ref, bf16[512,128]{1,0:T(8,128)(2,1)} %get-tuple-element.36.vec_ref, bf16[1024,512]{1,0:T(8,128)(2,1)} %tok_ref.5, bf16[1024,512]{1,0:T(8,128)(2,1)} %get-tuple-element.47.gq_ref, bf16[1024,1536]{1,0:T(8,128)(2,1)} %write_back.1.gkvc_ref, ...), custom_call_target="tpu_custom_call" | custom-call | flops 2147483648 | bytes 12582912 | tf_op jit(solution)/shard_map/input_grad/pallas_call | solution.py:570
  263.0 4.4 %collective-permute-done.47 = bf16[32,4736]{1,0:T(8,128)(2,1)S(1)} collective-permute-done((bf16[32,4736]{1,0:T(8,128)(2,1)}, bf16[32,4736]{1,0:T(8,128)(2,1)S(1)}, u32[]{:S(2)}, u32[]{:S(2)}) %collective-permute-start.47) | collective-permute-done | bytes 303136 | tf_op jit(solution)/shard_map/ppermute | solution.py:583
  267.4 24.3 %collective-permute-done.46 = bf16[32,4736]{1,0:T(8,128)(2,1)S(1)} collective-permute-done((bf16[32,4736]{1,0:T(8,128)(2,1)}, bf16[32,4736]{1,0:T(8,128)(2,1)S(1)}, u32[]{:S(2)}, u32[]{:S(2)}) %collective-permute-start.46) | collective-permute-done | bytes 303136 | tf_op jit(solution)/shard_map/ppermute | solution.py:583
  296.7 11.7 %collective-permute-done.49 = f32[32,4736]{1,0:T(8,128)S(1)} collective-permute-done((f32[32,4736]{1,0:T(8,128)S(1)}, f32[32,4736]{1,0:T(8,128)S(1)}, u32[]{:S(2)}, u32[]{:S(2)}) %collective-permute-start.49) | collective-permute-done | bytes 606240 | tf_op jit(solution)/shard_map/ppermute | solution.py:598
  (199 shorter events, 69.2 us)
Async XLA Ops:
  12.0 21.6 %collective-permute-start.9 = (bf16[32,2176]{1,0:T(8,128)(2,1)S(1)}, bf16[32,2176]{1,0:T(8,128)(2,1)S(1)}, u32[]{:S(2)}, u32[]{:S(2)}) collective-permute-start(bf16[32,2176]{1,0:T(8,128)(2,1)S(1)} %constant_dynamic-update-slice_fusion.refs_0_), channel_id=1, source_target_pairs={{0,20},{2,22},{4,16},{6,18},{8,28},{10,30},{12,24},{14,26},{16,4},... | collective-permute-start | bytes 417800 | tf_op jit(solution)/shard_map/ppermute | solution.py:583
  12.7 22.8 %collective-permute-start.7 = (bf16[32,2176]{1,0:T(8,128)(2,1)S(1)}, bf16[32,2176]{1,0:T(8,128)(2,1)S(1)}, u32[]{:S(2)}, u32[]{:S(2)}) collective-permute-start(bf16[32,2176]{1,0:T(8,128)(2,1)S(1)} %constant_dynamic-update-slice_fusion.refs_0_), channel_id=1, source_target_pairs={{0,16},{2,18},{4,20},{6,22},{8,24},{10,26},{12,28},{14,30},{16,0},... | collective-permute-start | bytes 417800 | tf_op jit(solution)/shard_map/ppermute | solution.py:583
  14.8 20.8 %collective-permute-start.5 = (bf16[32,2176]{1,0:T(8,128)(2,1)S(1)}, bf16[32,2176]{1,0:T(8,128)(2,1)S(1)}, u32[]{:S(2)}, u32[]{:S(2)}) collective-permute-start(bf16[32,2176]{1,0:T(8,128)(2,1)S(1)} %constant_dynamic-update-slice_fusion.refs_0_), channel_id=1, source_target_pairs={{0,12},{2,14},{4,8},{6,10},{8,4},{10,6},{12,0},{14,2},{16,28},{18,... | collective-permute-start | bytes 417800 | tf_op jit(solution)/shard_map/ppermute | solution.py:583
  42.1 35.4 %collective-permute-start.27 = (bf16[32,4608]{1,0:T(8,128)(2,1)S(1)}, bf16[32,4608]{1,0:T(8,128)(2,1)S(1)}, u32[]{:S(2)}, u32[]{:S(2)}) collective-permute-start(bf16[32,4608]{1,0:T(8,128)(2,1)S(1)} %constant_dynamic-update-slice_fusion.5.refs_0_), channel_id=1, source_target_pairs={{0,24},{2,26},{4,28},{6,30},{8,16},{10,18},{12,20},{14,22},{16,8},... | collective-permute-start | bytes 884744 | tf_op jit(solution)/shard_map/ppermute | solution.py:583
  43.5 45.1 %collective-permute-start.25 = (bf16[32,4608]{1,0:T(8,128)(2,1)S(1)}, bf16[32,4608]{1,0:T(8,128)(2,1)S(1)}, u32[]{:S(2)}, u32[]{:S(2)}) collective-permute-start(bf16[32,4608]{1,0:T(8,128)(2,1)S(1)} %constant_dynamic-update-slice_fusion.5.refs_0_), channel_id=1, source_target_pairs={{0,20},{2,22},{4,16},{6,18},{8,28},{10,30},{12,24},{14,26},{16,4},... | collective-permute-start | bytes 884744 | tf_op jit(solution)/shard_map/ppermute | solution.py:583
  43.6 50.0 %collective-permute-start.23 = (bf16[32,4608]{1,0:T(8,128)(2,1)S(1)}, bf16[32,4608]{1,0:T(8,128)(2,1)S(1)}, u32[]{:S(2)}, u32[]{:S(2)}) collective-permute-start(bf16[32,4608]{1,0:T(8,128)(2,1)S(1)} %constant_dynamic-update-slice_fusion.5.refs_0_), channel_id=1, source_target_pairs={{0,16},{2,18},{4,20},{6,22},{8,24},{10,26},{12,28},{14,30},{16,0},... | collective-permute-start | bytes 884744 | tf_op jit(solution)/shard_map/ppermute | solution.py:583
  47.3 46.3 %collective-permute-start.21 = (bf16[32,4608]{1,0:T(8,128)(2,1)S(1)}, bf16[32,4608]{1,0:T(8,128)(2,1)S(1)}, u32[]{:S(2)}, u32[]{:S(2)}) collective-permute-start(bf16[32,4608]{1,0:T(8,128)(2,1)S(1)} %constant_dynamic-update-slice_fusion.5.refs_0_), channel_id=1, source_target_pairs={{0,12},{2,14},{4,8},{6,10},{8,4},{10,6},{12,0},{14,2},{16,28},{18,... | collective-permute-start | bytes 884744 | tf_op jit(solution)/shard_map/ppermute | solution.py:583
  52.1 52.3 %collective-permute-start.19 = (bf16[32,4608]{1,0:T(8,128)(2,1)S(1)}, bf16[32,4608]{1,0:T(8,128)(2,1)S(1)}, u32[]{:S(2)}, u32[]{:S(2)}) collective-permute-start(bf16[32,4608]{1,0:T(8,128)(2,1)S(1)} %constant_dynamic-update-slice_fusion.5.refs_0_), channel_id=1, source_target_pairs={{0,8},{2,10},{4,12},{6,14},{8,0},{10,2},{12,4},{14,6},{16,24},{18,... | collective-permute-start | bytes 884744 | tf_op jit(solution)/shard_map/ppermute | solution.py:583
  77.5 30.4 %collective-permute-start.17 = (bf16[32,4608]{1,0:T(8,128)(2,1)S(1)}, bf16[32,4608]{1,0:T(8,128)(2,1)S(1)}, u32[]{:S(2)}, u32[]{:S(2)}) collective-permute-start(bf16[32,4608]{1,0:T(8,128)(2,1)S(1)} %constant_dynamic-update-slice_fusion.5.refs_0_), channel_id=1, source_target_pairs={{0,4},{2,6},{4,0},{6,2},{8,12},{10,14},{12,8},{14,10},{16,20},{18,... | collective-permute-start | bytes 884744 | tf_op jit(solution)/shard_map/ppermute | solution.py:583
  93.7 20.6 %collective-permute-start.30 = (bf16[32,4608]{1,0:T(8,128)(2,1)S(1)}, bf16[32,4608]{1,0:T(8,128)(2,1)S(1)}, u32[]{:S(2)}, u32[]{:S(2)}) collective-permute-start(bf16[32,4608]{1,0:T(8,128)(2,1)S(1)} %collective-permute-done.29.refs_14_), channel_id=1, source_target_pairs={{0,2},{2,0},{4,6},{6,4},{8,10},{10,8},{12,14},{14,12},{16,18},{18,... | collective-permute-start | bytes 884744 | tf_op jit(solution)/shard_map/ppermute | solution.py:583
  93.7 21.1 %collective-permute-start.28 = (bf16[32,4608]{1,0:T(8,128)(2,1)S(1)}, bf16[32,4608]{1,0:T(8,128)(2,1)S(1)}, u32[]{:S(2)}, u32[]{:S(2)}) collective-permute-start(bf16[32,4608]{1,0:T(8,128)(2,1)S(1)} %collective-permute-done.27.refs_12_), channel_id=1, source_target_pairs={{0,2},{2,0},{4,6},{6,4},{8,10},{10,8},{12,14},{14,12},{16,18},{18,... | collective-permute-start | bytes 884744 | tf_op jit(solution)/shard_map/ppermute | solution.py:583
  107.9 22.2 %collective-permute-start.26 = (bf16[32,4608]{1,0:T(8,128)(2,1)S(1)}, bf16[32,4608]{1,0:T(8,128)(2,1)S(1)}, u32[]{:S(2)}, u32[]{:S(2)}) collective-permute-start(bf16[32,4608]{1,0:T(8,128)(2,1)S(1)} %collective-permute-done.25.refs_10_), channel_id=1, source_target_pairs={{0,2},{2,0},{4,6},{6,4},{8,10},{10,8},{12,14},{14,12},{16,18},{18,... | collective-permute-start | bytes 884744 | tf_op jit(solution)/shard_map/ppermute | solution.py:583
  108.0 22.1 %collective-permute-start.24 = (bf16[32,4608]{1,0:T(8,128)(2,1)S(1)}, bf16[32,4608]{1,0:T(8,128)(2,1)S(1)}, u32[]{:S(2)}, u32[]{:S(2)}) collective-permute-start(bf16[32,4608]{1,0:T(8,128)(2,1)S(1)} %collective-permute-done.23.refs_8_), channel_id=1, source_target_pairs={{0,2},{2,0},{4,6},{6,4},{8,10},{10,8},{12,14},{14,12},{16,18},{18,... | collective-permute-start | bytes 884744 | tf_op jit(solution)/shard_map/ppermute | solution.py:583
  178.5 41.4 %collective-permute-start.41 = (bf16[8,32,4736]{2,1,0:T(8,128)(2,1)}, bf16[8,32,4736]{2,1,0:T(8,128)(2,1)S(1)}, u32[]{:S(2)}, u32[]{:S(2)}) collective-permute-start(bf16[8,32,4736]{2,1,0:T(8,128)(2,1)} %get-tuple-element.58), channel_id=1, source_target_pairs={{0,2},{2,0},{4,6},{6,4},{8,10},{10,8},{12,14},{14,12},{16,18},{18,... | collective-permute-start | bytes 7274504 | tf_op jit(solution)/shard_map/ppermute | solution.py:583
  219.9 24.5 %collective-permute-start.37 = (bf16[32,2048]{1,0:T(8,128)(2,1)S(1)}, bf16[32,2048]{1,0:T(8,128)(2,1)S(1)}, u32[]{:S(2)}, u32[]{:S(2)}) collective-permute-start(bf16[32,2048]{1,0:T(8,128)(2,1)S(1)} %get-tuple-element.71), channel_id=1, source_target_pairs={{0,20},{2,22},{4,16},{6,18},{8,28},{10,30},{12,24},{14,26},{16,4},... | collective-permute-start | bytes 393224 | tf_op jit(solution)/shard_map/ppermute | solution.py:583
  224.9 34.8 %collective-permute-start.42 = (bf16[32,4736]{1,0:T(8,128)(2,1)}, bf16[32,4736]{1,0:T(8,128)(2,1)S(1)}, u32[]{:S(2)}, u32[]{:S(2)}) collective-permute-start(bf16[32,4736]{1,0:T(8,128)(2,1)} %get-tuple-element.61), channel_id=1, source_target_pairs={{0,4},{2,6},{4,0},{6,2},{8,12},{10,14},{12,8},{14,10},{16,20},{18,... | collective-permute-start | bytes 909320 | tf_op jit(solution)/shard_map/ppermute | solution.py:583
  226.3 34.3 %collective-permute-start.48 = (bf16[32,4736]{1,0:T(8,128)(2,1)}, bf16[32,4736]{1,0:T(8,128)(2,1)}, u32[]{:S(2)}, u32[]{:S(2)}) collective-permute-start(bf16[32,4736]{1,0:T(8,128)(2,1)} %get-tuple-element.62), channel_id=1, source_target_pairs={{0,28},{2,30},{4,24},{6,26},{8,20},{10,22},{12,16},{14,18},{16,12}... | collective-permute-start | bytes 909320 | tf_op jit(solution)/shard_map/ppermute | solution.py:583
  229.3 25.9 %collective-permute-start.36 = (bf16[32,2048]{1,0:T(8,128)(2,1)}, bf16[32,2048]{1,0:T(8,128)(2,1)}, u32[]{:S(2)}, u32[]{:S(2)}) collective-permute-start(bf16[32,2048]{1,0:T(8,128)(2,1)} %get-tuple-element.72), channel_id=1, source_target_pairs={{0,16},{2,18},{4,20},{6,22},{8,24},{10,26},{12,28},{14,30},{16,0},... | collective-permute-start | bytes 393224 | tf_op jit(solution)/shard_map/ppermute | solution.py:583
  231.8 24.0 %collective-permute-start.35 = (bf16[32,2048]{1,0:T(8,128)(2,1)}, bf16[32,2048]{1,0:T(8,128)(2,1)}, u32[]{:S(2)}, u32[]{:S(2)}) collective-permute-start(bf16[32,2048]{1,0:T(8,128)(2,1)} %get-tuple-element.73), channel_id=1, source_target_pairs={{0,12},{2,14},{4,8},{6,10},{8,4},{10,6},{12,0},{14,2},{16,28},{18,... | collective-permute-start | bytes 393224 | tf_op jit(solution)/shard_map/ppermute | solution.py:583
  255.8 36.0 %collective-permute-start.46 = (bf16[32,4736]{1,0:T(8,128)(2,1)}, bf16[32,4736]{1,0:T(8,128)(2,1)S(1)}, u32[]{:S(2)}, u32[]{:S(2)}) collective-permute-start(bf16[32,4736]{1,0:T(8,128)(2,1)} %get-tuple-element.64), channel_id=1, source_target_pairs={{0,20},{2,22},{4,16},{6,18},{8,28},{10,30},{12,24},{14,26},{16,4},... | collective-permute-start | bytes 909320 | tf_op jit(solution)/shard_map/ppermute | solution.py:583
  257.8 36.1 %collective-permute-start.45 = (bf16[32,4736]{1,0:T(8,128)(2,1)}, bf16[32,4736]{1,0:T(8,128)(2,1)S(1)}, u32[]{:S(2)}, u32[]{:S(2)}) collective-permute-start(bf16[32,4736]{1,0:T(8,128)(2,1)} %get-tuple-element.65), channel_id=1, source_target_pairs={{0,16},{2,18},{4,20},{6,22},{8,24},{10,26},{12,28},{14,30},{16,0},... | collective-permute-start | bytes 909320 | tf_op jit(solution)/shard_map/ppermute | solution.py:583
  259.7 34.2 %collective-permute-start.44 = (bf16[32,4736]{1,0:T(8,128)(2,1)}, bf16[32,4736]{1,0:T(8,128)(2,1)S(1)}, u32[]{:S(2)}, u32[]{:S(2)}) collective-permute-start(bf16[32,4736]{1,0:T(8,128)(2,1)} %get-tuple-element.66), channel_id=1, source_target_pairs={{0,12},{2,14},{4,8},{6,10},{8,4},{10,6},{12,0},{14,2},{16,28},{18,... | collective-permute-start | bytes 909320 | tf_op jit(solution)/shard_map/ppermute | solution.py:583
  260.6 33.3 %collective-permute-start.43 = (bf16[32,4736]{1,0:T(8,128)(2,1)S(1)}, bf16[32,4736]{1,0:T(8,128)(2,1)S(1)}, u32[]{:S(2)}, u32[]{:S(2)}) collective-permute-start(bf16[32,4736]{1,0:T(8,128)(2,1)S(1)} %get-tuple-element.67), channel_id=1, source_target_pairs={{0,8},{2,10},{4,12},{6,14},{8,0},{10,2},{12,4},{14,6},{16,24},{18,... | collective-permute-start | bytes 909320 | tf_op jit(solution)/shard_map/ppermute | solution.py:583
  267.4 27.8 %collective-permute-start.40 = (f32[32,2048]{1,0:T(8,128)S(1)}, f32[32,2048]{1,0:T(8,128)S(1)}, u32[]{:S(2)}, u32[]{:S(2)}) collective-permute-start(f32[32,2048]{1,0:T(8,128)S(1)} %fusion.11), channel_id=1, source_target_pairs={{0,1},{1,0},{2,3},{3,2},{4,5},{5,4},{6,7},{7,6},{8,9},{9,8},{10,11... | collective-permute-start | bytes 786440 | tf_op jit(solution)/shard_map/ppermute | solution.py:598
  (70 other events, 1187.3 us)

commit v2 on v1

--- a/solution.py
+++ b/solution.py
@@ -115,9 +115,60 @@
     return mm_t(wide, tile).astype(BF16)
 
 
-def project_kernel(n, r, me_ref, tok_ref, *refs):
-    pieces = refs[:n]
-    att_ref, pack_ref, st_ref, w_ref, vec_out, kt_ref, mv_ref, tot_ref, vecs, sems, vsems = refs[n:]
+def piece_refs(where, refs):
+    return [refs[a] if row is None else refs[a].at[row] for a, row in where]
+
+
+def pack_kernel(q, k, v, c, o, up, down, gain_a, gain_f, b_up, b_down, first, second):
+    r, d = q.shape
+    ff = up.shape[1]
+    for p, ref in enumerate((q, k, v, c)):
+        first[:, p * d : (p + 1) * d] = ref[...]
+    tile = jnp.zeros((r, 128), F32)
+    row, col = iota((r, 128), 0), iota((r, 128), 1)
+    for i, ref in enumerate((gain_a, gain_f, b_up, b_down)):
+        length = ref.shape[1]
+        wide = jnp.broadcast_to(ref[...].astype(F32), (r, length))
+        if length < 128:
+            wide = jnp.concatenate([wide, jnp.zeros((r, 128 - length), F32)], axis=1)
+        tile = jnp.where(row == i, wide, tile)
+    first[:, 4 * d :] = tile.astype(BF16)
+    second[:, 2 * ff + d :] = tile.astype(BF16)
+    second[:, :ff] = up[...]
+    for m in range(ff // d):
+        second[:, ff + m * d : ff + (m + 1) * d] = down[m * r : (m + 1) * r, :]
+    second[:, 2 * ff : 2 * ff + d] = o[...]
+
+
+def pack(q, k, v, c, o, up, down, gain_a, gain_f, b_up, b_down):
+    r, d = q.shape
+    ff = up.shape[1]
+    return pl.pallas_call(
+        pack_kernel,
+        out_shape=[jax.ShapeDtypeStruct((r, 4 * d + 128), BF16), jax.ShapeDtypeStruct((r, 2 * ff + d + 128), BF16)],
+        cost_estimate=pl.CostEstimate(flops=0, bytes_accessed=1 << 20, transcendentals=0),
+        name="pack",
+    )(q, k, v, c, o, up, down, *(x.reshape(1, -1) for x in (gain_a, gain_f, b_up, b_down)))
+
+
+def stack_kernel(*refs):
+    for i, ref in enumerate(refs[:-1]):
+        refs[-1][i] = ref[...]
+
+
+def stack(items):
+    return pl.pallas_call(
+        stack_kernel,
+        out_shape=jax.ShapeDtypeStruct((len(items),) + items[0].shape, items[0].dtype),
+        cost_estimate=pl.CostEstimate(flops=0, bytes_accessed=2 << 20, transcendentals=0),
+        name="stack",
+    )(*items)
+
+
+def project_kernel(where, arrays, r, me_ref, tok_ref, *refs):
+    n = len(where)
+    pieces = piece_refs(where, refs)
+    att_ref, pack_ref, st_ref, w_ref, vec_out, kt_ref, mv_ref, tot_ref, vecs, sems, vsems = refs[arrays:]
     d = w_ref.shape[0]
     wide = w_ref.shape[1]
     me = me_ref[0]
@@ -159,18 +210,18 @@
         store_state(st_ref, kt_ref, mv_ref, tot_ref)
 
 
-def project(me, tokens, pieces, rows=256):
+def project(me, tokens, where, pieces, rows=256):
     t, d = tokens.shape
-    n = len(pieces)
-    r = pieces[0].shape[0]
+    n = len(where)
+    r = d // n
     wide = 4 * d
     g = d // QUAD
     const = lambda *shape: pl.BlockSpec(shape, lambda i: (0,) * len(shape))
     return pl.pallas_call(
-        partial(project_kernel, n, r),
+        partial(project_kernel, where, len(pieces), r),
         grid=(t // rows,),
         in_specs=[pl.BlockSpec(memory_space=pltpu.SMEM), pl.BlockSpec((rows, d), lambda i: (i, 0))]
-        + [pl.BlockSpec(memory_space=pl.ANY)] * n,
+        + [pl.BlockSpec(memory_space=pl.ANY)] * len(pieces),
         out_specs=[
             pl.BlockSpec((rows, d), lambda i: (i, 0)),
             pl.BlockSpec((rows, wide), lambda i: (i, 0)),
@@ -260,33 +311,30 @@
     )(packed, state)
 
 
-def ffn_kernel(n, r, me_ref, vec_ref, mixed_ref, tok_ref, cot_ref, *refs):
-    pieces = refs[:n]
-    out_ref, gres_ref, gmix_ref, even_ref, odd_ref = refs[n : n + 5]
-    w_out, w_up, w_down, hid, gpre, fin, gbr, grads, sems, osems = refs[n + 5 :]
+def ffn_kernel(n, mixed_ref, tok_ref, cot_ref, full_ref, out_ref, gres_ref, gmix_ref, grad_ref,
+               w_out, w_up, w_down, vecs, hid, gpre, fin, gbr, sems, osems):
     t, d = mixed_ref.shape
     ff = w_up.shape[1]
-    me = me_ref[0]
+    r = d // n
     mult = ff // d
-    copies = []
-    for j in range(n):
-        own = me ^ j
-        at = pl.multiple_of(own * r, r)
-        copies.append(pltpu.make_async_copy(pieces[j].at[:, pl.ds(0, ff)], w_up.at[pl.ds(at, r), :], sems.at[0, j]))
-        for m in range(mult):
-            to = pl.multiple_of(own * r * mult + m * r, r)
-            copies.append(
-                pltpu.make_async_copy(pieces[j].at[:, pl.ds(ff + m * d, d)], w_down.at[pl.ds(to, r), :], sems.at[2 + m, j])
-            )
-        copies.append(pltpu.make_async_copy(pieces[j].at[:, pl.ds(2 * ff, d)], w_out.at[pl.ds(at, r), :], sems.at[1, j]))
+
+    def moves(hbm, sem, out):
+        yield w_up, hbm.at[:, pl.ds(0, ff)], sem.at[0]
+        yield w_out, hbm.at[:, pl.ds(2 * ff, d)], sem.at[1]
+        yield vecs, hbm.at[:, pl.ds(2 * ff + d, 128)], sem.at[2]
+        for j in range(n):
+            for m in range(mult):
+                at = (j * mult + m) * r
+                yield w_down.at[pl.ds(at, r), :], hbm.at[pl.ds(j * r, r), pl.ds(ff + m * d, d)], sem.at[3 + j * mult + m]
+
+    copies = [pltpu.make_async_copy(h, v, s) for v, h, s in moves(full_ref, sems, False)]
     for c in copies:
         c.start()
-    vecs = vec_ref[...]
-    gain = spread_vector(vecs, me, n, r, 1, r, d)
-    b_up = spread_vector(vecs, me, n, r, 2, r * mult, ff)
-    b_down = spread_vector(vecs, me, n, r, 3, r, d)
     for c in copies:
         c.wait()
+    gain = spread_vector(vecs[...], 0, n, r, 1, r, d)
+    b_up = spread_vector(vecs[...], 0, n, r, 2, r * mult, ff)
+    b_down = spread_vector(vecs[...], 0, n, r, 3, r, d)
 
     rows = 256
     part = 512
@@ -335,68 +383,51 @@
         w_up[:, ps] = t_mm(fin[...], gpre[:, ps]).astype(BF16)
         w_down[ps, :] = t_mm(hid[:, ps], cot_ref[...]).astype(BF16)
     w_out[...] = t_mm(mixed_ref[...], gbr[...]).astype(BF16)
-    va = gather_vector(ggain, me, n, r)
-    vb = gather_vector(gbup, me, n, r * mult)
-    vc = gather_vector(gbdown, me, n, r)
-    row = iota((n, r, 128), 1)
-    grads[...] = jnp.where(
-        row == 1, va[:, None, :].astype(F32),
-        jnp.where(row == 2, vb[:, None, :].astype(F32), jnp.where(row == 3, vc[:, None, :].astype(F32), 0.0)),
-    ).astype(BF16)
-    outs = []
+    va = gather_vector(ggain, 0, n, r)
+    vb = gather_vector(gbup, 0, n, r * mult)
+    vc = gather_vector(gbdown, 0, n, r)
     for j in range(n):
-        own = me ^ j
-        at = pl.multiple_of(own * r, r)
-        dst = (odd_ref if j % 2 else even_ref).at[j // 2]
-        outs.append(pltpu.make_async_copy(w_up.at[pl.ds(at, r), :], dst.at[:, pl.ds(0, ff)], osems.at[0, j]))
-        for m in range(mult):
-            frm = pl.multiple_of(own * r * mult + m * r, r)
-            outs.append(
-                pltpu.make_async_copy(w_down.at[pl.ds(frm, r), :], dst.at[:, pl.ds(ff + m * d, d)], osems.at[3 + m, j])
-            )
-        outs.append(pltpu.make_async_copy(w_out.at[pl.ds(at, r), :], dst.at[:, pl.ds(2 * ff, d)], osems.at[1, j]))
-        outs.append(pltpu.make_async_copy(grads.at[j], dst.at[:, pl.ds(2 * ff + d, 128)], osems.at[2, j]))
-    for c in outs:
+        row = iota((r, 128), 0)
+        pick = lambda v, i, rest: jnp.where(row == i, jnp.broadcast_to(v[j : j + 1].astype(F32), (r, 128)), rest)
+        tile = pick(va, 1, pick(vb, 2, pick(vc, 3, jnp.zeros((r, 128), F32))))
+        vecs[j * r : (j + 1) * r, :] = tile.astype(BF16)
+    copies = [pltpu.make_async_copy(v, h, s) for v, h, s in moves(grad_ref, osems, True)]
+    for c in copies:
         c.start()
-    for c in outs:
+    for c in copies:
         c.wait()
 
 
-def ffn(me, vecs, mixed, tokens, cot, pieces, ff):
+def ffn(mixed, tokens, cot, full, ff, n):
     t, d = tokens.shape
-    n = len(pieces)
-    r = pieces[0].shape[0]
     whole = pl.BlockSpec(memory_space=pltpu.VMEM)
     hbm = pl.BlockSpec(memory_space=pl.ANY)
-    width = 2 * ff + d + 128
-    mult = ff // d
-    return pl.pallas_call(
-        partial(ffn_kernel, n, r),
-        in_specs=[pl.BlockSpec(memory_space=pltpu.SMEM)] + [whole] * 4 + [hbm] * n,
-        out_specs=[whole] * 3 + [hbm] * 2,
+    return pl.pallas_call(
+        partial(ffn_kernel, n),
+        in_specs=[whole] * 3 + [hbm],
+        out_specs=[whole] * 3 + [hbm],
         out_shape=[
             jax.ShapeDtypeStruct((t, d), BF16),
             jax.ShapeDtypeStruct((t, d), F32),
             jax.ShapeDtypeStruct((t, d), BF16),
-            jax.ShapeDtypeStruct((n // 2, r, width), BF16),
-            jax.ShapeDtypeStruct((n // 2, r, width), BF16),
+            jax.ShapeDtypeStruct(full.shape, BF16),
         ],
         scratch_shapes=[
             pltpu.VMEM((d, d), BF16),
             pltpu.VMEM((d, ff), BF16),
             pltpu.VMEM((ff, d), BF16),
+            pltpu.VMEM((d, 128), BF16),
             pltpu.VMEM((t, ff), BF16),
             pltpu.VMEM((t, ff), BF16),
             pltpu.VMEM((t, d), BF16),
             pltpu.VMEM((t, d), BF16),
-            pltpu.VMEM((n, r, 128), BF16),
-            pltpu.SemaphoreType.DMA((2 + mult, n)),
-            pltpu.SemaphoreType.DMA((3 + mult, n)),
+            pltpu.SemaphoreType.DMA((3 + n * (ff // d),)),
+            pltpu.SemaphoreType.DMA((3 + n * (ff // d),)),
         ],
         compiler_params=pltpu.CompilerParams(vmem_limit_bytes=VMEM_LIMIT),
         cost_estimate=pl.CostEstimate(flops=12 * t * d * ff, bytes_accessed=20 << 20, transcendentals=t * ff),
         name="ffn",
-    )(me, vecs, mixed, tokens, cot, *pieces)
+    )(mixed, tokens, cot, full)
 
 
 def read_back_kernel(pack_ref, gmix_ref, read_ref, score_ref, inv_ref, kts_ref, mvs_ref,
@@ -520,7 +551,9 @@
     )(packed, gmix, a, u, gtot, state)
 
 
-def weight_grad_kernel(n, r, me_ref, att_ref, gq_ref, gkvc_ref, even_ref, odd_ref, acc, sems):
+def weight_grad_kernel(n, r, me_ref, att_ref, gq_ref, gkvc_ref, *refs):
+    share_refs = refs[:4]
+    acc, sems = refs[4:]
     d = att_ref.shape[1]
     me = me_ref[0]
     acc[:, 0:d] = t_mm(att_ref[...], gq_ref[...]).astype(BF16)
@@ -529,7 +562,7 @@
     outs = []
     for j in range(n):
         at = pl.multiple_of((me ^ j) * r, r)
-        dst = (odd_ref if j % 2 else even_ref).at[j // 2]
+        dst = share_refs[j % 4].at[j // 4]
         outs.append(pltpu.make_async_copy(acc.at[pl.ds(at, r), :], dst, sems.at[j]))
     for c in outs:
         c.start()
@@ -545,8 +578,8 @@
     return pl.pallas_call(
         partial(weight_grad_kernel, n, r),
         in_specs=[pl.BlockSpec(memory_space=pltpu.SMEM)] + [whole] * 3,
-        out_specs=[hbm] * 2,
-        out_shape=[jax.ShapeDtypeStruct((n // 2, r, 4 * d), BF16)] * 2,
+        out_specs=[hbm] * 4,
+        out_shape=[jax.ShapeDtypeStruct((n // 4, r, 4 * d), BF16)] * 4,
         scratch_shapes=[pltpu.VMEM((d, 4 * d), BF16), pltpu.SemaphoreType.DMA((n,))],
         compiler_params=pltpu.CompilerParams(vmem_limit_bytes=VMEM_LIMIT),
         cost_estimate=pl.CostEstimate(flops=8 * t * d * d, bytes_accessed=7 << 20, transcendentals=0),
@@ -583,21 +616,20 @@
     return lax.ppermute(x, "fsdp", [(i, i ^ mask) for i in range(n)])
 
 
-def gather(shard, n):
-    even = [shard] + [swap(shard, 2 * i, n) for i in range(1, n // 2)]
-    odd = [swap(x, 1, n) for x in even]
-    return [x for pair in zip(even, odd) for x in pair]
-
-
-def scatter_sum(even, odd, n, seqs):
-    mine = (even.astype(F32) + swap(odd, 1, n).astype(F32)).astype(BF16)
-    parts = [mine[0]] + [swap(mine[i], 2 * i, n) for i in range(1, n // 2)]
-    total = sum(p.astype(F32) for p in parts)
-    step = 1
-    while step < seqs:
-        total = total + lax.ppermute(total, "seq", [(i, i ^ step) for i in range(seqs)])
-        step *= 2
-    return total
+def after(x, *first):
+    return lax.optimization_barrier((x, *first))[0]
+
+
+def add(*items):
+    return sum(x.astype(F32) for x in items).astype(BF16)
+
+
+def along_z(shard, n):
+    return [shard] + [swap(shard, 4 * k, n) for k in range(1, n // 4)]
+
+
+def along_x(own, n):
+    return [swap(x, 2, n) for x in own]
 
 
 def shift(x, by, seqs):
@@ -621,21 +653,39 @@
     ff = w_up.shape[1]
     mult = ff // d
     me = lax.axis_index("fsdp").astype(jnp.int32).reshape(1)
-    lanes = lambda v: jnp.pad(v, (0, 128 - v.shape[0]))
-    vec = jnp.pad(jnp.stack([lanes(gain_attn), lanes(gain_ffn), lanes(bias_up), lanes(bias_down)]), ((0, r - 4), (0, 0)))
-    first = jnp.concatenate([w_query, w_key, w_value, w_control, vec], axis=1)
-    second = jnp.concatenate([w_up] + [w_down[m * r : (m + 1) * r] for m in range(mult)] + [w_out], axis=1)
-    att_pieces = gather(first, n)
-    ffn_pieces = gather(second, n)
-    att, packed, state, w_att, vecs = project(me, tokens, att_pieces)
+    first, second = pack(w_query, w_key, w_value, w_control, w_out, w_up, w_down, gain_attn, gain_ffn, bias_up, bias_down)
+    depth = n // 4
+    own = along_z(first, n)
+    full = lax.all_gather(second, "fsdp", axis=0, tiled=True)
+    across = along_x(own, n)
+    cored = [[swap(x, 1, n) for x in group] for group in (own, across)]
+    att_pieces = [x for quad in zip(own, cored[0], across, cored[1]) for x in quad]
+    att_where = [(j, None) for j in range(n)]
+    att, packed, state, w_att, vecs = project(me, tokens, att_where, att_pieces)
     mixed, read, score, inv, kts, mvs = mix(packed, others(state, 1, seqs))
-    layer_out, gres, gmix, even, odd = ffn(me, vecs, mixed, tokens, cotangent, ffn_pieces, ff)
-    ffn_share = scatter_sum(even, odd, n, seqs)
+    layer_out, gres, gmix, ffn_grad = ffn(mixed, tokens, cotangent, full, ff, n)
+    ffn_sum = lax.psum_scatter(ffn_grad, "fsdp", scatter_dimension=0, tiled=True)
+
+    def core_sum(shares):
+        near, near_core, far, far_core = shares
+        return add(near, swap(near_core, 1, n)), add(far, swap(far_core, 1, n))
+
+    def seq_sum(x):
+        step = 1
+        while step < seqs:
+            x = add(x, lax.ppermute(x, "seq", [(i, i ^ step) for i in range(seqs)]))
+            step *= 2
+        return x.astype(F32)
+
     gq, a, u, gtot, gstate = read_back(packed, gmix, read, score, inv, kts, mvs)
     gkvc = write_back(packed, gmix, a, u, gtot, others(gstate, -1, seqs))
-    even, odd = weight_grad(me, att, gq, gkvc, n)
-    grad_tokens = input_grad(me, vecs, tokens, gq, gkvc, w_att, gres, n)
-    att_share = scatter_sum(even, odd, n, seqs)
+    shares = weight_grad(me, att, gq, gkvc, n)
+    near, far = core_sum(shares)
+    grad_tokens = input_grad(me, vecs, tokens, after(gq, near, far), gkvc, w_att, gres, n)
+    mine = {k: add(near[k], swap(far[k], 2, n)) for k in range(depth - 1, -1, -1)}
+    sent = {k: swap(mine[k], 4 * k, n) if k else mine[k] for k in range(depth)}
+    ffn_share = seq_sum(ffn_sum)
+    att_share = seq_sum(add(*sent.values()))
     gain_share = jnp.sum(att_share * first[:, : 4 * d].astype(F32), axis=1) / gain_attn.astype(F32)
     up, down, out, vec = (
         ffn_share[:, :ff],

time: 313 us -> 225 us (0.72)
  starting transfers between devices: 93.3 us -> 29.4 us
  waiting for transfers between devices: 90.4 us -> 70.9 us
  local copies, waits for them, and re-layouts: 18.6 us -> 5.17 us
  between operations: 1.21 us -> 14.4 us
  other arithmetic: 8.86 us -> 3.91 us
    ppermute x46 -> x24, starting transfers between devices: 88.5 us -> 21.9 us  [swap(): return lax.ppermute(x, 'fsdp', [(i, i ^ mask) for i in range(n)])]
    ppermute x46 -> x24, waiting for transfers between devices: 63.6 us -> 50.7 us  [swap(): return lax.ppermute(x, 'fsdp', [(i, i ^ mask) for i in range(n)])]
    unnamed x97 -> x40, local copies, waits for them, and re-layouts: 11.3 us -> 2.02 us
    ppermute x2, waiting for transfers between devices: 11.7 us -> 4.88 us  [seq_sum(): x = add(x, lax.ppermute(x, 'seq', [(i, i ^ step) for i in range(seqs)]))]
    pallas_call x2 -> x3, Pallas kernels: 41.8 us -> 43.2 us  [the longest x1 30.8 us: ffn(): pl.pallas_call(partial(ffn_kernel, n), in_specs=[whole] * 3 + [hbm], out_...]
  transfers between devices with their start and end apart: 50 -> 30, of which waited for: 15 -> 15; matrix products, arithmetic and copies ran while one was open for 5% -> 1% of each run, Pallas kernels for 17% -> 30%
where the time goes in v2:
time: 225 us; the launch traced here: 224 us
  Pallas kernels  100 us (44%)
  waiting for transfers between devices  70.9 us (32%)
  starting transfers between devices  29.4 us (13%)
  between operations  14.4 us (6%)
  local copies, waits for them, and re-layouts  5.17 us (2%)
  other arithmetic  3.91 us (2%)
    ppermute x24, waiting for transfers between devices, swap(): return lax.ppermute(x, 'fsdp', [(i, i ^ mask) for i in range(n)])  50.7 us
    pallas_call x1, Pallas kernels, ffn(): pl.pallas_call(partial(ffn_kernel, n), in_specs=[whole] * 3 + [hbm], out_...  30.8 us
    ppermute x24, starting transfers between devices, swap(): return lax.ppermute(x, 'fsdp', [(i, i ^ mask) for i in range(n)])  21.9 us
    ppermute x2, waiting for transfers between devices, shift(): lax.ppermute(x, 'seq', [(i, i + by) for i in range(seqs) if 0 <= i + by <...  15.2 us
    pallas_call x1, Pallas kernels, mix(): pl.pallas_call(mix_kernel, grid=(t // rows,), in_specs=[row(wide), const(...  14.8 us
    pallas_call x1, Pallas kernels, read_back(): pl.pallas_call(read_back_kernel, grid=(t // rows,), in_specs=[row(wide),...  14.2 us
    pallas_call x1, Pallas kernels, write_back(): pl.pallas_call(write_back_kernel, grid=(t // rows,), in_specs=[row(wide),...  13.9 us
    pallas_call x1, Pallas kernels, project(): pl.pallas_call(partial(project_kernel, where, len(pieces), r), grid=(t //...  10.4 us
  transfers between devices with their start and end apart: 30, of which 15 were waited for; matrix products, arithmetic and copies ran while one was open for 1% of the time, Pallas kernels for 30%

profile of v2, /device:TPU:0, one launch (start us, length us, event | category | flops | bytes accessed | tf_op | source)
XLA Modules:
  0.0 224.2 jit_solution(1819929466423414860)
XLA Ops:
  9.2 5.1 %collective-permute-start.11 = (bf16[32,2176]{1,0:T(8,128)(2,1)}, bf16[32,2176]{1,0:T(8,128)(2,1)S(1)}, u32[]{:S(2)}, u32[]{:S(2)}) collective-permute-start(bf16[32,2176]{1,0:T(8,128)(2,1)} %get-tuple-element.40.refs_0_), channel_id=1, source_target_pairs={{0,24},{2,26},{4,28},{6,30},{8,16},{10,18},{12,20},{14,22},{16,8},... | collective-permute-start | bytes 417800 | tf_op jit(solution)/shard_map/ppermute | solution.py:616
  16.6 2.5 %collective-permute-done.11.refs_12_ = bf16[32,2176]{1,0:T(8,128)(2,1)S(1)} collective-permute-done((bf16[32,2176]{1,0:T(8,128)(2,1)}, bf16[32,2176]{1,0:T(8,128)(2,1)S(1)}, u32[]{:S(2)}, u32[]{:S(2)}) %collective-permute-start.11) | collective-permute-done | bytes 139296 | tf_op jit(solution)/shard_map/ppermute | solution.py:616
  20.8 8.6 %collective-permute-done.7.refs_8_ = bf16[32,2176]{1,0:T(8,128)(2,1)S(1)} collective-permute-done((bf16[32,2176]{1,0:T(8,128)(2,1)}, bf16[32,2176]{1,0:T(8,128)(2,1)S(1)}, u32[]{:S(2)}, u32[]{:S(2)}) %collective-permute-start.7) | collective-permute-done | bytes 139296 | tf_op jit(solution)/shard_map/ppermute | solution.py:616
  32.2 3.7 %collective-permute-done.9.refs_10_ = bf16[32,2176]{1,0:T(8,128)(2,1)S(1)} collective-permute-done((bf16[32,2176]{1,0:T(8,128)(2,1)S(1)}, bf16[32,2176]{1,0:T(8,128)(2,1)S(1)}, u32[]{:S(2)}, u32[]{:S(2)}) %collective-permute-start.9) | collective-permute-done | bytes 139296 | tf_op jit(solution)/shard_map/ppermute | solution.py:616
  36.5 2.0 collective-permute-done.5.refs_6_
  40.5 10.4 %project.1 = (bf16[1024,512]{1,0:T(8,128)(2,1)}, bf16[1024,2048]{1,0:T(8,128)(2,1)}, f32[2,136,256]{2,1,0:T(8,128)}, bf16[512,2048]{1,0:T(8,128)(2,1)}, bf16[512,128]{1,0:T(8,128)(2,1)}) custom-call(s32[1]{0:T(128)} %bitcast.me_ref, bf16[1024,512]{1,0:T(8,128)(2,1)} %tok_ref.5, bf16[32,2176]{1,0:T(8,128)(2,1)} %get-tuple-element.40.refs_0_, ...), custom_call_target="tpu_custom_call" | custom-call | flops 2147483648 | bytes 12582912 | tf_op jit(solution)/shard_map/project/pallas_call | solution.py:220
  51.0 4.0 %collective-permute-start.15 = (f32[2,136,256]{2,1,0:T(8,128)}, f32[2,136,256]{2,1,0:T(8,128)S(1)}, u32[]{:S(2)}, u32[]{:S(2)}) collective-permute-start(f32[2,136,256]{2,1,0:T(8,128)} %get-tuple-element.42), channel_id=1, source_target_pairs={{0,1},{2,3},{4,5},{6,7},{8,9},{10,11},{12,13},{14,15},{16,17},{18,... | collective-permute-start | bytes 835592 | tf_op jit(solution)/shard_map/ppermute | solution.py:636
  54.9 6.4 %collective-permute-done.15.st_in = f32[2,136,256]{2,1,0:T(8,128)S(1)} collective-permute-done((f32[2,136,256]{2,1,0:T(8,128)}, f32[2,136,256]{2,1,0:T(8,128)S(1)}, u32[]{:S(2)}, u32[]{:S(2)}) %collective-permute-start.15) | collective-permute-done | bytes 278560 | tf_op jit(solution)/shard_map/ppermute | solution.py:636
  62.0 14.8 %mix.1 = (bf16[1024,512]{1,0:T(8,128)(2,1)}, f32[1024,512]{1,0:T(8,128)}, f32[1024,512]{1,0:T(8,128)}, f32[1024,512]{1,0:T(8,128)}, bf16[8,2,256,256]{3,2,1,0:T(8,128)(2,1)}, /*index=5*/bf16[8,2,256,256]{3,2,1,0:T(8,128)(2,1)}) custom-call(bf16[1024,2048]{1,0:T(8,128)(2,1)} %get-tuple-element.41.pack_ref, f32[2,136,256]{2,1,0:T(8,128)} %copy-done.3), custom_call_target="tpu_custom_call" | custom-call | flops 6000000000 | bytes 16777216 | tf_op jit(solution)/shard_map/mix/pallas_call | solution.py:300
  76.9 30.8 %ffn.1 = (bf16[1024,512]{1,0:T(8,128)(2,1)}, f32[1024,512]{1,0:T(8,128)}, bf16[1024,512]{1,0:T(8,128)(2,1)}, bf16[512,4736]{1,0:T(8,128)(2,1)}) custom-call(bf16[1024,512]{1,0:T(8,128)(2,1)} %get-tuple-element.43.mixed_ref, bf16[1024,512]{1,0:T(8,128)(2,1)} %tok_ref.5, bf16[1024,512]{1,0:T(8,128)(2,1)} %cot_ref.1, ...), custom_call_target="tpu_custom_call" | custom-call | flops 12884901888 | bytes 20971520 | tf_op jit(solution)/shard_map/ffn/pallas_call | solution.py:405
  107.7 14.2 %read_back.1 = (bf16[1024,512]{1,0:T(8,128)(2,1)}, bf16[1024,512]{1,0:T(8,128)(2,1)}, bf16[1024,512]{1,0:T(8,128)(2,1)}, f32[1024,512]{1,0:T(8,128)}, f32[2,136,256]{2,1,0:T(8,128)}) custom-call(bf16[1024,2048]{1,0:T(8,128)(2,1)} %get-tuple-element.41.pack_ref, bf16[1024,512]{1,0:T(8,128)(2,1)} %get-tuple-element.47.gmix_ref, ...), custom_call_target="tpu_custom_call" | custom-call | flops 6000000000 | bytes 20971520 | tf_op jit(solution)/shard_map/read_back/pallas_call | solution.py:482
  123.3 8.9 %collective-permute-done.16.st_in = f32[2,136,256]{2,1,0:T(8,128)S(1)} collective-permute-done((f32[2,136,256]{2,1,0:T(8,128)}, f32[2,136,256]{2,1,0:T(8,128)S(1)}, u32[]{:S(2)}, u32[]{:S(2)}) %collective-permute-start.16) | collective-permute-done | bytes 278560 | tf_op jit(solution)/shard_map/ppermute | solution.py:636
  132.9 13.9 %write_back.1.gkvc_ref = bf16[1024,1536]{1,0:T(8,128)(2,1)} custom-call(bf16[1024,2048]{1,0:T(8,128)(2,1)} %get-tuple-element.41.pack_ref, bf16[1024,512]{1,0:T(8,128)(2,1)} %get-tuple-element.47.gmix_ref, bf16[1024,512]{1,0:T(8,128)(2,1)} %get-tuple-element.55.a_ref, bf16[1024,512]{1,0:T(8,128)(2,1)} %get-tuple-element.56.u_ref, ...), custom_call_target="tpu_custom_call" | custom-call | flops 8999999488 | bytes 16777216 | tf_op jit(solution)/shard_map/write_back/pallas_call | solution.py:541
  146.8 6.4 %weight_grad.1 = (bf16[4,32,2048]{2,1,0:T(8,128)(2,1)}, bf16[4,32,2048]{2,1,0:T(8,128)(2,1)}, bf16[4,32,2048]{2,1,0:T(8,128)(2,1)}, bf16[4,32,2048]{2,1,0:T(8,128)(2,1)}) custom-call(s32[1]{0:T(128)} %bitcast.me_ref, bf16[1024,512]{1,0:T(8,128)(2,1)} %get-tuple-element.54.att_ref, bf16[1024,512]{1,0:T(8,128)(2,1)} %get-tuple-element.63.gq_ref, ...), custom_call_target="tpu_custom_call" | custom-call | flops 2147483648 | bytes 7340032 | tf_op jit(solution)/shard_map/weight_grad/pallas_call | solution.py:578
  160.9 5.0 %collective-permute-done.24 = bf16[32,2048]{1,0:T(8,128)(2,1)S(1)} collective-permute-done((bf16[32,2048]{1,0:T(8,128)(2,1)S(1)}, bf16[32,2048]{1,0:T(8,128)(2,1)S(1)}, u32[]{:S(2)}, u32[]{:S(2)}) %collective-permute-start.24) | collective-permute-done | bytes 131104 | tf_op jit(solution)/shard_map/ppermute | solution.py:616
  165.8 2.8 %collective-permute-done.22 = bf16[32,2048]{1,0:T(8,128)(2,1)S(1)} collective-permute-done((bf16[32,2048]{1,0:T(8,128)(2,1)S(1)}, bf16[32,2048]{1,0:T(8,128)(2,1)S(1)}, u32[]{:S(2)}, u32[]{:S(2)}) %collective-permute-start.22) | collective-permute-done | bytes 131104 | tf_op jit(solution)/shard_map/ppermute | solution.py:616
  168.6 2.0 collective-permute-done.20
  171.9 3.3 %collective-permute-start.25 = (bf16[32,2048]{1,0:T(8,128)(2,1)S(1)}, bf16[32,2048]{1,0:T(8,128)(2,1)S(1)}, u32[]{:S(2)}, u32[]{:S(2)}) collective-permute-start(bf16[32,2048]{1,0:T(8,128)(2,1)S(1)} %get-tuple-element.79), channel_id=1, source_target_pairs={{0,24},{2,26},{4,28},{6,30},{8,16},{10,18},{12,20},{14,22},{16,8},... | collective-permute-start | bytes 393224 | tf_op jit(solution)/shard_map/ppermute | solution.py:616
  175.6 1.9 collective-permute-done.21
  177.5 9.8 %collective-permute-done.25 = bf16[32,2048]{1,0:T(8,128)(2,1)S(1)} collective-permute-done((bf16[32,2048]{1,0:T(8,128)(2,1)S(1)}, bf16[32,2048]{1,0:T(8,128)(2,1)S(1)}, u32[]{:S(2)}, u32[]{:S(2)}) %collective-permute-start.25) | collective-permute-done | bytes 131104 | tf_op jit(solution)/shard_map/ppermute | solution.py:616
  187.3 9.4 %collective-permute-done.23 = bf16[32,2048]{1,0:T(8,128)(2,1)S(1)} collective-permute-done((bf16[32,2048]{1,0:T(8,128)(2,1)S(1)}, bf16[32,2048]{1,0:T(8,128)(2,1)S(1)}, u32[]{:S(2)}, u32[]{:S(2)}) %collective-permute-start.23) | collective-permute-done | bytes 131104 | tf_op jit(solution)/shard_map/ppermute | solution.py:616
  196.9 7.9 %input_grad.1 = f32[1024,512]{1,0:T(8,128)} custom-call(s32[1]{0:T(128)} %bitcast.me_ref, bf16[512,128]{1,0:T(8,128)(2,1)} %get-tuple-element.46.vec_ref, bf16[1024,512]{1,0:T(8,128)(2,1)} %tok_ref.5, bf16[1024,512]{1,0:T(8,128)(2,1)} %get-tuple-element.63.gq_ref, bf16[1024,1536]{1,0:T(8,128)(2,1)} %write_back.1.gkvc_ref, ...), custom_call_target="tpu_custom_call" | custom-call | flops 2147483648 | bytes 12582912 | tf_op jit(solution)/shard_map/input_grad/pallas_call | solution.py:603
  205.0 2.0 collective-permute-start.27
  208.3 4.9 %collective-permute-done.27 = bf16[32,4736]{1,0:T(8,128)(2,1)S(1)} collective-permute-done((bf16[32,4736]{1,0:T(8,128)(2,1)}, bf16[32,4736]{1,0:T(8,128)(2,1)S(1)}, u32[]{:S(2)}, u32[]{:S(2)}) %collective-permute-start.27) | collective-permute-done | bytes 303136 | tf_op jit(solution)/shard_map/ppermute | solution.py:676
  (100 shorter events, 29.0 us)
Async XLA Ops:
  7.2 69.7 %all-gather.2.cloned.1.call-start = ((), (), s32[]{:S(2)}) async-start(), calls=%async_computation.1 | async-start | bytes 5152768 | tf_op jit(solution)/shard_map/all_gather | solution.py:659
  9.1 195.9 %reduce-scatter.2.cloned.1.call-start = ((), (), s32[]{:S(2)}) async-start(), calls=%async_computation.2 | async-start | bytes 5152768 | tf_op jit(solution)/shard_map/reduce_scatter | solution.py:667
  9.2 9.9 %collective-permute-start.11 = (bf16[32,2176]{1,0:T(8,128)(2,1)}, bf16[32,2176]{1,0:T(8,128)(2,1)S(1)}, u32[]{:S(2)}, u32[]{:S(2)}) collective-permute-start(bf16[32,2176]{1,0:T(8,128)(2,1)} %get-tuple-element.40.refs_0_), channel_id=1, source_target_pairs={{0,24},{2,26},{4,28},{6,30},{8,16},{10,18},{12,20},{14,22},{16,8},... | collective-permute-start | bytes 417800 | tf_op jit(solution)/shard_map/ppermute | solution.py:616
  14.3 15.1 %collective-permute-start.7 = (bf16[32,2176]{1,0:T(8,128)(2,1)}, bf16[32,2176]{1,0:T(8,128)(2,1)S(1)}, u32[]{:S(2)}, u32[]{:S(2)}) collective-permute-start(bf16[32,2176]{1,0:T(8,128)(2,1)} %get-tuple-element.40.refs_0_), channel_id=1, source_target_pairs={{0,16},{2,18},{4,20},{6,22},{8,24},{10,26},{12,28},{14,30},{16,0},... | collective-permute-start | bytes 417800 | tf_op jit(solution)/shard_map/ppermute | solution.py:616
  14.3 15.1 %collective-permute-start.3 = (bf16[32,2176]{1,0:T(8,128)(2,1)}, bf16[32,2176]{1,0:T(8,128)(2,1)S(1)}, u32[]{:S(2)}, u32[]{:S(2)}) collective-permute-start(bf16[32,2176]{1,0:T(8,128)(2,1)} %get-tuple-element.40.refs_0_), channel_id=1, source_target_pairs={{0,8},{2,10},{4,12},{6,14},{8,0},{10,2},{12,4},{14,6},{16,24},{18,... | collective-permute-start | bytes 417800 | tf_op jit(solution)/shard_map/ppermute | solution.py:616
  14.9 16.3 %collective-permute-start.1 = (bf16[32,2176]{1,0:T(8,128)(2,1)}, bf16[32,2176]{1,0:T(8,128)(2,1)S(1)}, u32[]{:S(2)}, u32[]{:S(2)}) collective-permute-start(bf16[32,2176]{1,0:T(8,128)(2,1)} %get-tuple-element.40.refs_0_), channel_id=1, source_target_pairs={{0,4},{2,6},{4,0},{6,2},{8,12},{10,14},{12,8},{14,10},{16,20},{18,... | collective-permute-start | bytes 417800 | tf_op jit(solution)/shard_map/ppermute | solution.py:616
  16.6 14.8 %collective-permute-start = (bf16[32,2176]{1,0:T(8,128)(2,1)}, bf16[32,2176]{1,0:T(8,128)(2,1)S(1)}, u32[]{:S(2)}, u32[]{:S(2)}) collective-permute-start(bf16[32,2176]{1,0:T(8,128)(2,1)} %get-tuple-element.40.refs_0_), channel_id=1, source_target_pairs={{0,2},{2,0},{4,6},{6,4},{8,10},{10,8},{12,14},{14,12},{16,18},{18,... | collective-permute-start | bytes 417800 | tf_op jit(solution)/shard_map/ppermute | solution.py:616
  19.1 12.6 %collective-permute-start.13 = (bf16[32,2176]{1,0:T(8,128)(2,1)S(1)}, bf16[32,2176]{1,0:T(8,128)(2,1)S(1)}, u32[]{:S(2)}, u32[]{:S(2)}) collective-permute-start(bf16[32,2176]{1,0:T(8,128)(2,1)S(1)} %collective-permute-done.11.refs_12_), channel_id=1, source_target_pairs={{0,4},{2,6},{4,0},{6,2},{8,12},{10,14},{12,8},{14,10},{16,20},{18,... | collective-permute-start | bytes 417800 | tf_op jit(solution)/shard_map/ppermute | solution.py:616
  29.4 6.5 %collective-permute-start.9 = (bf16[32,2176]{1,0:T(8,128)(2,1)S(1)}, bf16[32,2176]{1,0:T(8,128)(2,1)S(1)}, u32[]{:S(2)}, u32[]{:S(2)}) collective-permute-start(bf16[32,2176]{1,0:T(8,128)(2,1)S(1)} %collective-permute-done.7.refs_8_), channel_id=1, source_target_pairs={{0,4},{2,6},{4,0},{6,2},{8,12},{10,14},{12,8},{14,10},{16,20},{18,... | collective-permute-start | bytes 417800 | tf_op jit(solution)/shard_map/ppermute | solution.py:616
  31.4 7.2 %collective-permute-start.5 = (bf16[32,2176]{1,0:T(8,128)(2,1)S(1)}, bf16[32,2176]{1,0:T(8,128)(2,1)S(1)}, u32[]{:S(2)}, u32[]{:S(2)}) collective-permute-start(bf16[32,2176]{1,0:T(8,128)(2,1)S(1)} %collective-permute-done.3.refs_4_), channel_id=1, source_target_pairs={{0,4},{2,6},{4,0},{6,2},{8,12},{10,14},{12,8},{14,10},{16,20},{18,... | collective-permute-start | bytes 417800 | tf_op jit(solution)/shard_map/ppermute | solution.py:616
  31.7 6.8 %collective-permute-start.4 = (bf16[32,2176]{1,0:T(8,128)(2,1)S(1)}, bf16[32,2176]{1,0:T(8,128)(2,1)S(1)}, u32[]{:S(2)}, u32[]{:S(2)}) collective-permute-start(bf16[32,2176]{1,0:T(8,128)(2,1)S(1)} %collective-permute-done.3.refs_4_), channel_id=1, source_target_pairs={{0,2},{2,0},{4,6},{6,4},{8,10},{10,8},{12,14},{14,12},{16,18},{18,... | collective-permute-start | bytes 417800 | tf_op jit(solution)/shard_map/ppermute | solution.py:616
  31.8 6.7 %collective-permute-start.2 = (bf16[32,2176]{1,0:T(8,128)(2,1)S(1)}, bf16[32,2176]{1,0:T(8,128)(2,1)S(1)}, u32[]{:S(2)}, u32[]{:S(2)}) collective-permute-start(bf16[32,2176]{1,0:T(8,128)(2,1)S(1)} %collective-permute-done.1.refs_2_), channel_id=1, source_target_pairs={{0,2},{2,0},{4,6},{6,4},{8,10},{10,8},{12,14},{14,12},{16,18},{18,... | collective-permute-start | bytes 417800 | tf_op jit(solution)/shard_map/ppermute | solution.py:616
  51.0 10.3 %collective-permute-start.15 = (f32[2,136,256]{2,1,0:T(8,128)}, f32[2,136,256]{2,1,0:T(8,128)S(1)}, u32[]{:S(2)}, u32[]{:S(2)}) collective-permute-start(f32[2,136,256]{2,1,0:T(8,128)} %get-tuple-element.42), channel_id=1, source_target_pairs={{0,1},{2,3},{4,5},{6,7},{8,9},{10,11},{12,13},{14,15},{16,17},{18,... | collective-permute-start | bytes 835592 | tf_op jit(solution)/shard_map/ppermute | solution.py:636
  122.0 10.2 %collective-permute-start.16 = (f32[2,136,256]{2,1,0:T(8,128)}, f32[2,136,256]{2,1,0:T(8,128)S(1)}, u32[]{:S(2)}, u32[]{:S(2)}) collective-permute-start(f32[2,136,256]{2,1,0:T(8,128)} %get-tuple-element.58), channel_id=1, source_target_pairs={{1,0},{3,2},{5,4},{7,6},{9,8},{11,10},{13,12},{15,14},{17,16},{19,... | collective-permute-start | bytes 835592 | tf_op jit(solution)/shard_map/ppermute | solution.py:636
  153.3 7.5 %collective-permute-start.17 = (bf16[4,32,2048]{2,1,0:T(8,128)(2,1)}, bf16[4,32,2048]{2,1,0:T(8,128)(2,1)S(1)}, u32[]{:S(2)}, u32[]{:S(2)}) collective-permute-start(bf16[4,32,2048]{2,1,0:T(8,128)(2,1)} %get-tuple-element.60), channel_id=1, source_target_pairs={{0,2},{2,0},{4,6},{6,4},{8,10},{10,8},{12,14},{14,12},{16,18},{18,... | collective-permute-start | bytes 1572872 | tf_op jit(solution)/shard_map/ppermute | solution.py:616
  156.6 19.0 %collective-permute-start.19 = (bf16[32,2048]{1,0:T(8,128)(2,1)S(1)}, bf16[32,2048]{1,0:T(8,128)(2,1)S(1)}, u32[]{:S(2)}, u32[]{:S(2)}) collective-permute-start(bf16[32,2048]{1,0:T(8,128)(2,1)S(1)} %get-tuple-element.74), channel_id=1, source_target_pairs={{0,4},{2,6},{4,0},{6,2},{8,12},{10,14},{12,8},{14,10},{16,20},{18,... | collective-permute-start | bytes 393224 | tf_op jit(solution)/shard_map/ppermute | solution.py:616
  158.1 7.7 %collective-permute-start.24 = (bf16[32,2048]{1,0:T(8,128)(2,1)S(1)}, bf16[32,2048]{1,0:T(8,128)(2,1)S(1)}, u32[]{:S(2)}, u32[]{:S(2)}) collective-permute-start(bf16[32,2048]{1,0:T(8,128)(2,1)S(1)} %get-tuple-element.75), channel_id=1, source_target_pairs={{0,4},{2,6},{4,0},{6,2},{8,12},{10,14},{12,8},{14,10},{16,20},{18,... | collective-permute-start | bytes 393224 | tf_op jit(solution)/shard_map/ppermute | solution.py:616
  158.7 9.9 %collective-permute-start.22 = (bf16[32,2048]{1,0:T(8,128)(2,1)S(1)}, bf16[32,2048]{1,0:T(8,128)(2,1)S(1)}, u32[]{:S(2)}, u32[]{:S(2)}) collective-permute-start(bf16[32,2048]{1,0:T(8,128)(2,1)S(1)} %get-tuple-element.76), channel_id=1, source_target_pairs={{0,4},{2,6},{4,0},{6,2},{8,12},{10,14},{12,8},{14,10},{16,20},{18,... | collective-permute-start | bytes 393224 | tf_op jit(solution)/shard_map/ppermute | solution.py:616
  160.1 10.5 %collective-permute-start.20 = (bf16[32,2048]{1,0:T(8,128)(2,1)S(1)}, bf16[32,2048]{1,0:T(8,128)(2,1)S(1)}, u32[]{:S(2)}, u32[]{:S(2)}) collective-permute-start(bf16[32,2048]{1,0:T(8,128)(2,1)S(1)} %get-tuple-element.77), channel_id=1, source_target_pairs={{0,4},{2,6},{4,0},{6,2},{8,12},{10,14},{12,8},{14,10},{16,20},{18,... | collective-permute-start | bytes 393224 | tf_op jit(solution)/shard_map/ppermute | solution.py:616
  170.7 6.8 %collective-permute-start.21 = (bf16[32,2048]{1,0:T(8,128)(2,1)S(1)}, bf16[32,2048]{1,0:T(8,128)(2,1)S(1)}, u32[]{:S(2)}, u32[]{:S(2)}) collective-permute-start(bf16[32,2048]{1,0:T(8,128)(2,1)S(1)} %get-tuple-element.78), channel_id=1, source_target_pairs={{0,8},{2,10},{4,12},{6,14},{8,0},{10,2},{12,4},{14,6},{16,24},{18,... | collective-permute-start | bytes 393224 | tf_op jit(solution)/shard_map/ppermute | solution.py:616
  171.9 15.5 %collective-permute-start.25 = (bf16[32,2048]{1,0:T(8,128)(2,1)S(1)}, bf16[32,2048]{1,0:T(8,128)(2,1)S(1)}, u32[]{:S(2)}, u32[]{:S(2)}) collective-permute-start(bf16[32,2048]{1,0:T(8,128)(2,1)S(1)} %get-tuple-element.79), channel_id=1, source_target_pairs={{0,24},{2,26},{4,28},{6,30},{8,16},{10,18},{12,20},{14,22},{16,8},... | collective-permute-start | bytes 393224 | tf_op jit(solution)/shard_map/ppermute | solution.py:616
  175.1 21.6 %collective-permute-start.23 = (bf16[32,2048]{1,0:T(8,128)(2,1)S(1)}, bf16[32,2048]{1,0:T(8,128)(2,1)S(1)}, u32[]{:S(2)}, u32[]{:S(2)}) collective-permute-start(bf16[32,2048]{1,0:T(8,128)(2,1)S(1)} %get-tuple-element.80), channel_id=1, source_target_pairs={{0,16},{2,18},{4,20},{6,22},{8,24},{10,26},{12,28},{14,30},{16,0},... | collective-permute-start | bytes 393224 | tf_op jit(solution)/shard_map/ppermute | solution.py:616
  196.8 8.1 %collective-permute-start.26 = (bf16[32,2048]{1,0:T(8,128)(2,1)S(1)}, bf16[32,2048]{1,0:T(8,128)(2,1)S(1)}, u32[]{:S(2)}, u32[]{:S(2)}) collective-permute-start(bf16[32,2048]{1,0:T(8,128)(2,1)S(1)} %add_convert_fusion.4), channel_id=1, source_target_pairs={{0,1},{1,0},{2,3},{3,2},{4,5},{5,4},{6,7},{7,6},{8,9},{9,8},{10,11... | collective-permute-start | bytes 393224 | tf_op jit(solution)/shard_map/ppermute | solution.py:676
  205.0 8.1 %collective-permute-start.27 = (bf16[32,4736]{1,0:T(8,128)(2,1)}, bf16[32,4736]{1,0:T(8,128)(2,1)S(1)}, u32[]{:S(2)}, u32[]{:S(2)}) collective-permute-start(bf16[32,4736]{1,0:T(8,128)(2,1)} %reduce-scatter.2.cloned.1.call-done), channel_id=1, source_target_pairs={{0,1},{1,0},{2,3},{3,2},{4,5},{5,4},{6,7},{7,6},{8,9},{9,8},{10,11... | collective-permute-start | bytes 909320 | tf_op jit(solution)/shard_map/ppermute | solution.py:676
  (26 other events, 134.0 us)
Sparse Core Ops, SparseCore 0:
  10.9 57.6 all-gather.1
  107.9 89.4 reduce-scatter.1

commit v3 on v2

v3 whole, which is shorter than its diff:
```python
from functools import partial
import jax
import jax.numpy as jnp
from jax import lax
from jax.experimental import pallas as pl
from jax.experimental.pallas import tpu as pltpu
from jax.sharding import PartitionSpec as P

F32 = jnp.float32
BF16 = jnp.bfloat16
HEAD = 64
QUAD = 256
SCALE = HEAD ** -0.5
CHUNK = 128
VMEM_LIMIT = 60 * 1024 * 1024


def mm(a, b):
    return lax.dot_general(a, b, (((1,), (0,)), ((), ())), preferred_element_type=F32)


def mm_t(a, b):
    return lax.dot_general(a, b, (((1,), (1,)), ((), ())), preferred_element_type=F32)


def t_mm(a, b):
    return lax.dot_general(a, b, (((0,), (0,)), ((), ())), preferred_element_type=F32)


def iota(shape, dim):
    return lax.broadcasted_iota(jnp.int32, shape, dim)


def normalize(x):
    centred = x - jnp.mean(x, axis=-1, keepdims=True)
    spread = jnp.mean(centred * centred, axis=-1, keepdims=True)
    factor = lax.rsqrt(spread + 1e-05)
    return centred * factor, factor


def norm_back(g, normed, factor):
    first = jnp.mean(g, axis=-1, keepdims=True)
    second = jnp.mean(g * normed, axis=-1, keepdims=True)
    return factor * (g - first - normed * second)


def blocks_of(x):
    lane = iota(x.shape, 1) // HEAD
    zero = jnp.zeros_like(x)
    return jnp.concatenate([jnp.where(lane == h, x, zero) for h in range(4)], axis=0)


def blocks_t(x):
    xt = x.T
    row = iota(xt.shape, 0) // HEAD
    zero = jnp.zeros_like(xt)
    return jnp.concatenate([jnp.where(row == h, xt, zero) for h in range(4)], axis=1)


def tri(x, lower):
    c = x.shape[0]
    row, col = iota(x.shape, 0), iota(x.shape, 1) % c
    keep = row >= col if lower else row <= col
    return jnp.where(keep, x, 0.0).astype(BF16)


def per_head(x, op, neutral):
    parts = []
    for p in range(x.shape[1] // 128):
        v = x[:, p * 128 : (p + 1) * 128]
        low = iota(v.shape, 1) < HEAD
        a = op(jnp.where(low, v, neutral), axis=-1, keepdims=True)
        b = op(jnp.where(low, neutral, v), axis=-1, keepdims=True)
        parts.append(jnp.where(low, a, b))
    return jnp.concatenate(parts, axis=1)


def head_square():
    return iota((QUAD, QUAD), 0) // HEAD == iota((QUAD, QUAD), 1) // HEAD


STATE = 2 * HEAD + 8


def store_state(st_ref, first, second, total):
    square = head_square()
    for g in range(st_ref.shape[0]):
        for k, ref in enumerate((first, second)):
            x = jnp.where(square, ref[g], 0.0)
            st_ref[g, k * HEAD : (k + 1) * HEAD, :] = x[0:64] + x[64:128] + x[128:192] + x[192:256]
        st_ref[g, 2 * HEAD :, :] = jnp.broadcast_to(total[0:1, g * QUAD : (g + 1) * QUAD], (8, QUAD))


def load_state(st_ref, first, second, total):
    square = head_square()
    for g in range(st_ref.shape[0]):
        for k, ref in enumerate((first, second)):
            x = st_ref[g, k * HEAD : (k + 1) * HEAD, :]
            ref[g] = jnp.where(square, jnp.concatenate([x] * 4, axis=0), 0.0)
        total[:, g * QUAD : (g + 1) * QUAD] = st_ref[g, 2 * HEAD :, :]


def hi_lo(x):
    hi = x.astype(BF16)
    return hi, (x - hi.astype(F32)).astype(BF16)


def spread_vector(vecs, me, n, r, k, each, total):
    pick = (iota((n, n * r), 1) == iota((n, n * r), 0) * r + k).astype(BF16)
    rows = mm(pick, vecs).astype(BF16)
    tile = (iota((128, total), 1) % each == iota((128, total), 0)).astype(BF16)
    wide = mm(rows, tile)
    own = iota((n, total), 1) // each == (iota((n, total), 0) ^ me)
    return jnp.sum(jnp.where(own, wide, 0.0), axis=0, keepdims=True)


def gather_vector(vec, me, n, each):
    total = vec.shape[1]
    own = iota((n, total), 1) // each == (iota((n, total), 0) ^ me)
    wide = jnp.where(own, vec, 0.0).astype(BF16)
    tile = (iota((128, total), 1) % each == iota((128, total), 0)).astype(BF16)
    return mm_t(wide, tile).astype(BF16)


def piece_refs(where, refs):
    return [refs[a] if row is None else refs[a].at[row] for a, row in where]


def pack_kernel(q, k, v, c, o, up, down, gain_a, gain_f, b_up, b_down, first, second):
    r, d = q.shape
    ff = up.shape[1]
    for p, ref in enumerate((q, k, v, c)):
        first[:, p * d : (p + 1) * d] = ref[...]
    tile = jnp.zeros((r, 128), F32)
    row, col = iota((r, 128), 0), iota((r, 128), 1)
    for i, ref in enumerate((gain_a, gain_f, b_up, b_down)):
        length = ref.shape[1]
        wide = jnp.broadcast_to(ref[...].astype(F32), (r, length))
        if length < 128:
            wide = jnp.concatenate([wide, jnp.zeros((r, 128 - length), F32)], axis=1)
        tile = jnp.where(row == i, wide, tile)
    first[:, 4 * d :] = tile.astype(BF16)
    second[:, 2 * ff + d :] = tile.astype(BF16)
    second[:, :ff] = up[...]
    for m in range(ff // d):
        second[:, ff + m * d : ff + (m + 1) * d] = down[m * r : (m + 1) * r, :]
    second[:, 2 * ff : 2 * ff + d] = o[...]


def pack(q, k, v, c, o, up, down, gain_a, gain_f, b_up, b_down):
    r, d = q.shape
    ff = up.shape[1]
    return pl.pallas_call(
        pack_kernel,
        out_shape=[jax.ShapeDtypeStruct((r, 4 * d + 128), BF16), jax.ShapeDtypeStruct((r, 2 * ff + d + 128), BF16)],
        cost_estimate=pl.CostEstimate(flops=0, bytes_accessed=1 << 20, transcendentals=0),
        name="pack",
    )(q, k, v, c, o, up, down, *(x.reshape(1, -1) for x in (gain_a, gain_f, b_up, b_down)))


def stack_kernel(*refs):
    for i, ref in enumerate(refs[:-1]):
        refs[-1][i] = ref[...]


def stack(items):
    return pl.pallas_call(
        stack_kernel,
        out_shape=jax.ShapeDtypeStruct((len(items),) + items[0].shape, items[0].dtype),
        cost_estimate=pl.CostEstimate(flops=0, bytes_accessed=2 << 20, transcendentals=0),
        name="stack",
    )(*items)


def project_kernel(where, arrays, r, me_ref, tok_hbm, *refs):
    n = len(where)
    pieces = piece_refs(where, refs)
    (att_hbm, pack_hbm, st_ref, w_hbm, gain_ref,
     tok, att, pack, w_all, vecs, normed, written, first, second, total, sems, vsems, tsem, osems) = refs[arrays:]
    t, d = att.shape
    wide = 4 * d
    rows = 256
    me = me_ref[0]
    load = pltpu.make_async_copy(tok_hbm, tok, tsem)
    load.start()
    vector_copies, copies = [], []
    for j in range(n):
        at = pl.multiple_of((me ^ j) * r, r)
        copies.append(pltpu.make_async_copy(pieces[j].at[:, pl.ds(0, wide)], w_all.at[pl.ds(at, r), :], sems.at[j]))
        vector_copies.append(pltpu.make_async_copy(pieces[j].at[:, pl.ds(wide, 128)], vecs.at[pl.ds(j * r, r), :], vsems.at[j]))
    for c in vector_copies + copies:
        c.start()
    sent = []

    def send(src, dst):
        copy = pltpu.make_async_copy(src, dst, osems.at[len(sent)])
        copy.start()
        sent.append(copy)

    load.wait()
    for i in range(t // rows):
        rs = pl.ds(i * rows, rows)
        normed[rs, :], _ = normalize(tok[rs, :].astype(F32))
    for c in vector_copies:
        c.wait()
    gain = spread_vector(vecs[...], me, n, r, 0, r, d)
    gain_ref[...] = jnp.broadcast_to(gain, gain_ref.shape)
    for c in copies:
        c.wait()
    send(w_all, w_hbm)
    sums = jnp.zeros((1, d), F32)
    for i in range(t // rows):
        rs = pl.ds(i * rows, rows)
        x = (normed[rs, :] * gain).astype(BF16)
        att[rs, :] = x
        send(att.at[rs, :], att_hbm.at[rs, :])
        for p in (3, 1, 2, 0):
            full = mm(x, w_all[:, p * d : (p + 1) * d]).astype(BF16)
            pack[rs, p * d : (p + 1) * d] = full
            if p == 3:
                new = jnp.exp(full.astype(F32)).astype(BF16)
                written[rs, :] = new
                sums += jnp.sum(new.astype(F32), axis=0, keepdims=True)
        send(pack.at[rs, :], pack_hbm.at[rs, :])
    for g in range(d // QUAD):
        s = slice(g * QUAD, (g + 1) * QUAD)
        first[g] = t_mm(pack[:, d + g * QUAD : d + (g + 1) * QUAD], written[:, s])
        second[g] = t_mm(written[:, s], pack[:, 2 * d + g * QUAD : 2 * d + (g + 1) * QUAD])
    total[...] = jnp.broadcast_to(sums, total.shape)
    store_state(st_ref, first, second, total)
    for c in sent:
        c.wait()


def project(me, tokens, where, pieces):
    t, d = tokens.shape
    n = len(where)
    r = d // n
    wide = 4 * d
    g = d // QUAD
    hbm = pl.BlockSpec(memory_space=pl.ANY)
    vmem = pl.BlockSpec(memory_space=pltpu.VMEM)
    return pl.pallas_call(
        partial(project_kernel, where, len(pieces), r),
        in_specs=[pl.BlockSpec(memory_space=pltpu.SMEM)] + [hbm] * (1 + len(pieces)),
        out_specs=[hbm, hbm, vmem, hbm, vmem],
        out_shape=[
            jax.ShapeDtypeStruct((t, d), BF16),
            jax.ShapeDtypeStruct((t, wide), BF16),
            jax.ShapeDtypeStruct((g, STATE, QUAD), F32),
            jax.ShapeDtypeStruct((d, wide), BF16),
            jax.ShapeDtypeStruct((8, d), F32),
        ],
        scratch_shapes=[
            pltpu.VMEM((t, d), BF16),
            pltpu.VMEM((t, d), BF16),
            pltpu.VMEM((t, wide), BF16),
            pltpu.VMEM((d, wide), BF16),
            pltpu.VMEM((n * r, 128), BF16),
            pltpu.VMEM((t, d), F32),
            pltpu.VMEM((t, d), BF16),
            pltpu.VMEM((g, QUAD, QUAD), F32),
            pltpu.VMEM((g, QUAD, QUAD), F32),
            pltpu.VMEM((8, d), F32),
            pltpu.SemaphoreType.DMA((n,)),
            pltpu.SemaphoreType.DMA((n,)),
            pltpu.SemaphoreType.DMA,
            pltpu.SemaphoreType.DMA((1 + 2 * (t // 256),)),
        ],
        compiler_params=pltpu.CompilerParams(vmem_limit_bytes=VMEM_LIMIT),
        cost_estimate=pl.CostEstimate(flops=2 * t * d * wide, bytes_accessed=12 << 20, transcendentals=t * d),
        name="project",
    )(me, tokens, *pieces)


def mix_kernel(pack_ref, st_in, mix_ref, read_ref, score_ref, inv_ref, kts_ref, mvs_ref, kt, mv, tot):
    d = mix_ref.shape[1]
    rows = mix_ref.shape[0]

    @pl.when(pl.program_id(0) == 0)
    def _():
        load_state(st_in, kt, mv, tot)

    c = CHUNK
    square = head_square()
    ones = (iota((c, c), 0) >= iota((c, c), 1)).astype(BF16)
    units = [(b, g) for b in range(rows // c) for g in range(d // QUAD)]
    at = {(b, g): (slice(b * c, (b + 1) * c), slice(g * QUAD, (g + 1) * QUAD)) for b, g in units}
    part = lambda p: {(b, g): pack_ref[at[b, g][0], p * d + g * QUAD : p * d + (g + 1) * QUAD] for b, g in units}
    q, k, v = part(0), part(1), part(2)
    written = {x: jnp.exp(y.astype(F32)).astype(BF16) for x, y in part(3).items()}
    wb = {x: blocks_of(written[x]) for x in units}
    pairs = {x: tri(mm(q[x], blocks_t(k[x])), True) for x in units}
    ktb, mvb, inv = {}, {}, {}
    for x in units:
        b, g = x
        ktb[x], mvb[x] = kt[g].astype(BF16), mv[g].astype(BF16)
        kts_ref[b, g] = ktb[x]
        mvs_ref[b, g] = mvb[x]
        kt[g] += jnp.where(square, t_mm(k[x], written[x]), 0.0)
        mv[g] += jnp.where(square, t_mm(written[x], v[x]), 0.0)
        total = mm(ones, written[x]) + tot[0:1, at[x][1]]
        tot[0:1, at[x][1]] = total[c - 1 : c, :]
        inv[x] = 1.0 / total
        inv_ref[at[x]] = inv[x]
    score = {x: (mm(pairs[x], wb[x]) + mm(q[x], ktb[x])) * SCALE * inv[x] for x in units}
    for x in units:
        score_ref[at[x]] = score[x]
    e = {x: jnp.exp(score[x] - per_head(score[x], jnp.max, -jnp.inf)) for x in units}
    read = {x: e[x] / per_head(e[x], jnp.sum, 0.0) for x in units}
    for x in units:
        read_ref[at[x]] = read[x]
    scaled = {x: (read[x] * inv[x]).astype(BF16) for x in units}
    recall = {x: tri(mm(scaled[x], blocks_t(written[x])), True) for x in units}
    for x in units:
        mix_ref[at[x]] = (mm(recall[x], blocks_of(v[x])) + mm(scaled[x], mvb[x])).astype(BF16)


def mix(packed, state, rows=256):
    t, wide = packed.shape
    d = wide // 4
    g = d // QUAD
    const = lambda *shape: pl.BlockSpec(shape, lambda i: (0,) * len(shape))
    per = rows // CHUNK
    row = lambda w: pl.BlockSpec((rows, w), lambda i: (i, 0))
    return pl.pallas_call(
        mix_kernel,
        grid=(t // rows,),
        in_specs=[row(wide), const(g, STATE, QUAD)],
        out_specs=[row(d)] * 4 + [pl.BlockSpec((per, g, QUAD, QUAD), lambda i: (i, 0, 0, 0))] * 2,
        out_shape=[jax.ShapeDtypeStruct((t, d), BF16)] + [jax.ShapeDtypeStruct((t, d), F32)] * 3
        + [jax.ShapeDtypeStruct((t // CHUNK, g, QUAD, QUAD), BF16)] * 2,
        scratch_shapes=[pltpu.VMEM((g, QUAD, QUAD), F32), pltpu.VMEM((g, QUAD, QUAD), F32), pltpu.VMEM((8, d), F32)],
        compiler_params=pltpu.CompilerParams(vmem_limit_bytes=VMEM_LIMIT),
        cost_estimate=pl.CostEstimate(flops=6 * 10**9, bytes_accessed=16 << 20, transcendentals=2 * t * d),
        name="mix",
    )(packed, state)


def ffn_kernel(n, mixed_hbm, tok_hbm, cot_hbm, full_ref, out_hbm, gres_hbm, gmix_hbm, grad_ref,
               mixed, tok, cot, outs, gres, gmix, w_out, w_up, w_down, vecs, hid, gpre, fin, gbr, sems, osems):
    t, d = mixed.shape
    ff = w_up.shape[1]
    r = d // n
    mult = ff // d
    rows = 256
    part = 512
    steps = t // rows
    parts = ff // part

    def load(src, dst, i):
        copy = pltpu.make_async_copy(src, dst, sems.at[i])
        copy.start()
        return copy

    down_sem = 3
    early = [
        load(full_ref.at[:, pl.ds(2 * ff, d)], w_out, 0),
        load(mixed_hbm, mixed, 1),
        load(tok_hbm, tok, 2),
        load(full_ref.at[:, pl.ds(2 * ff + d, 128)], vecs, 4),
        load(full_ref.at[:, pl.ds(0, ff)], w_up, 5),
    ]
    late = [load(cot_hbm, cot, 6)]
    down = []
    for j in range(n):
        for m in range(mult):
            down.append((full_ref.at[pl.ds(j * r, r), pl.ds(ff + m * d, d)], w_down.at[pl.ds((j * mult + m) * r, r), :]))
    late += [load(src, dst, 7 + i) for i, (src, dst) in enumerate(down)]
    for c in early:
        c.wait()
    gain = spread_vector(vecs[...], 0, n, r, 1, r, d)
    b_up = spread_vector(vecs[...], 0, n, r, 2, r * mult, ff)
    b_down = spread_vector(vecs[...], 0, n, r, 3, r, d)

    sent = []

    def send(src, dst):
        copy = pltpu.make_async_copy(src, dst, osems.at[len(sent)])
        copy.start()
        sent.append(copy)

    ggain = jnp.zeros((1, d), F32)
    gbdown = jnp.zeros((1, d), F32)
    gbup = [jnp.zeros((1, part), F32)] * parts
    for i in range(steps):
        rs = pl.ds(i * rows, rows)
        resid = tok[rs, :].astype(F32) + mm(mixed[rs, :], w_out[...])
        normed, factor = normalize(resid)
        ffn_in = (normed * gain).astype(BF16)
        fin[rs, :] = ffn_in
        if i == 0:
            for c in late:
                c.wait()
        cot_b = cot[rs, :]
        cotf = cot_b.astype(F32)

        def entry(p):
            ps = slice(p * part, (p + 1) * part)
            return mm(ffn_in, w_up[:, ps]) + b_up[:, ps], mm_t(cot_b, w_down[ps, :])

        ready = entry(0)
        total = gin = None
        for p in range(parts):
            ps = slice(p * part, (p + 1) * part)
            pre, gh = ready
            if p + 1 < parts:
                ready = entry(p + 1)
            sig = 0.5 * jnp.tanh(0.5 * pre) + 0.5
            act = pre * sig
            gp = gh * (sig + act * (1.0 - sig))
            gbup[p] = gbup[p] + jnp.sum(gp, axis=0, keepdims=True)
            act, gp = act.astype(BF16), gp.astype(BF16)
            hid[rs, ps] = act
            gpre[rs, ps] = gp
            x, y = mm(act, w_down[ps, :]), mm_t(gp, w_up[:, ps])
            total, gin = (x, y) if p == 0 else (total + x, gin + y)
        outs[rs, :] = (resid + (total + b_down)).astype(BF16)
        send(outs.at[rs, :], out_hbm.at[rs, :])
        back = cotf + norm_back(gin * gain, normed, factor)
        gres[rs, :] = back
        send(gres.at[rs, :], gres_hbm.at[rs, :])
        back = back.astype(BF16)
        gbr[rs, :] = back
        gmix[rs, :] = mm_t(back, w_out[...]).astype(BF16)
        send(gmix.at[rs, :], gmix_hbm.at[rs, :])
        ggain += jnp.sum(gin * normed, axis=0, keepdims=True)
        gbdown += jnp.sum(cotf, axis=0, keepdims=True)

    for p in range(parts):
        ps = slice(p * part, (p + 1) * part)
        w_up[:, ps] = t_mm(fin[...], gpre[:, ps]).astype(BF16)
        send(w_up.at[:, ps], grad_ref.at[:, ps])
    w_out[...] = t_mm(mixed[...], gbr[...]).astype(BF16)
    send(w_out, grad_ref.at[:, pl.ds(2 * ff, d)])
    va = gather_vector(ggain, 0, n, r)
    vb = gather_vector(jnp.concatenate(gbup, axis=1), 0, n, r * mult)
    vc = gather_vector(gbdown, 0, n, r)
    row = iota((r, 128), 0)
    pick = lambda v, j, i, rest: jnp.where(row == i, jnp.broadcast_to(v[j : j + 1].astype(F32), (r, 128)), rest)
    for j in range(n):
        tile = pick(va, j, 1, pick(vb, j, 2, pick(vc, j, 3, jnp.zeros((r, 128), F32))))
        vecs[j * r : (j + 1) * r, :] = tile.astype(BF16)
    send(vecs, grad_ref.at[:, pl.ds(2 * ff + d, 128)])
    for p in range(parts):
        ps = slice(p * part, (p + 1) * part)
        w_down[ps, :] = t_mm(hid[:, ps], cot[...]).astype(BF16)
        count = part // r
        for i in range(p * count, (p + 1) * count):
            send(down[i][1], grad_ref.at[pl.ds(i // mult * r, r), pl.ds(ff + i % mult * d, d)])
    for c in sent:
        c.wait()


def ffn(mixed, tokens, cot, full, ff, n):
    t, d = tokens.shape
    hbm = pl.BlockSpec(memory_space=pl.ANY)
    moves = n * (ff // d)
    return pl.pallas_call(
        partial(ffn_kernel, n),
        in_specs=[hbm] * 4,
        out_specs=[hbm] * 4,
        out_shape=[
            jax.ShapeDtypeStruct((t, d), BF16),
            jax.ShapeDtypeStruct((t, d), F32),
            jax.ShapeDtypeStruct((t, d), BF16),
            jax.ShapeDtypeStruct(full.shape, BF16),
        ],
        scratch_shapes=[pltpu.VMEM((t, d), BF16)] * 4
        + [pltpu.VMEM((t, d), F32), pltpu.VMEM((t, d), BF16)]
        + [
            pltpu.VMEM((d, d), BF16),
            pltpu.VMEM((d, ff), BF16),
            pltpu.VMEM((ff, d), BF16),
            pltpu.VMEM((d, 128), BF16),
            pltpu.VMEM((t, ff), BF16),
            pltpu.VMEM((t, ff), BF16),
            pltpu.VMEM((t, d), BF16),
            pltpu.VMEM((t, d), BF16),
            pltpu.SemaphoreType.DMA((7 + moves,)),
            pltpu.SemaphoreType.DMA((3 * (t // 256) + ff // 512 + 2 + moves,)),
        ],
        compiler_params=pltpu.CompilerParams(vmem_limit_bytes=VMEM_LIMIT),
        cost_estimate=pl.CostEstimate(flops=12 * t * d * ff, bytes_accessed=20 << 20, transcendentals=t * ff),
        name="ffn",
    )(mixed, tokens, cot, full)


def read_back_kernel(pack_ref, gmix_ref, read_ref, score_ref, inv_ref, kts_ref, mvs_ref,
                     gq_ref, a_ref, u_ref, gtot_ref, st_ref, gk_ref, gv_ref, gt_ref):
    rows, d = gmix_ref.shape

    @pl.when(pl.program_id(0) == 0)
    def _():
        gk_ref[...] = jnp.zeros_like(gk_ref)
        gv_ref[...] = jnp.zeros_like(gv_ref)
        gt_ref[...] = jnp.zeros_like(gt_ref)

    c = CHUNK
    units = [(b, g) for b in range(rows // c) for g in range(d // QUAD)]
    at = {(b, g): (slice(b * c, (b + 1) * c), slice(g * QUAD, (g + 1) * QUAD)) for b, g in units}
    part = lambda p: {(b, g): pack_ref[at[b, g][0], p * d + g * QUAD : p * d + (g + 1) * QUAD] for b, g in units}
    q, k, v = part(0), part(1), part(2)
    written = {x: jnp.exp(y.astype(F32)).astype(BF16) for x, y in part(3).items()}
    wb = {x: blocks_of(written[x]) for x in units}
    gm = {x: gmix_ref[at[x]] for x in units}
    gpair = {x: tri(mm(gm[x], blocks_t(v[x])), True) for x in units}
    weighted = {x: (mm(gpair[x], wb[x]) + mm_t(gm[x], mvs_ref[x])) * inv_ref[at[x]] * read_ref[at[x]] for x in units}
    gscore = {x: weighted[x] - read_ref[at[x]] * per_head(weighted[x], jnp.sum, 0.0) for x in units}
    a, u = {}, {}
    for x in units:
        inv = inv_ref[at[x]]
        a[x] = (gscore[x] * inv * SCALE).astype(BF16)
        u[x] = (read_ref[at[x]] * inv).astype(BF16)
        a_ref[at[x]] = a[x]
        u_ref[at[x]] = u[x]
        gtot = (gscore[x] * score_ref[at[x]] + weighted[x]) * inv
        gtot_ref[at[x]] = gtot
        gt_ref[0:1, at[x][1]] += jnp.sum(gtot, axis=0, keepdims=True)
    spair = {x: tri(mm(a[x], blocks_t(written[x])), True) for x in units}
    for x in units:
        gq_ref[at[x]] = (mm(spair[x], blocks_of(k[x])) + mm_t(a[x], kts_ref[x])).astype(BF16)
    for g in range(d // QUAD):
        s = slice(g * QUAD, (g + 1) * QUAD)
        every = lambda y: jnp.concatenate([y[b, g] for b in range(rows // c)], axis=0)
        gk_ref[g] += t_mm(every(a), every(q))
        gv_ref[g] += t_mm(every(u), every(gm))

    @pl.when(pl.program_id(0) == pl.num_programs(0) - 1)
    def _():
        store_state(st_ref, gk_ref, gv_ref, gt_ref)


def read_back(packed, gmix, read, score, inv, kts, mvs, rows=512):
    t, wide = packed.shape
    d = wide // 4
    g = d // QUAD
    const = lambda *shape: pl.BlockSpec(shape, lambda i: (0,) * len(shape))
    per = rows // CHUNK
    row = lambda w: pl.BlockSpec((rows, w), lambda i: (i, 0))
    st = pl.BlockSpec((per, g, QUAD, QUAD), lambda i: (i, 0, 0, 0))
    return pl.pallas_call(
        read_back_kernel,
        grid=(t // rows,),
        in_specs=[row(wide), row(d), row(d), row(d), row(d), st, st],
        out_specs=[row(d)] * 4 + [const(g, STATE, QUAD)],
        out_shape=[jax.ShapeDtypeStruct((t, d), BF16)] * 3 + [jax.ShapeDtypeStruct((t, d), F32)]
        + [jax.ShapeDtypeStruct((g, STATE, QUAD), F32)],
        scratch_shapes=[pltpu.VMEM((g, QUAD, QUAD), F32), pltpu.VMEM((g, QUAD, QUAD), F32), pltpu.VMEM((8, d), F32)],
        compiler_params=pltpu.CompilerParams(vmem_limit_bytes=VMEM_LIMIT),
        cost_estimate=pl.CostEstimate(flops=6 * 10**9, bytes_accessed=20 << 20, transcendentals=t * d),
        name="read_back",
    )(packed, gmix, read, score, inv, kts, mvs)


def write_back_kernel(n, me_ref, pack_ref, gmix_ref, a_ref, u_ref, gtot_ref, st_in, att_hbm, gq_hbm, out_ref, *refs):
    share_refs = refs[:4]
    gk, gv, gt, att, gq, grads, acc, isems, sems = refs[4:]
    rows, d = gmix_ref.shape
    loads = [pltpu.make_async_copy(att_hbm, att, isems.at[0]), pltpu.make_async_copy(gq_hbm, gq, isems.at[1])]

    @pl.when(pl.program_id(0) == 0)
    def _():
        for x in loads:
            x.start()
        load_state(st_in, gk, gv, gt)

    base = (pl.num_programs(0) - 1 - pl.program_id(0)) * rows
    c = CHUNK
    square = head_square()
    ones = (iota((c, c), 0) <= iota((c, c), 1)).astype(BF16)
    units = [(b, g) for b in reversed(range(rows // c)) for g in range(d // QUAD)]
    at = {(b, g): (slice(b * c, (b + 1) * c), slice(g * QUAD, (g + 1) * QUAD)) for b, g in units}
    part = lambda p: {(b, g): pack_ref[at[b, g][0], p * d + g * QUAD : p * d + (g + 1) * QUAD] for b, g in units}
    q, k, v = part(0), part(1), part(2)
    wf = {x: jnp.exp(y.astype(F32)) for x, y in part(3).items()}
    written = {x: wf[x].astype(BF16) for x in units}
    gm, a, u = ({x: ref[at[x]] for x in units} for ref in (gmix_ref, a_ref, u_ref))
    qb, gb, ab, ub = ({x: blocks_of(y[x]) for x in units} for y in (q, gm, a, u))
    gkb, gvb, after = {}, {}, {}
    for x in units:
        g = x[1]
        gkb[x], gvb[x] = gk[g].astype(BF16), gv[g].astype(BF16)
        gk[g] += jnp.where(square, t_mm(a[x], q[x]), 0.0)
        gv[g] += jnp.where(square, t_mm(u[x], gm[x]), 0.0)
        hi, lo = hi_lo(gtot_ref[at[x]])
        after[x] = mm(ones, hi) + mm(ones, lo) + gt[0:1, at[x][1]]
        gt[0:1, at[x][1]] = after[x][0:1, :]

    def out(p, x, y):
        y = y.astype(BF16)
        cols = slice(p * d + x[1] * QUAD, p * d + (x[1] + 1) * QUAD)
        out_ref[at[x][0], cols] = y
        grads[pl.ds(pl.multiple_of(base + x[0] * c, c), c), cols] = y

    st = {x: tri(mm(written[x], blocks_t(a[x])), False) for x in units}
    rt = {x: tri(mm(written[x], blocks_t(u[x])), False) for x in units}
    for x in units:
        out(0, x, mm(st[x], qb[x]) + mm(written[x], gkb[x]))
    for x in units:
        out(1, x, mm(rt[x], gb[x]) + mm(written[x], gvb[x]))
    pt = {x: tri(mm(k[x], blocks_t(q[x])), False) for x in units}
    gp = {x: tri(mm(v[x], blocks_t(gm[x])), False) for x in units}
    for x in units:
        gw = mm(pt[x], ab[x]) + mm(gp[x], ub[x]) + mm_t(k[x], gkb[x]) + mm_t(v[x], gvb[x])
        out(2, x, wf[x] * (gw - after[x]))

    @pl.when(pl.program_id(0) == pl.num_programs(0) - 1)
    def _():
        for x in loads:
            x.wait()
        r = d // n
        me = me_ref[0]
        acc[:, 0:d] = t_mm(att[...], gq[...]).astype(BF16)
        for p in range(3):
            acc[:, (p + 1) * d : (p + 2) * d] = t_mm(att[...], grads[:, p * d : (p + 1) * d]).astype(BF16)
        outs = []
        for j in range(n):
            frm = pl.multiple_of((me ^ j) * r, r)
            dst = share_refs[j % 4].at[j // 4]
            outs.append(pltpu.make_async_copy(acc.at[pl.ds(frm, r), :], dst, sems.at[j]))
        for x in outs:
            x.start()
        for x in outs:
            x.wait()


def write_back(me, packed, gmix, a, u, gtot, state, att, gq, n, rows=256):
    t, wide = packed.shape
    d = wide // 4
    g = d // QUAD
    r = d // n
    last = t // rows - 1
    const = lambda *shape: pl.BlockSpec(shape, lambda i: (0,) * len(shape))
    row = lambda w: pl.BlockSpec((rows, w), lambda i: (last - i, 0))
    hbm = pl.BlockSpec(memory_space=pl.ANY)
    return pl.pallas_call(
        partial(write_back_kernel, n),
        grid=(t // rows,),
        in_specs=[pl.BlockSpec(memory_space=pltpu.SMEM), row(wide), row(d), row(d), row(d), row(d), const(g, STATE, QUAD), hbm, hbm],
        out_specs=[row(3 * d)] + [hbm] * 4,
        out_shape=[jax.ShapeDtypeStruct((t, 3 * d), BF16)] + [jax.ShapeDtypeStruct((n // 4, r, wide), BF16)] * 4,
        scratch_shapes=[
            pltpu.VMEM((g, QUAD, QUAD), F32),
            pltpu.VMEM((g, QUAD, QUAD), F32),
            pltpu.VMEM((8, d), F32),
            pltpu.VMEM((t, d), BF16),
            pltpu.VMEM((t, d), BF16),
            pltpu.VMEM((t, 3 * d), BF16),
            pltpu.VMEM((d, wide), BF16),
            pltpu.SemaphoreType.DMA((2,)),
            pltpu.SemaphoreType.DMA((n,)),
        ],
        compiler_params=pltpu.CompilerParams(vmem_limit_bytes=VMEM_LIMIT),
        cost_estimate=pl.CostEstimate(flops=11 * 10**9, bytes_accessed=18 << 20, transcendentals=t * d),
        name="write_back",
    )(me, packed, gmix, a, u, gtot, state, att, gq)


def input_grad_kernel(gain_ref, tok_ref, gq_ref, gkvc_ref, w_ref, gres_ref, out_ref):
    d = tok_ref.shape[1]
    gain = gain_ref[0:1, :]
    gin = mm_t(gq_ref[...], w_ref[:, 0:d]) + mm_t(gkvc_ref[...], w_ref[:, d:])
    normed, factor = normalize(tok_ref[...].astype(F32))
    out_ref[...] = gres_ref[...] + norm_back(gin * gain, normed, factor)


def input_grad(gain, tokens, gq, gkvc, w, gres, rows=256):
    t, d = tokens.shape
    const = lambda *shape: pl.BlockSpec(shape, lambda i: (0,) * len(shape))
    row = lambda w: pl.BlockSpec((rows, w), lambda i: (i, 0))
    return pl.pallas_call(
        input_grad_kernel,
        grid=(t // rows,),
        in_specs=[const(8, d), row(d), row(d), row(3 * d), const(d, 4 * d), row(d)],
        out_specs=row(d),
        out_shape=jax.ShapeDtypeStruct((t, d), F32),
        compiler_params=pltpu.CompilerParams(vmem_limit_bytes=VMEM_LIMIT),
        cost_estimate=pl.CostEstimate(flops=8 * t * d * d, bytes_accessed=12 << 20, transcendentals=0),
        name="input_grad",
    )(gain, tokens, gq, gkvc, w, gres)


def swap(x, mask, n):
    return lax.ppermute(x, "fsdp", [(i, i ^ mask) for i in range(n)])


def after(x, *first):
    return lax.optimization_barrier((x, *first))[0]


def add(*items):
    return sum(x.astype(F32) for x in items).astype(BF16)


def along_z(shard, n):
    return [shard] + [swap(shard, 4 * k, n) for k in range(1, n // 4)]


def along_x(own, n):
    return [swap(x, 2, n) for x in own]


def shift(x, by, seqs):
    return lax.ppermute(x, "seq", [(i, i + by) for i in range(seqs) if 0 <= i + by < seqs])


def others(state, direction, seqs):
    if seqs == 1:
        return jnp.zeros_like(state)
    total = shift(state, direction, seqs)
    step = 1
    while step < seqs - 1:
        total = total + shift(total, direction * step, seqs)
        step *= 2
    return total


def on_device(n, seqs, tokens, w_query, w_key, w_value, w_control, w_out, w_up, w_down,
              gain_attn, gain_ffn, bias_up, bias_down, cotangent):
    r, d = w_query.shape
    ff = w_up.shape[1]
    mult = ff // d
    me = lax.axis_index("fsdp").astype(jnp.int32).reshape(1)
    first, second = pack(w_query, w_key, w_value, w_control, w_out, w_up, w_down, gain_attn, gain_ffn, bias_up, bias_down)
    depth = n // 4
    own = along_z(first, n)
    full = lax.all_gather(second, "fsdp", axis=0, tiled=True)
    across = along_x(own, n)
    cored = [[swap(x, 1, n) for x in group] for group in (own, across)]
    att_pieces = [x for quad in zip(own, cored[0], across, cored[1]) for x in quad]
    att_where = [(j, None) for j in range(n)]
    att, packed, state, w_att, gain = project(me, tokens, att_where, att_pieces)
    mixed, read, score, inv, kts, mvs = mix(packed, others(state, 1, seqs))
    layer_out, gres, gmix, ffn_grad = ffn(mixed, tokens, cotangent, full, ff, n)
    ffn_sum = lax.psum_scatter(ffn_grad, "fsdp", scatter_dimension=0, tiled=True)

    def core_sum(shares):
        near, near_core, far, far_core = shares
        return add(near, swap(near_core, 1, n)), add(far, swap(far_core, 1, n))

    def seq_sum(x):
        step = 1
        while step < seqs:
            x = add(x, lax.ppermute(x, "seq", [(i, i ^ step) for i in range(seqs)]))
            step *= 2
        return x.astype(F32)

    gq, a, u, gtot, gstate = read_back(packed, gmix, read, score, inv, kts, mvs)
    gkvc, *shares = write_back(me, packed, gmix, a, u, gtot, others(gstate, -1, seqs), att, gq, n)
    near, far = core_sum(shares)
    grad_tokens = input_grad(gain, tokens, after(gq, near, far), gkvc, w_att, gres)
    mine = {k: add(near[k], swap(far[k], 2, n)) for k in range(depth - 1, -1, -1)}
    sent = {k: swap(mine[k], 4 * k, n) if k else mine[k] for k in range(depth)}
    ffn_share = seq_sum(ffn_sum)
    att_share = seq_sum(add(*sent.values()))
    gain_share = jnp.sum(att_share * first[:, : 4 * d].astype(F32), axis=1) / gain_attn.astype(F32)
    up, down, out, vec = (
        ffn_share[:, :ff],
        ffn_share[:, ff : 2 * ff],
        ffn_share[:, 2 * ff : 2 * ff + d],
        ffn_share[:, 2 * ff + d :],
    )
    down = jnp.concatenate([down[:, m * d : (m + 1) * d] for m in range(mult)], axis=0)
    return (
        layer_out,
        grad_tokens,
        att_share[:, 0:d],
        att_share[:, d : 2 * d],
        att_share[:, 2 * d : 3 * d],
        att_share[:, 3 * d :],
        out,
        up,
        down,
        gain_share,
        vec[1, :r],
        vec[2, : r * mult],
        vec[3, :r],
    )


def solution(mesh):
    tokens = P(("fsdp", "seq"), None)
    matrix = P("fsdp", None)
    vector = P("fsdp")
    return jax.shard_map(
        partial(on_device, mesh.shape["fsdp"], mesh.shape["seq"]),
        mesh=mesh,
        in_specs=(tokens,) + (matrix,) * 7 + (vector,) * 4 + (tokens,),
        out_specs=(tokens, tokens) + (matrix,) * 7 + (vector,) * 4,
        check_vma=False,
    )
```

time: 225 us -> 202 us (0.90)
  Pallas kernels: 100 us -> 77.6 us
    pallas_call x5 -> x4, Pallas kernels: 69.5 us -> 55.3 us  [the longest x1 23.5 us: ffn(): pl.pallas_call(partial(ffn_kernel, n), in_specs=[hbm] * 4, out_specs=[hbm...]
    ppermute x24, waiting for transfers between devices: 50.7 us -> 46.1 us  [swap(): return lax.ppermute(x, 'fsdp', [(i, i ^ mask) for i in range(n)])]
    pallas_call x1, Pallas kernels: 14.8 us -> 10.2 us  [mix(): pl.pallas_call(mix_kernel, grid=(t // rows,), in_specs=[row(wide), const(...]
    pallas_call x1, Pallas kernels: 14.2 us -> 10.3 us  [read_back(): pl.pallas_call(read_back_kernel, grid=(t // rows,), in_specs=[row(wide),...]
    reduce_scatter x1, waiting for transfers between devices: 0.01 us -> 3.42 us  [on_device(): lax.psum_scatter(ffn_grad, 'fsdp', scatter_dimension=0, tiled=True)]
    ppermute x2, starting transfers between devices: 2.11 us -> 4.76 us  [seq_sum(): x = add(x, lax.ppermute(x, 'seq', [(i, i ^ step) for i in range(seqs)]))]
  transfers between devices with their start and end apart: 30 -> 30, of which waited for: 15 -> 16; matrix products, arithmetic and copies ran while one was open for 1% -> 1% of each run, Pallas kernels for 30% -> 26%
where the time goes in v3:
time: 202 us
  Pallas kernels  77.6 us (38%)
  waiting for transfers between devices  70.5 us (35%)
  starting transfers between devices  30.5 us (15%)
  between operations  14.4 us (7%)
  local copies, waits for them, and re-layouts  5.21 us (3%)
  other arithmetic  3.92 us (2%)
    ppermute x24, waiting for transfers between devices, swap(): return lax.ppermute(x, 'fsdp', [(i, i ^ mask) for i in range(n)])  46.1 us
    pallas_call x1, Pallas kernels, ffn(): pl.pallas_call(partial(ffn_kernel, n), in_specs=[hbm] * 4, out_specs=[hbm...  23.5 us
    ppermute x24, starting transfers between devices, swap(): return lax.ppermute(x, 'fsdp', [(i, i ^ mask) for i in range(n)])  21 us
    pallas_call x1, Pallas kernels, write_back(): pl.pallas_call(partial(write_back_kernel, n), grid=(t // rows,), in_specs...  16.2 us
    ppermute x2, waiting for transfers between devices, shift(): lax.ppermute(x, 'seq', [(i, i + by) for i in range(seqs) if 0 <= i + by <...  15.4 us
    pallas_call x1, Pallas kernels, read_back(): pl.pallas_call(read_back_kernel, grid=(t // rows,), in_specs=[row(wide),...  10.3 us
    pallas_call x1, Pallas kernels, mix(): pl.pallas_call(mix_kernel, grid=(t // rows,), in_specs=[row(wide), const(...  10.2 us
    pallas_call x1, Pallas kernels, project(): pl.pallas_call(partial(project_kernel, where, len(pieces), r), in_specs=[...  7.91 us
  transfers between devices with their start and end apart: 30, of which 16 were waited for; matrix products, arithmetic and copies ran while one was open for 1% of the time, Pallas kernels for 26%

profile of v3, /device:TPU:0, one launch (start us, length us, event | category | flops | bytes accessed | tf_op | source)
XLA Modules:
  0.0 202.1 jit_solution(10434917233525435524)
XLA Ops:
  9.2 5.1 %collective-permute-start.11 = (bf16[32,2176]{1,0:T(8,128)(2,1)}, bf16[32,2176]{1,0:T(8,128)(2,1)S(1)}, u32[]{:S(2)}, u32[]{:S(2)}) collective-permute-start(bf16[32,2176]{1,0:T(8,128)(2,1)} %get-tuple-element.41.refs_0_), channel_id=1, source_target_pairs={{0,24},{2,26},{4,28},{6,30},{8,16},{10,18},{12,20},{14,22},{16,8},... | collective-permute-start | bytes 417800 | tf_op jit(solution)/shard_map/ppermute | solution.py:685
  16.6 2.5 %collective-permute-done.11.refs_12_ = bf16[32,2176]{1,0:T(8,128)(2,1)S(1)} collective-permute-done((bf16[32,2176]{1,0:T(8,128)(2,1)}, bf16[32,2176]{1,0:T(8,128)(2,1)S(1)}, u32[]{:S(2)}, u32[]{:S(2)}) %collective-permute-start.11) | collective-permute-done | bytes 139296 | tf_op jit(solution)/shard_map/ppermute | solution.py:685
  20.8 8.6 %collective-permute-done.7.refs_8_ = bf16[32,2176]{1,0:T(8,128)(2,1)S(1)} collective-permute-done((bf16[32,2176]{1,0:T(8,128)(2,1)}, bf16[32,2176]{1,0:T(8,128)(2,1)S(1)}, u32[]{:S(2)}, u32[]{:S(2)}) %collective-permute-start.7) | collective-permute-done | bytes 139296 | tf_op jit(solution)/shard_map/ppermute | solution.py:685
  32.2 3.7 %collective-permute-done.9.refs_10_ = bf16[32,2176]{1,0:T(8,128)(2,1)S(1)} collective-permute-done((bf16[32,2176]{1,0:T(8,128)(2,1)S(1)}, bf16[32,2176]{1,0:T(8,128)(2,1)S(1)}, u32[]{:S(2)}, u32[]{:S(2)}) %collective-permute-start.9) | collective-permute-done | bytes 139296 | tf_op jit(solution)/shard_map/ppermute | solution.py:685
  36.5 2.0 collective-permute-done.5.refs_6_
  40.5 7.9 %project.1 = (bf16[1024,512]{1,0:T(8,128)(2,1)}, bf16[1024,2048]{1,0:T(8,128)(2,1)}, f32[2,136,256]{2,1,0:T(8,128)}, bf16[512,2048]{1,0:T(8,128)(2,1)}, f32[8,512]{1,0:T(8,128)}) custom-call(s32[1]{0:T(128)} %bitcast.me_ref, bf16[1024,512]{1,0:T(8,128)(2,1)} %tok_ref.1, bf16[32,2176]{1,0:T(8,128)(2,1)} %get-tuple-element.41.refs_0_, ...), custom_call_target="tpu_custom_call" | custom-call | flops 2147483648 | bytes 12582912 | tf_op jit(solution)/shard_map/project/pallas_call | solution.py:243
  48.4 3.3 %collective-permute-start.15 = (f32[2,136,256]{2,1,0:T(8,128)}, f32[2,136,256]{2,1,0:T(8,128)S(1)}, u32[]{:S(2)}, u32[]{:S(2)}) collective-permute-start(f32[2,136,256]{2,1,0:T(8,128)} %get-tuple-element.43), channel_id=1, source_target_pairs={{0,1},{2,3},{4,5},{6,7},{8,9},{10,11},{12,13},{14,15},{16,17},{18,... | collective-permute-start | bytes 835592 | tf_op jit(solution)/shard_map/ppermute | solution.py:705
  51.8 6.5 %collective-permute-done.15.st_in = f32[2,136,256]{2,1,0:T(8,128)S(1)} collective-permute-done((f32[2,136,256]{2,1,0:T(8,128)}, f32[2,136,256]{2,1,0:T(8,128)S(1)}, u32[]{:S(2)}, u32[]{:S(2)}) %collective-permute-start.15) | collective-permute-done | bytes 278560 | tf_op jit(solution)/shard_map/ppermute | solution.py:705
  59.0 10.2 %mix.1 = (bf16[1024,512]{1,0:T(8,128)(2,1)}, f32[1024,512]{1,0:T(8,128)}, f32[1024,512]{1,0:T(8,128)}, f32[1024,512]{1,0:T(8,128)}, bf16[8,2,256,256]{3,2,1,0:T(8,128)(2,1)}, /*index=5*/bf16[8,2,256,256]{3,2,1,0:T(8,128)(2,1)}) custom-call(bf16[1024,2048]{1,0:T(8,128)(2,1)} %get-tuple-element.42.pack_ref, f32[2,136,256]{2,1,0:T(8,128)} %copy-done.4), custom_call_target="tpu_custom_call" | custom-call | flops 6000000000 | bytes 16777216 | tf_op jit(solution)/shard_map/mix/pallas_call | solution.py:326
  69.2 23.5 %ffn.1 = (bf16[1024,512]{1,0:T(8,128)(2,1)}, f32[1024,512]{1,0:T(8,128)}, bf16[1024,512]{1,0:T(8,128)(2,1)}, bf16[512,4736]{1,0:T(8,128)(2,1)}) custom-call(bf16[1024,512]{1,0:T(8,128)(2,1)} %get-tuple-element.44.mixed_hbm, bf16[1024,512]{1,0:T(8,128)(2,1)} %tok_ref.1, bf16[1024,512]{1,0:T(8,128)(2,1)} %cot_hbm.1, ...), custom_call_target="tpu_custom_call" | custom-call | flops 12884901888 | bytes 20971520 | tf_op jit(solution)/shard_map/ffn/pallas_call | solution.py:459
  92.7 10.3 %read_back.1 = (bf16[1024,512]{1,0:T(8,128)(2,1)}, bf16[1024,512]{1,0:T(8,128)(2,1)}, bf16[1024,512]{1,0:T(8,128)(2,1)}, f32[1024,512]{1,0:T(8,128)}, f32[2,136,256]{2,1,0:T(8,128)}) custom-call(bf16[1024,2048]{1,0:T(8,128)(2,1)} %get-tuple-element.42.pack_ref, bf16[1024,512]{1,0:T(8,128)(2,1)} %get-tuple-element.48.gmix_ref, ...), custom_call_target="tpu_custom_call" | custom-call | flops 6000000000 | bytes 20971520 | tf_op jit(solution)/shard_map/read_back/pallas_call | solution.py:542
  104.3 9.0 %collective-permute-done.16.st_in = f32[2,136,256]{2,1,0:T(8,128)S(1)} collective-permute-done((f32[2,136,256]{2,1,0:T(8,128)}, f32[2,136,256]{2,1,0:T(8,128)S(1)}, u32[]{:S(2)}, u32[]{:S(2)}) %collective-permute-start.16) | collective-permute-done | bytes 278560 | tf_op jit(solution)/shard_map/ppermute | solution.py:705
  114.0 16.2 %write_back.1 = (bf16[1024,1536]{1,0:T(8,128)(2,1)}, bf16[4,32,2048]{2,1,0:T(8,128)(2,1)}, bf16[4,32,2048]{2,1,0:T(8,128)(2,1)}, bf16[4,32,2048]{2,1,0:T(8,128)(2,1)}, bf16[4,32,2048]{2,1,0:T(8,128)(2,1)}) custom-call(s32[1]{0:T(128)} %bitcast.me_ref, bf16[1024,2048]{1,0:T(8,128)(2,1)} %get-tuple-element.42.pack_ref, ...), custom_call_target="tpu_custom_call" | custom-call | flops 11000000512 | bytes 18874368 | tf_op jit(solution)/shard_map/write_back/pallas_call | solution.py:637
  137.9 9.0 %collective-permute-done.24 = bf16[32,2048]{1,0:T(8,128)(2,1)S(1)} collective-permute-done((bf16[32,2048]{1,0:T(8,128)(2,1)S(1)}, bf16[32,2048]{1,0:T(8,128)(2,1)S(1)}, u32[]{:S(2)}, u32[]{:S(2)}) %collective-permute-start.24) | collective-permute-done | bytes 131104 | tf_op jit(solution)/shard_map/ppermute | solution.py:685
  146.9 2.8 %collective-permute-done.22 = bf16[32,2048]{1,0:T(8,128)(2,1)S(1)} collective-permute-done((bf16[32,2048]{1,0:T(8,128)(2,1)S(1)}, bf16[32,2048]{1,0:T(8,128)(2,1)S(1)}, u32[]{:S(2)}, u32[]{:S(2)}) %collective-permute-start.22) | collective-permute-done | bytes 131104 | tf_op jit(solution)/shard_map/ppermute | solution.py:685
  149.7 2.5 %collective-permute-done.20 = bf16[32,2048]{1,0:T(8,128)(2,1)S(1)} collective-permute-done((bf16[32,2048]{1,0:T(8,128)(2,1)S(1)}, bf16[32,2048]{1,0:T(8,128)(2,1)S(1)}, u32[]{:S(2)}, u32[]{:S(2)}) %collective-permute-start.20) | collective-permute-done | bytes 131104 | tf_op jit(solution)/shard_map/ppermute | solution.py:685
  153.9 2.4 %collective-permute-start.25 = (bf16[32,2048]{1,0:T(8,128)(2,1)S(1)}, bf16[32,2048]{1,0:T(8,128)(2,1)S(1)}, u32[]{:S(2)}, u32[]{:S(2)}) collective-permute-start(bf16[32,2048]{1,0:T(8,128)(2,1)S(1)} %get-tuple-element.81), channel_id=1, source_target_pairs={{0,24},{2,26},{4,28},{6,30},{8,16},{10,18},{12,20},{14,22},{16,8},... | collective-permute-start | bytes 393224 | tf_op jit(solution)/shard_map/ppermute | solution.py:685
  156.3 3.8 %collective-permute-done.21 = bf16[32,2048]{1,0:T(8,128)(2,1)S(1)} collective-permute-done((bf16[32,2048]{1,0:T(8,128)(2,1)S(1)}, bf16[32,2048]{1,0:T(8,128)(2,1)S(1)}, u32[]{:S(2)}, u32[]{:S(2)}) %collective-permute-start.21) | collective-permute-done | bytes 131104 | tf_op jit(solution)/shard_map/ppermute | solution.py:685
  160.1 3.5 %collective-permute-done.25 = bf16[32,2048]{1,0:T(8,128)(2,1)S(1)} collective-permute-done((bf16[32,2048]{1,0:T(8,128)(2,1)S(1)}, bf16[32,2048]{1,0:T(8,128)(2,1)S(1)}, u32[]{:S(2)}, u32[]{:S(2)}) %collective-permute-start.25) | collective-permute-done | bytes 131104 | tf_op jit(solution)/shard_map/ppermute | solution.py:685
  163.6 4.7 %collective-permute-done.23 = bf16[32,2048]{1,0:T(8,128)(2,1)S(1)} collective-permute-done((bf16[32,2048]{1,0:T(8,128)(2,1)S(1)}, bf16[32,2048]{1,0:T(8,128)(2,1)S(1)}, u32[]{:S(2)}, u32[]{:S(2)}) %collective-permute-start.23) | collective-permute-done | bytes 131104 | tf_op jit(solution)/shard_map/ppermute | solution.py:685
  168.3 3.3 %collective-permute-start.26 = (bf16[32,2048]{1,0:T(8,128)(2,1)S(1)}, bf16[32,2048]{1,0:T(8,128)(2,1)S(1)}, u32[]{:S(2)}, u32[]{:S(2)}) collective-permute-start(bf16[32,2048]{1,0:T(8,128)(2,1)S(1)} %add_convert_fusion.4), channel_id=1, source_target_pairs={{0,1},{1,0},{2,3},{3,2},{4,5},{5,4},{6,7},{7,6},{8,9},{9,8},{10,11... | collective-permute-start | bytes 393224 | tf_op jit(solution)/shard_map/ppermute | solution.py:745
  171.6 7.6 %input_grad.1 = f32[1024,512]{1,0:T(8,128)} custom-call(f32[8,512]{1,0:T(8,128)} %get-tuple-element.47.gain_ref, bf16[1024,512]{1,0:T(8,128)(2,1)} %tok_ref.1, bf16[1024,512]{1,0:T(8,128)(2,1)} %get-tuple-element.64.gq_hbm.gq_ref, bf16[1024,1536]{1,0:T(8,128)(2,1)} %get-tuple-element.65.gkvc_ref, bf16[512,2048]{1,0:T(8,128)(2,1)} %get-tuple-element.66.w_ref, ...), custom_call_target="tpu_custom_call" | custom-call | flops 2147483648 | bytes 12582912 | tf_op jit(solution)/shard_map/input_grad/pallas_call | solution.py:672
  179.4 3.4 %reduce-scatter.2.cloned.1.call-done = bf16[32,4736]{1,0:T(8,128)(2,1)} async-done(((bf16[512,4736]{1,0:T(8,128)(2,1)}), bf16[32,4736]{1,0:T(8,128)(2,1)}) %reduce-scatter.2.cloned.1.call-update) | async-done | bytes 303120 | tf_op jit(solution)/shard_map/reduce_scatter | solution.py:736
  185.5 5.5 %collective-permute-done.27 = bf16[32,4736]{1,0:T(8,128)(2,1)S(1)} collective-permute-done((bf16[32,4736]{1,0:T(8,128)(2,1)}, bf16[32,4736]{1,0:T(8,128)(2,1)S(1)}, u32[]{:S(2)}, u32[]{:S(2)}) %collective-permute-start.27) | collective-permute-done | bytes 303136 | tf_op jit(solution)/shard_map/ppermute | solution.py:745
  (99 shorter events, 30.3 us)
Async XLA Ops:
  7.2 62.0 %all-gather.2.cloned.1.call-start = ((), (), s32[]{:S(2)}) async-start(), calls=%async_computation.1 | async-start | bytes 5152768 | tf_op jit(solution)/shard_map/all_gather | solution.py:728
  9.1 173.7 %reduce-scatter.2.cloned.1.call-start = ((), (), s32[]{:S(2)}) async-start(), calls=%async_computation.2 | async-start | bytes 5152768 | tf_op jit(solution)/shard_map/reduce_scatter | solution.py:736
  9.2 9.9 %collective-permute-start.11 = (bf16[32,2176]{1,0:T(8,128)(2,1)}, bf16[32,2176]{1,0:T(8,128)(2,1)S(1)}, u32[]{:S(2)}, u32[]{:S(2)}) collective-permute-start(bf16[32,2176]{1,0:T(8,128)(2,1)} %get-tuple-element.41.refs_0_), channel_id=1, source_target_pairs={{0,24},{2,26},{4,28},{6,30},{8,16},{10,18},{12,20},{14,22},{16,8},... | collective-permute-start | bytes 417800 | tf_op jit(solution)/shard_map/ppermute | solution.py:685
  14.3 15.1 %collective-permute-start.7 = (bf16[32,2176]{1,0:T(8,128)(2,1)}, bf16[32,2176]{1,0:T(8,128)(2,1)S(1)}, u32[]{:S(2)}, u32[]{:S(2)}) collective-permute-start(bf16[32,2176]{1,0:T(8,128)(2,1)} %get-tuple-element.41.refs_0_), channel_id=1, source_target_pairs={{0,16},{2,18},{4,20},{6,22},{8,24},{10,26},{12,28},{14,30},{16,0},... | collective-permute-start | bytes 417800 | tf_op jit(solution)/shard_map/ppermute | solution.py:685
  14.3 15.1 %collective-permute-start.3 = (bf16[32,2176]{1,0:T(8,128)(2,1)}, bf16[32,2176]{1,0:T(8,128)(2,1)S(1)}, u32[]{:S(2)}, u32[]{:S(2)}) collective-permute-start(bf16[32,2176]{1,0:T(8,128)(2,1)} %get-tuple-element.41.refs_0_), channel_id=1, source_target_pairs={{0,8},{2,10},{4,12},{6,14},{8,0},{10,2},{12,4},{14,6},{16,24},{18,... | collective-permute-start | bytes 417800 | tf_op jit(solution)/shard_map/ppermute | solution.py:685
  14.9 16.3 %collective-permute-start.1 = (bf16[32,2176]{1,0:T(8,128)(2,1)}, bf16[32,2176]{1,0:T(8,128)(2,1)S(1)}, u32[]{:S(2)}, u32[]{:S(2)}) collective-permute-start(bf16[32,2176]{1,0:T(8,128)(2,1)} %get-tuple-element.41.refs_0_), channel_id=1, source_target_pairs={{0,4},{2,6},{4,0},{6,2},{8,12},{10,14},{12,8},{14,10},{16,20},{18,... | collective-permute-start | bytes 417800 | tf_op jit(solution)/shard_map/ppermute | solution.py:685
  16.6 14.8 %collective-permute-start = (bf16[32,2176]{1,0:T(8,128)(2,1)}, bf16[32,2176]{1,0:T(8,128)(2,1)S(1)}, u32[]{:S(2)}, u32[]{:S(2)}) collective-permute-start(bf16[32,2176]{1,0:T(8,128)(2,1)} %get-tuple-element.41.refs_0_), channel_id=1, source_target_pairs={{0,2},{2,0},{4,6},{6,4},{8,10},{10,8},{12,14},{14,12},{16,18},{18,... | collective-permute-start | bytes 417800 | tf_op jit(solution)/shard_map/ppermute | solution.py:685
  19.1 12.6 %collective-permute-start.13 = (bf16[32,2176]{1,0:T(8,128)(2,1)S(1)}, bf16[32,2176]{1,0:T(8,128)(2,1)S(1)}, u32[]{:S(2)}, u32[]{:S(2)}) collective-permute-start(bf16[32,2176]{1,0:T(8,128)(2,1)S(1)} %collective-permute-done.11.refs_12_), channel_id=1, source_target_pairs={{0,4},{2,6},{4,0},{6,2},{8,12},{10,14},{12,8},{14,10},{16,20},{18,... | collective-permute-start | bytes 417800 | tf_op jit(solution)/shard_map/ppermute | solution.py:685
  29.4 6.5 %collective-permute-start.9 = (bf16[32,2176]{1,0:T(8,128)(2,1)S(1)}, bf16[32,2176]{1,0:T(8,128)(2,1)S(1)}, u32[]{:S(2)}, u32[]{:S(2)}) collective-permute-start(bf16[32,2176]{1,0:T(8,128)(2,1)S(1)} %collective-permute-done.7.refs_8_), channel_id=1, source_target_pairs={{0,4},{2,6},{4,0},{6,2},{8,12},{10,14},{12,8},{14,10},{16,20},{18,... | collective-permute-start | bytes 417800 | tf_op jit(solution)/shard_map/ppermute | solution.py:685
  31.4 7.2 %collective-permute-start.5 = (bf16[32,2176]{1,0:T(8,128)(2,1)S(1)}, bf16[32,2176]{1,0:T(8,128)(2,1)S(1)}, u32[]{:S(2)}, u32[]{:S(2)}) collective-permute-start(bf16[32,2176]{1,0:T(8,128)(2,1)S(1)} %collective-permute-done.3.refs_4_), channel_id=1, source_target_pairs={{0,4},{2,6},{4,0},{6,2},{8,12},{10,14},{12,8},{14,10},{16,20},{18,... | collective-permute-start | bytes 417800 | tf_op jit(solution)/shard_map/ppermute | solution.py:685
  31.7 6.8 %collective-permute-start.4 = (bf16[32,2176]{1,0:T(8,128)(2,1)S(1)}, bf16[32,2176]{1,0:T(8,128)(2,1)S(1)}, u32[]{:S(2)}, u32[]{:S(2)}) collective-permute-start(bf16[32,2176]{1,0:T(8,128)(2,1)S(1)} %collective-permute-done.3.refs_4_), channel_id=1, source_target_pairs={{0,2},{2,0},{4,6},{6,4},{8,10},{10,8},{12,14},{14,12},{16,18},{18,... | collective-permute-start | bytes 417800 | tf_op jit(solution)/shard_map/ppermute | solution.py:685
  31.8 6.7 %collective-permute-start.2 = (bf16[32,2176]{1,0:T(8,128)(2,1)S(1)}, bf16[32,2176]{1,0:T(8,128)(2,1)S(1)}, u32[]{:S(2)}, u32[]{:S(2)}) collective-permute-start(bf16[32,2176]{1,0:T(8,128)(2,1)S(1)} %collective-permute-done.1.refs_2_), channel_id=1, source_target_pairs={{0,2},{2,0},{4,6},{6,4},{8,10},{10,8},{12,14},{14,12},{16,18},{18,... | collective-permute-start | bytes 417800 | tf_op jit(solution)/shard_map/ppermute | solution.py:685
  48.4 9.8 %collective-permute-start.15 = (f32[2,136,256]{2,1,0:T(8,128)}, f32[2,136,256]{2,1,0:T(8,128)S(1)}, u32[]{:S(2)}, u32[]{:S(2)}) collective-permute-start(f32[2,136,256]{2,1,0:T(8,128)} %get-tuple-element.43), channel_id=1, source_target_pairs={{0,1},{2,3},{4,5},{6,7},{8,9},{10,11},{12,13},{14,15},{16,17},{18,... | collective-permute-start | bytes 835592 | tf_op jit(solution)/shard_map/ppermute | solution.py:705
  103.0 10.3 %collective-permute-start.16 = (f32[2,136,256]{2,1,0:T(8,128)}, f32[2,136,256]{2,1,0:T(8,128)S(1)}, u32[]{:S(2)}, u32[]{:S(2)}) collective-permute-start(f32[2,136,256]{2,1,0:T(8,128)} %get-tuple-element.58), channel_id=1, source_target_pairs={{1,0},{3,2},{5,4},{7,6},{9,8},{11,10},{13,12},{15,14},{17,16},{19,... | collective-permute-start | bytes 835592 | tf_op jit(solution)/shard_map/ppermute | solution.py:705
  130.3 7.5 %collective-permute-start.17 = (bf16[4,32,2048]{2,1,0:T(8,128)(2,1)}, bf16[4,32,2048]{2,1,0:T(8,128)(2,1)S(1)}, u32[]{:S(2)}, u32[]{:S(2)}) collective-permute-start(bf16[4,32,2048]{2,1,0:T(8,128)(2,1)} %get-tuple-element.61), channel_id=1, source_target_pairs={{0,2},{2,0},{4,6},{6,4},{8,10},{10,8},{12,14},{14,12},{16,18},{18,... | collective-permute-start | bytes 1572872 | tf_op jit(solution)/shard_map/ppermute | solution.py:685
  133.7 22.7 %collective-permute-start.19 = (bf16[32,2048]{1,0:T(8,128)(2,1)S(1)}, bf16[32,2048]{1,0:T(8,128)(2,1)S(1)}, u32[]{:S(2)}, u32[]{:S(2)}) collective-permute-start(bf16[32,2048]{1,0:T(8,128)(2,1)S(1)} %get-tuple-element.76), channel_id=1, source_target_pairs={{0,4},{2,6},{4,0},{6,2},{8,12},{10,14},{12,8},{14,10},{16,20},{18,... | collective-permute-start | bytes 393224 | tf_op jit(solution)/shard_map/ppermute | solution.py:685
  135.4 11.5 %collective-permute-start.24 = (bf16[32,2048]{1,0:T(8,128)(2,1)S(1)}, bf16[32,2048]{1,0:T(8,128)(2,1)S(1)}, u32[]{:S(2)}, u32[]{:S(2)}) collective-permute-start(bf16[32,2048]{1,0:T(8,128)(2,1)S(1)} %get-tuple-element.77), channel_id=1, source_target_pairs={{0,4},{2,6},{4,0},{6,2},{8,12},{10,14},{12,8},{14,10},{16,20},{18,... | collective-permute-start | bytes 393224 | tf_op jit(solution)/shard_map/ppermute | solution.py:685
  135.8 14.0 %collective-permute-start.22 = (bf16[32,2048]{1,0:T(8,128)(2,1)S(1)}, bf16[32,2048]{1,0:T(8,128)(2,1)S(1)}, u32[]{:S(2)}, u32[]{:S(2)}) collective-permute-start(bf16[32,2048]{1,0:T(8,128)(2,1)S(1)} %get-tuple-element.78), channel_id=1, source_target_pairs={{0,4},{2,6},{4,0},{6,2},{8,12},{10,14},{12,8},{14,10},{16,20},{18,... | collective-permute-start | bytes 393224 | tf_op jit(solution)/shard_map/ppermute | solution.py:685
  137.4 14.9 %collective-permute-start.20 = (bf16[32,2048]{1,0:T(8,128)(2,1)S(1)}, bf16[32,2048]{1,0:T(8,128)(2,1)S(1)}, u32[]{:S(2)}, u32[]{:S(2)}) collective-permute-start(bf16[32,2048]{1,0:T(8,128)(2,1)S(1)} %get-tuple-element.79), channel_id=1, source_target_pairs={{0,4},{2,6},{4,0},{6,2},{8,12},{10,14},{12,8},{14,10},{16,20},{18,... | collective-permute-start | bytes 393224 | tf_op jit(solution)/shard_map/ppermute | solution.py:685
  152.4 7.7 %collective-permute-start.21 = (bf16[32,2048]{1,0:T(8,128)(2,1)S(1)}, bf16[32,2048]{1,0:T(8,128)(2,1)S(1)}, u32[]{:S(2)}, u32[]{:S(2)}) collective-permute-start(bf16[32,2048]{1,0:T(8,128)(2,1)S(1)} %get-tuple-element.80), channel_id=1, source_target_pairs={{0,8},{2,10},{4,12},{6,14},{8,0},{10,2},{12,4},{14,6},{16,24},{18,... | collective-permute-start | bytes 393224 | tf_op jit(solution)/shard_map/ppermute | solution.py:685
  153.9 9.6 %collective-permute-start.25 = (bf16[32,2048]{1,0:T(8,128)(2,1)S(1)}, bf16[32,2048]{1,0:T(8,128)(2,1)S(1)}, u32[]{:S(2)}, u32[]{:S(2)}) collective-permute-start(bf16[32,2048]{1,0:T(8,128)(2,1)S(1)} %get-tuple-element.81), channel_id=1, source_target_pairs={{0,24},{2,26},{4,28},{6,30},{8,16},{10,18},{12,20},{14,22},{16,8},... | collective-permute-start | bytes 393224 | tf_op jit(solution)/shard_map/ppermute | solution.py:685
  156.3 11.9 %collective-permute-start.23 = (bf16[32,2048]{1,0:T(8,128)(2,1)S(1)}, bf16[32,2048]{1,0:T(8,128)(2,1)S(1)}, u32[]{:S(2)}, u32[]{:S(2)}) collective-permute-start(bf16[32,2048]{1,0:T(8,128)(2,1)S(1)} %get-tuple-element.82), channel_id=1, source_target_pairs={{0,16},{2,18},{4,20},{6,22},{8,24},{10,26},{12,28},{14,30},{16,0},... | collective-permute-start | bytes 393224 | tf_op jit(solution)/shard_map/ppermute | solution.py:685
  168.3 11.0 %collective-permute-start.26 = (bf16[32,2048]{1,0:T(8,128)(2,1)S(1)}, bf16[32,2048]{1,0:T(8,128)(2,1)S(1)}, u32[]{:S(2)}, u32[]{:S(2)}) collective-permute-start(bf16[32,2048]{1,0:T(8,128)(2,1)S(1)} %add_convert_fusion.4), channel_id=1, source_target_pairs={{0,1},{1,0},{2,3},{3,2},{4,5},{5,4},{6,7},{7,6},{8,9},{9,8},{10,11... | collective-permute-start | bytes 393224 | tf_op jit(solution)/shard_map/ppermute | solution.py:745
  182.9 8.2 %collective-permute-start.27 = (bf16[32,4736]{1,0:T(8,128)(2,1)}, bf16[32,4736]{1,0:T(8,128)(2,1)S(1)}, u32[]{:S(2)}, u32[]{:S(2)}) collective-permute-start(bf16[32,4736]{1,0:T(8,128)(2,1)} %reduce-scatter.2.cloned.1.call-done), channel_id=1, source_target_pairs={{0,1},{1,0},{2,3},{3,2},{4,5},{5,4},{6,7},{7,6},{8,9},{9,8},{10,11... | collective-permute-start | bytes 909320 | tf_op jit(solution)/shard_map/ppermute | solution.py:745
  (26 other events, 136.1 us)
Sparse Core Ops, SparseCore 0:
  10.9 57.6 all-gather.1
  92.8 89.9 reduce-scatter.1

commit v4 on v3

--- a/solution.py
+++ b/solution.py
@@ -79,7 +79,7 @@
     return iota((QUAD, QUAD), 0) // HEAD == iota((QUAD, QUAD), 1) // HEAD
 
 
-STATE = 2 * HEAD + 8
+STATE = 2 * HEAD + 16
 
 
 def store_state(st_ref, first, second, total):
@@ -87,17 +87,21 @@
     for g in range(st_ref.shape[0]):
         for k, ref in enumerate((first, second)):
             x = jnp.where(square, ref[g], 0.0)
-            st_ref[g, k * HEAD : (k + 1) * HEAD, :] = x[0:64] + x[64:128] + x[128:192] + x[192:256]
-        st_ref[g, 2 * HEAD :, :] = jnp.broadcast_to(total[0:1, g * QUAD : (g + 1) * QUAD], (8, QUAD))
+            st_ref[g, k * HEAD : (k + 1) * HEAD, :] = (x[0:64] + x[64:128] + x[128:192] + x[192:256]).astype(BF16)
+        hi, lo = hi_lo(total[0:1, g * QUAD : (g + 1) * QUAD])
+        row = iota((16, QUAD), 0)
+        spread = lambda x: jnp.broadcast_to(x.astype(F32), (16, QUAD))
+        st_ref[g, 2 * HEAD :, :] = jnp.where(row == 0, spread(hi), jnp.where(row == 1, spread(lo), 0.0)).astype(BF16)
 
 
 def load_state(st_ref, first, second, total):
     square = head_square()
     for g in range(st_ref.shape[0]):
         for k, ref in enumerate((first, second)):
-            x = st_ref[g, k * HEAD : (k + 1) * HEAD, :]
+            x = st_ref[g, k * HEAD : (k + 1) * HEAD, :].astype(F32)
             ref[g] = jnp.where(square, jnp.concatenate([x] * 4, axis=0), 0.0)
-        total[:, g * QUAD : (g + 1) * QUAD] = st_ref[g, 2 * HEAD :, :]
+        both = jnp.sum(st_ref[g, 2 * HEAD :, :].astype(F32), axis=0, keepdims=True)
+        total[:, g * QUAD : (g + 1) * QUAD] = jnp.broadcast_to(both, (8, QUAD))
 
 
 def hi_lo(x):
@@ -247,7 +251,7 @@
         out_shape=[
             jax.ShapeDtypeStruct((t, d), BF16),
             jax.ShapeDtypeStruct((t, wide), BF16),
-            jax.ShapeDtypeStruct((g, STATE, QUAD), F32),
+            jax.ShapeDtypeStruct((g, STATE, QUAD), BF16),
             jax.ShapeDtypeStruct((d, wide), BF16),
             jax.ShapeDtypeStruct((8, d), F32),
         ],
@@ -337,8 +341,10 @@
     )(packed, state)
 
 
-def ffn_kernel(n, mixed_hbm, tok_hbm, cot_hbm, full_ref, out_hbm, gres_hbm, gmix_hbm, grad_ref,
-               mixed, tok, cot, outs, gres, gmix, w_out, w_up, w_down, vecs, hid, gpre, fin, gbr, sems, osems):
+def ffn_kernel(n, me_ref, mixed_hbm, tok_hbm, cot_hbm, full_ref, out_hbm, gres_hbm, gmix_hbm, *refs):
+    share_refs = refs[:4]
+    (mixed, tok, cot, outs, gres, gmix, w_out, w_up, w_down, vecs, hid, gpre, fin, gbr, sems, osems) = refs[4:]
+    me = me_ref[0]
     t, d = mixed.shape
     ff = w_up.shape[1]
     r = d // n
@@ -427,12 +433,16 @@
         ggain += jnp.sum(gin * normed, axis=0, keepdims=True)
         gbdown += jnp.sum(cotf, axis=0, keepdims=True)
 
+    def share(j, rows_of, ref, at, width):
+        send(ref.at[rows_of(me ^ j), :], share_refs[j % 4].at[j // 4, :, pl.ds(at, width)])
+
+    own_rows = lambda f: pl.ds(pl.multiple_of(f * r, r), r)
     for p in range(parts):
         ps = slice(p * part, (p + 1) * part)
         w_up[:, ps] = t_mm(fin[...], gpre[:, ps]).astype(BF16)
-        send(w_up.at[:, ps], grad_ref.at[:, ps])
+    for j in range(n):
+        share(j, own_rows, w_up, 0, ff)
     w_out[...] = t_mm(mixed[...], gbr[...]).astype(BF16)
-    send(w_out, grad_ref.at[:, pl.ds(2 * ff, d)])
     va = gather_vector(ggain, 0, n, r)
     vb = gather_vector(jnp.concatenate(gbup, axis=1), 0, n, r * mult)
     vc = gather_vector(gbdown, 0, n, r)
@@ -441,31 +451,33 @@
     for j in range(n):
         tile = pick(va, j, 1, pick(vb, j, 2, pick(vc, j, 3, jnp.zeros((r, 128), F32))))
         vecs[j * r : (j + 1) * r, :] = tile.astype(BF16)
-    send(vecs, grad_ref.at[:, pl.ds(2 * ff + d, 128)])
+    for j in range(n):
+        share(j, own_rows, w_out, 2 * ff, d)
+        share(j, own_rows, vecs, 2 * ff + d, 128)
     for p in range(parts):
         ps = slice(p * part, (p + 1) * part)
         w_down[ps, :] = t_mm(hid[:, ps], cot[...]).astype(BF16)
-        count = part // r
-        for i in range(p * count, (p + 1) * count):
-            send(down[i][1], grad_ref.at[pl.ds(i // mult * r, r), pl.ds(ff + i % mult * d, d)])
+    for j in range(n):
+        for m in range(mult):
+            share(j, lambda f: pl.ds(pl.multiple_of((f * mult + m) * r, r), r), w_down, ff + m * d, d)
     for c in sent:
         c.wait()
 
 
-def ffn(mixed, tokens, cot, full, ff, n):
+def ffn(me, mixed, tokens, cot, full, ff, n):
     t, d = tokens.shape
     hbm = pl.BlockSpec(memory_space=pl.ANY)
     moves = n * (ff // d)
     return pl.pallas_call(
         partial(ffn_kernel, n),
-        in_specs=[hbm] * 4,
-        out_specs=[hbm] * 4,
+        in_specs=[pl.BlockSpec(memory_space=pltpu.SMEM)] + [hbm] * 4,
+        out_specs=[hbm] * 7,
         out_shape=[
             jax.ShapeDtypeStruct((t, d), BF16),
             jax.ShapeDtypeStruct((t, d), F32),
             jax.ShapeDtypeStruct((t, d), BF16),
-            jax.ShapeDtypeStruct(full.shape, BF16),
-        ],
+        ]
+        + [jax.ShapeDtypeStruct((n // 4, d // n, full.shape[1]), BF16)] * 4,
         scratch_shapes=[pltpu.VMEM((t, d), BF16)] * 4
         + [pltpu.VMEM((t, d), F32), pltpu.VMEM((t, d), BF16)]
         + [
@@ -478,12 +490,12 @@
             pltpu.VMEM((t, d), BF16),
             pltpu.VMEM((t, d), BF16),
             pltpu.SemaphoreType.DMA((7 + moves,)),
-            pltpu.SemaphoreType.DMA((3 * (t // 256) + ff // 512 + 2 + moves,)),
+            pltpu.SemaphoreType.DMA((3 * (t // 256) + 3 * n + moves,)),
         ],
         compiler_params=pltpu.CompilerParams(vmem_limit_bytes=VMEM_LIMIT),
         cost_estimate=pl.CostEstimate(flops=12 * t * d * ff, bytes_accessed=20 << 20, transcendentals=t * ff),
         name="ffn",
-    )(mixed, tokens, cot, full)
+    )(me, mixed, tokens, cot, full)
 
 
 def read_back_kernel(pack_ref, gmix_ref, read_ref, score_ref, inv_ref, kts_ref, mvs_ref,
@@ -545,7 +557,7 @@
         in_specs=[row(wide), row(d), row(d), row(d), row(d), st, st],
         out_specs=[row(d)] * 4 + [const(g, STATE, QUAD)],
         out_shape=[jax.ShapeDtypeStruct((t, d), BF16)] * 3 + [jax.ShapeDtypeStruct((t, d), F32)]
-        + [jax.ShapeDtypeStruct((g, STATE, QUAD), F32)],
+        + [jax.ShapeDtypeStruct((g, STATE, QUAD), BF16)],
         scratch_shapes=[pltpu.VMEM((g, QUAD, QUAD), F32), pltpu.VMEM((g, QUAD, QUAD), F32), pltpu.VMEM((8, d), F32)],
         compiler_params=pltpu.CompilerParams(vmem_limit_bytes=VMEM_LIMIT),
         cost_estimate=pl.CostEstimate(flops=6 * 10**9, bytes_accessed=20 << 20, transcendentals=t * d),
@@ -708,6 +720,8 @@
 def others(state, direction, seqs):
     if seqs == 1:
         return jnp.zeros_like(state)
+    if seqs > 2:
+        state = state.astype(F32)
     total = shift(state, direction, seqs)
     step = 1
     while step < seqs - 1:
@@ -732,12 +746,20 @@
     att_where = [(j, None) for j in range(n)]
     att, packed, state, w_att, gain = project(me, tokens, att_where, att_pieces)
     mixed, read, score, inv, kts, mvs = mix(packed, others(state, 1, seqs))
-    layer_out, gres, gmix, ffn_grad = ffn(mixed, tokens, cotangent, full, ff, n)
-    ffn_sum = lax.psum_scatter(ffn_grad, "fsdp", scatter_dimension=0, tiled=True)
-
-    def core_sum(shares):
+    layer_out, gres, gmix, *ffn_shares = ffn(me, mixed, tokens, cotangent, full, ff, n)
+    order = range(depth - 1, -1, -1)
+
+    def start_sum(shares):
         near, near_core, far, far_core = shares
-        return add(near, swap(near_core, 1, n)), add(far, swap(far_core, 1, n))
+        far_core = swap(far_core, 1, n)
+        near_core = swap(near_core, 1, n)
+        return near, near_core, {k: add(far[k], far_core[k]) for k in order}
+
+    def cross(far, keys, *first):
+        return {k: swap(after(far[k], *first) if first else far[k], 2, n) for k in keys}
+
+    def along(part, k):
+        return swap(part, 4 * k, n) if k else part
 
     def seq_sum(x):
         step = 1
@@ -746,14 +768,23 @@
             step *= 2
         return x.astype(F32)
 
-    gq, a, u, gtot, gstate = read_back(packed, gmix, read, score, inv, kts, mvs)
-    gkvc, *shares = write_back(me, packed, gmix, a, u, gtot, others(gstate, -1, seqs), att, gq, n)
-    near, far = core_sum(shares)
-    grad_tokens = input_grad(gain, tokens, after(gq, near, far), gkvc, w_att, gres)
-    mine = {k: add(near[k], swap(far[k], 2, n)) for k in range(depth - 1, -1, -1)}
-    sent = {k: swap(mine[k], 4 * k, n) if k else mine[k] for k in range(depth)}
-    ffn_share = seq_sum(ffn_sum)
-    att_share = seq_sum(add(*sent.values()))
+    high, low = [k for k in order if k >= depth // 2], [k for k in order if k < depth // 2]
+    near, near_core, far = start_sum(ffn_shares)
+    crossed = cross(far, high)
+    gq, a, u, gtot, gstate = read_back(packed, after(gmix, *far.values()), read, score, inv, kts, mvs)
+    crossed |= cross(far, low, gq)
+    mine = {k: add(after(near[k], gq), near_core[k], crossed[k]) for k in high}
+    gkvc, *shares = write_back(
+        me, packed, gmix, a, u, gtot, after(others(gstate, -1, seqs), *mine.values()), att, gq, n
+    )
+    mine |= {k: add(after(near[k], gkvc), near_core[k], crossed[k]) for k in low}
+    ffn_parts = [along(mine[k], k) for k in order]
+    near, near_core, far = start_sum(shares)
+    crossed = cross(far, order)
+    grad_tokens = input_grad(gain, tokens, after(gq, *far.values()), gkvc, w_att, gres)
+    att_parts = [along(add(after(near[k], grad_tokens), near_core[k], crossed[k]), k) for k in order]
+    ffn_share = seq_sum(add(*ffn_parts))
+    att_share = seq_sum(add(*att_parts))
     gain_share = jnp.sum(att_share * first[:, : 4 * d].astype(F32), axis=1) / gain_attn.astype(F32)
     up, down, out, vec = (
         ffn_share[:, :ff],

time: 202 us -> 189 us (0.936)
  waiting for transfers between devices: 70.5 us -> 44.5 us
  starting transfers between devices: 30.5 us -> 37.9 us
  other arithmetic: 3.92 us -> 6.56 us
    ppermute x2, waiting for transfers between devices: 15.4 us -> 3.66 us  [shift(): lax.ppermute(x, 'seq', [(i, i + by) for i in range(seqs) if 0 <= i + by <...]
    ppermute x24 -> x33, waiting for transfers between devices: 46.1 us -> 35.6 us  [swap(): return lax.ppermute(x, 'fsdp', [(i, i ^ mask) for i in range(n)])]
    ppermute x24 -> x33, starting transfers between devices: 21 us -> 30.3 us  [swap(): return lax.ppermute(x, 'fsdp', [(i, i ^ mask) for i in range(n)])]
    convert_element_type x4 -> x7, other arithmetic: 1.48 us -> 5.08 us  [add(): return sum((x.astype(F32) for x in items)).astype(BF16)]
    reduce_scatter x1 -> x0, waiting for transfers between devices: 3.42 us -> none  [on_device(): lax.psum_scatter(ffn_grad, 'fsdp', scatter_dimension=0, tiled=True)]
    ppermute x2, waiting for transfers between devices: 5.53 us -> 2.71 us  [seq_sum(): x = add(x, lax.ppermute(x, 'seq', [(i, i ^ step) for i in range(seqs)]))]
    all_gather x1, waiting for transfers between devices: 0.02 us -> 2.56 us  [on_device(): full = lax.all_gather(second, 'fsdp', axis=0, tiled=True)]
    squeeze x1 -> x2, local copies, waits for them, and re-layouts: 0.04 us -> 2.45 us  [on_device(): near[k]]
  transfers between devices with their start and end apart: 30 -> 38, of which waited for: 16 -> 15; matrix products, arithmetic and copies ran while one was open for 1% -> 6% of each run, Pallas kernels for 26% -> 27%
where the time goes in v4:
time: 189 us; the launch traced here: 188 us
  Pallas kernels  77.9 us (41%)
  waiting for transfers between devices  44.5 us (24%)
  starting transfers between devices  37.9 us (20%)
  between operations  14.4 us (8%)
  local copies, waits for them, and re-layouts  6.83 us (4%)
  other arithmetic  6.56 us (3%)
    ppermute x33, waiting for transfers between devices, swap(): return lax.ppermute(x, 'fsdp', [(i, i ^ mask) for i in range(n)])  35.6 us
    ppermute x33, starting transfers between devices, swap(): return lax.ppermute(x, 'fsdp', [(i, i ^ mask) for i in range(n)])  30.3 us
    pallas_call x1, Pallas kernels, ffn(): pl.pallas_call(partial(ffn_kernel, n), in_specs=[pl.BlockSpec(memory_spac...  24.6 us
    pallas_call x1, Pallas kernels, write_back(): pl.pallas_call(partial(write_back_kernel, n), grid=(t // rows,), in_specs...  15.9 us
    pallas_call x1, Pallas kernels, read_back(): pl.pallas_call(read_back_kernel, grid=(t // rows,), in_specs=[row(wide),...  10.2 us
    pallas_call x1, Pallas kernels, mix(): pl.pallas_call(mix_kernel, grid=(t // rows,), in_specs=[row(wide), const(...  10.2 us
    pallas_call x1, Pallas kernels, project(): pl.pallas_call(partial(project_kernel, where, len(pieces), r), in_specs=[...  7.64 us
    pallas_call x1, Pallas kernels, input_grad(): pl.pallas_call(input_grad_kernel, grid=(t // rows,), in_specs=[const(8, d...  7.55 us
  transfers between devices with their start and end apart: 38, of which 15 were waited for; matrix products, arithmetic and copies ran while one was open for 6% of the time, Pallas kernels for 27%

profile of v4, /device:TPU:0, one launch (start us, length us, event | category | flops | bytes accessed | tf_op | source)
XLA Modules:
  0.0 188.1 jit_solution(41297896267339186)
XLA Ops:
  9.1 5.1 %collective-permute-start.11 = (bf16[32,2176]{1,0:T(8,128)(2,1)}, bf16[32,2176]{1,0:T(8,128)(2,1)S(1)}, u32[]{:S(2)}, u32[]{:S(2)}) collective-permute-start(bf16[32,2176]{1,0:T(8,128)(2,1)} %get-tuple-element.56.refs_0_), channel_id=1, source_target_pairs={{0,24},{2,26},{4,28},{6,30},{8,16},{10,18},{12,20},{14,22},{16,8},... | collective-permute-start | bytes 417800 | tf_op jit(solution)/shard_map/ppermute | solution.py:697
  16.5 2.5 %collective-permute-done.11.refs_12_ = bf16[32,2176]{1,0:T(8,128)(2,1)S(1)} collective-permute-done((bf16[32,2176]{1,0:T(8,128)(2,1)}, bf16[32,2176]{1,0:T(8,128)(2,1)S(1)}, u32[]{:S(2)}, u32[]{:S(2)}) %collective-permute-start.11) | collective-permute-done | bytes 139296 | tf_op jit(solution)/shard_map/ppermute | solution.py:697
  20.8 8.4 %collective-permute-done.7.refs_8_ = bf16[32,2176]{1,0:T(8,128)(2,1)S(1)} collective-permute-done((bf16[32,2176]{1,0:T(8,128)(2,1)}, bf16[32,2176]{1,0:T(8,128)(2,1)S(1)}, u32[]{:S(2)}, u32[]{:S(2)}) %collective-permute-start.7) | collective-permute-done | bytes 139296 | tf_op jit(solution)/shard_map/ppermute | solution.py:697
  32.0 3.7 %collective-permute-done.9.refs_10_ = bf16[32,2176]{1,0:T(8,128)(2,1)S(1)} collective-permute-done((bf16[32,2176]{1,0:T(8,128)(2,1)S(1)}, bf16[32,2176]{1,0:T(8,128)(2,1)S(1)}, u32[]{:S(2)}, u32[]{:S(2)}) %collective-permute-start.9) | collective-permute-done | bytes 139296 | tf_op jit(solution)/shard_map/ppermute | solution.py:697
  40.3 7.6 %project.1 = (bf16[1024,512]{1,0:T(8,128)(2,1)}, bf16[1024,2048]{1,0:T(8,128)(2,1)}, bf16[2,144,256]{2,1,0:T(8,128)(2,1)}, bf16[512,2048]{1,0:T(8,128)(2,1)}, f32[8,512]{1,0:T(8,128)}) custom-call(s32[1]{0:T(128)} %bitcast.me_ref, bf16[1024,512]{1,0:T(8,128)(2,1)} %tok_ref.1, bf16[32,2176]{1,0:T(8,128)(2,1)} %get-tuple-element.56.refs_0_, ...), custom_call_target="tpu_custom_call" | custom-call | flops 2147483648 | bytes 12582912 | tf_op jit(solution)/shard_map/project/pallas_call | solution.py:247
  47.9 3.5 %collective-permute-start.15 = (bf16[2,144,256]{2,1,0:T(8,128)(2,1)}, bf16[2,144,256]{2,1,0:T(8,128)(2,1)S(1)}, u32[]{:S(2)}, u32[]{:S(2)}) collective-permute-start(bf16[2,144,256]{2,1,0:T(8,128)(2,1)} %get-tuple-element.58), channel_id=1, source_target_pairs={{0,1},{2,3},{4,5},{6,7},{8,9},{10,11},{12,13},{14,15},{16,17},{18,... | collective-permute-start | bytes 442376 | tf_op jit(solution)/shard_map/ppermute | solution.py:717
  51.4 3.7 %collective-permute-done.15.st_in = bf16[2,144,256]{2,1,0:T(8,128)(2,1)S(1)} collective-permute-done((bf16[2,144,256]{2,1,0:T(8,128)(2,1)}, bf16[2,144,256]{2,1,0:T(8,128)(2,1)S(1)}, u32[]{:S(2)}, u32[]{:S(2)}) %collective-permute-start.15) | collective-permute-done | bytes 147488 | tf_op jit(solution)/shard_map/ppermute | solution.py:717
  55.8 10.2 %mix.1 = (bf16[1024,512]{1,0:T(8,128)(2,1)}, f32[1024,512]{1,0:T(8,128)}, f32[1024,512]{1,0:T(8,128)}, f32[1024,512]{1,0:T(8,128)}, bf16[8,2,256,256]{3,2,1,0:T(8,128)(2,1)}, /*index=5*/bf16[8,2,256,256]{3,2,1,0:T(8,128)(2,1)}) custom-call(bf16[1024,2048]{1,0:T(8,128)(2,1)} %get-tuple-element.57.pack_ref, bf16[2,144,256]{2,1,0:T(8,128)(2,1)} %copy-done.4), custom_call_target="tpu_custom_call" | custom-call | flops 6000000000 | bytes 16777216 | tf_op jit(solution)/shard_map/mix/pallas_call | solution.py:330
  65.9 2.6 %all-gather.2.cloned.1.call-done.full_ref = bf16[512,4736]{1,0:T(8,128)(2,1)} async-done(((bf16[32,4736]{1,0:T(8,128)(2,1)}), bf16[512,4736]{1,0:T(8,128)(2,1)}) %all-gather.2.cloned.1.call-update) | async-done | bytes 4849680 | tf_op jit(solution)/shard_map/all_gather | solution.py:742
  68.5 24.6 %ffn.1 = (bf16[1024,512]{1,0:T(8,128)(2,1)}, f32[1024,512]{1,0:T(8,128)}, bf16[1024,512]{1,0:T(8,128)(2,1)}, bf16[4,32,4736]{2,1,0:T(8,128)(2,1)}, bf16[4,32,473...) custom-call(s32[1]{0:T(128)} %bitcast.me_ref, ...), custom_call_target="tpu_custom_call" | custom-call | flops 12884901888 | bytes 20971520 | tf_op jit(solution)/shard_map/ffn/pallas_call | solution.py:471
  98.6 10.2 %read_back.1 = (bf16[1024,512]{1,0:T(8,128)(2,1)}, bf16[1024,512]{1,0:T(8,128)(2,1)}, bf16[1024,512]{1,0:T(8,128)(2,1)}, f32[1024,512]{1,0:T(8,128)}, bf16[2,144,256]{2,1,0:T(8,128)(2,1)}) custom-call(bf16[1024,2048]{1,0:T(8,128)(2,1)} %get-tuple-element.57.pack_ref, bf16[1024,512]{1,0:T(8,128)(2,1)} %get-tuple-element.66.gmix_ref, ...), custom_call_target="tpu_custom_call" | custom-call | flops 6000000000 | bytes 20971520 | tf_op jit(solution)/shard_map/read_back/pallas_call | solution.py:554
  112.6 2.0 %fusion.5 = (bf16[32,4736]{1,0:T(8,128)(2,1)}, bf16[32,4736]{1,0:T(8,128)(2,1)S(1)}) fusion(bf16[32,4736]{1,0:T(8,128)(2,1)} %collective-permute-done.20, bf16[32,4736]{1,0:T(8,128)(2,1)S(1)} %get-tuple-element.80, bf16[4,32,4736]{2,1,0:T(8,128)(2,1)S(1)} %collective-permute-done.18, bf16[32,4736]{1,0:T(8,128)(2,1)} %collective-permute-done.19, ...), kind=kLoop, calls=%fused_computation.8 | loop fusion | flops 1818624 | bytes 2424832 | tf_op jit(solution)/shard_map/convert_element_type | solution.py:705
  116.5 2.0 %collective-permute-start.31 = (bf16[32,4736]{1,0:T(8,128)(2,1)S(1)}, bf16[32,4736]{1,0:T(8,128)(2,1)}, u32[]{:S(2)}, u32[]{:S(2)}) collective-permute-start(bf16[32,4736]{1,0:T(8,128)(2,1)S(1)} %get-tuple-element.108), channel_id=1, source_target_pairs={{0,24},{2,26},{4,28},{6,30},{8,16},{10,18},{12,20},{14,22},{16,8},... | collective-permute-start | bytes 909320 | tf_op jit(solution)/shard_map/ppermute | solution.py:697
  118.5 15.9 %write_back.1 = (bf16[1024,1536]{1,0:T(8,128)(2,1)}, bf16[4,32,2048]{2,1,0:T(8,128)(2,1)}, bf16[4,32,2048]{2,1,0:T(8,128)(2,1)}, bf16[4,32,2048]{2,1,0:T(8,128)(2,1)}, bf16[4,32,2048]{2,1,0:T(8,128)(2,1)}) custom-call(s32[1]{0:T(128)} %bitcast.me_ref, bf16[1024,2048]{1,0:T(8,128)(2,1)} %get-tuple-element.57.pack_ref, ...), custom_call_target="tpu_custom_call" | custom-call | flops 11000000512 | bytes 18874368 | tf_op jit(solution)/shard_map/write_back/pallas_call | solution.py:649
  137.4 6.8 %collective-permute-done.34 = bf16[32,4736]{1,0:T(8,128)(2,1)S(1)} collective-permute-done((bf16[32,4736]{1,0:T(8,128)(2,1)S(1)}, bf16[32,4736]{1,0:T(8,128)(2,1)S(1)}, u32[]{:S(2)}, u32[]{:S(2)}) %collective-permute-start.34) | collective-permute-done | bytes 303136 | tf_op jit(solution)/shard_map/ppermute | solution.py:697
  145.5 2.4 %collective-permute-start.36 = (bf16[32,4736]{1,0:T(8,128)(2,1)S(1)}, bf16[32,4736]{1,0:T(8,128)(2,1)S(1)}, u32[]{:S(2)}, u32[]{:S(2)}) collective-permute-start(bf16[32,4736]{1,0:T(8,128)(2,1)S(1)} %add_convert_fusion.1), channel_id=1, source_target_pairs={{0,1},{1,0},{2,3},{3,2},{4,5},{5,4},{6,7},{7,6},{8,9},{9,8},{10,11... | collective-permute-start | bytes 909320 | tf_op jit(solution)/shard_map/ppermute | solution.py:767
  150.6 7.5 %input_grad.1 = f32[1024,512]{1,0:T(8,128)} custom-call(f32[8,512]{1,0:T(8,128)} %get-tuple-element.62.gain_ref, bf16[1024,512]{1,0:T(8,128)(2,1)} %tok_ref.1, bf16[1024,512]{1,0:T(8,128)(2,1)} %get-tuple-element.85.gq_hbm.gq_ref, bf16[1024,1536]{1,0:T(8,128)(2,1)} %get-tuple-element.86.gkvc_ref, bf16[512,2048]{1,0:T(8,128)(2,1)} %get-tuple-element.87.w_ref, ...), custom_call_target="tpu_custom_call" | custom-call | flops 2147483648 | bytes 12582912 | tf_op jit(solution)/shard_map/input_grad/pallas_call | solution.py:684
  160.5 2.7 %collective-permute-done.23 = bf16[32,2048]{1,0:T(8,128)(2,1)S(1)} collective-permute-done((bf16[32,2048]{1,0:T(8,128)(2,1)S(1)}, bf16[32,2048]{1,0:T(8,128)(2,1)S(1)}, u32[]{:S(2)}, u32[]{:S(2)}) %collective-permute-start.23) | collective-permute-done | bytes 131104 | tf_op jit(solution)/shard_map/ppermute | solution.py:697
  163.4 2.3 %collective-permute-start.24 = (bf16[32,2048]{1,0:T(8,128)(2,1)S(1)}, bf16[32,2048]{1,0:T(8,128)(2,1)S(1)}, u32[]{:S(2)}, u32[]{:S(2)}) collective-permute-start(bf16[32,2048]{1,0:T(8,128)(2,1)S(1)} %get-tuple-element.124), channel_id=1, source_target_pairs={{0,24},{2,26},{4,28},{6,30},{8,16},{10,18},{12,20},{14,22},{16,8},... | collective-permute-start | bytes 393224 | tf_op jit(solution)/shard_map/ppermute | solution.py:697
  165.7 2.1 %collective-permute-start.26 = (bf16[32,2048]{1,0:T(8,128)(2,1)S(1)}, bf16[32,2048]{1,0:T(8,128)(2,1)S(1)}, u32[]{:S(2)}, u32[]{:S(2)}) collective-permute-start(bf16[32,2048]{1,0:T(8,128)(2,1)S(1)} %get-tuple-element.126), channel_id=1, source_target_pairs={{0,16},{2,18},{4,20},{6,22},{8,24},{10,26},{12,28},{14,30},{16,0},... | collective-permute-start | bytes 393224 | tf_op jit(solution)/shard_map/ppermute | solution.py:697
  168.3 2.1 %collective-permute-done.24 = bf16[32,2048]{1,0:T(8,128)(2,1)S(1)} collective-permute-done((bf16[32,2048]{1,0:T(8,128)(2,1)S(1)}, bf16[32,2048]{1,0:T(8,128)(2,1)S(1)}, u32[]{:S(2)}, u32[]{:S(2)}) %collective-permute-start.24) | collective-permute-done | bytes 131104 | tf_op jit(solution)/shard_map/ppermute | solution.py:697
  170.4 2.0 %collective-permute-done.28 = bf16[32,2048]{1,0:T(8,128)(2,1)S(1)} collective-permute-done((bf16[32,2048]{1,0:T(8,128)(2,1)S(1)}, bf16[32,2048]{1,0:T(8,128)(2,1)S(1)}, u32[]{:S(2)}, u32[]{:S(2)}) %collective-permute-start.28) | collective-permute-done | bytes 131104 | tf_op jit(solution)/shard_map/ppermute | solution.py:697
  172.4 2.3 %collective-permute-done.26 = bf16[32,2048]{1,0:T(8,128)(2,1)S(1)} collective-permute-done((bf16[32,2048]{1,0:T(8,128)(2,1)S(1)}, bf16[32,2048]{1,0:T(8,128)(2,1)S(1)}, u32[]{:S(2)}, u32[]{:S(2)}) %collective-permute-start.26) | collective-permute-done | bytes 131104 | tf_op jit(solution)/shard_map/ppermute | solution.py:697
  177.2 2.7 %collective-permute-done.30 = bf16[32,2048]{1,0:T(8,128)(2,1)S(1)} collective-permute-done((bf16[32,2048]{1,0:T(8,128)(2,1)S(1)}, bf16[32,2048]{1,0:T(8,128)(2,1)S(1)}, u32[]{:S(2)}, u32[]{:S(2)}) %collective-permute-start.30) | collective-permute-done | bytes 131104 | tf_op jit(solution)/shard_map/ppermute | solution.py:767
  (118 shorter events, 38.6 us)
Async XLA Ops:
  7.2 61.3 %all-gather.2.cloned.1.call-start = ((), (), s32[]{:S(2)}) async-start(), calls=%async_computation | async-start | bytes 5152768 | tf_op jit(solution)/shard_map/all_gather | solution.py:742
  9.1 9.9 %collective-permute-start.11 = (bf16[32,2176]{1,0:T(8,128)(2,1)}, bf16[32,2176]{1,0:T(8,128)(2,1)S(1)}, u32[]{:S(2)}, u32[]{:S(2)}) collective-permute-start(bf16[32,2176]{1,0:T(8,128)(2,1)} %get-tuple-element.56.refs_0_), channel_id=1, source_target_pairs={{0,24},{2,26},{4,28},{6,30},{8,16},{10,18},{12,20},{14,22},{16,8},... | collective-permute-start | bytes 417800 | tf_op jit(solution)/shard_map/ppermute | solution.py:697
  14.2 14.9 %collective-permute-start.7 = (bf16[32,2176]{1,0:T(8,128)(2,1)}, bf16[32,2176]{1,0:T(8,128)(2,1)S(1)}, u32[]{:S(2)}, u32[]{:S(2)}) collective-permute-start(bf16[32,2176]{1,0:T(8,128)(2,1)} %get-tuple-element.56.refs_0_), channel_id=1, source_target_pairs={{0,16},{2,18},{4,20},{6,22},{8,24},{10,26},{12,28},{14,30},{16,0},... | collective-permute-start | bytes 417800 | tf_op jit(solution)/shard_map/ppermute | solution.py:697
  14.2 14.9 %collective-permute-start.3 = (bf16[32,2176]{1,0:T(8,128)(2,1)}, bf16[32,2176]{1,0:T(8,128)(2,1)S(1)}, u32[]{:S(2)}, u32[]{:S(2)}) collective-permute-start(bf16[32,2176]{1,0:T(8,128)(2,1)} %get-tuple-element.56.refs_0_), channel_id=1, source_target_pairs={{0,8},{2,10},{4,12},{6,14},{8,0},{10,2},{12,4},{14,6},{16,24},{18,... | collective-permute-start | bytes 417800 | tf_op jit(solution)/shard_map/ppermute | solution.py:697
  14.9 16.0 %collective-permute-start.1 = (bf16[32,2176]{1,0:T(8,128)(2,1)}, bf16[32,2176]{1,0:T(8,128)(2,1)S(1)}, u32[]{:S(2)}, u32[]{:S(2)}) collective-permute-start(bf16[32,2176]{1,0:T(8,128)(2,1)} %get-tuple-element.56.refs_0_), channel_id=1, source_target_pairs={{0,4},{2,6},{4,0},{6,2},{8,12},{10,14},{12,8},{14,10},{16,20},{18,... | collective-permute-start | bytes 417800 | tf_op jit(solution)/shard_map/ppermute | solution.py:697
  16.5 14.5 %collective-permute-start = (bf16[32,2176]{1,0:T(8,128)(2,1)}, bf16[32,2176]{1,0:T(8,128)(2,1)S(1)}, u32[]{:S(2)}, u32[]{:S(2)}) collective-permute-start(bf16[32,2176]{1,0:T(8,128)(2,1)} %get-tuple-element.56.refs_0_), channel_id=1, source_target_pairs={{0,2},{2,0},{4,6},{6,4},{8,10},{10,8},{12,14},{14,12},{16,18},{18,... | collective-permute-start | bytes 417800 | tf_op jit(solution)/shard_map/ppermute | solution.py:697
  19.1 12.4 %collective-permute-start.13 = (bf16[32,2176]{1,0:T(8,128)(2,1)S(1)}, bf16[32,2176]{1,0:T(8,128)(2,1)S(1)}, u32[]{:S(2)}, u32[]{:S(2)}) collective-permute-start(bf16[32,2176]{1,0:T(8,128)(2,1)S(1)} %collective-permute-done.11.refs_12_), channel_id=1, source_target_pairs={{0,4},{2,6},{4,0},{6,2},{8,12},{10,14},{12,8},{14,10},{16,20},{18,... | collective-permute-start | bytes 417800 | tf_op jit(solution)/shard_map/ppermute | solution.py:697
  31.0 7.2 %collective-permute-start.5 = (bf16[32,2176]{1,0:T(8,128)(2,1)S(1)}, bf16[32,2176]{1,0:T(8,128)(2,1)S(1)}, u32[]{:S(2)}, u32[]{:S(2)}) collective-permute-start(bf16[32,2176]{1,0:T(8,128)(2,1)S(1)} %collective-permute-done.3.refs_4_), channel_id=1, source_target_pairs={{0,4},{2,6},{4,0},{6,2},{8,12},{10,14},{12,8},{14,10},{16,20},{18,... | collective-permute-start | bytes 417800 | tf_op jit(solution)/shard_map/ppermute | solution.py:697
  93.4 17.3 %collective-permute-start.18 = (bf16[4,32,4736]{2,1,0:T(8,128)(2,1)}, bf16[4,32,4736]{2,1,0:T(8,128)(2,1)S(1)}, u32[]{:S(2)}, u32[]{:S(2)}) collective-permute-start(bf16[4,32,4736]{2,1,0:T(8,128)(2,1)} %get-tuple-element.79), channel_id=1, source_target_pairs={{0,2},{2,0},{4,6},{6,4},{8,10},{10,8},{12,14},{14,12},{16,18},{18,... | collective-permute-start | bytes 3637256 | tf_op jit(solution)/shard_map/ppermute | solution.py:697
  96.6 15.7 %collective-permute-start.20 = (bf16[32,4736]{1,0:T(8,128)(2,1)S(1)}, bf16[32,4736]{1,0:T(8,128)(2,1)}, u32[]{:S(2)}, u32[]{:S(2)}) collective-permute-start(bf16[32,4736]{1,0:T(8,128)(2,1)S(1)} %get-tuple-element.101), channel_id=1, source_target_pairs={{0,4},{2,6},{4,0},{6,2},{8,12},{10,14},{12,8},{14,10},{16,20},{18,... | collective-permute-start | bytes 909320 | tf_op jit(solution)/shard_map/ppermute | solution.py:697
  97.2 15.4 %collective-permute-start.19 = (bf16[32,4736]{1,0:T(8,128)(2,1)S(1)}, bf16[32,4736]{1,0:T(8,128)(2,1)}, u32[]{:S(2)}, u32[]{:S(2)}) collective-permute-start(bf16[32,4736]{1,0:T(8,128)(2,1)S(1)} %get-tuple-element.102), channel_id=1, source_target_pairs={{0,4},{2,6},{4,0},{6,2},{8,12},{10,14},{12,8},{14,10},{16,20},{18,... | collective-permute-start | bytes 909320 | tf_op jit(solution)/shard_map/ppermute | solution.py:697
  108.8 9.6 %collective-permute-start.17 = (bf16[2,144,256]{2,1,0:T(8,128)(2,1)}, bf16[2,144,256]{2,1,0:T(8,128)(2,1)}, u32[]{:S(2)}, u32[]{:S(2)}) collective-permute-start(bf16[2,144,256]{2,1,0:T(8,128)(2,1)} %get-tuple-element.76), channel_id=1, source_target_pairs={{1,0},{3,2},{5,4},{7,6},{9,8},{11,10},{13,12},{15,14},{17,16},{19,... | collective-permute-start | bytes 442376 | tf_op jit(solution)/shard_map/ppermute | solution.py:717
  110.1 24.3 %collective-permute-start.33 = (bf16[32,4736]{1,0:T(8,128)(2,1)S(1)}, bf16[32,4736]{1,0:T(8,128)(2,1)}, u32[]{:S(2)}, u32[]{:S(2)}) collective-permute-start(bf16[32,4736]{1,0:T(8,128)(2,1)S(1)} %get-tuple-element.96), channel_id=1, source_target_pairs={{0,4},{2,6},{4,0},{6,2},{8,12},{10,14},{12,8},{14,10},{16,20},{18,... | collective-permute-start | bytes 909320 | tf_op jit(solution)/shard_map/ppermute | solution.py:697
  110.8 26.1 %collective-permute-start.35 = (bf16[32,4736]{1,0:T(8,128)(2,1)S(1)}, bf16[32,4736]{1,0:T(8,128)(2,1)S(1)}, u32[]{:S(2)}, u32[]{:S(2)}) collective-permute-start(bf16[32,4736]{1,0:T(8,128)(2,1)S(1)} %get-tuple-element.98), channel_id=1, source_target_pairs={{0,4},{2,6},{4,0},{6,2},{8,12},{10,14},{12,8},{14,10},{16,20},{18,... | collective-permute-start | bytes 909320 | tf_op jit(solution)/shard_map/ppermute | solution.py:697
  114.6 29.6 %collective-permute-start.32 = (bf16[32,4736]{1,0:T(8,128)(2,1)}, bf16[32,4736]{1,0:T(8,128)(2,1)S(1)}, u32[]{:S(2)}, u32[]{:S(2)}) collective-permute-start(bf16[32,4736]{1,0:T(8,128)(2,1)} %get-tuple-element.107), channel_id=1, source_target_pairs={{0,16},{2,18},{4,20},{6,22},{8,24},{10,26},{12,28},{14,30},{16,0},... | collective-permute-start | bytes 909320 | tf_op jit(solution)/shard_map/ppermute | solution.py:697
  116.5 27.8 %collective-permute-start.31 = (bf16[32,4736]{1,0:T(8,128)(2,1)S(1)}, bf16[32,4736]{1,0:T(8,128)(2,1)}, u32[]{:S(2)}, u32[]{:S(2)}) collective-permute-start(bf16[32,4736]{1,0:T(8,128)(2,1)S(1)} %get-tuple-element.108), channel_id=1, source_target_pairs={{0,24},{2,26},{4,28},{6,30},{8,16},{10,18},{12,20},{14,22},{16,8},... | collective-permute-start | bytes 909320 | tf_op jit(solution)/shard_map/ppermute | solution.py:697
  135.6 8.7 %collective-permute-start.34 = (bf16[32,4736]{1,0:T(8,128)(2,1)S(1)}, bf16[32,4736]{1,0:T(8,128)(2,1)S(1)}, u32[]{:S(2)}, u32[]{:S(2)}) collective-permute-start(bf16[32,4736]{1,0:T(8,128)(2,1)S(1)} %fusion.3), channel_id=1, source_target_pairs={{0,8},{2,10},{4,12},{6,14},{8,0},{10,2},{12,4},{14,6},{16,24},{18,... | collective-permute-start | bytes 909320 | tf_op jit(solution)/shard_map/ppermute | solution.py:697
  135.7 12.2 %collective-permute-start.21 = (bf16[4,32,2048]{2,1,0:T(8,128)(2,1)}, bf16[4,32,2048]{2,1,0:T(8,128)(2,1)S(1)}, u32[]{:S(2)}, u32[]{:S(2)}) collective-permute-start(bf16[4,32,2048]{2,1,0:T(8,128)(2,1)} %get-tuple-element.84), channel_id=1, source_target_pairs={{0,2},{2,0},{4,6},{6,4},{8,10},{10,8},{12,14},{14,12},{16,18},{18,... | collective-permute-start | bytes 1572872 | tf_op jit(solution)/shard_map/ppermute | solution.py:697
  136.9 23.6 %collective-permute-start.22 = (bf16[4,32,2048]{2,1,0:T(8,128)(2,1)}, bf16[4,32,2048]{2,1,0:T(8,128)(2,1)S(1)}, u32[]{:S(2)}, u32[]{:S(2)}) collective-permute-start(bf16[4,32,2048]{2,1,0:T(8,128)(2,1)} %get-tuple-element.91), channel_id=1, source_target_pairs={{0,2},{2,0},{4,6},{6,4},{8,10},{10,8},{12,14},{14,12},{16,18},{18,... | collective-permute-start | bytes 1572872 | tf_op jit(solution)/shard_map/ppermute | solution.py:697
  145.5 12.7 %collective-permute-start.36 = (bf16[32,4736]{1,0:T(8,128)(2,1)S(1)}, bf16[32,4736]{1,0:T(8,128)(2,1)S(1)}, u32[]{:S(2)}, u32[]{:S(2)}) collective-permute-start(bf16[32,4736]{1,0:T(8,128)(2,1)S(1)} %add_convert_fusion.1), channel_id=1, source_target_pairs={{0,1},{1,0},{2,3},{3,2},{4,5},{5,4},{6,7},{7,6},{8,9},{9,8},{10,11... | collective-permute-start | bytes 909320 | tf_op jit(solution)/shard_map/ppermute | solution.py:767
  148.0 20.4 %collective-permute-start.29 = (bf16[32,2048]{1,0:T(8,128)(2,1)S(1)}, bf16[32,2048]{1,0:T(8,128)(2,1)S(1)}, u32[]{:S(2)}, u32[]{:S(2)}) collective-permute-start(bf16[32,2048]{1,0:T(8,128)(2,1)S(1)} %get-tuple-element.109), channel_id=1, source_target_pairs={{0,4},{2,6},{4,0},{6,2},{8,12},{10,14},{12,8},{14,10},{16,20},{18,... | collective-permute-start | bytes 393224 | tf_op jit(solution)/shard_map/ppermute | solution.py:697
  148.6 11.9 %collective-permute-start.27 = (bf16[32,2048]{1,0:T(8,128)(2,1)S(1)}, bf16[32,2048]{1,0:T(8,128)(2,1)S(1)}, u32[]{:S(2)}, u32[]{:S(2)}) collective-permute-start(bf16[32,2048]{1,0:T(8,128)(2,1)S(1)} %get-tuple-element.110), channel_id=1, source_target_pairs={{0,4},{2,6},{4,0},{6,2},{8,12},{10,14},{12,8},{14,10},{16,20},{18,... | collective-permute-start | bytes 393224 | tf_op jit(solution)/shard_map/ppermute | solution.py:697
  150.1 10.4 %collective-permute-start.25 = (bf16[32,2048]{1,0:T(8,128)(2,1)S(1)}, bf16[32,2048]{1,0:T(8,128)(2,1)S(1)}, u32[]{:S(2)}, u32[]{:S(2)}) collective-permute-start(bf16[32,2048]{1,0:T(8,128)(2,1)S(1)} %get-tuple-element.111), channel_id=1, source_target_pairs={{0,4},{2,6},{4,0},{6,2},{8,12},{10,14},{12,8},{14,10},{16,20},{18,... | collective-permute-start | bytes 393224 | tf_op jit(solution)/shard_map/ppermute | solution.py:697
  165.7 9.0 %collective-permute-start.26 = (bf16[32,2048]{1,0:T(8,128)(2,1)S(1)}, bf16[32,2048]{1,0:T(8,128)(2,1)S(1)}, u32[]{:S(2)}, u32[]{:S(2)}) collective-permute-start(bf16[32,2048]{1,0:T(8,128)(2,1)S(1)} %get-tuple-element.126), channel_id=1, source_target_pairs={{0,16},{2,18},{4,20},{6,22},{8,24},{10,26},{12,28},{14,30},{16,0},... | collective-permute-start | bytes 393224 | tf_op jit(solution)/shard_map/ppermute | solution.py:697
  (34 other events, 215.9 us)
Sparse Core Ops, SparseCore 0:
  10.9 57.5 all-gather.1

commit v5 on v4

--- a/solution.py
+++ b/solution.py
@@ -124,6 +124,23 @@
     wide = jnp.where(own, vec, 0.0).astype(BF16)
     tile = (iota((128, total), 1) % each == iota((128, total), 0)).astype(BF16)
     return mm_t(wide, tile).astype(BF16)
+
+
+def share_ref(refs, j, n):
+    near, low, high, high_core, rest_core = refs
+    a, k, half = j % 4, j // 4, n // 8
+    if a == 0:
+        return near.at[k]
+    if a == 1:
+        return rest_core.at[k]
+    if k >= half:
+        return (high if a == 2 else high_core).at[k - half]
+    return low.at[k] if a == 2 else rest_core.at[2 * half + k]
+
+
+def share_shapes(n, r, width):
+    half = n // 8
+    return [jax.ShapeDtypeStruct((c, r, width), BF16) for c in (2 * half, half, half, half, 3 * half)]
 
 
 def piece_refs(where, refs):
@@ -341,15 +358,15 @@
     )(packed, state)
 
 
-def ffn_kernel(n, me_ref, mixed_hbm, tok_hbm, cot_hbm, full_ref, out_hbm, gres_hbm, gmix_hbm, *refs):
-    share_refs = refs[:4]
-    (mixed, tok, cot, outs, gres, gmix, w_out, w_up, w_down, vecs, hid, gpre, fin, gbr, sems, osems) = refs[4:]
+def ffn_kernel(n, me_ref, mixed_hbm, tok_hbm, cot_hbm, full_ref, kept_hbm, gres_hbm, gmix_hbm, hid_hbm, down_hbm, *refs):
+    share_refs = refs[:5]
+    (mixed, tok, cot, kept, gres, gmix, w_out, w_up, w_down, vecs, hid, gpre, fin, gbr, normed_f, sems, osems, dsem) = refs[5:]
     me = me_ref[0]
     t, d = mixed.shape
     ff = w_up.shape[1]
     r = d // n
     mult = ff // d
-    rows = 256
+    rows = 512
     part = 512
     steps = t // rows
     parts = ff // part
@@ -365,9 +382,8 @@
         load(mixed_hbm, mixed, 1),
         load(tok_hbm, tok, 2),
         load(full_ref.at[:, pl.ds(2 * ff + d, 128)], vecs, 4),
-        load(full_ref.at[:, pl.ds(0, ff)], w_up, 5),
     ]
-    late = [load(cot_hbm, cot, 6)]
+    late = [load(full_ref.at[:, pl.ds(0, ff)], w_up, 5), load(cot_hbm, cot, 6)]
     down = []
     for j in range(n):
         for m in range(mult):
@@ -389,15 +405,23 @@
     ggain = jnp.zeros((1, d), F32)
     gbdown = jnp.zeros((1, d), F32)
     gbup = [jnp.zeros((1, part), F32)] * parts
+    factors = []
     for i in range(steps):
         rs = pl.ds(i * rows, rows)
         resid = tok[rs, :].astype(F32) + mm(mixed[rs, :], w_out[...])
-        normed, factor = normalize(resid)
-        ffn_in = (normed * gain).astype(BF16)
-        fin[rs, :] = ffn_in
-        if i == 0:
-            for c in late:
-                c.wait()
+        kept[rs, :] = resid + b_down
+        send(kept.at[rs, :], kept_hbm.at[rs, :])
+        x, factor = normalize(resid)
+        normed_f[rs, :] = x
+        factors.append(factor)
+        fin[rs, :] = (x * gain).astype(BF16)
+    for c in late:
+        c.wait()
+    keep_down = pltpu.make_async_copy(w_down, down_hbm, dsem)
+    keep_down.start()
+    for i in range(steps):
+        rs = pl.ds(i * rows, rows)
+        ffn_in, normed, factor = fin[rs, :], normed_f[rs, :], factors[i]
         cot_b = cot[rs, :]
         cotf = cot_b.astype(F32)
 
@@ -406,7 +430,7 @@
             return mm(ffn_in, w_up[:, ps]) + b_up[:, ps], mm_t(cot_b, w_down[ps, :])
 
         ready = entry(0)
-        total = gin = None
+        gin = None
         for p in range(parts):
             ps = slice(p * part, (p + 1) * part)
             pre, gh = ready
@@ -419,10 +443,9 @@
             act, gp = act.astype(BF16), gp.astype(BF16)
             hid[rs, ps] = act
             gpre[rs, ps] = gp
-            x, y = mm(act, w_down[ps, :]), mm_t(gp, w_up[:, ps])
-            total, gin = (x, y) if p == 0 else (total + x, gin + y)
-        outs[rs, :] = (resid + (total + b_down)).astype(BF16)
-        send(outs.at[rs, :], out_hbm.at[rs, :])
+            x = mm_t(gp, w_up[:, ps])
+            gin = x if p == 0 else gin + x
+        send(hid.at[rs, :], hid_hbm.at[rs, :])
         back = cotf + norm_back(gin * gain, normed, factor)
         gres[rs, :] = back
         send(gres.at[rs, :], gres_hbm.at[rs, :])
@@ -434,14 +457,16 @@
         gbdown += jnp.sum(cotf, axis=0, keepdims=True)
 
     def share(j, rows_of, ref, at, width):
-        send(ref.at[rows_of(me ^ j), :], share_refs[j % 4].at[j // 4, :, pl.ds(at, width)])
+        send(ref.at[rows_of(me ^ j), :], share_ref(share_refs, j, n).at[:, pl.ds(at, width)])
 
     own_rows = lambda f: pl.ds(pl.multiple_of(f * r, r), r)
+    keep_down.wait()
     for p in range(parts):
         ps = slice(p * part, (p + 1) * part)
-        w_up[:, ps] = t_mm(fin[...], gpre[:, ps]).astype(BF16)
+        w_down[ps, :] = t_mm(hid[:, ps], cot[...]).astype(BF16)
     for j in range(n):
-        share(j, own_rows, w_up, 0, ff)
+        for m in range(mult):
+            share(j, lambda f: pl.ds(pl.multiple_of((f * mult + m) * r, r), r), w_down, ff + m * d, d)
     w_out[...] = t_mm(mixed[...], gbr[...]).astype(BF16)
     va = gather_vector(ggain, 0, n, r)
     vb = gather_vector(jnp.concatenate(gbup, axis=1), 0, n, r * mult)
@@ -456,10 +481,9 @@
         share(j, own_rows, vecs, 2 * ff + d, 128)
     for p in range(parts):
         ps = slice(p * part, (p + 1) * part)
-        w_down[ps, :] = t_mm(hid[:, ps], cot[...]).astype(BF16)
+        w_up[:, ps] = t_mm(fin[...], gpre[:, ps]).astype(BF16)
     for j in range(n):
-        for m in range(mult):
-            share(j, lambda f: pl.ds(pl.multiple_of((f * mult + m) * r, r), r), w_down, ff + m * d, d)
+        share(j, own_rows, w_up, 0, ff)
     for c in sent:
         c.wait()
 
@@ -471,15 +495,17 @@
     return pl.pallas_call(
         partial(ffn_kernel, n),
         in_specs=[pl.BlockSpec(memory_space=pltpu.SMEM)] + [hbm] * 4,
-        out_specs=[hbm] * 7,
+        out_specs=[hbm] * 10,
         out_shape=[
-            jax.ShapeDtypeStruct((t, d), BF16),
+            jax.ShapeDtypeStruct((t, d), F32),
             jax.ShapeDtypeStruct((t, d), F32),
             jax.ShapeDtypeStruct((t, d), BF16),
+            jax.ShapeDtypeStruct((t, ff), BF16),
+            jax.ShapeDtypeStruct((ff, d), BF16),
         ]
-        + [jax.ShapeDtypeStruct((n // 4, d // n, full.shape[1]), BF16)] * 4,
-        scratch_shapes=[pltpu.VMEM((t, d), BF16)] * 4
-        + [pltpu.VMEM((t, d), F32), pltpu.VMEM((t, d), BF16)]
+        + share_shapes(n, d // n, full.shape[1]),
+        scratch_shapes=[pltpu.VMEM((t, d), BF16)] * 3
+        + [pltpu.VMEM((t, d), F32), pltpu.VMEM((t, d), F32), pltpu.VMEM((t, d), BF16)]
         + [
             pltpu.VMEM((d, d), BF16),
             pltpu.VMEM((d, ff), BF16),
@@ -489,13 +515,35 @@
             pltpu.VMEM((t, ff), BF16),
             pltpu.VMEM((t, d), BF16),
             pltpu.VMEM((t, d), BF16),
+            pltpu.VMEM((t, d), F32),
             pltpu.SemaphoreType.DMA((7 + moves,)),
-            pltpu.SemaphoreType.DMA((3 * (t // 256) + 3 * n + moves,)),
+            pltpu.SemaphoreType.DMA((4 * (t // 256) + 3 * n + moves,)),
+            pltpu.SemaphoreType.DMA,
         ],
         compiler_params=pltpu.CompilerParams(vmem_limit_bytes=VMEM_LIMIT),
-        cost_estimate=pl.CostEstimate(flops=12 * t * d * ff, bytes_accessed=20 << 20, transcendentals=t * ff),
+        cost_estimate=pl.CostEstimate(flops=11 * t * d * ff, bytes_accessed=20 << 20, transcendentals=t * ff),
         name="ffn",
     )(me, mixed, tokens, cot, full)
+
+
+def ffn_out_kernel(hid_ref, kept_ref, down_ref, out_ref):
+    out_ref[...] = (kept_ref[...] + mm(hid_ref[...], down_ref[...])).astype(BF16)
+
+
+def ffn_out(hid, kept, down, rows=256):
+    t, ff = hid.shape
+    d = kept.shape[1]
+    row = lambda w: pl.BlockSpec((rows, w), lambda i: (i, 0))
+    return pl.pallas_call(
+        ffn_out_kernel,
+        grid=(t // rows,),
+        in_specs=[row(ff), row(d), pl.BlockSpec((ff, d), lambda i: (0, 0))],
+        out_specs=row(d),
+        out_shape=jax.ShapeDtypeStruct((t, d), BF16),
+        compiler_params=pltpu.CompilerParams(vmem_limit_bytes=VMEM_LIMIT),
+        cost_estimate=pl.CostEstimate(flops=2 * t * d * ff, bytes_accessed=9 << 20, transcendentals=0),
+        name="ffn_out",
+    )(hid, kept, down)
 
 
 def read_back_kernel(pack_ref, gmix_ref, read_ref, score_ref, inv_ref, kts_ref, mvs_ref,
@@ -566,8 +614,8 @@
 
 
 def write_back_kernel(n, me_ref, pack_ref, gmix_ref, a_ref, u_ref, gtot_ref, st_in, att_hbm, gq_hbm, out_ref, *refs):
-    share_refs = refs[:4]
-    gk, gv, gt, att, gq, grads, acc, isems, sems = refs[4:]
+    share_refs = refs[:5]
+    gk, gv, gt, att, gq, grads, acc, isems, sems = refs[5:]
     rows, d = gmix_ref.shape
     loads = [pltpu.make_async_copy(att_hbm, att, isems.at[0]), pltpu.make_async_copy(gq_hbm, gq, isems.at[1])]
 
@@ -629,7 +677,7 @@
         outs = []
         for j in range(n):
             frm = pl.multiple_of((me ^ j) * r, r)
-            dst = share_refs[j % 4].at[j // 4]
+            dst = share_ref(share_refs, j, n)
             outs.append(pltpu.make_async_copy(acc.at[pl.ds(frm, r), :], dst, sems.at[j]))
         for x in outs:
             x.start()
@@ -650,8 +698,8 @@
         partial(write_back_kernel, n),
         grid=(t // rows,),
         in_specs=[pl.BlockSpec(memory_space=pltpu.SMEM), row(wide), row(d), row(d), row(d), row(d), const(g, STATE, QUAD), hbm, hbm],
-        out_specs=[row(3 * d)] + [hbm] * 4,
-        out_shape=[jax.ShapeDtypeStruct((t, 3 * d), BF16)] + [jax.ShapeDtypeStruct((n // 4, r, wide), BF16)] * 4,
+        out_specs=[row(3 * d)] + [hbm] * 5,
+        out_shape=[jax.ShapeDtypeStruct((t, 3 * d), BF16)] + share_shapes(n, r, wide),
         scratch_shapes=[
             pltpu.VMEM((g, QUAD, QUAD), F32),
             pltpu.VMEM((g, QUAD, QUAD), F32),
@@ -746,17 +794,19 @@
     att_where = [(j, None) for j in range(n)]
     att, packed, state, w_att, gain = project(me, tokens, att_where, att_pieces)
     mixed, read, score, inv, kts, mvs = mix(packed, others(state, 1, seqs))
-    layer_out, gres, gmix, *ffn_shares = ffn(me, mixed, tokens, cotangent, full, ff, n)
-    order = range(depth - 1, -1, -1)
-
-    def start_sum(shares):
-        near, near_core, far, far_core = shares
-        far_core = swap(far_core, 1, n)
-        near_core = swap(near_core, 1, n)
-        return near, near_core, {k: add(far[k], far_core[k]) for k in order}
-
-    def cross(far, keys, *first):
-        return {k: swap(after(far[k], *first) if first else far[k], 2, n) for k in keys}
+    kept, gres, gmix, hid, full_down, *ffn_shares = ffn(me, mixed, tokens, cotangent, full, ff, n)
+    half = depth // 2
+
+    def start_sum(shares, *first):
+        near, low, high, high_core, rest = shares
+        high = add(after(high, *first) if first else high, swap(high_core, 1, n))
+        rest = swap(rest, 1, n)
+        return (near, rest), add(low, rest[depth:]), high
+
+    def joined(near, crossed, base, *first):
+        own, core = near
+        own = after(own, *first)
+        return {base + i: add(own[base + i], core[base + i], crossed[i]) for i in range(half)}
 
     def along(part, k):
         return swap(part, 4 * k, n) if k else part
@@ -768,23 +818,26 @@
             step *= 2
         return x.astype(F32)
 
-    high, low = [k for k in order if k >= depth // 2], [k for k in order if k < depth // 2]
-    near, near_core, far = start_sum(ffn_shares)
-    crossed = cross(far, high)
-    gq, a, u, gtot, gstate = read_back(packed, after(gmix, *far.values()), read, score, inv, kts, mvs)
-    crossed |= cross(far, low, gq)
-    mine = {k: add(after(near[k], gq), near_core[k], crossed[k]) for k in high}
+    near, low, high = start_sum(ffn_shares)
+    crossed_high = swap(high, 2, n)
+    gq, a, u, gtot, gstate = read_back(packed, after(gmix, high), read, score, inv, kts, mvs)
+    crossed_low = swap(after(low, gq), 2, n)
+    mine = joined(near, crossed_high, half, gq)
+    ffn_parts = [along(mine[k], k) for k in range(half, depth)]
     gkvc, *shares = write_back(
         me, packed, gmix, a, u, gtot, after(others(gstate, -1, seqs), *mine.values()), att, gq, n
     )
-    mine |= {k: add(after(near[k], gkvc), near_core[k], crossed[k]) for k in low}
-    ffn_parts = [along(mine[k], k) for k in order]
-    near, near_core, far = start_sum(shares)
-    crossed = cross(far, order)
-    grad_tokens = input_grad(gain, tokens, after(gq, *far.values()), gkvc, w_att, gres)
-    att_parts = [along(add(after(near[k], grad_tokens), near_core[k], crossed[k]), k) for k in order]
-    ffn_share = seq_sum(add(*ffn_parts))
-    att_share = seq_sum(add(*att_parts))
+    mine = joined(near, crossed_low, 0, gkvc)
+    att_near, att_low, att_high = start_sum(shares, *ffn_parts, *mine.values())
+    ffn_parts += [along(mine[k], k) for k in range(half)]
+    crossed_high, crossed_low = swap(att_high, 2, n), swap(att_low, 2, n)
+    grad_tokens = input_grad(gain, tokens, after(gq, att_low, *mine.values()), gkvc, w_att, gres)
+    ffn_sum = add(after(mine[0], grad_tokens), *(p for p in ffn_parts if p is not mine[0]))
+    mine = joined(att_near, crossed_high, half, grad_tokens, ffn_sum) | joined(att_near, crossed_low, 0, grad_tokens)
+    att_parts = [along(mine[k], k) for k in range(depth)]
+    layer_out = ffn_out(after(hid, *mine.values()), kept, full_down)
+    ffn_share = seq_sum(ffn_sum)
+    att_share = seq_sum(add(*[after(p, layer_out) for p in att_parts]))
     gain_share = jnp.sum(att_share * first[:, : 4 * d].astype(F32), axis=1) / gain_attn.astype(F32)
     up, down, out, vec = (
         ffn_share[:, :ff],

time: 189 us -> 179 us (0.947)
  waiting for transfers between devices: 44.5 us -> 34.1 us
  Pallas kernels: 77.9 us -> 81.1 us
  starting transfers between devices: 37.9 us -> 34.9 us
  other arithmetic: 6.56 us -> 9.46 us
  local copies, waits for them, and re-layouts: 6.83 us -> 4.39 us
    ppermute x33 -> x29, waiting for transfers between devices: 35.6 us -> 29 us  [swap(): return lax.ppermute(x, 'fsdp', [(i, i ^ mask) for i in range(n)])]
    pallas_call x0 -> x1, Pallas kernels: none -> 6.5 us  [ffn_out(): pl.pallas_call(ffn_out_kernel, grid=(t // rows,), in_specs=[row(ff), row(...]
    ppermute x33 -> x29, starting transfers between devices: 30.3 us -> 26.7 us  [swap(): return lax.ppermute(x, 'fsdp', [(i, i ^ mask) for i in range(n)])]
    pallas_call x1, Pallas kernels: 24.6 us -> 21.2 us  [ffn(): pl.pallas_call(partial(ffn_kernel, n), in_specs=[pl.BlockSpec(memory_spac...]
    convert_element_type x7 -> x9, other arithmetic: 5.08 us -> 7.98 us  [add(): return sum((x.astype(F32) for x in items)).astype(BF16)]
    squeeze x2 -> x0, local copies, waits for them, and re-layouts: 2.45 us -> none  [on_device(): near[k]]
    ppermute x2, waiting for transfers between devices: 2.71 us -> 0.38 us  [seq_sum(): x = add(x, lax.ppermute(x, 'seq', [(i, i ^ step) for i in range(seqs)]))]
  transfers between devices with their start and end apart: 38 -> 34, of which waited for: 15 -> 12; matrix products, arithmetic and copies ran while one was open for 6% -> 6% of each run, Pallas kernels for 27% -> 32%
where the time goes in v5:
time: 179 us; the launch traced here: 178 us
  Pallas kernels  81.1 us (45%)
  starting transfers between devices  34.9 us (19%)
  waiting for transfers between devices  34.1 us (19%)
  between operations  14.4 us (8%)
  other arithmetic  9.46 us (5%)
  local copies, waits for them, and re-layouts  4.39 us (2%)
    ppermute x29, waiting for transfers between devices, swap(): return lax.ppermute(x, 'fsdp', [(i, i ^ mask) for i in range(n)])  29 us
    ppermute x29, starting transfers between devices, swap(): return lax.ppermute(x, 'fsdp', [(i, i ^ mask) for i in range(n)])  26.7 us
    pallas_call x1, Pallas kernels, ffn(): pl.pallas_call(partial(ffn_kernel, n), in_specs=[pl.BlockSpec(memory_spac...  21.2 us
    pallas_call x1, Pallas kernels, write_back(): pl.pallas_call(partial(write_back_kernel, n), grid=(t // rows,), in_specs...  15.6 us
    pallas_call x1, Pallas kernels, read_back(): pl.pallas_call(read_back_kernel, grid=(t // rows,), in_specs=[row(wide),...  10.3 us
    pallas_call x1, Pallas kernels, mix(): pl.pallas_call(mix_kernel, grid=(t // rows,), in_specs=[row(wide), const(...  10.3 us
    convert_element_type x9, other arithmetic, add(): return sum((x.astype(F32) for x in items)).astype(BF16)  7.98 us
    pallas_call x1, Pallas kernels, input_grad(): pl.pallas_call(input_grad_kernel, grid=(t // rows,), in_specs=[const(8, d...  7.6 us
  transfers between devices with their start and end apart: 34, of which 12 were waited for; matrix products, arithmetic and copies ran while one was open for 6% of the time, Pallas kernels for 32%

profile of v5, /device:TPU:0, one launch (start us, length us, event | category | flops | bytes accessed | tf_op | source)
XLA Modules:
  0.0 178.3 jit_solution(17314548048229523346)
XLA Ops:
  7.2 1.9 %pack.1 = (bf16[32,2176]{1,0:T(8,128)(2,1)}, bf16[32,4736]{1,0:T(8,128)(2,1)}) custom-call(bf16[32,512]{1,0:T(8,128)(2,1)} %q.1, bf16[32,512]{1,0:T(8,128)(2,1)} %k.1, bf16[32,512]{1,0:T(8,128)(2,1)} %v.1, bf16[32,512]{1,0:T(8,128)(2,1)} %c.1, bf16[32,512]{1,0:T(8,128)(2,1)} %o.1, bf16[32,2048]{1,0:T(8,128)(2,1)} %up.1, bf16[128,512]{1,0:T(8,128)(2,1)} %down.1, ...), custom_call_target="tpu_custom_call" | custom-call | bytes 1048576 | tf_op jit(solution)/shard_map/pack/pallas_call | solution.py:174
  9.1 5.1 %collective-permute-start.11 = (bf16[32,2176]{1,0:T(8,128)(2,1)}, bf16[32,2176]{1,0:T(8,128)(2,1)S(1)}, u32[]{:S(2)}, u32[]{:S(2)}) collective-permute-start(bf16[32,2176]{1,0:T(8,128)(2,1)} %get-tuple-element.62.refs_0_), channel_id=1, source_target_pairs={{0,24},{2,26},{4,28},{6,30},{8,16},{10,18},{12,20},{14,22},{16,8},... | collective-permute-start | bytes 417800 | tf_op jit(solution)/shard_map/ppermute | solution.py:745
  16.5 2.5 %collective-permute-done.11.refs_12_ = bf16[32,2176]{1,0:T(8,128)(2,1)S(1)} collective-permute-done((bf16[32,2176]{1,0:T(8,128)(2,1)}, bf16[32,2176]{1,0:T(8,128)(2,1)S(1)}, u32[]{:S(2)}, u32[]{:S(2)}) %collective-permute-start.11) | collective-permute-done | bytes 139296 | tf_op jit(solution)/shard_map/ppermute | solution.py:745
  20.8 9.7 %collective-permute-done.7.refs_8_ = bf16[32,2176]{1,0:T(8,128)(2,1)S(1)} collective-permute-done((bf16[32,2176]{1,0:T(8,128)(2,1)}, bf16[32,2176]{1,0:T(8,128)(2,1)S(1)}, u32[]{:S(2)}, u32[]{:S(2)}) %collective-permute-start.7) | collective-permute-done | bytes 139296 | tf_op jit(solution)/shard_map/ppermute | solution.py:745
  30.5 1.8 %collective-permute-start.9 = (bf16[32,2176]{1,0:T(8,128)(2,1)S(1)}, bf16[32,2176]{1,0:T(8,128)(2,1)S(1)}, u32[]{:S(2)}, u32[]{:S(2)}) collective-permute-start(bf16[32,2176]{1,0:T(8,128)(2,1)S(1)} %collective-permute-done.7.refs_8_), channel_id=1, source_target_pairs={{0,4},{2,6},{4,0},{6,2},{8,12},{10,14},{12,8},{14,10},{16,20},{18,... | collective-permute-start | bytes 417800 | tf_op jit(solution)/shard_map/ppermute | solution.py:745
  33.4 3.7 %collective-permute-done.9.refs_10_ = bf16[32,2176]{1,0:T(8,128)(2,1)S(1)} collective-permute-done((bf16[32,2176]{1,0:T(8,128)(2,1)S(1)}, bf16[32,2176]{1,0:T(8,128)(2,1)S(1)}, u32[]{:S(2)}, u32[]{:S(2)}) %collective-permute-start.9) | collective-permute-done | bytes 139296 | tf_op jit(solution)/shard_map/ppermute | solution.py:745
  37.6 2.0 %collective-permute-done.5.refs_6_ = bf16[32,2176]{1,0:T(8,128)(2,1)S(1)} collective-permute-done((bf16[32,2176]{1,0:T(8,128)(2,1)S(1)}, bf16[32,2176]{1,0:T(8,128)(2,1)S(1)}, u32[]{:S(2)}, u32[]{:S(2)}) %collective-permute-start.5) | collective-permute-done | bytes 139296 | tf_op jit(solution)/shard_map/ppermute | solution.py:745
  41.6 7.6 %project.1 = (bf16[1024,512]{1,0:T(8,128)(2,1)}, bf16[1024,2048]{1,0:T(8,128)(2,1)}, bf16[2,144,256]{2,1,0:T(8,128)(2,1)}, bf16[512,2048]{1,0:T(8,128)(2,1)}, f32[8,512]{1,0:T(8,128)}) custom-call(s32[1]{0:T(128)} %bitcast.me_ref, bf16[1024,512]{1,0:T(8,128)(2,1)} %tok_ref.1, bf16[32,2176]{1,0:T(8,128)(2,1)} %get-tuple-element.62.refs_0_, ...), custom_call_target="tpu_custom_call" | custom-call | flops 2147483648 | bytes 12582912 | tf_op jit(solution)/shard_map/project/pallas_call | solution.py:264
  49.2 3.8 %collective-permute-start.15 = (bf16[2,144,256]{2,1,0:T(8,128)(2,1)}, bf16[2,144,256]{2,1,0:T(8,128)(2,1)S(1)}, u32[]{:S(2)}, u32[]{:S(2)}) collective-permute-start(bf16[2,144,256]{2,1,0:T(8,128)(2,1)} %get-tuple-element.64), channel_id=1, source_target_pairs={{0,1},{2,3},{4,5},{6,7},{8,9},{10,11},{12,13},{14,15},{16,17},{18,... | collective-permute-start | bytes 442376 | tf_op jit(solution)/shard_map/ppermute | solution.py:765
  53.0 3.7 %collective-permute-done.15.st_in = bf16[2,144,256]{2,1,0:T(8,128)(2,1)S(1)} collective-permute-done((bf16[2,144,256]{2,1,0:T(8,128)(2,1)}, bf16[2,144,256]{2,1,0:T(8,128)(2,1)S(1)}, u32[]{:S(2)}, u32[]{:S(2)}) %collective-permute-start.15) | collective-permute-done | bytes 147488 | tf_op jit(solution)/shard_map/ppermute | solution.py:765
  57.4 10.3 %mix.1 = (bf16[1024,512]{1,0:T(8,128)(2,1)}, f32[1024,512]{1,0:T(8,128)}, f32[1024,512]{1,0:T(8,128)}, f32[1024,512]{1,0:T(8,128)}, bf16[8,2,256,256]{3,2,1,0:T(8,128)(2,1)}, /*index=5*/bf16[8,2,256,256]{3,2,1,0:T(8,128)(2,1)}) custom-call(bf16[1024,2048]{1,0:T(8,128)(2,1)} %get-tuple-element.63.pack_ref, bf16[2,144,256]{2,1,0:T(8,128)(2,1)} %copy-done.8), custom_call_target="tpu_custom_call" | custom-call | flops 6000000000 | bytes 16777216 | tf_op jit(solution)/shard_map/mix/pallas_call | solution.py:347
  68.6 21.2 %ffn.1 = (f32[1024,512]{1,0:T(8,128)}, f32[1024,512]{1,0:T(8,128)}, bf16[1024,512]{1,0:T(8,128)(2,1)}, bf16[1024,2048]{1,0:T(8,128)(2,1)}, bf16[2048,512]{1,0:T(...) custom-call(s32[1]{0:T(128)} %bitcast.me_ref, ...), custom_call_target="tpu_custom_call" | custom-call | flops 11811160064 | bytes 20971520 | tf_op jit(solution)/shard_map/ffn/pallas_call | solution.py:495
  90.4 1.7 collective-permute-done.16
  94.1 10.3 %read_back.1 = (bf16[1024,512]{1,0:T(8,128)(2,1)}, bf16[1024,512]{1,0:T(8,128)(2,1)}, bf16[1024,512]{1,0:T(8,128)(2,1)}, f32[1024,512]{1,0:T(8,128)}, bf16[2,144,256]{2,1,0:T(8,128)(2,1)}) custom-call(bf16[1024,2048]{1,0:T(8,128)(2,1)} %get-tuple-element.63.pack_ref, bf16[1024,512]{1,0:T(8,128)(2,1)} %get-tuple-element.71.gmix_ref, ...), custom_call_target="tpu_custom_call" | custom-call | flops 6000000000 | bytes 20971520 | tf_op jit(solution)/shard_map/read_back/pallas_call | solution.py:602
  105.9 3.5 %collective-permute-done.19 = bf16[2,32,4736]{2,1,0:T(8,128)(2,1)} collective-permute-done((bf16[2,32,4736]{2,1,0:T(8,128)(2,1)S(1)}, bf16[2,32,4736]{2,1,0:T(8,128)(2,1)}, u32[]{:S(2)}, u32[]{:S(2)}) %collective-permute-start.19) | collective-permute-done | bytes 606240 | tf_op jit(solution)/shard_map/ppermute | solution.py:745
  109.4 2.1 %fusion.1 = (bf16[32,4736]{1,0:T(8,128)(2,1)}, bf16[32,4736]{1,0:T(8,128)(2,1)}) fusion(bf16[2,32,4736]{2,1,0:T(8,128)(2,1)} %collective-permute-done.19, bf16[6,32,4736]{2,1,0:T(8,128)(2,1)S(1)} %collective-permute-done.18, bf16[4,32,4736]{2,1,0:T(8,128)(2,1)S(1)} %copy-done), kind=kLoop, calls=%fused_computation.11 | loop fusion | flops 1818624 | bytes 2424832 | tf_op jit(solution)/shard_map/convert_element_type | solution.py:753
  111.5 3.8 %collective-permute-start.23 = (bf16[32,4736]{1,0:T(8,128)(2,1)}, bf16[32,4736]{1,0:T(8,128)(2,1)}, u32[]{:S(2)}, u32[]{:S(2)}) collective-permute-start(bf16[32,4736]{1,0:T(8,128)(2,1)} %get-tuple-element.113), channel_id=1, source_target_pairs={{0,24},{2,26},{4,28},{6,30},{8,16},{10,18},{12,20},{14,22},{16,8},... | collective-permute-start | bytes 909320 | tf_op jit(solution)/shard_map/ppermute | solution.py:745
  117.8 15.6 %write_back.1 = (bf16[1024,1536]{1,0:T(8,128)(2,1)}, bf16[4,32,2048]{2,1,0:T(8,128)(2,1)}, bf16[2,32,2048]{2,1,0:T(8,128)(2,1)}, bf16[2,32,2048]{2,1,0:T(8,128)(...) custom-call(s32[1]{0:T(128)} %bitcast.me_ref, bf16[1024,2048]{1,0:T(8,128)(2,1)} %get-tuple-element.63.pack_ref, ...), custom_call_target="tpu_custom_call" | custom-call | flops 11000000512 | bytes 18874368 | tf_op jit(solution)/shard_map/write_back/pallas_call | solution.py:697
  134.0 2.0 %fusion.3 = (bf16[32,4736]{1,0:T(8,128)(2,1)}, bf16[32,4736]{1,0:T(8,128)(2,1)S(1)}) fusion(bf16[2,32,4736]{2,1,0:T(8,128)(2,1)} %collective-permute-done.21, bf16[6,32,4736]{2,1,0:T(8,128)(2,1)S(1)} %collective-permute-done.18, bf16[4,32,4736]{2,1,0:T(8,128)(2,1)S(1)} %copy-done), kind=kLoop, calls=%fused_computation.13 | loop fusion | flops 1818624 | bytes 2424832 | tf_op jit(solution)/shard_map/convert_element_type | solution.py:753
  136.6 4.2 %collective-permute-done.22 = bf16[32,4736]{1,0:T(8,128)(2,1)} collective-permute-done((bf16[32,4736]{1,0:T(8,128)(2,1)}, bf16[32,4736]{1,0:T(8,128)(2,1)}, u32[]{:S(2)}, u32[]{:S(2)}) %collective-permute-start.22) | collective-permute-done | bytes 303136 | tf_op jit(solution)/shard_map/ppermute | solution.py:745
  143.1 7.6 %input_grad.1 = f32[1024,512]{1,0:T(8,128)} custom-call(f32[8,512]{1,0:T(8,128)} %get-tuple-element.88.gain_ref, bf16[1024,512]{1,0:T(8,128)(2,1)} %tok_ref.1, bf16[1024,512]{1,0:T(8,128)(2,1)} %get-tuple-element.95.gq_hbm.gq_ref, bf16[1024,1536]{1,0:T(8,128)(2,1)} %get-tuple-element.91.gkvc_ref, bf16[512,2048]{1,0:T(8,128)(2,1)} %get-tuple-element.96.w_ref, ...), custom_call_target="tpu_custom_call" | custom-call | flops 2147483648 | bytes 12582912 | tf_op jit(solution)/shard_map/input_grad/pallas_call | solution.py:732
  153.8 2.3 %collective-permute-start.29 = (bf16[32,2048]{1,0:T(8,128)(2,1)S(1)}, bf16[32,2048]{1,0:T(8,128)(2,1)S(1)}, u32[]{:S(2)}, u32[]{:S(2)}) collective-permute-start(bf16[32,2048]{1,0:T(8,128)(2,1)S(1)} %get-tuple-element.119), channel_id=1, source_target_pairs={{0,16},{2,18},{4,20},{6,22},{8,24},{10,26},{12,28},{14,30},{16,0},... | collective-permute-start | bytes 393224 | tf_op jit(solution)/shard_map/ppermute | solution.py:745
  156.1 2.1 %collective-permute-start.30 = (bf16[32,2048]{1,0:T(8,128)(2,1)S(1)}, bf16[32,2048]{1,0:T(8,128)(2,1)S(1)}, u32[]{:S(2)}, u32[]{:S(2)}) collective-permute-start(bf16[32,2048]{1,0:T(8,128)(2,1)S(1)} %get-tuple-element.120), channel_id=1, source_target_pairs={{0,24},{2,26},{4,28},{6,30},{8,16},{10,18},{12,20},{14,22},{16,8},... | collective-permute-start | bytes 393224 | tf_op jit(solution)/shard_map/ppermute | solution.py:745
  158.2 6.5 %ffn_out.1 = bf16[1024,512]{1,0:T(8,128)(2,1)} custom-call(bf16[1024,2048]{1,0:T(8,128)(2,1)} %get-tuple-element.104.hid_ref, f32[1024,512]{1,0:T(8,128)} %get-tuple-element.105.kept_ref, bf16[2048,512]{1,0:T(8,128)(2,1)} %get-tuple-element.106.down_ref), custom_call_target="tpu_custom_call" | custom-call | flops 2147483648 | bytes 9437184 | tf_op jit(solution)/shard_map/ffn_out/pallas_call | solution.py:537
  (119 shorter events, 28.8 us)
Async XLA Ops:
  7.2 61.5 %all-gather.2.cloned.1.call-start = ((), (), s32[]{:S(2)}) async-start(), calls=%async_computation | async-start | bytes 5152768 | tf_op jit(solution)/shard_map/all_gather | solution.py:790
  9.1 9.9 %collective-permute-start.11 = (bf16[32,2176]{1,0:T(8,128)(2,1)}, bf16[32,2176]{1,0:T(8,128)(2,1)S(1)}, u32[]{:S(2)}, u32[]{:S(2)}) collective-permute-start(bf16[32,2176]{1,0:T(8,128)(2,1)} %get-tuple-element.62.refs_0_), channel_id=1, source_target_pairs={{0,24},{2,26},{4,28},{6,30},{8,16},{10,18},{12,20},{14,22},{16,8},... | collective-permute-start | bytes 417800 | tf_op jit(solution)/shard_map/ppermute | solution.py:745
  14.3 16.2 %collective-permute-start.7 = (bf16[32,2176]{1,0:T(8,128)(2,1)}, bf16[32,2176]{1,0:T(8,128)(2,1)S(1)}, u32[]{:S(2)}, u32[]{:S(2)}) collective-permute-start(bf16[32,2176]{1,0:T(8,128)(2,1)} %get-tuple-element.62.refs_0_), channel_id=1, source_target_pairs={{0,16},{2,18},{4,20},{6,22},{8,24},{10,26},{12,28},{14,30},{16,0},... | collective-permute-start | bytes 417800 | tf_op jit(solution)/shard_map/ppermute | solution.py:745
  14.3 16.2 %collective-permute-start.3 = (bf16[32,2176]{1,0:T(8,128)(2,1)}, bf16[32,2176]{1,0:T(8,128)(2,1)S(1)}, u32[]{:S(2)}, u32[]{:S(2)}) collective-permute-start(bf16[32,2176]{1,0:T(8,128)(2,1)} %get-tuple-element.62.refs_0_), channel_id=1, source_target_pairs={{0,8},{2,10},{4,12},{6,14},{8,0},{10,2},{12,4},{14,6},{16,24},{18,... | collective-permute-start | bytes 417800 | tf_op jit(solution)/shard_map/ppermute | solution.py:745
  14.9 17.5 %collective-permute-start.1 = (bf16[32,2176]{1,0:T(8,128)(2,1)}, bf16[32,2176]{1,0:T(8,128)(2,1)S(1)}, u32[]{:S(2)}, u32[]{:S(2)}) collective-permute-start(bf16[32,2176]{1,0:T(8,128)(2,1)} %get-tuple-element.62.refs_0_), channel_id=1, source_target_pairs={{0,4},{2,6},{4,0},{6,2},{8,12},{10,14},{12,8},{14,10},{16,20},{18,... | collective-permute-start | bytes 417800 | tf_op jit(solution)/shard_map/ppermute | solution.py:745
  16.5 16.0 %collective-permute-start = (bf16[32,2176]{1,0:T(8,128)(2,1)}, bf16[32,2176]{1,0:T(8,128)(2,1)S(1)}, u32[]{:S(2)}, u32[]{:S(2)}) collective-permute-start(bf16[32,2176]{1,0:T(8,128)(2,1)} %get-tuple-element.62.refs_0_), channel_id=1, source_target_pairs={{0,2},{2,0},{4,6},{6,4},{8,10},{10,8},{12,14},{14,12},{16,18},{18,... | collective-permute-start | bytes 417800 | tf_op jit(solution)/shard_map/ppermute | solution.py:745
  19.1 13.8 %collective-permute-start.13 = (bf16[32,2176]{1,0:T(8,128)(2,1)S(1)}, bf16[32,2176]{1,0:T(8,128)(2,1)S(1)}, u32[]{:S(2)}, u32[]{:S(2)}) collective-permute-start(bf16[32,2176]{1,0:T(8,128)(2,1)S(1)} %collective-permute-done.11.refs_12_), channel_id=1, source_target_pairs={{0,4},{2,6},{4,0},{6,2},{8,12},{10,14},{12,8},{14,10},{16,20},{18,... | collective-permute-start | bytes 417800 | tf_op jit(solution)/shard_map/ppermute | solution.py:745
  32.5 7.1 %collective-permute-start.5 = (bf16[32,2176]{1,0:T(8,128)(2,1)S(1)}, bf16[32,2176]{1,0:T(8,128)(2,1)S(1)}, u32[]{:S(2)}, u32[]{:S(2)}) collective-permute-start(bf16[32,2176]{1,0:T(8,128)(2,1)S(1)} %collective-permute-done.3.refs_4_), channel_id=1, source_target_pairs={{0,4},{2,6},{4,0},{6,2},{8,12},{10,14},{12,8},{14,10},{16,20},{18,... | collective-permute-start | bytes 417800 | tf_op jit(solution)/shard_map/ppermute | solution.py:745
  49.2 7.5 %collective-permute-start.15 = (bf16[2,144,256]{2,1,0:T(8,128)(2,1)}, bf16[2,144,256]{2,1,0:T(8,128)(2,1)S(1)}, u32[]{:S(2)}, u32[]{:S(2)}) collective-permute-start(bf16[2,144,256]{2,1,0:T(8,128)(2,1)} %get-tuple-element.64), channel_id=1, source_target_pairs={{0,1},{2,3},{4,5},{6,7},{8,9},{10,11},{12,13},{14,15},{16,17},{18,... | collective-permute-start | bytes 442376 | tf_op jit(solution)/shard_map/ppermute | solution.py:765
  90.2 19.2 %collective-permute-start.18 = (bf16[6,32,4736]{2,1,0:T(8,128)(2,1)}, bf16[6,32,4736]{2,1,0:T(8,128)(2,1)S(1)}, u32[]{:S(2)}, u32[]{:S(2)}) collective-permute-start(bf16[6,32,4736]{2,1,0:T(8,128)(2,1)} %get-tuple-element.84), channel_id=1, source_target_pairs={{0,2},{2,0},{4,6},{6,4},{8,10},{10,8},{12,14},{14,12},{16,18},{18,... | collective-permute-start | bytes 5455880 | tf_op jit(solution)/shard_map/ppermute | solution.py:745
  93.4 16.0 %collective-permute-start.19 = (bf16[2,32,4736]{2,1,0:T(8,128)(2,1)S(1)}, bf16[2,32,4736]{2,1,0:T(8,128)(2,1)}, u32[]{:S(2)}, u32[]{:S(2)}) collective-permute-start(bf16[2,32,4736]{2,1,0:T(8,128)(2,1)S(1)} %add_convert_fusion.1), channel_id=1, source_target_pairs={{0,4},{2,6},{4,0},{6,2},{8,12},{10,14},{12,8},{14,10},{16,20},{18,... | collective-permute-start | bytes 1818632 | tf_op jit(solution)/shard_map/ppermute | solution.py:745
  104.4 10.9 %collective-permute-start.17 = (bf16[2,144,256]{2,1,0:T(8,128)(2,1)}, bf16[2,144,256]{2,1,0:T(8,128)(2,1)S(1)}, u32[]{:S(2)}, u32[]{:S(2)}) collective-permute-start(bf16[2,144,256]{2,1,0:T(8,128)(2,1)} %get-tuple-element.80), channel_id=1, source_target_pairs={{1,0},{3,2},{5,4},{7,6},{9,8},{11,10},{13,12},{15,14},{17,16},{19,... | collective-permute-start | bytes 442376 | tf_op jit(solution)/shard_map/ppermute | solution.py:765
  111.5 25.0 %collective-permute-start.23 = (bf16[32,4736]{1,0:T(8,128)(2,1)}, bf16[32,4736]{1,0:T(8,128)(2,1)}, u32[]{:S(2)}, u32[]{:S(2)}) collective-permute-start(bf16[32,4736]{1,0:T(8,128)(2,1)} %get-tuple-element.113), channel_id=1, source_target_pairs={{0,24},{2,26},{4,28},{6,30},{8,16},{10,18},{12,20},{14,22},{16,8},... | collective-permute-start | bytes 909320 | tf_op jit(solution)/shard_map/ppermute | solution.py:745
  115.3 25.4 %collective-permute-start.22 = (bf16[32,4736]{1,0:T(8,128)(2,1)}, bf16[32,4736]{1,0:T(8,128)(2,1)}, u32[]{:S(2)}, u32[]{:S(2)}) collective-permute-start(bf16[32,4736]{1,0:T(8,128)(2,1)} %get-tuple-element.114), channel_id=1, source_target_pairs={{0,16},{2,18},{4,20},{6,22},{8,24},{10,26},{12,28},{14,30},{16,0},... | collective-permute-start | bytes 909320 | tf_op jit(solution)/shard_map/ppermute | solution.py:745
  116.3 17.7 %collective-permute-start.21 = (bf16[2,32,4736]{2,1,0:T(8,128)(2,1)}, bf16[2,32,4736]{2,1,0:T(8,128)(2,1)}, u32[]{:S(2)}, u32[]{:S(2)}) collective-permute-start(bf16[2,32,4736]{2,1,0:T(8,128)(2,1)} %add_convert_fusion), channel_id=1, source_target_pairs={{0,4},{2,6},{4,0},{6,2},{8,12},{10,14},{12,8},{14,10},{16,20},{18,... | collective-permute-start | bytes 1818632 | tf_op jit(solution)/shard_map/ppermute | solution.py:745
  133.4 7.3 %collective-permute-start.25 = (bf16[2,32,2048]{2,1,0:T(8,128)(2,1)}, bf16[2,32,2048]{2,1,0:T(8,128)(2,1)S(1)}, u32[]{:S(2)}, u32[]{:S(2)}) collective-permute-start(bf16[2,32,2048]{2,1,0:T(8,128)(2,1)} %get-tuple-element.102), channel_id=1, source_target_pairs={{0,2},{2,0},{4,6},{6,4},{8,10},{10,8},{12,14},{14,12},{16,18},{18,... | collective-permute-start | bytes 786440 | tf_op jit(solution)/shard_map/ppermute | solution.py:745
  133.5 7.9 %collective-permute-start.20 = (bf16[6,32,2048]{2,1,0:T(8,128)(2,1)}, bf16[6,32,2048]{2,1,0:T(8,128)(2,1)S(1)}, u32[]{:S(2)}, u32[]{:S(2)}) collective-permute-start(bf16[6,32,2048]{2,1,0:T(8,128)(2,1)} %get-tuple-element.90), channel_id=1, source_target_pairs={{0,2},{2,0},{4,6},{6,4},{8,10},{10,8},{12,14},{14,12},{16,18},{18,... | collective-permute-start | bytes 2359304 | tf_op jit(solution)/shard_map/ppermute | solution.py:745
  136.0 14.6 %collective-permute-start.24 = (bf16[32,4736]{1,0:T(8,128)(2,1)}, bf16[32,4736]{1,0:T(8,128)(2,1)S(1)}, u32[]{:S(2)}, u32[]{:S(2)}) collective-permute-start(bf16[32,4736]{1,0:T(8,128)(2,1)} %get-tuple-element.111), channel_id=1, source_target_pairs={{0,8},{2,10},{4,12},{6,14},{8,0},{10,2},{12,4},{14,6},{16,24},{18,... | collective-permute-start | bytes 909320 | tf_op jit(solution)/shard_map/ppermute | solution.py:745
  140.8 12.6 %collective-permute-start.26 = (bf16[2,32,2048]{2,1,0:T(8,128)(2,1)S(1)}, bf16[2,32,2048]{2,1,0:T(8,128)(2,1)S(1)}, u32[]{:S(2)}, u32[]{:S(2)}) collective-permute-start(bf16[2,32,2048]{2,1,0:T(8,128)(2,1)S(1)} %add_convert_fusion.8), channel_id=1, source_target_pairs={{0,4},{2,6},{4,0},{6,2},{8,12},{10,14},{12,8},{14,10},{16,20},{18,... | collective-permute-start | bytes 786440 | tf_op jit(solution)/shard_map/ppermute | solution.py:745
  141.5 11.9 %collective-permute-start.27 = (bf16[2,32,2048]{2,1,0:T(8,128)(2,1)S(1)}, bf16[2,32,2048]{2,1,0:T(8,128)(2,1)S(1)}, u32[]{:S(2)}, u32[]{:S(2)}) collective-permute-start(bf16[2,32,2048]{2,1,0:T(8,128)(2,1)S(1)} %add_convert_fusion.9), channel_id=1, source_target_pairs={{0,4},{2,6},{4,0},{6,2},{8,12},{10,14},{12,8},{14,10},{16,20},{18,... | collective-permute-start | bytes 786440 | tf_op jit(solution)/shard_map/ppermute | solution.py:745
  151.9 14.6 %collective-permute-start.32 = (bf16[32,4736]{1,0:T(8,128)(2,1)S(1)}, bf16[32,4736]{1,0:T(8,128)(2,1)S(1)}, u32[]{:S(2)}, u32[]{:S(2)}) collective-permute-start(bf16[32,4736]{1,0:T(8,128)(2,1)S(1)} %add_convert_fusion.3), channel_id=1, source_target_pairs={{0,1},{1,0},{2,3},{3,2},{4,5},{5,4},{6,7},{7,6},{8,9},{9,8},{10,11... | collective-permute-start | bytes 909320 | tf_op jit(solution)/shard_map/ppermute | solution.py:817
  153.7 11.0 %collective-permute-start.28 = (bf16[32,2048]{1,0:T(8,128)(2,1)S(1)}, bf16[32,2048]{1,0:T(8,128)(2,1)S(1)}, u32[]{:S(2)}, u32[]{:S(2)}) collective-permute-start(bf16[32,2048]{1,0:T(8,128)(2,1)S(1)} %get-tuple-element.115), channel_id=1, source_target_pairs={{0,8},{2,10},{4,12},{6,14},{8,0},{10,2},{12,4},{14,6},{16,24},{18,... | collective-permute-start | bytes 393224 | tf_op jit(solution)/shard_map/ppermute | solution.py:745
  153.8 11.2 %collective-permute-start.29 = (bf16[32,2048]{1,0:T(8,128)(2,1)S(1)}, bf16[32,2048]{1,0:T(8,128)(2,1)S(1)}, u32[]{:S(2)}, u32[]{:S(2)}) collective-permute-start(bf16[32,2048]{1,0:T(8,128)(2,1)S(1)} %get-tuple-element.119), channel_id=1, source_target_pairs={{0,16},{2,18},{4,20},{6,22},{8,24},{10,26},{12,28},{14,30},{16,0},... | collective-permute-start | bytes 393224 | tf_op jit(solution)/shard_map/ppermute | solution.py:745
  156.1 8.9 %collective-permute-start.30 = (bf16[32,2048]{1,0:T(8,128)(2,1)S(1)}, bf16[32,2048]{1,0:T(8,128)(2,1)S(1)}, u32[]{:S(2)}, u32[]{:S(2)}) collective-permute-start(bf16[32,2048]{1,0:T(8,128)(2,1)S(1)} %get-tuple-element.120), channel_id=1, source_target_pairs={{0,24},{2,26},{4,28},{6,30},{8,16},{10,18},{12,20},{14,22},{16,8},... | collective-permute-start | bytes 393224 | tf_op jit(solution)/shard_map/ppermute | solution.py:745
  (34 other events, 198.9 us)
Sparse Core Ops, SparseCore 0:
  10.3 58.2 all-gather.1

commit v6 on v5

--- a/solution.py
+++ b/solution.py
@@ -828,16 +828,19 @@
         me, packed, gmix, a, u, gtot, after(others(gstate, -1, seqs), *mine.values()), att, gq, n
     )
     mine = joined(near, crossed_low, 0, gkvc)
-    att_near, att_low, att_high = start_sum(shares, *ffn_parts, *mine.values())
+    att_near, att_low, att_high = start_sum(shares, *ffn_parts[-1:], *mine.values())
     ffn_parts += [along(mine[k], k) for k in range(half)]
     crossed_high, crossed_low = swap(att_high, 2, n), swap(att_low, 2, n)
-    grad_tokens = input_grad(gain, tokens, after(gq, att_low, *mine.values()), gkvc, w_att, gres)
-    ffn_sum = add(after(mine[0], grad_tokens), *(p for p in ffn_parts if p is not mine[0]))
-    mine = joined(att_near, crossed_high, half, grad_tokens, ffn_sum) | joined(att_near, crossed_low, 0, grad_tokens)
-    att_parts = [along(mine[k], k) for k in range(depth)]
-    layer_out = ffn_out(after(hid, *mine.values()), kept, full_down)
+    layer_out = ffn_out(after(hid, att_low, mine[0]), kept, full_down)
+    ffn_sum = add(after(mine[0], layer_out), *(p for p in ffn_parts if p is not mine[0]))
+    mine = joined(att_near, crossed_high, half, layer_out)
+    att_parts = [along(mine[k], k) for k in range(half, depth)]
+    mine = joined(att_near, crossed_low, 0, layer_out, *mine.values())
+    att_parts += [along(mine[k], k) for k in range(half)]
+    grad_tokens = input_grad(gain, tokens, after(gq, *mine.values(), ffn_sum), gkvc, w_att, gres)
     ffn_share = seq_sum(ffn_sum)
-    att_share = seq_sum(add(*[after(p, layer_out) for p in att_parts]))
+    att_sum = add(*[after(p, grad_tokens) for p in att_parts])
+    att_share = seq_sum(att_sum)
     gain_share = jnp.sum(att_share * first[:, : 4 * d].astype(F32), axis=1) / gain_attn.astype(F32)
     up, down, out, vec = (
         ffn_share[:, :ff],

time: 179 us -> 176 us (0.983)
  waiting for transfers between devices: 34.1 us -> 31.5 us
    ppermute x29, waiting for transfers between devices: 29 us -> 25.1 us  [swap(): return lax.ppermute(x, 'fsdp', [(i, i ^ mask) for i in range(n)])]
    convert_element_type x9 -> x10, other arithmetic: 7.98 us -> 7.91 us  [add(): return sum((x.astype(F32) for x in items)).astype(BF16)]
  transfers between devices with their start and end apart: 34 -> 34, of which waited for: 12 -> 11; matrix products, arithmetic and copies ran while one was open for 6% -> 6% of each run, Pallas kernels for 32% -> 33%
where the time goes in v6:
time: 176 us; the launch traced here: 175 us
  Pallas kernels  80.9 us (46%)
  starting transfers between devices  34.6 us (20%)
  waiting for transfers between devices  31.5 us (18%)
  between operations  14.4 us (8%)
  other arithmetic  9.39 us (5%)
  local copies, waits for them, and re-layouts  4.39 us (2%)
    ppermute x29, starting transfers between devices, swap(): return lax.ppermute(x, 'fsdp', [(i, i ^ mask) for i in range(n)])  26.8 us
    ppermute x29, waiting for transfers between devices, swap(): return lax.ppermute(x, 'fsdp', [(i, i ^ mask) for i in range(n)])  25.1 us
    pallas_call x1, Pallas kernels, ffn(): pl.pallas_call(partial(ffn_kernel, n), in_specs=[pl.BlockSpec(memory_spac...  21.3 us
    pallas_call x1, Pallas kernels, write_back(): pl.pallas_call(partial(write_back_kernel, n), grid=(t // rows,), in_specs...  15.6 us
    pallas_call x1, Pallas kernels, mix(): pl.pallas_call(mix_kernel, grid=(t // rows,), in_specs=[row(wide), const(...  10.3 us
    pallas_call x1, Pallas kernels, read_back(): pl.pallas_call(read_back_kernel, grid=(t // rows,), in_specs=[row(wide),...  10.3 us
    convert_element_type x10, other arithmetic, add(): return sum((x.astype(F32) for x in items)).astype(BF16)  7.91 us
    pallas_call x1, Pallas kernels, project(): pl.pallas_call(partial(project_kernel, where, len(pieces), r), in_specs=[...  7.58 us
  transfers between devices with their start and end apart: 34, of which 11 were waited for; matrix products, arithmetic and copies ran while one was open for 6% of the time, Pallas kernels for 33%

profile of v6, /device:TPU:0, one launch (start us, length us, event | category | flops | bytes accessed | tf_op | source)
XLA Modules:
  0.0 175.3 jit_solution(4272694333553989368)
XLA Ops:
  7.2 1.9 %pack.1 = (bf16[32,2176]{1,0:T(8,128)(2,1)}, bf16[32,4736]{1,0:T(8,128)(2,1)}) custom-call(bf16[32,512]{1,0:T(8,128)(2,1)} %q.1, bf16[32,512]{1,0:T(8,128)(2,1)} %k.1, bf16[32,512]{1,0:T(8,128)(2,1)} %v.1, bf16[32,512]{1,0:T(8,128)(2,1)} %c.1, bf16[32,512]{1,0:T(8,128)(2,1)} %o.1, bf16[32,2048]{1,0:T(8,128)(2,1)} %up.1, bf16[128,512]{1,0:T(8,128)(2,1)} %down.1, ...), custom_call_target="tpu_custom_call" | custom-call | bytes 1048576 | tf_op jit(solution)/shard_map/pack/pallas_call | solution.py:174
  9.1 5.1 %collective-permute-start.11 = (bf16[32,2176]{1,0:T(8,128)(2,1)}, bf16[32,2176]{1,0:T(8,128)(2,1)S(1)}, u32[]{:S(2)}, u32[]{:S(2)}) collective-permute-start(bf16[32,2176]{1,0:T(8,128)(2,1)} %get-tuple-element.62.refs_0_), channel_id=1, source_target_pairs={{0,24},{2,26},{4,28},{6,30},{8,16},{10,18},{12,20},{14,22},{16,8},... | collective-permute-start | bytes 417800 | tf_op jit(solution)/shard_map/ppermute | solution.py:745
  16.5 2.5 %collective-permute-done.11.refs_12_ = bf16[32,2176]{1,0:T(8,128)(2,1)S(1)} collective-permute-done((bf16[32,2176]{1,0:T(8,128)(2,1)}, bf16[32,2176]{1,0:T(8,128)(2,1)S(1)}, u32[]{:S(2)}, u32[]{:S(2)}) %collective-permute-start.11) | collective-permute-done | bytes 139296 | tf_op jit(solution)/shard_map/ppermute | solution.py:745
  20.8 9.7 %collective-permute-done.7.refs_8_ = bf16[32,2176]{1,0:T(8,128)(2,1)S(1)} collective-permute-done((bf16[32,2176]{1,0:T(8,128)(2,1)}, bf16[32,2176]{1,0:T(8,128)(2,1)S(1)}, u32[]{:S(2)}, u32[]{:S(2)}) %collective-permute-start.7) | collective-permute-done | bytes 139296 | tf_op jit(solution)/shard_map/ppermute | solution.py:745
  30.5 1.8 %collective-permute-start.9 = (bf16[32,2176]{1,0:T(8,128)(2,1)S(1)}, bf16[32,2176]{1,0:T(8,128)(2,1)S(1)}, u32[]{:S(2)}, u32[]{:S(2)}) collective-permute-start(bf16[32,2176]{1,0:T(8,128)(2,1)S(1)} %collective-permute-done.7.refs_8_), channel_id=1, source_target_pairs={{0,4},{2,6},{4,0},{6,2},{8,12},{10,14},{12,8},{14,10},{16,20},{18,... | collective-permute-start | bytes 417800 | tf_op jit(solution)/shard_map/ppermute | solution.py:745
  33.4 3.6 %collective-permute-done.9.refs_10_ = bf16[32,2176]{1,0:T(8,128)(2,1)S(1)} collective-permute-done((bf16[32,2176]{1,0:T(8,128)(2,1)S(1)}, bf16[32,2176]{1,0:T(8,128)(2,1)S(1)}, u32[]{:S(2)}, u32[]{:S(2)}) %collective-permute-start.9) | collective-permute-done | bytes 139296 | tf_op jit(solution)/shard_map/ppermute | solution.py:745
  37.6 2.0 %collective-permute-done.5.refs_6_ = bf16[32,2176]{1,0:T(8,128)(2,1)S(1)} collective-permute-done((bf16[32,2176]{1,0:T(8,128)(2,1)S(1)}, bf16[32,2176]{1,0:T(8,128)(2,1)S(1)}, u32[]{:S(2)}, u32[]{:S(2)}) %collective-permute-start.5) | collective-permute-done | bytes 139296 | tf_op jit(solution)/shard_map/ppermute | solution.py:745
  41.6 7.6 %project.1 = (bf16[1024,512]{1,0:T(8,128)(2,1)}, bf16[1024,2048]{1,0:T(8,128)(2,1)}, bf16[2,144,256]{2,1,0:T(8,128)(2,1)}, bf16[512,2048]{1,0:T(8,128)(2,1)}, f32[8,512]{1,0:T(8,128)}) custom-call(s32[1]{0:T(128)} %bitcast.me_ref, bf16[1024,512]{1,0:T(8,128)(2,1)} %tok_ref.1, bf16[32,2176]{1,0:T(8,128)(2,1)} %get-tuple-element.62.refs_0_, ...), custom_call_target="tpu_custom_call" | custom-call | flops 2147483648 | bytes 12582912 | tf_op jit(solution)/shard_map/project/pallas_call | solution.py:264
  49.2 3.8 %collective-permute-start.15 = (bf16[2,144,256]{2,1,0:T(8,128)(2,1)}, bf16[2,144,256]{2,1,0:T(8,128)(2,1)S(1)}, u32[]{:S(2)}, u32[]{:S(2)}) collective-permute-start(bf16[2,144,256]{2,1,0:T(8,128)(2,1)} %get-tuple-element.64), channel_id=1, source_target_pairs={{0,1},{2,3},{4,5},{6,7},{8,9},{10,11},{12,13},{14,15},{16,17},{18,... | collective-permute-start | bytes 442376 | tf_op jit(solution)/shard_map/ppermute | solution.py:765
  53.0 3.7 %collective-permute-done.15.st_in = bf16[2,144,256]{2,1,0:T(8,128)(2,1)S(1)} collective-permute-done((bf16[2,144,256]{2,1,0:T(8,128)(2,1)}, bf16[2,144,256]{2,1,0:T(8,128)(2,1)S(1)}, u32[]{:S(2)}, u32[]{:S(2)}) %collective-permute-start.15) | collective-permute-done | bytes 147488 | tf_op jit(solution)/shard_map/ppermute | solution.py:765
  57.4 10.3 %mix.1 = (bf16[1024,512]{1,0:T(8,128)(2,1)}, f32[1024,512]{1,0:T(8,128)}, f32[1024,512]{1,0:T(8,128)}, f32[1024,512]{1,0:T(8,128)}, bf16[8,2,256,256]{3,2,1,0:T(8,128)(2,1)}, /*index=5*/bf16[8,2,256,256]{3,2,1,0:T(8,128)(2,1)}) custom-call(bf16[1024,2048]{1,0:T(8,128)(2,1)} %get-tuple-element.63.pack_ref, bf16[2,144,256]{2,1,0:T(8,128)(2,1)} %copy-done.8), custom_call_target="tpu_custom_call" | custom-call | flops 6000000000 | bytes 16777216 | tf_op jit(solution)/shard_map/mix/pallas_call | solution.py:347
  68.6 21.3 %ffn.1 = (f32[1024,512]{1,0:T(8,128)}, f32[1024,512]{1,0:T(8,128)}, bf16[1024,512]{1,0:T(8,128)(2,1)}, bf16[1024,2048]{1,0:T(8,128)(2,1)}, bf16[2048,512]{1,0:T(...) custom-call(s32[1]{0:T(128)} %bitcast.me_ref, ...), custom_call_target="tpu_custom_call" | custom-call | flops 11811160064 | bytes 20971520 | tf_op jit(solution)/shard_map/ffn/pallas_call | solution.py:495
  90.5 1.7 collective-permute-done.16
  94.1 10.3 %read_back.1 = (bf16[1024,512]{1,0:T(8,128)(2,1)}, bf16[1024,512]{1,0:T(8,128)(2,1)}, bf16[1024,512]{1,0:T(8,128)(2,1)}, f32[1024,512]{1,0:T(8,128)}, bf16[2,144,256]{2,1,0:T(8,128)(2,1)}) custom-call(bf16[1024,2048]{1,0:T(8,128)(2,1)} %get-tuple-element.63.pack_ref, bf16[1024,512]{1,0:T(8,128)(2,1)} %get-tuple-element.71.gmix_ref, ...), custom_call_target="tpu_custom_call" | custom-call | flops 6000000000 | bytes 20971520 | tf_op jit(solution)/shard_map/read_back/pallas_call | solution.py:602
  105.8 3.6 %collective-permute-done.19 = bf16[2,32,4736]{2,1,0:T(8,128)(2,1)} collective-permute-done((bf16[2,32,4736]{2,1,0:T(8,128)(2,1)S(1)}, bf16[2,32,4736]{2,1,0:T(8,128)(2,1)}, u32[]{:S(2)}, u32[]{:S(2)}) %collective-permute-start.19) | collective-permute-done | bytes 606240 | tf_op jit(solution)/shard_map/ppermute | solution.py:745
  109.4 2.1 %fusion.1 = (bf16[32,4736]{1,0:T(8,128)(2,1)}, bf16[32,4736]{1,0:T(8,128)(2,1)}) fusion(bf16[2,32,4736]{2,1,0:T(8,128)(2,1)} %collective-permute-done.19, bf16[6,32,4736]{2,1,0:T(8,128)(2,1)S(1)} %collective-permute-done.18, bf16[4,32,4736]{2,1,0:T(8,128)(2,1)S(1)} %copy-done), kind=kLoop, calls=%fused_computation.11 | loop fusion | flops 1818624 | bytes 2424832 | tf_op jit(solution)/shard_map/convert_element_type | solution.py:753
  111.6 3.6 %collective-permute-start.22 = (bf16[32,4736]{1,0:T(8,128)(2,1)}, bf16[32,4736]{1,0:T(8,128)(2,1)}, u32[]{:S(2)}, u32[]{:S(2)}) collective-permute-start(bf16[32,4736]{1,0:T(8,128)(2,1)} %get-tuple-element.113), channel_id=1, source_target_pairs={{0,24},{2,26},{4,28},{6,30},{8,16},{10,18},{12,20},{14,22},{16,8},... | collective-permute-start | bytes 909320 | tf_op jit(solution)/shard_map/ppermute | solution.py:745
  117.7 15.6 %write_back.1 = (bf16[1024,1536]{1,0:T(8,128)(2,1)}, bf16[4,32,2048]{2,1,0:T(8,128)(2,1)}, bf16[2,32,2048]{2,1,0:T(8,128)(2,1)}, bf16[2,32,2048]{2,1,0:T(8,128)(...) custom-call(s32[1]{0:T(128)} %bitcast.me_ref, bf16[1024,2048]{1,0:T(8,128)(2,1)} %get-tuple-element.63.pack_ref, ...), custom_call_target="tpu_custom_call" | custom-call | flops 11000000512 | bytes 18874368 | tf_op jit(solution)/shard_map/write_back/pallas_call | solution.py:697
  133.9 2.0 %fusion.3 = (bf16[32,4736]{1,0:T(8,128)(2,1)}, bf16[32,4736]{1,0:T(8,128)(2,1)S(1)}) fusion(bf16[2,32,4736]{2,1,0:T(8,128)(2,1)} %collective-permute-done.21, bf16[6,32,4736]{2,1,0:T(8,128)(2,1)S(1)} %collective-permute-done.18, bf16[4,32,4736]{2,1,0:T(8,128)(2,1)S(1)} %copy-done), kind=kLoop, calls=%fused_computation.13 | loop fusion | flops 1818624 | bytes 2424832 | tf_op jit(solution)/shard_map/convert_element_type | solution.py:753
  138.8 6.5 %ffn_out.1 = bf16[1024,512]{1,0:T(8,128)(2,1)} custom-call(bf16[1024,2048]{1,0:T(8,128)(2,1)} %get-tuple-element.93.hid_ref, f32[1024,512]{1,0:T(8,128)} %get-tuple-element.94.kept_ref, bf16[2048,512]{1,0:T(8,128)(2,1)} %get-tuple-element.95.down_ref), custom_call_target="tpu_custom_call" | custom-call | flops 2147483648 | bytes 9437184 | tf_op jit(solution)/shard_map/ffn_out/pallas_call | solution.py:537
  145.9 3.9 %collective-permute-start.29 = (bf16[32,2048]{1,0:T(8,128)(2,1)S(1)}, bf16[32,2048]{1,0:T(8,128)(2,1)S(1)}, u32[]{:S(2)}, u32[]{:S(2)}) collective-permute-start(bf16[32,2048]{1,0:T(8,128)(2,1)S(1)} %get-tuple-element.117), channel_id=1, source_target_pairs={{0,24},{2,26},{4,28},{6,30},{8,16},{10,18},{12,20},{14,22},{16,8},... | collective-permute-start | bytes 393224 | tf_op jit(solution)/shard_map/ppermute | solution.py:745
  151.1 2.5 %collective-permute-start.32 = (bf16[32,4736]{1,0:T(8,128)(2,1)S(1)}, bf16[32,4736]{1,0:T(8,128)(2,1)S(1)}, u32[]{:S(2)}, u32[]{:S(2)}) collective-permute-start(bf16[32,4736]{1,0:T(8,128)(2,1)S(1)} %add_convert_fusion.3), channel_id=1, source_target_pairs={{0,1},{1,0},{2,3},{3,2},{4,5},{5,4},{6,7},{7,6},{8,9},{9,8},{10,11... | collective-permute-start | bytes 909320 | tf_op jit(solution)/shard_map/ppermute | solution.py:817
  154.3 7.5 %input_grad.1 = f32[1024,512]{1,0:T(8,128)} custom-call(f32[8,512]{1,0:T(8,128)} %get-tuple-element.96.gain_ref, bf16[1024,512]{1,0:T(8,128)(2,1)} %tok_ref.1, bf16[1024,512]{1,0:T(8,128)(2,1)} %get-tuple-element.104.gq_hbm.gq_ref, bf16[1024,1536]{1,0:T(8,128)(2,1)} %get-tuple-element.89.gkvc_ref, bf16[512,2048]{1,0:T(8,128)(2,1)} %get-tuple-element.105.w_ref, ...), custom_call_target="tpu_custom_call" | custom-call | flops 2147483648 | bytes 12582912 | tf_op jit(solution)/shard_map/input_grad/pallas_call | solution.py:732
  165.3 1.7 collective-permute-done.31
  (120 shorter events, 26.4 us)
Async XLA Ops:
  7.2 61.5 %all-gather.2.cloned.1.call-start = ((), (), s32[]{:S(2)}) async-start(), calls=%async_computation | async-start | bytes 5152768 | tf_op jit(solution)/shard_map/all_gather | solution.py:790
  9.1 9.9 %collective-permute-start.11 = (bf16[32,2176]{1,0:T(8,128)(2,1)}, bf16[32,2176]{1,0:T(8,128)(2,1)S(1)}, u32[]{:S(2)}, u32[]{:S(2)}) collective-permute-start(bf16[32,2176]{1,0:T(8,128)(2,1)} %get-tuple-element.62.refs_0_), channel_id=1, source_target_pairs={{0,24},{2,26},{4,28},{6,30},{8,16},{10,18},{12,20},{14,22},{16,8},... | collective-permute-start | bytes 417800 | tf_op jit(solution)/shard_map/ppermute | solution.py:745
  14.2 16.2 %collective-permute-start.7 = (bf16[32,2176]{1,0:T(8,128)(2,1)}, bf16[32,2176]{1,0:T(8,128)(2,1)S(1)}, u32[]{:S(2)}, u32[]{:S(2)}) collective-permute-start(bf16[32,2176]{1,0:T(8,128)(2,1)} %get-tuple-element.62.refs_0_), channel_id=1, source_target_pairs={{0,16},{2,18},{4,20},{6,22},{8,24},{10,26},{12,28},{14,30},{16,0},... | collective-permute-start | bytes 417800 | tf_op jit(solution)/shard_map/ppermute | solution.py:745
  14.3 16.2 %collective-permute-start.3 = (bf16[32,2176]{1,0:T(8,128)(2,1)}, bf16[32,2176]{1,0:T(8,128)(2,1)S(1)}, u32[]{:S(2)}, u32[]{:S(2)}) collective-permute-start(bf16[32,2176]{1,0:T(8,128)(2,1)} %get-tuple-element.62.refs_0_), channel_id=1, source_target_pairs={{0,8},{2,10},{4,12},{6,14},{8,0},{10,2},{12,4},{14,6},{16,24},{18,... | collective-permute-start | bytes 417800 | tf_op jit(solution)/shard_map/ppermute | solution.py:745
  14.9 17.5 %collective-permute-start.1 = (bf16[32,2176]{1,0:T(8,128)(2,1)}, bf16[32,2176]{1,0:T(8,128)(2,1)S(1)}, u32[]{:S(2)}, u32[]{:S(2)}) collective-permute-start(bf16[32,2176]{1,0:T(8,128)(2,1)} %get-tuple-element.62.refs_0_), channel_id=1, source_target_pairs={{0,4},{2,6},{4,0},{6,2},{8,12},{10,14},{12,8},{14,10},{16,20},{18,... | collective-permute-start | bytes 417800 | tf_op jit(solution)/shard_map/ppermute | solution.py:745
  16.5 16.0 %collective-permute-start = (bf16[32,2176]{1,0:T(8,128)(2,1)}, bf16[32,2176]{1,0:T(8,128)(2,1)S(1)}, u32[]{:S(2)}, u32[]{:S(2)}) collective-permute-start(bf16[32,2176]{1,0:T(8,128)(2,1)} %get-tuple-element.62.refs_0_), channel_id=1, source_target_pairs={{0,2},{2,0},{4,6},{6,4},{8,10},{10,8},{12,14},{14,12},{16,18},{18,... | collective-permute-start | bytes 417800 | tf_op jit(solution)/shard_map/ppermute | solution.py:745
  19.1 13.8 %collective-permute-start.13 = (bf16[32,2176]{1,0:T(8,128)(2,1)S(1)}, bf16[32,2176]{1,0:T(8,128)(2,1)S(1)}, u32[]{:S(2)}, u32[]{:S(2)}) collective-permute-start(bf16[32,2176]{1,0:T(8,128)(2,1)S(1)} %collective-permute-done.11.refs_12_), channel_id=1, source_target_pairs={{0,4},{2,6},{4,0},{6,2},{8,12},{10,14},{12,8},{14,10},{16,20},{18,... | collective-permute-start | bytes 417800 | tf_op jit(solution)/shard_map/ppermute | solution.py:745
  32.5 7.1 %collective-permute-start.5 = (bf16[32,2176]{1,0:T(8,128)(2,1)S(1)}, bf16[32,2176]{1,0:T(8,128)(2,1)S(1)}, u32[]{:S(2)}, u32[]{:S(2)}) collective-permute-start(bf16[32,2176]{1,0:T(8,128)(2,1)S(1)} %collective-permute-done.3.refs_4_), channel_id=1, source_target_pairs={{0,4},{2,6},{4,0},{6,2},{8,12},{10,14},{12,8},{14,10},{16,20},{18,... | collective-permute-start | bytes 417800 | tf_op jit(solution)/shard_map/ppermute | solution.py:745
  32.9 6.7 %collective-permute-start.4 = (bf16[32,2176]{1,0:T(8,128)(2,1)S(1)}, bf16[32,2176]{1,0:T(8,128)(2,1)S(1)}, u32[]{:S(2)}, u32[]{:S(2)}) collective-permute-start(bf16[32,2176]{1,0:T(8,128)(2,1)S(1)} %collective-permute-done.3.refs_4_), channel_id=1, source_target_pairs={{0,2},{2,0},{4,6},{6,4},{8,10},{10,8},{12,14},{14,12},{16,18},{18,... | collective-permute-start | bytes 417800 | tf_op jit(solution)/shard_map/ppermute | solution.py:745
  33.0 6.7 %collective-permute-start.2 = (bf16[32,2176]{1,0:T(8,128)(2,1)S(1)}, bf16[32,2176]{1,0:T(8,128)(2,1)S(1)}, u32[]{:S(2)}, u32[]{:S(2)}) collective-permute-start(bf16[32,2176]{1,0:T(8,128)(2,1)S(1)} %collective-permute-done.1.refs_2_), channel_id=1, source_target_pairs={{0,2},{2,0},{4,6},{6,4},{8,10},{10,8},{12,14},{14,12},{16,18},{18,... | collective-permute-start | bytes 417800 | tf_op jit(solution)/shard_map/ppermute | solution.py:745
  49.2 7.5 %collective-permute-start.15 = (bf16[2,144,256]{2,1,0:T(8,128)(2,1)}, bf16[2,144,256]{2,1,0:T(8,128)(2,1)S(1)}, u32[]{:S(2)}, u32[]{:S(2)}) collective-permute-start(bf16[2,144,256]{2,1,0:T(8,128)(2,1)} %get-tuple-element.64), channel_id=1, source_target_pairs={{0,1},{2,3},{4,5},{6,7},{8,9},{10,11},{12,13},{14,15},{16,17},{18,... | collective-permute-start | bytes 442376 | tf_op jit(solution)/shard_map/ppermute | solution.py:765
  90.2 19.2 %collective-permute-start.18 = (bf16[6,32,4736]{2,1,0:T(8,128)(2,1)}, bf16[6,32,4736]{2,1,0:T(8,128)(2,1)S(1)}, u32[]{:S(2)}, u32[]{:S(2)}) collective-permute-start(bf16[6,32,4736]{2,1,0:T(8,128)(2,1)} %get-tuple-element.84), channel_id=1, source_target_pairs={{0,2},{2,0},{4,6},{6,4},{8,10},{10,8},{12,14},{14,12},{16,18},{18,... | collective-permute-start | bytes 5455880 | tf_op jit(solution)/shard_map/ppermute | solution.py:745
  93.4 16.0 %collective-permute-start.19 = (bf16[2,32,4736]{2,1,0:T(8,128)(2,1)S(1)}, bf16[2,32,4736]{2,1,0:T(8,128)(2,1)}, u32[]{:S(2)}, u32[]{:S(2)}) collective-permute-start(bf16[2,32,4736]{2,1,0:T(8,128)(2,1)S(1)} %add_convert_fusion.1), channel_id=1, source_target_pairs={{0,4},{2,6},{4,0},{6,2},{8,12},{10,14},{12,8},{14,10},{16,20},{18,... | collective-permute-start | bytes 1818632 | tf_op jit(solution)/shard_map/ppermute | solution.py:745
  104.4 10.8 %collective-permute-start.17 = (bf16[2,144,256]{2,1,0:T(8,128)(2,1)}, bf16[2,144,256]{2,1,0:T(8,128)(2,1)S(1)}, u32[]{:S(2)}, u32[]{:S(2)}) collective-permute-start(bf16[2,144,256]{2,1,0:T(8,128)(2,1)} %get-tuple-element.80), channel_id=1, source_target_pairs={{1,0},{3,2},{5,4},{7,6},{9,8},{11,10},{13,12},{15,14},{17,16},{19,... | collective-permute-start | bytes 442376 | tf_op jit(solution)/shard_map/ppermute | solution.py:765
  111.6 24.9 %collective-permute-start.22 = (bf16[32,4736]{1,0:T(8,128)(2,1)}, bf16[32,4736]{1,0:T(8,128)(2,1)}, u32[]{:S(2)}, u32[]{:S(2)}) collective-permute-start(bf16[32,4736]{1,0:T(8,128)(2,1)} %get-tuple-element.113), channel_id=1, source_target_pairs={{0,24},{2,26},{4,28},{6,30},{8,16},{10,18},{12,20},{14,22},{16,8},... | collective-permute-start | bytes 909320 | tf_op jit(solution)/shard_map/ppermute | solution.py:745
  115.1 34.7 %collective-permute-start.26 = (bf16[32,4736]{1,0:T(8,128)(2,1)}, bf16[32,4736]{1,0:T(8,128)(2,1)}, u32[]{:S(2)}, u32[]{:S(2)}) collective-permute-start(bf16[32,4736]{1,0:T(8,128)(2,1)} %get-tuple-element.114), channel_id=1, source_target_pairs={{0,16},{2,18},{4,20},{6,22},{8,24},{10,26},{12,28},{14,30},{16,0},... | collective-permute-start | bytes 909320 | tf_op jit(solution)/shard_map/ppermute | solution.py:745
  116.1 17.8 %collective-permute-start.21 = (bf16[2,32,4736]{2,1,0:T(8,128)(2,1)}, bf16[2,32,4736]{2,1,0:T(8,128)(2,1)}, u32[]{:S(2)}, u32[]{:S(2)}) collective-permute-start(bf16[2,32,4736]{2,1,0:T(8,128)(2,1)} %add_convert_fusion), channel_id=1, source_target_pairs={{0,4},{2,6},{4,0},{6,2},{8,12},{10,14},{12,8},{14,10},{16,20},{18,... | collective-permute-start | bytes 1818632 | tf_op jit(solution)/shard_map/ppermute | solution.py:745
  135.9 13.9 %collective-permute-start.27 = (bf16[32,4736]{1,0:T(8,128)(2,1)}, bf16[32,4736]{1,0:T(8,128)(2,1)S(1)}, u32[]{:S(2)}, u32[]{:S(2)}) collective-permute-start(bf16[32,4736]{1,0:T(8,128)(2,1)} %get-tuple-element.111), channel_id=1, source_target_pairs={{0,8},{2,10},{4,12},{6,14},{8,0},{10,2},{12,4},{14,6},{16,24},{18,... | collective-permute-start | bytes 909320 | tf_op jit(solution)/shard_map/ppermute | solution.py:745
  136.6 9.3 %collective-permute-start.24 = (bf16[2,32,2048]{2,1,0:T(8,128)(2,1)S(1)}, bf16[2,32,2048]{2,1,0:T(8,128)(2,1)S(1)}, u32[]{:S(2)}, u32[]{:S(2)}) collective-permute-start(bf16[2,32,2048]{2,1,0:T(8,128)(2,1)S(1)} %add_convert_fusion.8), channel_id=1, source_target_pairs={{0,4},{2,6},{4,0},{6,2},{8,12},{10,14},{12,8},{14,10},{16,20},{18,... | collective-permute-start | bytes 786440 | tf_op jit(solution)/shard_map/ppermute | solution.py:745
  137.4 16.1 %collective-permute-start.25 = (bf16[2,32,2048]{2,1,0:T(8,128)(2,1)S(1)}, bf16[2,32,2048]{2,1,0:T(8,128)(2,1)S(1)}, u32[]{:S(2)}, u32[]{:S(2)}) collective-permute-start(bf16[2,32,2048]{2,1,0:T(8,128)(2,1)S(1)} %add_convert_fusion.9), channel_id=1, source_target_pairs={{0,4},{2,6},{4,0},{6,2},{8,12},{10,14},{12,8},{14,10},{16,20},{18,... | collective-permute-start | bytes 786440 | tf_op jit(solution)/shard_map/ppermute | solution.py:745
  145.9 15.9 %collective-permute-start.29 = (bf16[32,2048]{1,0:T(8,128)(2,1)S(1)}, bf16[32,2048]{1,0:T(8,128)(2,1)S(1)}, u32[]{:S(2)}, u32[]{:S(2)}) collective-permute-start(bf16[32,2048]{1,0:T(8,128)(2,1)S(1)} %get-tuple-element.117), channel_id=1, source_target_pairs={{0,24},{2,26},{4,28},{6,30},{8,16},{10,18},{12,20},{14,22},{16,8},... | collective-permute-start | bytes 393224 | tf_op jit(solution)/shard_map/ppermute | solution.py:745
  149.8 12.1 %collective-permute-start.28 = (bf16[32,2048]{1,0:T(8,128)(2,1)S(1)}, bf16[32,2048]{1,0:T(8,128)(2,1)S(1)}, u32[]{:S(2)}, u32[]{:S(2)}) collective-permute-start(bf16[32,2048]{1,0:T(8,128)(2,1)S(1)} %get-tuple-element.118), channel_id=1, source_target_pairs={{0,16},{2,18},{4,20},{6,22},{8,24},{10,26},{12,28},{14,30},{16,0},... | collective-permute-start | bytes 393224 | tf_op jit(solution)/shard_map/ppermute | solution.py:745
  151.1 11.0 %collective-permute-start.32 = (bf16[32,4736]{1,0:T(8,128)(2,1)S(1)}, bf16[32,4736]{1,0:T(8,128)(2,1)S(1)}, u32[]{:S(2)}, u32[]{:S(2)}) collective-permute-start(bf16[32,4736]{1,0:T(8,128)(2,1)S(1)} %add_convert_fusion.3), channel_id=1, source_target_pairs={{0,1},{1,0},{2,3},{3,2},{4,5},{5,4},{6,7},{7,6},{8,9},{9,8},{10,11... | collective-permute-start | bytes 909320 | tf_op jit(solution)/shard_map/ppermute | solution.py:817
  153.6 8.3 %collective-permute-start.30 = (bf16[32,2048]{1,0:T(8,128)(2,1)S(1)}, bf16[32,2048]{1,0:T(8,128)(2,1)S(1)}, u32[]{:S(2)}, u32[]{:S(2)}) collective-permute-start(bf16[32,2048]{1,0:T(8,128)(2,1)S(1)} %get-tuple-element.115), channel_id=1, source_target_pairs={{0,8},{2,10},{4,12},{6,14},{8,0},{10,2},{12,4},{14,6},{16,24},{18,... | collective-permute-start | bytes 393224 | tf_op jit(solution)/shard_map/ppermute | solution.py:745
  (34 other events, 180.5 us)
Sparse Core Ops, SparseCore 0:
  10.3 58.2 all-gather.1

commit v7 on v6

--- a/solution.py
+++ b/solution.py
@@ -530,7 +530,7 @@
     out_ref[...] = (kept_ref[...] + mm(hid_ref[...], down_ref[...])).astype(BF16)
 
 
-def ffn_out(hid, kept, down, rows=256):
+def ffn_out(hid, kept, down, rows=512):
     t, ff = hid.shape
     d = kept.shape[1]
     row = lambda w: pl.BlockSpec((rows, w), lambda i: (i, 0))
@@ -718,14 +718,20 @@
 
 
 def input_grad_kernel(gain_ref, tok_ref, gq_ref, gkvc_ref, w_ref, gres_ref, out_ref):
-    d = tok_ref.shape[1]
+    rows, d = tok_ref.shape
     gain = gain_ref[0:1, :]
-    gin = mm_t(gq_ref[...], w_ref[:, 0:d]) + mm_t(gkvc_ref[...], w_ref[:, d:])
-    normed, factor = normalize(tok_ref[...].astype(F32))
-    out_ref[...] = gres_ref[...] + norm_back(gin * gain, normed, factor)
-
-
-def input_grad(gain, tokens, gq, gkvc, w, gres, rows=256):
+    part = 256
+    cuts = [slice(i, i + part) for i in range(0, rows, part)]
+    product = lambda s: mm_t(gq_ref[s, :], w_ref[:, 0:d]) + mm_t(gkvc_ref[s, :], w_ref[:, d:])
+    gin = product(cuts[0])
+    for i, s in enumerate(cuts):
+        coming = product(cuts[i + 1]) if i + 1 < len(cuts) else None
+        normed, factor = normalize(tok_ref[s, :].astype(F32))
+        out_ref[s, :] = gres_ref[s, :] + norm_back(gin * gain, normed, factor)
+        gin = coming
+
+
+def input_grad(gain, tokens, gq, gkvc, w, gres, rows=512):
     t, d = tokens.shape
     const = lambda *shape: pl.BlockSpec(shape, lambda i: (0,) * len(shape))
     row = lambda w: pl.BlockSpec((rows, w), lambda i: (i, 0))

time: 176 us -> 175 us (level)
  transfers between devices with their start and end apart: 34 -> 34, of which waited for: 11 -> 11; matrix products, arithmetic and copies ran while one was open for 6% -> 6% of each run, Pallas kernels for 33% -> 32%
where the time goes in v7:
time: 175 us
  Pallas kernels  79.6 us (45%)
  starting transfers between devices  34.7 us (20%)
  waiting for transfers between devices  32 us (18%)
  between operations  14.4 us (8%)
  other arithmetic  9.39 us (5%)
  local copies, waits for them, and re-layouts  4.39 us (3%)
    ppermute x29, starting transfers between devices, swap(): return lax.ppermute(x, 'fsdp', [(i, i ^ mask) for i in range(n)])  26.8 us
    ppermute x29, waiting for transfers between devices, swap(): return lax.ppermute(x, 'fsdp', [(i, i ^ mask) for i in range(n)])  25.7 us
    pallas_call x1, Pallas kernels, ffn(): pl.pallas_call(partial(ffn_kernel, n), in_specs=[pl.BlockSpec(memory_spac...  21.3 us
    pallas_call x1, Pallas kernels, write_back(): pl.pallas_call(partial(write_back_kernel, n), grid=(t // rows,), in_specs...  15.6 us
    pallas_call x1, Pallas kernels, mix(): pl.pallas_call(mix_kernel, grid=(t // rows,), in_specs=[row(wide), const(...  10.3 us
    pallas_call x1, Pallas kernels, read_back(): pl.pallas_call(read_back_kernel, grid=(t // rows,), in_specs=[row(wide),...  10.3 us
    convert_element_type x10, other arithmetic, add(): return sum((x.astype(F32) for x in items)).astype(BF16)  7.91 us
    pallas_call x1, Pallas kernels, project(): pl.pallas_call(partial(project_kernel, where, len(pieces), r), in_specs=[...  7.58 us
  transfers between devices with their start and end apart: 34, of which 11 were waited for; matrix products, arithmetic and copies ran while one was open for 6% of the time, Pallas kernels for 32%

profile of v7, /device:TPU:0, one launch (start us, length us, event | category | flops | bytes accessed | tf_op | source)
XLA Modules:
  0.0 174.6 jit_solution(1327831061766639627)
XLA Ops:
  7.2 1.9 %pack.1 = (bf16[32,2176]{1,0:T(8,128)(2,1)}, bf16[32,4736]{1,0:T(8,128)(2,1)}) custom-call(bf16[32,512]{1,0:T(8,128)(2,1)} %q.1, bf16[32,512]{1,0:T(8,128)(2,1)} %k.1, bf16[32,512]{1,0:T(8,128)(2,1)} %v.1, bf16[32,512]{1,0:T(8,128)(2,1)} %c.1, bf16[32,512]{1,0:T(8,128)(2,1)} %o.1, bf16[32,2048]{1,0:T(8,128)(2,1)} %up.1, bf16[128,512]{1,0:T(8,128)(2,1)} %down.1, ...), custom_call_target="tpu_custom_call" | custom-call | bytes 1048576 | tf_op jit(solution)/shard_map/pack/pallas_call | solution.py:174
  9.1 5.1 %collective-permute-start.11 = (bf16[32,2176]{1,0:T(8,128)(2,1)}, bf16[32,2176]{1,0:T(8,128)(2,1)S(1)}, u32[]{:S(2)}, u32[]{:S(2)}) collective-permute-start(bf16[32,2176]{1,0:T(8,128)(2,1)} %get-tuple-element.62.refs_0_), channel_id=1, source_target_pairs={{0,24},{2,26},{4,28},{6,30},{8,16},{10,18},{12,20},{14,22},{16,8},... | collective-permute-start | bytes 417800 | tf_op jit(solution)/shard_map/ppermute | solution.py:751
  16.5 2.5 %collective-permute-done.11.refs_12_ = bf16[32,2176]{1,0:T(8,128)(2,1)S(1)} collective-permute-done((bf16[32,2176]{1,0:T(8,128)(2,1)}, bf16[32,2176]{1,0:T(8,128)(2,1)S(1)}, u32[]{:S(2)}, u32[]{:S(2)}) %collective-permute-start.11) | collective-permute-done | bytes 139296 | tf_op jit(solution)/shard_map/ppermute | solution.py:751
  19.1 1.7 collective-permute-start.13
  20.8 9.7 %collective-permute-done.7.refs_8_ = bf16[32,2176]{1,0:T(8,128)(2,1)S(1)} collective-permute-done((bf16[32,2176]{1,0:T(8,128)(2,1)}, bf16[32,2176]{1,0:T(8,128)(2,1)S(1)}, u32[]{:S(2)}, u32[]{:S(2)}) %collective-permute-start.7) | collective-permute-done | bytes 139296 | tf_op jit(solution)/shard_map/ppermute | solution.py:751
  30.5 1.8 %collective-permute-start.9 = (bf16[32,2176]{1,0:T(8,128)(2,1)S(1)}, bf16[32,2176]{1,0:T(8,128)(2,1)S(1)}, u32[]{:S(2)}, u32[]{:S(2)}) collective-permute-start(bf16[32,2176]{1,0:T(8,128)(2,1)S(1)} %collective-permute-done.7.refs_8_), channel_id=1, source_target_pairs={{0,4},{2,6},{4,0},{6,2},{8,12},{10,14},{12,8},{14,10},{16,20},{18,... | collective-permute-start | bytes 417800 | tf_op jit(solution)/shard_map/ppermute | solution.py:751
  33.4 3.6 %collective-permute-done.9.refs_10_ = bf16[32,2176]{1,0:T(8,128)(2,1)S(1)} collective-permute-done((bf16[32,2176]{1,0:T(8,128)(2,1)S(1)}, bf16[32,2176]{1,0:T(8,128)(2,1)S(1)}, u32[]{:S(2)}, u32[]{:S(2)}) %collective-permute-start.9) | collective-permute-done | bytes 139296 | tf_op jit(solution)/shard_map/ppermute | solution.py:751
  37.6 2.0 %collective-permute-done.5.refs_6_ = bf16[32,2176]{1,0:T(8,128)(2,1)S(1)} collective-permute-done((bf16[32,2176]{1,0:T(8,128)(2,1)S(1)}, bf16[32,2176]{1,0:T(8,128)(2,1)S(1)}, u32[]{:S(2)}, u32[]{:S(2)}) %collective-permute-start.5) | collective-permute-done | bytes 139296 | tf_op jit(solution)/shard_map/ppermute | solution.py:751
  41.6 7.6 %project.1 = (bf16[1024,512]{1,0:T(8,128)(2,1)}, bf16[1024,2048]{1,0:T(8,128)(2,1)}, bf16[2,144,256]{2,1,0:T(8,128)(2,1)}, bf16[512,2048]{1,0:T(8,128)(2,1)}, f32[8,512]{1,0:T(8,128)}) custom-call(s32[1]{0:T(128)} %bitcast.me_ref, bf16[1024,512]{1,0:T(8,128)(2,1)} %tok_ref.1, bf16[32,2176]{1,0:T(8,128)(2,1)} %get-tuple-element.62.refs_0_, ...), custom_call_target="tpu_custom_call" | custom-call | flops 2147483648 | bytes 12582912 | tf_op jit(solution)/shard_map/project/pallas_call | solution.py:264
  49.2 3.8 %collective-permute-start.15 = (bf16[2,144,256]{2,1,0:T(8,128)(2,1)}, bf16[2,144,256]{2,1,0:T(8,128)(2,1)S(1)}, u32[]{:S(2)}, u32[]{:S(2)}) collective-permute-start(bf16[2,144,256]{2,1,0:T(8,128)(2,1)} %get-tuple-element.64), channel_id=1, source_target_pairs={{0,1},{2,3},{4,5},{6,7},{8,9},{10,11},{12,13},{14,15},{16,17},{18,... | collective-permute-start | bytes 442376 | tf_op jit(solution)/shard_map/ppermute | solution.py:771
  53.0 3.7 %collective-permute-done.15.st_in = bf16[2,144,256]{2,1,0:T(8,128)(2,1)S(1)} collective-permute-done((bf16[2,144,256]{2,1,0:T(8,128)(2,1)}, bf16[2,144,256]{2,1,0:T(8,128)(2,1)S(1)}, u32[]{:S(2)}, u32[]{:S(2)}) %collective-permute-start.15) | collective-permute-done | bytes 147488 | tf_op jit(solution)/shard_map/ppermute | solution.py:771
  57.4 10.3 %mix.1 = (bf16[1024,512]{1,0:T(8,128)(2,1)}, f32[1024,512]{1,0:T(8,128)}, f32[1024,512]{1,0:T(8,128)}, f32[1024,512]{1,0:T(8,128)}, bf16[8,2,256,256]{3,2,1,0:T(8,128)(2,1)}, /*index=5*/bf16[8,2,256,256]{3,2,1,0:T(8,128)(2,1)}) custom-call(bf16[1024,2048]{1,0:T(8,128)(2,1)} %get-tuple-element.63.pack_ref, bf16[2,144,256]{2,1,0:T(8,128)(2,1)} %copy-done.8), custom_call_target="tpu_custom_call" | custom-call | flops 6000000000 | bytes 16777216 | tf_op jit(solution)/shard_map/mix/pallas_call | solution.py:347
  68.6 21.3 %ffn.1 = (f32[1024,512]{1,0:T(8,128)}, f32[1024,512]{1,0:T(8,128)}, bf16[1024,512]{1,0:T(8,128)(2,1)}, bf16[1024,2048]{1,0:T(8,128)(2,1)}, bf16[2048,512]{1,0:T(...) custom-call(s32[1]{0:T(128)} %bitcast.me_ref, ...), custom_call_target="tpu_custom_call" | custom-call | flops 11811160064 | bytes 20971520 | tf_op jit(solution)/shard_map/ffn/pallas_call | solution.py:495
  90.5 1.7 collective-permute-done.16
  94.1 10.3 %read_back.1 = (bf16[1024,512]{1,0:T(8,128)(2,1)}, bf16[1024,512]{1,0:T(8,128)(2,1)}, bf16[1024,512]{1,0:T(8,128)(2,1)}, f32[1024,512]{1,0:T(8,128)}, bf16[2,144,256]{2,1,0:T(8,128)(2,1)}) custom-call(bf16[1024,2048]{1,0:T(8,128)(2,1)} %get-tuple-element.63.pack_ref, bf16[1024,512]{1,0:T(8,128)(2,1)} %get-tuple-element.71.gmix_ref, ...), custom_call_target="tpu_custom_call" | custom-call | flops 6000000000 | bytes 20971520 | tf_op jit(solution)/shard_map/read_back/pallas_call | solution.py:602
  105.8 3.6 %collective-permute-done.19 = bf16[2,32,4736]{2,1,0:T(8,128)(2,1)} collective-permute-done((bf16[2,32,4736]{2,1,0:T(8,128)(2,1)S(1)}, bf16[2,32,4736]{2,1,0:T(8,128)(2,1)}, u32[]{:S(2)}, u32[]{:S(2)}) %collective-permute-start.19) | collective-permute-done | bytes 606240 | tf_op jit(solution)/shard_map/ppermute | solution.py:751
  109.4 2.1 %fusion.1 = (bf16[32,4736]{1,0:T(8,128)(2,1)}, bf16[32,4736]{1,0:T(8,128)(2,1)}) fusion(bf16[2,32,4736]{2,1,0:T(8,128)(2,1)} %collective-permute-done.19, bf16[6,32,4736]{2,1,0:T(8,128)(2,1)S(1)} %collective-permute-done.18, bf16[4,32,4736]{2,1,0:T(8,128)(2,1)S(1)} %copy-done), kind=kLoop, calls=%fused_computation.11 | loop fusion | flops 1818624 | bytes 2424832 | tf_op jit(solution)/shard_map/convert_element_type | solution.py:759
  111.6 3.6 %collective-permute-start.22 = (bf16[32,4736]{1,0:T(8,128)(2,1)}, bf16[32,4736]{1,0:T(8,128)(2,1)}, u32[]{:S(2)}, u32[]{:S(2)}) collective-permute-start(bf16[32,4736]{1,0:T(8,128)(2,1)} %get-tuple-element.113), channel_id=1, source_target_pairs={{0,24},{2,26},{4,28},{6,30},{8,16},{10,18},{12,20},{14,22},{16,8},... | collective-permute-start | bytes 909320 | tf_op jit(solution)/shard_map/ppermute | solution.py:751
  117.7 15.6 %write_back.1 = (bf16[1024,1536]{1,0:T(8,128)(2,1)}, bf16[4,32,2048]{2,1,0:T(8,128)(2,1)}, bf16[2,32,2048]{2,1,0:T(8,128)(2,1)}, bf16[2,32,2048]{2,1,0:T(8,128)(...) custom-call(s32[1]{0:T(128)} %bitcast.me_ref, bf16[1024,2048]{1,0:T(8,128)(2,1)} %get-tuple-element.63.pack_ref, ...), custom_call_target="tpu_custom_call" | custom-call | flops 11000000512 | bytes 18874368 | tf_op jit(solution)/shard_map/write_back/pallas_call | solution.py:697
  133.9 2.0 %fusion.3 = (bf16[32,4736]{1,0:T(8,128)(2,1)}, bf16[32,4736]{1,0:T(8,128)(2,1)S(1)}) fusion(bf16[2,32,4736]{2,1,0:T(8,128)(2,1)} %collective-permute-done.21, bf16[6,32,4736]{2,1,0:T(8,128)(2,1)S(1)} %collective-permute-done.18, bf16[4,32,4736]{2,1,0:T(8,128)(2,1)S(1)} %copy-done), kind=kLoop, calls=%fused_computation.13 | loop fusion | flops 1818624 | bytes 2424832 | tf_op jit(solution)/shard_map/convert_element_type | solution.py:759
  138.8 5.9 %ffn_out.1 = bf16[1024,512]{1,0:T(8,128)(2,1)} custom-call(bf16[1024,2048]{1,0:T(8,128)(2,1)} %get-tuple-element.93.hid_ref, f32[1024,512]{1,0:T(8,128)} %get-tuple-element.94.kept_ref, bf16[2048,512]{1,0:T(8,128)(2,1)} %get-tuple-element.95.down_ref), custom_call_target="tpu_custom_call" | custom-call | flops 2147483648 | bytes 9437184 | tf_op jit(solution)/shard_map/ffn_out/pallas_call | solution.py:537
  145.9 3.9 %collective-permute-start.29 = (bf16[32,2048]{1,0:T(8,128)(2,1)S(1)}, bf16[32,2048]{1,0:T(8,128)(2,1)S(1)}, u32[]{:S(2)}, u32[]{:S(2)}) collective-permute-start(bf16[32,2048]{1,0:T(8,128)(2,1)S(1)} %get-tuple-element.117), channel_id=1, source_target_pairs={{0,24},{2,26},{4,28},{6,30},{8,16},{10,18},{12,20},{14,22},{16,8},... | collective-permute-start | bytes 393224 | tf_op jit(solution)/shard_map/ppermute | solution.py:751
  151.1 2.5 %collective-permute-start.32 = (bf16[32,4736]{1,0:T(8,128)(2,1)S(1)}, bf16[32,4736]{1,0:T(8,128)(2,1)S(1)}, u32[]{:S(2)}, u32[]{:S(2)}) collective-permute-start(bf16[32,4736]{1,0:T(8,128)(2,1)S(1)} %add_convert_fusion.3), channel_id=1, source_target_pairs={{0,1},{1,0},{2,3},{3,2},{4,5},{5,4},{6,7},{7,6},{8,9},{9,8},{10,11... | collective-permute-start | bytes 909320 | tf_op jit(solution)/shard_map/ppermute | solution.py:823
  154.3 6.9 %input_grad.1 = f32[1024,512]{1,0:T(8,128)} custom-call(f32[8,512]{1,0:T(8,128)} %get-tuple-element.96.gain_ref, bf16[1024,512]{1,0:T(8,128)(2,1)} %tok_ref.1, bf16[1024,512]{1,0:T(8,128)(2,1)} %get-tuple-element.104.gq_hbm.gq_ref, bf16[1024,1536]{1,0:T(8,128)(2,1)} %get-tuple-element.89.gkvc_ref, bf16[512,2048]{1,0:T(8,128)(2,1)} %get-tuple-element.105.w_ref, ...), custom_call_target="tpu_custom_call" | custom-call | flops 2147483648 | bytes 12582912 | tf_op jit(solution)/shard_map/input_grad/pallas_call | solution.py:738
  (120 shorter events, 27.1 us)
Async XLA Ops:
  7.2 61.5 %all-gather.2.cloned.1.call-start = ((), (), s32[]{:S(2)}) async-start(), calls=%async_computation | async-start | bytes 5152768 | tf_op jit(solution)/shard_map/all_gather | solution.py:796
  9.1 9.9 %collective-permute-start.11 = (bf16[32,2176]{1,0:T(8,128)(2,1)}, bf16[32,2176]{1,0:T(8,128)(2,1)S(1)}, u32[]{:S(2)}, u32[]{:S(2)}) collective-permute-start(bf16[32,2176]{1,0:T(8,128)(2,1)} %get-tuple-element.62.refs_0_), channel_id=1, source_target_pairs={{0,24},{2,26},{4,28},{6,30},{8,16},{10,18},{12,20},{14,22},{16,8},... | collective-permute-start | bytes 417800 | tf_op jit(solution)/shard_map/ppermute | solution.py:751
  14.2 16.2 %collective-permute-start.7 = (bf16[32,2176]{1,0:T(8,128)(2,1)}, bf16[32,2176]{1,0:T(8,128)(2,1)S(1)}, u32[]{:S(2)}, u32[]{:S(2)}) collective-permute-start(bf16[32,2176]{1,0:T(8,128)(2,1)} %get-tuple-element.62.refs_0_), channel_id=1, source_target_pairs={{0,16},{2,18},{4,20},{6,22},{8,24},{10,26},{12,28},{14,30},{16,0},... | collective-permute-start | bytes 417800 | tf_op jit(solution)/shard_map/ppermute | solution.py:751
  14.3 16.2 %collective-permute-start.3 = (bf16[32,2176]{1,0:T(8,128)(2,1)}, bf16[32,2176]{1,0:T(8,128)(2,1)S(1)}, u32[]{:S(2)}, u32[]{:S(2)}) collective-permute-start(bf16[32,2176]{1,0:T(8,128)(2,1)} %get-tuple-element.62.refs_0_), channel_id=1, source_target_pairs={{0,8},{2,10},{4,12},{6,14},{8,0},{10,2},{12,4},{14,6},{16,24},{18,... | collective-permute-start | bytes 417800 | tf_op jit(solution)/shard_map/ppermute | solution.py:751
  14.9 17.5 %collective-permute-start.1 = (bf16[32,2176]{1,0:T(8,128)(2,1)}, bf16[32,2176]{1,0:T(8,128)(2,1)S(1)}, u32[]{:S(2)}, u32[]{:S(2)}) collective-permute-start(bf16[32,2176]{1,0:T(8,128)(2,1)} %get-tuple-element.62.refs_0_), channel_id=1, source_target_pairs={{0,4},{2,6},{4,0},{6,2},{8,12},{10,14},{12,8},{14,10},{16,20},{18,... | collective-permute-start | bytes 417800 | tf_op jit(solution)/shard_map/ppermute | solution.py:751
  16.5 16.0 %collective-permute-start = (bf16[32,2176]{1,0:T(8,128)(2,1)}, bf16[32,2176]{1,0:T(8,128)(2,1)S(1)}, u32[]{:S(2)}, u32[]{:S(2)}) collective-permute-start(bf16[32,2176]{1,0:T(8,128)(2,1)} %get-tuple-element.62.refs_0_), channel_id=1, source_target_pairs={{0,2},{2,0},{4,6},{6,4},{8,10},{10,8},{12,14},{14,12},{16,18},{18,... | collective-permute-start | bytes 417800 | tf_op jit(solution)/shard_map/ppermute | solution.py:751
  19.1 13.8 %collective-permute-start.13 = (bf16[32,2176]{1,0:T(8,128)(2,1)S(1)}, bf16[32,2176]{1,0:T(8,128)(2,1)S(1)}, u32[]{:S(2)}, u32[]{:S(2)}) collective-permute-start(bf16[32,2176]{1,0:T(8,128)(2,1)S(1)} %collective-permute-done.11.refs_12_), channel_id=1, source_target_pairs={{0,4},{2,6},{4,0},{6,2},{8,12},{10,14},{12,8},{14,10},{16,20},{18,... | collective-permute-start | bytes 417800 | tf_op jit(solution)/shard_map/ppermute | solution.py:751
  32.5 7.1 %collective-permute-start.5 = (bf16[32,2176]{1,0:T(8,128)(2,1)S(1)}, bf16[32,2176]{1,0:T(8,128)(2,1)S(1)}, u32[]{:S(2)}, u32[]{:S(2)}) collective-permute-start(bf16[32,2176]{1,0:T(8,128)(2,1)S(1)} %collective-permute-done.3.refs_4_), channel_id=1, source_target_pairs={{0,4},{2,6},{4,0},{6,2},{8,12},{10,14},{12,8},{14,10},{16,20},{18,... | collective-permute-start | bytes 417800 | tf_op jit(solution)/shard_map/ppermute | solution.py:751
  32.9 6.7 %collective-permute-start.4 = (bf16[32,2176]{1,0:T(8,128)(2,1)S(1)}, bf16[32,2176]{1,0:T(8,128)(2,1)S(1)}, u32[]{:S(2)}, u32[]{:S(2)}) collective-permute-start(bf16[32,2176]{1,0:T(8,128)(2,1)S(1)} %collective-permute-done.3.refs_4_), channel_id=1, source_target_pairs={{0,2},{2,0},{4,6},{6,4},{8,10},{10,8},{12,14},{14,12},{16,18},{18,... | collective-permute-start | bytes 417800 | tf_op jit(solution)/shard_map/ppermute | solution.py:751
  33.0 6.7 %collective-permute-start.2 = (bf16[32,2176]{1,0:T(8,128)(2,1)S(1)}, bf16[32,2176]{1,0:T(8,128)(2,1)S(1)}, u32[]{:S(2)}, u32[]{:S(2)}) collective-permute-start(bf16[32,2176]{1,0:T(8,128)(2,1)S(1)} %collective-permute-done.1.refs_2_), channel_id=1, source_target_pairs={{0,2},{2,0},{4,6},{6,4},{8,10},{10,8},{12,14},{14,12},{16,18},{18,... | collective-permute-start | bytes 417800 | tf_op jit(solution)/shard_map/ppermute | solution.py:751
  49.2 7.5 %collective-permute-start.15 = (bf16[2,144,256]{2,1,0:T(8,128)(2,1)}, bf16[2,144,256]{2,1,0:T(8,128)(2,1)S(1)}, u32[]{:S(2)}, u32[]{:S(2)}) collective-permute-start(bf16[2,144,256]{2,1,0:T(8,128)(2,1)} %get-tuple-element.64), channel_id=1, source_target_pairs={{0,1},{2,3},{4,5},{6,7},{8,9},{10,11},{12,13},{14,15},{16,17},{18,... | collective-permute-start | bytes 442376 | tf_op jit(solution)/shard_map/ppermute | solution.py:771
  90.2 19.2 %collective-permute-start.18 = (bf16[6,32,4736]{2,1,0:T(8,128)(2,1)}, bf16[6,32,4736]{2,1,0:T(8,128)(2,1)S(1)}, u32[]{:S(2)}, u32[]{:S(2)}) collective-permute-start(bf16[6,32,4736]{2,1,0:T(8,128)(2,1)} %get-tuple-element.84), channel_id=1, source_target_pairs={{0,2},{2,0},{4,6},{6,4},{8,10},{10,8},{12,14},{14,12},{16,18},{18,... | collective-permute-start | bytes 5455880 | tf_op jit(solution)/shard_map/ppermute | solution.py:751
  93.4 16.0 %collective-permute-start.19 = (bf16[2,32,4736]{2,1,0:T(8,128)(2,1)S(1)}, bf16[2,32,4736]{2,1,0:T(8,128)(2,1)}, u32[]{:S(2)}, u32[]{:S(2)}) collective-permute-start(bf16[2,32,4736]{2,1,0:T(8,128)(2,1)S(1)} %add_convert_fusion.1), channel_id=1, source_target_pairs={{0,4},{2,6},{4,0},{6,2},{8,12},{10,14},{12,8},{14,10},{16,20},{18,... | collective-permute-start | bytes 1818632 | tf_op jit(solution)/shard_map/ppermute | solution.py:751
  104.4 10.8 %collective-permute-start.17 = (bf16[2,144,256]{2,1,0:T(8,128)(2,1)}, bf16[2,144,256]{2,1,0:T(8,128)(2,1)S(1)}, u32[]{:S(2)}, u32[]{:S(2)}) collective-permute-start(bf16[2,144,256]{2,1,0:T(8,128)(2,1)} %get-tuple-element.80), channel_id=1, source_target_pairs={{1,0},{3,2},{5,4},{7,6},{9,8},{11,10},{13,12},{15,14},{17,16},{19,... | collective-permute-start | bytes 442376 | tf_op jit(solution)/shard_map/ppermute | solution.py:771
  111.6 24.9 %collective-permute-start.22 = (bf16[32,4736]{1,0:T(8,128)(2,1)}, bf16[32,4736]{1,0:T(8,128)(2,1)}, u32[]{:S(2)}, u32[]{:S(2)}) collective-permute-start(bf16[32,4736]{1,0:T(8,128)(2,1)} %get-tuple-element.113), channel_id=1, source_target_pairs={{0,24},{2,26},{4,28},{6,30},{8,16},{10,18},{12,20},{14,22},{16,8},... | collective-permute-start | bytes 909320 | tf_op jit(solution)/shard_map/ppermute | solution.py:751
  115.1 34.7 %collective-permute-start.26 = (bf16[32,4736]{1,0:T(8,128)(2,1)}, bf16[32,4736]{1,0:T(8,128)(2,1)}, u32[]{:S(2)}, u32[]{:S(2)}) collective-permute-start(bf16[32,4736]{1,0:T(8,128)(2,1)} %get-tuple-element.114), channel_id=1, source_target_pairs={{0,16},{2,18},{4,20},{6,22},{8,24},{10,26},{12,28},{14,30},{16,0},... | collective-permute-start | bytes 909320 | tf_op jit(solution)/shard_map/ppermute | solution.py:751
  116.1 17.8 %collective-permute-start.21 = (bf16[2,32,4736]{2,1,0:T(8,128)(2,1)}, bf16[2,32,4736]{2,1,0:T(8,128)(2,1)}, u32[]{:S(2)}, u32[]{:S(2)}) collective-permute-start(bf16[2,32,4736]{2,1,0:T(8,128)(2,1)} %add_convert_fusion), channel_id=1, source_target_pairs={{0,4},{2,6},{4,0},{6,2},{8,12},{10,14},{12,8},{14,10},{16,20},{18,... | collective-permute-start | bytes 1818632 | tf_op jit(solution)/shard_map/ppermute | solution.py:751
  135.9 13.9 %collective-permute-start.27 = (bf16[32,4736]{1,0:T(8,128)(2,1)}, bf16[32,4736]{1,0:T(8,128)(2,1)S(1)}, u32[]{:S(2)}, u32[]{:S(2)}) collective-permute-start(bf16[32,4736]{1,0:T(8,128)(2,1)} %get-tuple-element.111), channel_id=1, source_target_pairs={{0,8},{2,10},{4,12},{6,14},{8,0},{10,2},{12,4},{14,6},{16,24},{18,... | collective-permute-start | bytes 909320 | tf_op jit(solution)/shard_map/ppermute | solution.py:751
  136.6 9.3 %collective-permute-start.24 = (bf16[2,32,2048]{2,1,0:T(8,128)(2,1)S(1)}, bf16[2,32,2048]{2,1,0:T(8,128)(2,1)S(1)}, u32[]{:S(2)}, u32[]{:S(2)}) collective-permute-start(bf16[2,32,2048]{2,1,0:T(8,128)(2,1)S(1)} %add_convert_fusion.8), channel_id=1, source_target_pairs={{0,4},{2,6},{4,0},{6,2},{8,12},{10,14},{12,8},{14,10},{16,20},{18,... | collective-permute-start | bytes 786440 | tf_op jit(solution)/shard_map/ppermute | solution.py:751
  137.4 16.1 %collective-permute-start.25 = (bf16[2,32,2048]{2,1,0:T(8,128)(2,1)S(1)}, bf16[2,32,2048]{2,1,0:T(8,128)(2,1)S(1)}, u32[]{:S(2)}, u32[]{:S(2)}) collective-permute-start(bf16[2,32,2048]{2,1,0:T(8,128)(2,1)S(1)} %add_convert_fusion.9), channel_id=1, source_target_pairs={{0,4},{2,6},{4,0},{6,2},{8,12},{10,14},{12,8},{14,10},{16,20},{18,... | collective-permute-start | bytes 786440 | tf_op jit(solution)/shard_map/ppermute | solution.py:751
  145.9 15.3 %collective-permute-start.29 = (bf16[32,2048]{1,0:T(8,128)(2,1)S(1)}, bf16[32,2048]{1,0:T(8,128)(2,1)S(1)}, u32[]{:S(2)}, u32[]{:S(2)}) collective-permute-start(bf16[32,2048]{1,0:T(8,128)(2,1)S(1)} %get-tuple-element.117), channel_id=1, source_target_pairs={{0,24},{2,26},{4,28},{6,30},{8,16},{10,18},{12,20},{14,22},{16,8},... | collective-permute-start | bytes 393224 | tf_op jit(solution)/shard_map/ppermute | solution.py:751
  149.8 11.4 %collective-permute-start.28 = (bf16[32,2048]{1,0:T(8,128)(2,1)S(1)}, bf16[32,2048]{1,0:T(8,128)(2,1)S(1)}, u32[]{:S(2)}, u32[]{:S(2)}) collective-permute-start(bf16[32,2048]{1,0:T(8,128)(2,1)S(1)} %get-tuple-element.118), channel_id=1, source_target_pairs={{0,16},{2,18},{4,20},{6,22},{8,24},{10,26},{12,28},{14,30},{16,0},... | collective-permute-start | bytes 393224 | tf_op jit(solution)/shard_map/ppermute | solution.py:751
  151.1 10.5 %collective-permute-start.32 = (bf16[32,4736]{1,0:T(8,128)(2,1)S(1)}, bf16[32,4736]{1,0:T(8,128)(2,1)S(1)}, u32[]{:S(2)}, u32[]{:S(2)}) collective-permute-start(bf16[32,4736]{1,0:T(8,128)(2,1)S(1)} %add_convert_fusion.3), channel_id=1, source_target_pairs={{0,1},{1,0},{2,3},{3,2},{4,5},{5,4},{6,7},{7,6},{8,9},{9,8},{10,11... | collective-permute-start | bytes 909320 | tf_op jit(solution)/shard_map/ppermute | solution.py:823
  153.6 7.6 %collective-permute-start.30 = (bf16[32,2048]{1,0:T(8,128)(2,1)S(1)}, bf16[32,2048]{1,0:T(8,128)(2,1)S(1)}, u32[]{:S(2)}, u32[]{:S(2)}) collective-permute-start(bf16[32,2048]{1,0:T(8,128)(2,1)S(1)} %get-tuple-element.115), channel_id=1, source_target_pairs={{0,8},{2,10},{4,12},{6,14},{8,0},{10,2},{12,4},{14,6},{16,24},{18,... | collective-permute-start | bytes 393224 | tf_op jit(solution)/shard_map/ppermute | solution.py:751
  (34 other events, 180.5 us)
Sparse Core Ops, SparseCore 0:
  10.3 58.2 all-gather.1

commit v8 on v6

--- a/solution.py
+++ b/solution.py
@@ -530,7 +530,7 @@
     out_ref[...] = (kept_ref[...] + mm(hid_ref[...], down_ref[...])).astype(BF16)
 
 
-def ffn_out(hid, kept, down, rows=256):
+def ffn_out(hid, kept, down, rows=512):
     t, ff = hid.shape
     d = kept.shape[1]
     row = lambda w: pl.BlockSpec((rows, w), lambda i: (i, 0))

time: 176 us -> 176 us (level)
  no operation moved by 1% of the time
where the time goes in v8:
time: 176 us; the launch traced here: 175 us
  Pallas kernels  80.3 us (46%)
  starting transfers between devices  34.6 us (20%)
  waiting for transfers between devices  32.2 us (18%)
  between operations  14.4 us (8%)
  other arithmetic  9.39 us (5%)
  local copies, waits for them, and re-layouts  4.39 us (2%)
    ppermute x29, starting transfers between devices, swap(): return lax.ppermute(x, 'fsdp', [(i, i ^ mask) for i in range(n)])  26.8 us
    ppermute x29, waiting for transfers between devices, swap(): return lax.ppermute(x, 'fsdp', [(i, i ^ mask) for i in range(n)])  25.7 us
    pallas_call x1, Pallas kernels, ffn(): pl.pallas_call(partial(ffn_kernel, n), in_specs=[pl.BlockSpec(memory_spac...  21.3 us
    pallas_call x1, Pallas kernels, write_back(): pl.pallas_call(partial(write_back_kernel, n), grid=(t // rows,), in_specs...  15.6 us
    pallas_call x1, Pallas kernels, mix(): pl.pallas_call(mix_kernel, grid=(t // rows,), in_specs=[row(wide), const(...  10.3 us
    pallas_call x1, Pallas kernels, read_back(): pl.pallas_call(read_back_kernel, grid=(t // rows,), in_specs=[row(wide),...  10.3 us
    convert_element_type x10, other arithmetic, add(): return sum((x.astype(F32) for x in items)).astype(BF16)  7.91 us
    pallas_call x1, Pallas kernels, project(): pl.pallas_call(partial(project_kernel, where, len(pieces), r), in_specs=[...  7.58 us
  transfers between devices with their start and end apart: 34, of which 11 were waited for; matrix products, arithmetic and copies ran while one was open for 6% of the time, Pallas kernels for 33%

profile of v8, /device:TPU:0, one launch (start us, length us, event | category | flops | bytes accessed | tf_op | source)
XLA Modules:
  0.0 175.3 jit_solution(16614659076844233316)
XLA Ops:
  7.2 1.9 %pack.1 = (bf16[32,2176]{1,0:T(8,128)(2,1)}, bf16[32,4736]{1,0:T(8,128)(2,1)}) custom-call(bf16[32,512]{1,0:T(8,128)(2,1)} %q.1, bf16[32,512]{1,0:T(8,128)(2,1)} %k.1, bf16[32,512]{1,0:T(8,128)(2,1)} %v.1, bf16[32,512]{1,0:T(8,128)(2,1)} %c.1, bf16[32,512]{1,0:T(8,128)(2,1)} %o.1, bf16[32,2048]{1,0:T(8,128)(2,1)} %up.1, bf16[128,512]{1,0:T(8,128)(2,1)} %down.1, ...), custom_call_target="tpu_custom_call" | custom-call | bytes 1048576 | tf_op jit(solution)/shard_map/pack/pallas_call | solution.py:174
  9.1 5.1 %collective-permute-start.11 = (bf16[32,2176]{1,0:T(8,128)(2,1)}, bf16[32,2176]{1,0:T(8,128)(2,1)S(1)}, u32[]{:S(2)}, u32[]{:S(2)}) collective-permute-start(bf16[32,2176]{1,0:T(8,128)(2,1)} %get-tuple-element.62.refs_0_), channel_id=1, source_target_pairs={{0,24},{2,26},{4,28},{6,30},{8,16},{10,18},{12,20},{14,22},{16,8},... | collective-permute-start | bytes 417800 | tf_op jit(solution)/shard_map/ppermute | solution.py:745
  16.5 2.5 %collective-permute-done.11.refs_12_ = bf16[32,2176]{1,0:T(8,128)(2,1)S(1)} collective-permute-done((bf16[32,2176]{1,0:T(8,128)(2,1)}, bf16[32,2176]{1,0:T(8,128)(2,1)S(1)}, u32[]{:S(2)}, u32[]{:S(2)}) %collective-permute-start.11) | collective-permute-done | bytes 139296 | tf_op jit(solution)/shard_map/ppermute | solution.py:745
  20.8 9.7 %collective-permute-done.7.refs_8_ = bf16[32,2176]{1,0:T(8,128)(2,1)S(1)} collective-permute-done((bf16[32,2176]{1,0:T(8,128)(2,1)}, bf16[32,2176]{1,0:T(8,128)(2,1)S(1)}, u32[]{:S(2)}, u32[]{:S(2)}) %collective-permute-start.7) | collective-permute-done | bytes 139296 | tf_op jit(solution)/shard_map/ppermute | solution.py:745
  30.5 1.8 %collective-permute-start.9 = (bf16[32,2176]{1,0:T(8,128)(2,1)S(1)}, bf16[32,2176]{1,0:T(8,128)(2,1)S(1)}, u32[]{:S(2)}, u32[]{:S(2)}) collective-permute-start(bf16[32,2176]{1,0:T(8,128)(2,1)S(1)} %collective-permute-done.7.refs_8_), channel_id=1, source_target_pairs={{0,4},{2,6},{4,0},{6,2},{8,12},{10,14},{12,8},{14,10},{16,20},{18,... | collective-permute-start | bytes 417800 | tf_op jit(solution)/shard_map/ppermute | solution.py:745
  33.4 3.6 %collective-permute-done.9.refs_10_ = bf16[32,2176]{1,0:T(8,128)(2,1)S(1)} collective-permute-done((bf16[32,2176]{1,0:T(8,128)(2,1)S(1)}, bf16[32,2176]{1,0:T(8,128)(2,1)S(1)}, u32[]{:S(2)}, u32[]{:S(2)}) %collective-permute-start.9) | collective-permute-done | bytes 139296 | tf_op jit(solution)/shard_map/ppermute | solution.py:745
  37.6 2.0 %collective-permute-done.5.refs_6_ = bf16[32,2176]{1,0:T(8,128)(2,1)S(1)} collective-permute-done((bf16[32,2176]{1,0:T(8,128)(2,1)S(1)}, bf16[32,2176]{1,0:T(8,128)(2,1)S(1)}, u32[]{:S(2)}, u32[]{:S(2)}) %collective-permute-start.5) | collective-permute-done | bytes 139296 | tf_op jit(solution)/shard_map/ppermute | solution.py:745
  41.6 7.6 %project.1 = (bf16[1024,512]{1,0:T(8,128)(2,1)}, bf16[1024,2048]{1,0:T(8,128)(2,1)}, bf16[2,144,256]{2,1,0:T(8,128)(2,1)}, bf16[512,2048]{1,0:T(8,128)(2,1)}, f32[8,512]{1,0:T(8,128)}) custom-call(s32[1]{0:T(128)} %bitcast.me_ref, bf16[1024,512]{1,0:T(8,128)(2,1)} %tok_ref.1, bf16[32,2176]{1,0:T(8,128)(2,1)} %get-tuple-element.62.refs_0_, ...), custom_call_target="tpu_custom_call" | custom-call | flops 2147483648 | bytes 12582912 | tf_op jit(solution)/shard_map/project/pallas_call | solution.py:264
  49.2 3.8 %collective-permute-start.15 = (bf16[2,144,256]{2,1,0:T(8,128)(2,1)}, bf16[2,144,256]{2,1,0:T(8,128)(2,1)S(1)}, u32[]{:S(2)}, u32[]{:S(2)}) collective-permute-start(bf16[2,144,256]{2,1,0:T(8,128)(2,1)} %get-tuple-element.64), channel_id=1, source_target_pairs={{0,1},{2,3},{4,5},{6,7},{8,9},{10,11},{12,13},{14,15},{16,17},{18,... | collective-permute-start | bytes 442376 | tf_op jit(solution)/shard_map/ppermute | solution.py:765
  53.0 3.7 %collective-permute-done.15.st_in = bf16[2,144,256]{2,1,0:T(8,128)(2,1)S(1)} collective-permute-done((bf16[2,144,256]{2,1,0:T(8,128)(2,1)}, bf16[2,144,256]{2,1,0:T(8,128)(2,1)S(1)}, u32[]{:S(2)}, u32[]{:S(2)}) %collective-permute-start.15) | collective-permute-done | bytes 147488 | tf_op jit(solution)/shard_map/ppermute | solution.py:765
  57.4 10.3 %mix.1 = (bf16[1024,512]{1,0:T(8,128)(2,1)}, f32[1024,512]{1,0:T(8,128)}, f32[1024,512]{1,0:T(8,128)}, f32[1024,512]{1,0:T(8,128)}, bf16[8,2,256,256]{3,2,1,0:T(8,128)(2,1)}, /*index=5*/bf16[8,2,256,256]{3,2,1,0:T(8,128)(2,1)}) custom-call(bf16[1024,2048]{1,0:T(8,128)(2,1)} %get-tuple-element.63.pack_ref, bf16[2,144,256]{2,1,0:T(8,128)(2,1)} %copy-done.8), custom_call_target="tpu_custom_call" | custom-call | flops 6000000000 | bytes 16777216 | tf_op jit(solution)/shard_map/mix/pallas_call | solution.py:347
  68.6 21.3 %ffn.1 = (f32[1024,512]{1,0:T(8,128)}, f32[1024,512]{1,0:T(8,128)}, bf16[1024,512]{1,0:T(8,128)(2,1)}, bf16[1024,2048]{1,0:T(8,128)(2,1)}, bf16[2048,512]{1,0:T(...) custom-call(s32[1]{0:T(128)} %bitcast.me_ref, ...), custom_call_target="tpu_custom_call" | custom-call | flops 11811160064 | bytes 20971520 | tf_op jit(solution)/shard_map/ffn/pallas_call | solution.py:495
  90.5 1.7 collective-permute-done.16
  94.1 10.3 %read_back.1 = (bf16[1024,512]{1,0:T(8,128)(2,1)}, bf16[1024,512]{1,0:T(8,128)(2,1)}, bf16[1024,512]{1,0:T(8,128)(2,1)}, f32[1024,512]{1,0:T(8,128)}, bf16[2,144,256]{2,1,0:T(8,128)(2,1)}) custom-call(bf16[1024,2048]{1,0:T(8,128)(2,1)} %get-tuple-element.63.pack_ref, bf16[1024,512]{1,0:T(8,128)(2,1)} %get-tuple-element.71.gmix_ref, ...), custom_call_target="tpu_custom_call" | custom-call | flops 6000000000 | bytes 20971520 | tf_op jit(solution)/shard_map/read_back/pallas_call | solution.py:602
  105.8 3.6 %collective-permute-done.19 = bf16[2,32,4736]{2,1,0:T(8,128)(2,1)} collective-permute-done((bf16[2,32,4736]{2,1,0:T(8,128)(2,1)S(1)}, bf16[2,32,4736]{2,1,0:T(8,128)(2,1)}, u32[]{:S(2)}, u32[]{:S(2)}) %collective-permute-start.19) | collective-permute-done | bytes 606240 | tf_op jit(solution)/shard_map/ppermute | solution.py:745
  109.4 2.1 %fusion.1 = (bf16[32,4736]{1,0:T(8,128)(2,1)}, bf16[32,4736]{1,0:T(8,128)(2,1)}) fusion(bf16[2,32,4736]{2,1,0:T(8,128)(2,1)} %collective-permute-done.19, bf16[6,32,4736]{2,1,0:T(8,128)(2,1)S(1)} %collective-permute-done.18, bf16[4,32,4736]{2,1,0:T(8,128)(2,1)S(1)} %copy-done), kind=kLoop, calls=%fused_computation.11 | loop fusion | flops 1818624 | bytes 2424832 | tf_op jit(solution)/shard_map/convert_element_type | solution.py:753
  111.6 3.6 %collective-permute-start.22 = (bf16[32,4736]{1,0:T(8,128)(2,1)}, bf16[32,4736]{1,0:T(8,128)(2,1)}, u32[]{:S(2)}, u32[]{:S(2)}) collective-permute-start(bf16[32,4736]{1,0:T(8,128)(2,1)} %get-tuple-element.113), channel_id=1, source_target_pairs={{0,24},{2,26},{4,28},{6,30},{8,16},{10,18},{12,20},{14,22},{16,8},... | collective-permute-start | bytes 909320 | tf_op jit(solution)/shard_map/ppermute | solution.py:745
  117.7 15.6 %write_back.1 = (bf16[1024,1536]{1,0:T(8,128)(2,1)}, bf16[4,32,2048]{2,1,0:T(8,128)(2,1)}, bf16[2,32,2048]{2,1,0:T(8,128)(2,1)}, bf16[2,32,2048]{2,1,0:T(8,128)(...) custom-call(s32[1]{0:T(128)} %bitcast.me_ref, bf16[1024,2048]{1,0:T(8,128)(2,1)} %get-tuple-element.63.pack_ref, ...), custom_call_target="tpu_custom_call" | custom-call | flops 11000000512 | bytes 18874368 | tf_op jit(solution)/shard_map/write_back/pallas_call | solution.py:697
  133.9 2.0 %fusion.3 = (bf16[32,4736]{1,0:T(8,128)(2,1)}, bf16[32,4736]{1,0:T(8,128)(2,1)S(1)}) fusion(bf16[2,32,4736]{2,1,0:T(8,128)(2,1)} %collective-permute-done.21, bf16[6,32,4736]{2,1,0:T(8,128)(2,1)S(1)} %collective-permute-done.18, bf16[4,32,4736]{2,1,0:T(8,128)(2,1)S(1)} %copy-done), kind=kLoop, calls=%fused_computation.13 | loop fusion | flops 1818624 | bytes 2424832 | tf_op jit(solution)/shard_map/convert_element_type | solution.py:753
  138.8 5.9 %ffn_out.1 = bf16[1024,512]{1,0:T(8,128)(2,1)} custom-call(bf16[1024,2048]{1,0:T(8,128)(2,1)} %get-tuple-element.93.hid_ref, f32[1024,512]{1,0:T(8,128)} %get-tuple-element.94.kept_ref, bf16[2048,512]{1,0:T(8,128)(2,1)} %get-tuple-element.95.down_ref), custom_call_target="tpu_custom_call" | custom-call | flops 2147483648 | bytes 9437184 | tf_op jit(solution)/shard_map/ffn_out/pallas_call | solution.py:537
  145.9 3.9 %collective-permute-start.29 = (bf16[32,2048]{1,0:T(8,128)(2,1)S(1)}, bf16[32,2048]{1,0:T(8,128)(2,1)S(1)}, u32[]{:S(2)}, u32[]{:S(2)}) collective-permute-start(bf16[32,2048]{1,0:T(8,128)(2,1)S(1)} %get-tuple-element.117), channel_id=1, source_target_pairs={{0,24},{2,26},{4,28},{6,30},{8,16},{10,18},{12,20},{14,22},{16,8},... | collective-permute-start | bytes 393224 | tf_op jit(solution)/shard_map/ppermute | solution.py:745
  151.1 2.5 %collective-permute-start.32 = (bf16[32,4736]{1,0:T(8,128)(2,1)S(1)}, bf16[32,4736]{1,0:T(8,128)(2,1)S(1)}, u32[]{:S(2)}, u32[]{:S(2)}) collective-permute-start(bf16[32,4736]{1,0:T(8,128)(2,1)S(1)} %add_convert_fusion.3), channel_id=1, source_target_pairs={{0,1},{1,0},{2,3},{3,2},{4,5},{5,4},{6,7},{7,6},{8,9},{9,8},{10,11... | collective-permute-start | bytes 909320 | tf_op jit(solution)/shard_map/ppermute | solution.py:817
  154.3 7.5 %input_grad.1 = f32[1024,512]{1,0:T(8,128)} custom-call(f32[8,512]{1,0:T(8,128)} %get-tuple-element.96.gain_ref, bf16[1024,512]{1,0:T(8,128)(2,1)} %tok_ref.1, bf16[1024,512]{1,0:T(8,128)(2,1)} %get-tuple-element.104.gq_hbm.gq_ref, bf16[1024,1536]{1,0:T(8,128)(2,1)} %get-tuple-element.89.gkvc_ref, bf16[512,2048]{1,0:T(8,128)(2,1)} %get-tuple-element.105.w_ref, ...), custom_call_target="tpu_custom_call" | custom-call | flops 2147483648 | bytes 12582912 | tf_op jit(solution)/shard_map/input_grad/pallas_call | solution.py:732
  165.3 1.7 collective-permute-done.31
  (120 shorter events, 27.1 us)
Async XLA Ops:
  7.2 61.5 %all-gather.2.cloned.1.call-start = ((), (), s32[]{:S(2)}) async-start(), calls=%async_computation | async-start | bytes 5152768 | tf_op jit(solution)/shard_map/all_gather | solution.py:790
  9.1 9.9 %collective-permute-start.11 = (bf16[32,2176]{1,0:T(8,128)(2,1)}, bf16[32,2176]{1,0:T(8,128)(2,1)S(1)}, u32[]{:S(2)}, u32[]{:S(2)}) collective-permute-start(bf16[32,2176]{1,0:T(8,128)(2,1)} %get-tuple-element.62.refs_0_), channel_id=1, source_target_pairs={{0,24},{2,26},{4,28},{6,30},{8,16},{10,18},{12,20},{14,22},{16,8},... | collective-permute-start | bytes 417800 | tf_op jit(solution)/shard_map/ppermute | solution.py:745
  14.2 16.2 %collective-permute-start.7 = (bf16[32,2176]{1,0:T(8,128)(2,1)}, bf16[32,2176]{1,0:T(8,128)(2,1)S(1)}, u32[]{:S(2)}, u32[]{:S(2)}) collective-permute-start(bf16[32,2176]{1,0:T(8,128)(2,1)} %get-tuple-element.62.refs_0_), channel_id=1, source_target_pairs={{0,16},{2,18},{4,20},{6,22},{8,24},{10,26},{12,28},{14,30},{16,0},... | collective-permute-start | bytes 417800 | tf_op jit(solution)/shard_map/ppermute | solution.py:745
  14.3 16.2 %collective-permute-start.3 = (bf16[32,2176]{1,0:T(8,128)(2,1)}, bf16[32,2176]{1,0:T(8,128)(2,1)S(1)}, u32[]{:S(2)}, u32[]{:S(2)}) collective-permute-start(bf16[32,2176]{1,0:T(8,128)(2,1)} %get-tuple-element.62.refs_0_), channel_id=1, source_target_pairs={{0,8},{2,10},{4,12},{6,14},{8,0},{10,2},{12,4},{14,6},{16,24},{18,... | collective-permute-start | bytes 417800 | tf_op jit(solution)/shard_map/ppermute | solution.py:745
  14.9 17.5 %collective-permute-start.1 = (bf16[32,2176]{1,0:T(8,128)(2,1)}, bf16[32,2176]{1,0:T(8,128)(2,1)S(1)}, u32[]{:S(2)}, u32[]{:S(2)}) collective-permute-start(bf16[32,2176]{1,0:T(8,128)(2,1)} %get-tuple-element.62.refs_0_), channel_id=1, source_target_pairs={{0,4},{2,6},{4,0},{6,2},{8,12},{10,14},{12,8},{14,10},{16,20},{18,... | collective-permute-start | bytes 417800 | tf_op jit(solution)/shard_map/ppermute | solution.py:745
  16.5 16.0 %collective-permute-start = (bf16[32,2176]{1,0:T(8,128)(2,1)}, bf16[32,2176]{1,0:T(8,128)(2,1)S(1)}, u32[]{:S(2)}, u32[]{:S(2)}) collective-permute-start(bf16[32,2176]{1,0:T(8,128)(2,1)} %get-tuple-element.62.refs_0_), channel_id=1, source_target_pairs={{0,2},{2,0},{4,6},{6,4},{8,10},{10,8},{12,14},{14,12},{16,18},{18,... | collective-permute-start | bytes 417800 | tf_op jit(solution)/shard_map/ppermute | solution.py:745
  19.1 13.8 %collective-permute-start.13 = (bf16[32,2176]{1,0:T(8,128)(2,1)S(1)}, bf16[32,2176]{1,0:T(8,128)(2,1)S(1)}, u32[]{:S(2)}, u32[]{:S(2)}) collective-permute-start(bf16[32,2176]{1,0:T(8,128)(2,1)S(1)} %collective-permute-done.11.refs_12_), channel_id=1, source_target_pairs={{0,4},{2,6},{4,0},{6,2},{8,12},{10,14},{12,8},{14,10},{16,20},{18,... | collective-permute-start | bytes 417800 | tf_op jit(solution)/shard_map/ppermute | solution.py:745
  32.5 7.1 %collective-permute-start.5 = (bf16[32,2176]{1,0:T(8,128)(2,1)S(1)}, bf16[32,2176]{1,0:T(8,128)(2,1)S(1)}, u32[]{:S(2)}, u32[]{:S(2)}) collective-permute-start(bf16[32,2176]{1,0:T(8,128)(2,1)S(1)} %collective-permute-done.3.refs_4_), channel_id=1, source_target_pairs={{0,4},{2,6},{4,0},{6,2},{8,12},{10,14},{12,8},{14,10},{16,20},{18,... | collective-permute-start | bytes 417800 | tf_op jit(solution)/shard_map/ppermute | solution.py:745
  32.9 6.7 %collective-permute-start.4 = (bf16[32,2176]{1,0:T(8,128)(2,1)S(1)}, bf16[32,2176]{1,0:T(8,128)(2,1)S(1)}, u32[]{:S(2)}, u32[]{:S(2)}) collective-permute-start(bf16[32,2176]{1,0:T(8,128)(2,1)S(1)} %collective-permute-done.3.refs_4_), channel_id=1, source_target_pairs={{0,2},{2,0},{4,6},{6,4},{8,10},{10,8},{12,14},{14,12},{16,18},{18,... | collective-permute-start | bytes 417800 | tf_op jit(solution)/shard_map/ppermute | solution.py:745
  33.0 6.7 %collective-permute-start.2 = (bf16[32,2176]{1,0:T(8,128)(2,1)S(1)}, bf16[32,2176]{1,0:T(8,128)(2,1)S(1)}, u32[]{:S(2)}, u32[]{:S(2)}) collective-permute-start(bf16[32,2176]{1,0:T(8,128)(2,1)S(1)} %collective-permute-done.1.refs_2_), channel_id=1, source_target_pairs={{0,2},{2,0},{4,6},{6,4},{8,10},{10,8},{12,14},{14,12},{16,18},{18,... | collective-permute-start | bytes 417800 | tf_op jit(solution)/shard_map/ppermute | solution.py:745
  49.2 7.5 %collective-permute-start.15 = (bf16[2,144,256]{2,1,0:T(8,128)(2,1)}, bf16[2,144,256]{2,1,0:T(8,128)(2,1)S(1)}, u32[]{:S(2)}, u32[]{:S(2)}) collective-permute-start(bf16[2,144,256]{2,1,0:T(8,128)(2,1)} %get-tuple-element.64), channel_id=1, source_target_pairs={{0,1},{2,3},{4,5},{6,7},{8,9},{10,11},{12,13},{14,15},{16,17},{18,... | collective-permute-start | bytes 442376 | tf_op jit(solution)/shard_map/ppermute | solution.py:765
  90.2 19.2 %collective-permute-start.18 = (bf16[6,32,4736]{2,1,0:T(8,128)(2,1)}, bf16[6,32,4736]{2,1,0:T(8,128)(2,1)S(1)}, u32[]{:S(2)}, u32[]{:S(2)}) collective-permute-start(bf16[6,32,4736]{2,1,0:T(8,128)(2,1)} %get-tuple-element.84), channel_id=1, source_target_pairs={{0,2},{2,0},{4,6},{6,4},{8,10},{10,8},{12,14},{14,12},{16,18},{18,... | collective-permute-start | bytes 5455880 | tf_op jit(solution)/shard_map/ppermute | solution.py:745
  93.4 16.0 %collective-permute-start.19 = (bf16[2,32,4736]{2,1,0:T(8,128)(2,1)S(1)}, bf16[2,32,4736]{2,1,0:T(8,128)(2,1)}, u32[]{:S(2)}, u32[]{:S(2)}) collective-permute-start(bf16[2,32,4736]{2,1,0:T(8,128)(2,1)S(1)} %add_convert_fusion.1), channel_id=1, source_target_pairs={{0,4},{2,6},{4,0},{6,2},{8,12},{10,14},{12,8},{14,10},{16,20},{18,... | collective-permute-start | bytes 1818632 | tf_op jit(solution)/shard_map/ppermute | solution.py:745
  104.4 10.8 %collective-permute-start.17 = (bf16[2,144,256]{2,1,0:T(8,128)(2,1)}, bf16[2,144,256]{2,1,0:T(8,128)(2,1)S(1)}, u32[]{:S(2)}, u32[]{:S(2)}) collective-permute-start(bf16[2,144,256]{2,1,0:T(8,128)(2,1)} %get-tuple-element.80), channel_id=1, source_target_pairs={{1,0},{3,2},{5,4},{7,6},{9,8},{11,10},{13,12},{15,14},{17,16},{19,... | collective-permute-start | bytes 442376 | tf_op jit(solution)/shard_map/ppermute | solution.py:765
  111.6 24.9 %collective-permute-start.22 = (bf16[32,4736]{1,0:T(8,128)(2,1)}, bf16[32,4736]{1,0:T(8,128)(2,1)}, u32[]{:S(2)}, u32[]{:S(2)}) collective-permute-start(bf16[32,4736]{1,0:T(8,128)(2,1)} %get-tuple-element.113), channel_id=1, source_target_pairs={{0,24},{2,26},{4,28},{6,30},{8,16},{10,18},{12,20},{14,22},{16,8},... | collective-permute-start | bytes 909320 | tf_op jit(solution)/shard_map/ppermute | solution.py:745
  115.1 34.7 %collective-permute-start.26 = (bf16[32,4736]{1,0:T(8,128)(2,1)}, bf16[32,4736]{1,0:T(8,128)(2,1)}, u32[]{:S(2)}, u32[]{:S(2)}) collective-permute-start(bf16[32,4736]{1,0:T(8,128)(2,1)} %get-tuple-element.114), channel_id=1, source_target_pairs={{0,16},{2,18},{4,20},{6,22},{8,24},{10,26},{12,28},{14,30},{16,0},... | collective-permute-start | bytes 909320 | tf_op jit(solution)/shard_map/ppermute | solution.py:745
  116.1 17.8 %collective-permute-start.21 = (bf16[2,32,4736]{2,1,0:T(8,128)(2,1)}, bf16[2,32,4736]{2,1,0:T(8,128)(2,1)}, u32[]{:S(2)}, u32[]{:S(2)}) collective-permute-start(bf16[2,32,4736]{2,1,0:T(8,128)(2,1)} %add_convert_fusion), channel_id=1, source_target_pairs={{0,4},{2,6},{4,0},{6,2},{8,12},{10,14},{12,8},{14,10},{16,20},{18,... | collective-permute-start | bytes 1818632 | tf_op jit(solution)/shard_map/ppermute | solution.py:745
  135.9 13.9 %collective-permute-start.27 = (bf16[32,4736]{1,0:T(8,128)(2,1)}, bf16[32,4736]{1,0:T(8,128)(2,1)S(1)}, u32[]{:S(2)}, u32[]{:S(2)}) collective-permute-start(bf16[32,4736]{1,0:T(8,128)(2,1)} %get-tuple-element.111), channel_id=1, source_target_pairs={{0,8},{2,10},{4,12},{6,14},{8,0},{10,2},{12,4},{14,6},{16,24},{18,... | collective-permute-start | bytes 909320 | tf_op jit(solution)/shard_map/ppermute | solution.py:745
  136.6 9.3 %collective-permute-start.24 = (bf16[2,32,2048]{2,1,0:T(8,128)(2,1)S(1)}, bf16[2,32,2048]{2,1,0:T(8,128)(2,1)S(1)}, u32[]{:S(2)}, u32[]{:S(2)}) collective-permute-start(bf16[2,32,2048]{2,1,0:T(8,128)(2,1)S(1)} %add_convert_fusion.8), channel_id=1, source_target_pairs={{0,4},{2,6},{4,0},{6,2},{8,12},{10,14},{12,8},{14,10},{16,20},{18,... | collective-permute-start | bytes 786440 | tf_op jit(solution)/shard_map/ppermute | solution.py:745
  137.4 16.1 %collective-permute-start.25 = (bf16[2,32,2048]{2,1,0:T(8,128)(2,1)S(1)}, bf16[2,32,2048]{2,1,0:T(8,128)(2,1)S(1)}, u32[]{:S(2)}, u32[]{:S(2)}) collective-permute-start(bf16[2,32,2048]{2,1,0:T(8,128)(2,1)S(1)} %add_convert_fusion.9), channel_id=1, source_target_pairs={{0,4},{2,6},{4,0},{6,2},{8,12},{10,14},{12,8},{14,10},{16,20},{18,... | collective-permute-start | bytes 786440 | tf_op jit(solution)/shard_map/ppermute | solution.py:745
  145.9 15.9 %collective-permute-start.29 = (bf16[32,2048]{1,0:T(8,128)(2,1)S(1)}, bf16[32,2048]{1,0:T(8,128)(2,1)S(1)}, u32[]{:S(2)}, u32[]{:S(2)}) collective-permute-start(bf16[32,2048]{1,0:T(8,128)(2,1)S(1)} %get-tuple-element.117), channel_id=1, source_target_pairs={{0,24},{2,26},{4,28},{6,30},{8,16},{10,18},{12,20},{14,22},{16,8},... | collective-permute-start | bytes 393224 | tf_op jit(solution)/shard_map/ppermute | solution.py:745
  149.8 12.1 %collective-permute-start.28 = (bf16[32,2048]{1,0:T(8,128)(2,1)S(1)}, bf16[32,2048]{1,0:T(8,128)(2,1)S(1)}, u32[]{:S(2)}, u32[]{:S(2)}) collective-permute-start(bf16[32,2048]{1,0:T(8,128)(2,1)S(1)} %get-tuple-element.118), channel_id=1, source_target_pairs={{0,16},{2,18},{4,20},{6,22},{8,24},{10,26},{12,28},{14,30},{16,0},... | collective-permute-start | bytes 393224 | tf_op jit(solution)/shard_map/ppermute | solution.py:745
  151.1 11.0 %collective-permute-start.32 = (bf16[32,4736]{1,0:T(8,128)(2,1)S(1)}, bf16[32,4736]{1,0:T(8,128)(2,1)S(1)}, u32[]{:S(2)}, u32[]{:S(2)}) collective-permute-start(bf16[32,4736]{1,0:T(8,128)(2,1)S(1)} %add_convert_fusion.3), channel_id=1, source_target_pairs={{0,1},{1,0},{2,3},{3,2},{4,5},{5,4},{6,7},{7,6},{8,9},{9,8},{10,11... | collective-permute-start | bytes 909320 | tf_op jit(solution)/shard_map/ppermute | solution.py:817
  153.6 8.3 %collective-permute-start.30 = (bf16[32,2048]{1,0:T(8,128)(2,1)S(1)}, bf16[32,2048]{1,0:T(8,128)(2,1)S(1)}, u32[]{:S(2)}, u32[]{:S(2)}) collective-permute-start(bf16[32,2048]{1,0:T(8,128)(2,1)S(1)} %get-tuple-element.115), channel_id=1, source_target_pairs={{0,8},{2,10},{4,12},{6,14},{8,0},{10,2},{12,4},{14,6},{16,24},{18,... | collective-permute-start | bytes 393224 | tf_op jit(solution)/shard_map/ppermute | solution.py:745
  (34 other events, 180.5 us)
Sparse Core Ops, SparseCore 0:
  10.3 58.2 all-gather.1
